TPU v7x, 32 devices: a whole 2x2x4 slice. The times are simulated.
32 devices in a mesh: dp: 8 (over y, x, core), tensor: 4 (over z).
Axes of the slice: x: 2, y: 2, z: 4, core: 2. Of those that a mesh axis runs over, the one named last changes fastest.
Arguments:
- layer_input: bfloat16 [2048, 2048], P('dp'), may hold values from -20 to 20
- doc_ids: int32 [2048], P('dp'), may hold values from 0 to 2047, as said below
- expert_ids: int32 [2048, 4], P('dp'), may hold values from 0 to 7, all different within a row; in each aligned block of 256 rows (0 to 255, 256 to 511, ...) at most 192 rows name the same one
- route_weights: float32 [2048, 4], P('dp'), may hold values from 0.05 to 0.6
- attn_gain: bfloat16 [2048], replicated, may hold values from 0.5 to 1.5
- qkv_weight: bfloat16 [2048, 6144], P(None, 'tensor'), may hold values from -0.125 to 0.125
- qkv_bias: bfloat16 [16, 384], P('tensor'), may hold values from -2 to 2
- out_weight: bfloat16 [2048, 2048], P('tensor'), may hold values from -0.5 to 0.5
- mlp_gain: bfloat16 [2048], replicated, may hold values from 0.5 to 1.5
- expert_gate_up: bfloat16 [8, 2048, 2, 1408], P(None, None, None, 'tensor'), may hold values from -0.125 to 0.125
- expert_down: bfloat16 [8, 1408, 2048], P(None, 'tensor'), may hold values from -0.15625 to 0.15625
- shared_gate_up: bfloat16 [2048, 2, 5632], P(None, None, 'tensor'), may hold values from -0.125 to 0.125
- shared_down: bfloat16 [5632, 2048], P('tensor'), may hold values from -0.078125 to 0.078125
- shared_gate: bfloat16 [2048], replicated, may hold values from -0.125 to 0.125
- cotangent: bfloat16 [2048, 2048], P('dp'), may hold values from -6 to 6
Outputs:
- layer_output: bfloat16 [2048, 2048], P('dp')
- input_grad: bfloat16 [2048, 2048], P('dp')
- attn_gain_grad: float32 [2048], P('dp')
- qkv_weight_grad: float32 [2048, 6144], P('dp', 'tensor')
- qkv_bias_grad: float32 [16, 384], P('tensor', 'dp')
- out_weight_grad: float32 [2048, 2048], P('tensor', 'dp')
- mlp_gain_grad: float32 [2048], P('dp')
- expert_gate_up_grad: float32 [8, 2048, 2, 1408], P(None, 'dp', None, 'tensor')
- expert_down_grad: float32 [8, 1408, 2048], P(None, 'tensor', 'dp')
- shared_gate_up_grad: float32 [2048, 2, 5632], P('dp', None, 'tensor')
- shared_down_grad: float32 [5632, 2048], P('tensor', 'dp')
- shared_gate_grad: float32 [2048], P('dp')
Inputs may be any that keep to these rules, and one draw needn't show every extreme that they name: `doc_ids`: never falling; a sequence's label is the index of its first token; every block of 256 tokens (one index of dp) begins a new sequence, so no sequence crosses blocks; a sequence has 1 to 256 tokens, one has exactly 256, and the last token forms a sequence of its own. `expert_ids`: each row names 4 different experts; within the rows of one device no expert is named by more than 192 rows, a bound that some block reaches.
All inputs are finite; a program needn't handle non-finite values.
Results may differ from a plain program's by a relative error of at most 0.015.
Values sent between devices are 32-bit elements; how exact they have to be, the bound alone decides.
No kernel may reach another device: no remote copies, remote signals or barrier semaphores. Data moves between devices by JAX's collectives and lax.ppermute only.
A program may use at most 384 MiB of HBM per device.

v0:
```python
import jax
import jax.numpy as jnp
from jax import lax
from jax.sharding import PartitionSpec as P

EPS = 1e-06
ROPE_BASE = 1000000.0
NEG = -1e30


def rms_norm(values_in, gain_vec):
    factor = lax.rsqrt(jnp.mean(values_in * values_in, axis=-1, keepdims=True) + EPS)
    return (values_in * factor * gain_vec, factor)


def norm_back(values_in, factor, gain_vec, upstream):
    scaled = gain_vec * upstream
    inner = jnp.mean(scaled * values_in, axis=-1, keepdims=True)
    return factor * scaled - values_in * factor**3 * inner


def rope_tables(doc_ids, head_dim):
    count = doc_ids.shape[0]
    index = jnp.arange(count, dtype=jnp.int32)
    begins = jnp.concatenate([jnp.ones((1,), dtype=bool), doc_ids[1:] != doc_ids[:-1]])
    first = lax.cummax(jnp.where(begins, index, jnp.zeros_like(index)), axis=0)
    place = (index - first).astype(jnp.float32)
    freq = ROPE_BASE ** (-(jnp.arange(head_dim // 2, dtype=jnp.float32) * 2.0 / head_dim))
    angle = place[:, None] * freq[None, :]
    cosine = jnp.concatenate([jnp.cos(angle), jnp.cos(angle)], axis=-1)
    sine = jnp.concatenate([jnp.sin(angle), jnp.sin(angle)], axis=-1)
    return (cosine, sine)


def rotate_half(values_in):
    middle = values_in.shape[-1] // 2
    return jnp.concatenate([-values_in[..., middle:], values_in[..., :middle]], axis=-1)


def rotary_apply(values_in, cosine, sine):
    return values_in * cosine[:, None, :] + rotate_half(values_in) * sine[:, None, :]


def rotary_back(upstream, cosine, sine):
    return upstream * cosine[:, None, :] - rotate_half(upstream * sine[:, None, :])


def silu_back(gate_part, up_part, upstream):
    sigma = jax.nn.sigmoid(gate_part)
    gate_grad = upstream * up_part * sigma * (1.0 + gate_part * (1.0 - sigma))
    up_grad = upstream * gate_part * sigma
    return jnp.stack([gate_grad, up_grad], axis=1).astype(jnp.bfloat16)


def inner_rows(left, right):
    return lax.dot_general(
        left, right, (((0,), (0,)), ((), ())), preferred_element_type=jnp.float32
    )


def inner_cols(left, right):
    return lax.dot_general(
        left, right, (((1,), (1,)), ((), ())), preferred_element_type=jnp.float32
    )


def shards(
    layer_input,
    doc_ids,
    expert_ids,
    route_weights,
    attn_gain,
    qkv_weight,
    qkv_bias,
    out_weight,
    mlp_gain,
    expert_gate_up,
    expert_down,
    shared_gate_up,
    shared_down,
    shared_gate,
    cotangent,
):
    count = layer_input.shape[0]
    heads_here = qkv_bias.shape[0]
    head_dim = qkv_bias.shape[1] // 3
    experts = expert_down.shape[0]
    routes_per = expert_ids.shape[1]
    capacity = count * routes_per * 3 // (2 * experts)
    scale = head_dim ** (-0.5)
    block_rows = min(512, count)
    inputs = layer_input.astype(jnp.float32)
    gain_one = attn_gain.astype(jnp.float32)
    gain_two = mlp_gain.astype(jnp.float32)
    normed_one, factor_one = rms_norm(inputs, gain_one)
    normed_one_low = normed_one.astype(jnp.bfloat16)
    projected = jnp.dot(
        normed_one_low, qkv_weight, preferred_element_type=jnp.float32
    ) + qkv_bias.reshape(-1).astype(jnp.float32)
    projected = projected.reshape(count, heads_here, 3, head_dim)
    cosine, sine = rope_tables(doc_ids, head_dim)
    query_low = rotary_apply(projected[:, :, 0], cosine, sine).astype(jnp.bfloat16)
    key_low = rotary_apply(projected[:, :, 1], cosine, sine).astype(jnp.bfloat16)
    value_low = projected[:, :, 2].astype(jnp.bfloat16)
    col_index = jnp.arange(count, dtype=jnp.int32)

    def block_scores(offset):
        row_index = offset + jnp.arange(block_rows, dtype=jnp.int32)
        allowed = (doc_ids[:, None] == doc_ids[None, :]) & (
            col_index[None, :] <= row_index[:, None]
        )
        scores = (
            jnp.einsum("qhd,khd->hqk", query_low, key_low, preferred_element_type=jnp.float32)
            * scale
        )
        return (jnp.where(allowed[None], scores, NEG), query_low)

    number = 0
    offset = number * block_rows
    scores, queries = block_scores(offset)
    row_peak = jnp.max(scores, axis=-1, keepdims=True)
    exponent = jnp.exp(scores - row_peak)
    row_mass = jnp.sum(exponent, axis=-1, keepdims=True)
    probs_low = (exponent / row_mass).astype(jnp.bfloat16)
    log_totals = [row_peak + jnp.log(row_mass)]
    outputs = jnp.einsum("hqk,khd->qhd", probs_low, value_low, preferred_element_type=jnp.float32)
    attended = outputs.astype(jnp.bfloat16).reshape(count, heads_here * head_dim)
    attn_part = jnp.dot(attended, out_weight, preferred_element_type=jnp.float32)
    attn_sum = lax.psum(attn_part, "tensor")
    residual = inputs + attn_sum
    normed_two, factor_two = rms_norm(residual, gain_two)
    normed_two_low = normed_two.astype(jnp.bfloat16)
    choose = expert_ids[:, :, None] == jnp.arange(experts, dtype=jnp.int32)[None, None, :]
    route = jnp.sum(route_weights[:, :, None] * choose.astype(jnp.float32), axis=1)
    unused = 1 - jnp.any(choose, axis=1).astype(jnp.int32).T
    slot_rows = jnp.argsort(unused, axis=1, stable=True)[:, :capacity]
    slot_weight = jnp.take_along_axis(route.T, slot_rows, axis=1)
    mixture = jnp.zeros((count, inputs.shape[1]), dtype=jnp.float32)
    kept_mix = []
    kept_act = []
    kept_rows = []
    for expert in range(experts):
        picked = slot_rows[expert]
        rows_in = normed_two_low[picked]
        mix_here = jnp.einsum(
            "td,dcf->tcf", rows_in, expert_gate_up[expert], preferred_element_type=jnp.float32
        )
        act_here = (jax.nn.silu(mix_here[:, 0]) * mix_here[:, 1]).astype(jnp.bfloat16)
        out_here = jnp.dot(act_here, expert_down[expert], preferred_element_type=jnp.float32)
        mixture = mixture.at[picked].add(slot_weight[expert][:, None] * out_here)
        kept_mix.append(mix_here)
        kept_act.append(act_here)
        kept_rows.append(rows_in)
    shared_mix = jnp.einsum(
        "td,dcf->tcf", normed_two_low, shared_gate_up, preferred_element_type=jnp.float32
    )
    shared_act = (jax.nn.silu(shared_mix[:, 0]) * shared_mix[:, 1]).astype(jnp.bfloat16)
    shared_out = jnp.dot(shared_act, shared_down, preferred_element_type=jnp.float32)
    gate_open = jax.nn.sigmoid(
        jnp.dot(normed_two_low, shared_gate, preferred_element_type=jnp.float32)
    )
    mlp_part = mixture + gate_open[:, None] * shared_out
    mlp_sum = lax.psum(mlp_part, "tensor")
    layer_output = (residual + mlp_sum).astype(jnp.bfloat16)
    upstream = cotangent.astype(jnp.float32)
    shared_branch = (gate_open[:, None] * upstream).astype(jnp.bfloat16)
    shared_down_grad = inner_rows(shared_act, shared_branch)
    shared_mix_grad = silu_back(
        shared_mix[:, 0], shared_mix[:, 1], inner_cols(shared_branch, shared_down)
    )
    shared_gate_up_grad = jnp.einsum(
        "td,tcf->dcf", normed_two_low, shared_mix_grad, preferred_element_type=jnp.float32
    )
    normed_two_grad = jnp.einsum(
        "tcf,dcf->td", shared_mix_grad, shared_gate_up, preferred_element_type=jnp.float32
    )
    logit_grad = gate_open * (1.0 - gate_open) * jnp.sum(upstream * shared_out, axis=-1)
    normed_two_grad = (
        normed_two_grad + logit_grad[:, None] * shared_gate.astype(jnp.float32)[None, :]
    )
    mix_grads = []
    down_grads = []
    for expert in range(experts):
        picked = slot_rows[expert]
        expert_branch = (
            slot_weight[expert][:, None] * cotangent[picked].astype(jnp.float32)
        ).astype(jnp.bfloat16)
        down_grads.append(inner_rows(kept_act[expert], expert_branch))
        mix_here = kept_mix[expert]
        expert_mix_grad = silu_back(
            mix_here[:, 0], mix_here[:, 1], inner_cols(expert_branch, expert_down[expert])
        )
        mix_grads.append(
            jnp.einsum(
                "td,tcf->dcf",
                kept_rows[expert],
                expert_mix_grad,
                preferred_element_type=jnp.float32,
            )
        )
        normed_two_grad = normed_two_grad.at[picked].add(
            jnp.einsum(
                "tcf,dcf->td",
                expert_mix_grad,
                expert_gate_up[expert],
                preferred_element_type=jnp.float32,
            )
        )
    expert_gate_up_grad = jnp.stack(mix_grads, axis=0)
    expert_down_grad = jnp.stack(down_grads, axis=0)
    normed_two_total, logit_total = lax.psum((normed_two_grad, logit_grad), "tensor")
    mlp_gain_grad = jnp.sum(normed_two_total * residual * factor_two, axis=0)
    shared_gate_grad = jnp.dot(
        logit_total, normed_two_low.astype(jnp.float32), precision=lax.Precision.HIGHEST
    )
    residual_grad = upstream + norm_back(residual, factor_two, gain_two, normed_two_total)
    branch_grad = residual_grad.astype(jnp.bfloat16)
    out_weight_grad = inner_rows(attended, branch_grad)
    attended_grad = (
        inner_cols(branch_grad, out_weight)
        .astype(jnp.bfloat16)
        .reshape(count, heads_here, head_dim)
    )
    number = 0
    offset = number * block_rows
    scores, queries = block_scores(offset)
    probs = jnp.exp(scores - log_totals[number])
    probs_low = probs.astype(jnp.bfloat16)
    prob_grad = jnp.einsum(
        "qhd,khd->hqk", attended_grad, value_low, preferred_element_type=jnp.float32
    )
    inner = jnp.sum(probs * prob_grad, axis=-1, keepdims=True)
    score_low = (probs * (prob_grad - inner) * scale).astype(jnp.bfloat16)
    query_grads = jnp.einsum("hqk,khd->qhd", score_low, key_low, preferred_element_type=jnp.float32)
    key_grad = jnp.einsum("hqk,qhd->khd", score_low, queries, preferred_element_type=jnp.float32)
    value_grad = jnp.einsum(
        "hqk,qhd->khd", probs_low, attended_grad, preferred_element_type=jnp.float32
    )
    query_round = lax.optimization_barrier(query_grads.astype(jnp.bfloat16)).astype(jnp.float32)
    key_round = lax.optimization_barrier(key_grad.astype(jnp.bfloat16)).astype(jnp.float32)
    projected_grad = jnp.stack(
        [rotary_back(query_round, cosine, sine), rotary_back(key_round, cosine, sine), value_grad],
        axis=2,
    )
    projected_grad = projected_grad.astype(jnp.bfloat16).reshape(count, heads_here * 3 * head_dim)
    qkv_bias_grad = jnp.sum(projected_grad, axis=0, dtype=jnp.float32).reshape(
        heads_here, 3 * head_dim
    )
    qkv_weight_grad = inner_rows(normed_one_low, projected_grad)
    normed_one_grad = inner_cols(projected_grad, qkv_weight)
    normed_one_total = lax.psum(normed_one_grad, "tensor")
    attn_gain_grad = jnp.sum(normed_one_total * inputs * factor_one, axis=0)
    input_grad = (residual_grad + norm_back(inputs, factor_one, gain_one, normed_one_total)).astype(
        jnp.bfloat16
    )
    summed = (
        lax.psum_scatter(attn_gain_grad, "dp", scatter_dimension=0, tiled=True),
        lax.psum_scatter(qkv_weight_grad, "dp", scatter_dimension=0, tiled=True),
        lax.psum_scatter(qkv_bias_grad, "dp", scatter_dimension=1, tiled=True),
        lax.psum_scatter(out_weight_grad, "dp", scatter_dimension=1, tiled=True),
        lax.psum_scatter(mlp_gain_grad, "dp", scatter_dimension=0, tiled=True),
        lax.psum_scatter(expert_gate_up_grad, "dp", scatter_dimension=1, tiled=True),
        lax.psum_scatter(expert_down_grad, "dp", scatter_dimension=2, tiled=True),
        lax.psum_scatter(shared_gate_up_grad, "dp", scatter_dimension=0, tiled=True),
        lax.psum_scatter(shared_down_grad, "dp", scatter_dimension=1, tiled=True),
        lax.psum_scatter(shared_gate_grad, "dp", scatter_dimension=0, tiled=True),
    )
    (
        attn_gain_grad,
        qkv_weight_grad,
        qkv_bias_grad,
        out_weight_grad,
        mlp_gain_grad,
        expert_gate_up_grad,
        expert_down_grad,
        shared_gate_up_grad,
        shared_down_grad,
        shared_gate_grad,
    ) = summed
    return (
        layer_output,
        input_grad,
        attn_gain_grad,
        qkv_weight_grad,
        qkv_bias_grad,
        out_weight_grad,
        mlp_gain_grad,
        expert_gate_up_grad,
        expert_down_grad,
        shared_gate_up_grad,
        shared_down_grad,
        shared_gate_grad,
    )


def solution(mesh):
    placed = (
        P("dp", None),
        P("dp"),
        P("dp", None),
        P("dp", None),
        P(),
        P(None, "tensor"),
        P("tensor", None),
        P("tensor", None),
        P(),
        P(None, None, None, "tensor"),
        P(None, "tensor", None),
        P(None, None, "tensor"),
        P("tensor", None),
        P(),
        P("dp", None),
    )
    return jax.shard_map(
        shards,
        mesh=mesh,
        in_specs=placed,
        out_specs=(
            P("dp", None),
            P("dp", None),
            P("dp"),
            P("dp", "tensor"),
            P("tensor", "dp"),
            P("tensor", "dp"),
            P("dp"),
            P(None, "dp", None, "tensor"),
            P(None, "tensor", "dp"),
            P("dp", None, "tensor"),
            P("tensor", "dp"),
            P("dp"),
        ),
        check_vma=False,
    )
```

profile of v0, /device:TPU:0, one launch (start us, length us, event | category | flops | bytes accessed | tf_op | source)
XLA Modules:
  0.0 1243.8 jit_solution(14847507831882475313)
XLA Ops:
  16.0 6.1 convolution_add_fusion
  34.5 10.8 gather_fusion.16
  61.9 59.1 %all-reduce.9.cloned.1.call-done = f32[256,2048]{1,0:T(8,128)} async-done(((f32[256,2048]{1,0:T(8,128)}), f32[256,2048]{1,0:T(8,128)}) %all-reduce.9.cloned.1.call-update) | async-done | bytes 2097168 | tf_op jit(solution)/shard_map/psum | solution.py:129
  231.9 6.6 scatter_fusion.8
  238.6 6.6 scatter_fusion.9
  245.2 6.6 scatter_fusion.10
  251.9 6.6 scatter_fusion.11
  258.5 6.9 scatter_fusion.12
  265.4 6.6 scatter_fusion.13
  272.0 6.6 scatter_fusion.14
  278.7 6.6 scatter_fusion.15
  285.4 6.7 scatter_fusion
  295.2 7.1 scatter_fusion.1
  305.5 6.7 scatter_fusion.2
  315.3 6.7 scatter_fusion.3
  325.1 6.7 scatter_fusion.4
  335.0 6.9 scatter_fusion.5
  345.1 6.7 scatter_fusion.6
  354.9 6.7 scatter_fusion.7
  361.6 8.9 all-reduce.11.cloned.1.call-done
  392.7 5.9 fusion.401
  399.9 10.8 fusion.150
  416.5 7.4 fusion.196
  424.6 7.9 fusion.200
  487.6 11.4 psum.39
  500.9 52.2 %all-reduce.13.cloned.1.call-done = (f32[256,2048]{1,0:T(8,128)}, f32[256,2048]{1,0:T(8,128)}) async-done(((f32[256,2048]{1,0:T(8,128)}, f32[256,2048]{1,0:T(8,128)}), (f32[256,2048]{1,0:T(8,128)}, f32[256,2048]{1,0:T(8,128)})) %all-reduce.13.cloned.1.call-update) | async-done | bytes 4194320 | tf_op jit(solution)/shard_map/psum | solution.py:163
  555.5 24.7 %all-reduce.3 = (f32[2048]{0:T(1024)S(1)}, f32[2048]{0:T(1024)S(1)}, f32[2048]{0:T(1024)S(1)}) all-reduce(f32[2048]{0:T(1024)S(1)} %get-tuple-element.64, f32[2048]{0:T(1024)S(1)} %get-tuple-element.62, f32[2048]{0:T(1024)S(1)} %bitcast.790), channel_id=2, replica_groups=mesh['dp'=8,'tensor'=4] {'dp'}, use_global_device_ids=true, to_apply=%region_34.35.clone | all-reduce | flops 6144 | bytes 49152
  594.3 36.0 %reduce-scatter.12.cloned.1.call-done = f32[512,256]{1,0:T(8,128)} async-done(((f32[512,2048]{1,0:T(8,128)}), f32[512,256]{1,0:T(8,128)}) %reduce-scatter.12.cloned.1.call-update) | async-done | bytes 524304 | tf_op jit(solution)/shard_map/reduce_scatter | solution.py:260
  630.3 90.7 %reduce-scatter.20.cloned.1.call-done = f32[1408,256]{1,0:T(8,128)} async-done(((f32[1408,2048]{1,0:T(8,128)}), f32[1408,256]{1,0:T(8,128)}) %reduce-scatter.20.cloned.1.call-update) | async-done | bytes 1441808 | tf_op jit(solution)/shard_map/reduce_scatter | solution.py:265
  721.0 96.4 %reduce-scatter.10.cloned.1.call-done = f32[256,1536]{1,0:T(8,128)} async-done(((f32[2048,1536]{1,0:T(8,128)}), f32[256,1536]{1,0:T(8,128)}) %reduce-scatter.10.cloned.1.call-update) | async-done | bytes 1572880 | tf_op jit(solution)/shard_map/reduce_scatter | solution.py:258
  817.3 150.2 %reduce-scatter.16.cloned.1.call-done = f32[8,352,256]{2,1,0:T(8,128)} async-done(((f32[8,352,2048]{2,1,0:T(8,128)}), f32[8,352,256]{2,1,0:T(8,128)}) %reduce-scatter.16.cloned.1.call-update) | async-done | bytes 2883600 | tf_op jit(solution)/shard_map/reduce_scatter | solution.py:263
  967.5 268.5 %reduce-scatter.14.cloned.1.call-done = f32[8,256,2,352]{1,3,2,0:T(8,128)} async-done(((f32[8,2048,2,352]{1,3,2,0:T(8,128)}), f32[8,256,2,352]{1,3,2,0:T(8,128)}) %reduce-scatter.14.cloned.1.call-update) | async-done | bytes 5767184 | tf_op jit(solution)/shard_map/reduce_scatter | solution.py:262
  (490 shorter events, 270.9 us)
Async XLA Ops:
  8.0 22.1 %copy-start = (bf16[512,2048]{1,0:T(8,128)(2,1)S(1)}, bf16[512,2048]{1,0:T(8,128)(2,1)}, u32[]{:S(2)}) copy-start(bf16[512,2048]{1,0:T(8,128)(2,1)} %param.22) | copy-start | bytes 6291460
  8.0 25.7 %sort.19.cloned.1.call-start = ((), (), s32[]{:S(2)}) async-start(), calls=%async_computation.17 | async-start | bytes 49184 | tf_op jit(solution)/shard_map/jit(argsort)/sort | solution.py:136
  10.1 110.9 %all-reduce.9.cloned.1.call-start = ((), (), s32[]{:S(2)}) async-start(), calls=%async_computation.7 | async-start | bytes 4194304 | tf_op jit(solution)/shard_map/psum | solution.py:129
  32.2 338.2 %all-reduce.11.cloned.1.call-start = ((), (), s32[]{:S(2)}) async-start(), calls=%async_computation.8 | async-start | bytes 4194304 | tf_op jit(solution)/shard_map/psum | solution.py:211
  32.9 90.9 %copy-start.112 = (f32[2048]{0:T(1024)}, f32[2048]{0:T(1024)S(1)}, u32[]{:S(2)}) copy-start(f32[2048]{0:T(1024)S(1)} %convert_element_type.251) | copy-start | bytes 24580
  61.8 108.6 %copy-start.142 = (f32[1,192]{1,0:T(1,128)}, f32[1,192]{1,0:T(1,128)S(1)}, u32[]{:S(2)}) copy-start(f32[1,192]{1,0:T(1,128)S(1)} %get-tuple-element.118) | copy-start | bytes 2308
  61.9 230.2 %copy-start.135 = (f32[1,192]{1,0:T(1,128)}, f32[1,192]{1,0:T(1,128)S(1)}, u32[]{:S(2)}) copy-start(f32[1,192]{1,0:T(1,128)S(1)} %get-tuple-element.117) | copy-start | bytes 2308
  61.9 240.5 %copy-start.133 = (f32[1,192]{1,0:T(1,128)}, f32[1,192]{1,0:T(1,128)S(1)}, u32[]{:S(2)}) copy-start(f32[1,192]{1,0:T(1,128)S(1)} %get-tuple-element.116) | copy-start | bytes 2308
  61.9 250.3 %copy-start.131 = (f32[1,192]{1,0:T(1,128)}, f32[1,192]{1,0:T(1,128)S(1)}, u32[]{:S(2)}) copy-start(f32[1,192]{1,0:T(1,128)S(1)} %get-tuple-element.115) | copy-start | bytes 2308
  61.9 260.1 %copy-start.129 = (f32[1,192]{1,0:T(1,128)}, f32[1,192]{1,0:T(1,128)S(1)}, u32[]{:S(2)}) copy-start(f32[1,192]{1,0:T(1,128)S(1)} %get-tuple-element.114) | copy-start | bytes 2308
  61.9 270.0 %copy-start.127 = (f32[1,192]{1,0:T(1,128)}, f32[1,192]{1,0:T(1,128)S(1)}, u32[]{:S(2)}) copy-start(f32[1,192]{1,0:T(1,128)S(1)} %get-tuple-element.113) | copy-start | bytes 2308
  61.9 280.1 %copy-start.125 = (f32[1,192]{1,0:T(1,128)}, f32[1,192]{1,0:T(1,128)S(1)}, u32[]{:S(2)}) copy-start(f32[1,192]{1,0:T(1,128)S(1)} %get-tuple-element.112) | copy-start | bytes 2308
  124.8 48.0 %copy-start.1 = (bf16[256,2048]{1,0:T(8,128)(2,1)}, bf16[256,2048]{1,0:T(8,128)(2,1)S(1)}, u32[]{:S(2)}) copy-start(bf16[256,2048]{1,0:T(8,128)(2,1)S(1)} %multiply_convert_fusion) | copy-start | bytes 3145732
  144.7 76.2 %copy-start.59 = (f32[192,2,352]{2,0,1:T(8,128)}, f32[192,2,352]{2,0,1:T(8,128)S(1)}, u32[]{:S(2)}) copy-start(f32[192,2,352]{2,0,1:T(8,128)S(1)} %fusion.15) | copy-start | bytes 1622020
  148.1 66.5 %copy-start.62 = (f32[192,2,352]{2,0,1:T(8,128)}, f32[192,2,352]{2,0,1:T(8,128)S(1)}, u32[]{:S(2)}) copy-start(f32[192,2,352]{2,0,1:T(8,128)S(1)} %fusion.19) | copy-start | bytes 1622020
  151.2 58.7 %copy-start.65 = (f32[192,2,352]{2,0,1:T(8,128)}, f32[192,2,352]{2,0,1:T(8,128)S(1)}, u32[]{:S(2)}) copy-start(f32[192,2,352]{2,0,1:T(8,128)S(1)} %fusion.23) | copy-start | bytes 1622020
  154.4 50.7 %copy-start.68 = (f32[192,2,352]{2,0,1:T(8,128)}, f32[192,2,352]{2,0,1:T(8,128)S(1)}, u32[]{:S(2)}) copy-start(f32[192,2,352]{2,0,1:T(8,128)S(1)} %fusion.27) | copy-start | bytes 1622020
  157.6 42.8 %copy-start.71 = (f32[192,2,352]{2,0,1:T(8,128)}, f32[192,2,352]{2,0,1:T(8,128)S(1)}, u32[]{:S(2)}) copy-start(f32[192,2,352]{2,0,1:T(8,128)S(1)} %fusion.31) | copy-start | bytes 1622020
  160.7 34.9 %copy-start.74 = (f32[192,2,352]{2,0,1:T(8,128)}, f32[192,2,352]{2,0,1:T(8,128)S(1)}, u32[]{:S(2)}) copy-start(f32[192,2,352]{2,0,1:T(8,128)S(1)} %fusion.35) | copy-start | bytes 1622020
  163.9 27.0 %copy-start.77 = (f32[192,2,352]{2,0,1:T(8,128)}, f32[192,2,352]{2,0,1:T(8,128)S(1)}, u32[]{:S(2)}) copy-start(f32[192,2,352]{2,0,1:T(8,128)S(1)} %fusion.39) | copy-start | bytes 1622020
  179.4 47.7 %copy-start.139 = (f32[256]{0:T(256)}, f32[256]{0:T(256)S(1)}, u32[]{:S(2)}) copy-start(f32[256]{0:T(256)S(1)} %get-tuple-element.73) | copy-start | bytes 3076
  184.9 42.2 %copy-start.55 = (bf16[256,1,1408]{2,0,1:T(8,128)(2,1)}, bf16[256,1,1408]{2,0,1:T(8,128)(2,1)S(1)}, u32[]{:S(2)}) copy-start(bf16[256,1,1408]{2,0,1:T(8,128)(2,1)S(1)} %get-tuple-element.77) | copy-start | bytes 2162692
  184.9 42.2 %copy-start.56 = (bf16[256,1,1408]{2,0,1:T(8,128)(2,1)}, bf16[256,1,1408]{2,0,1:T(8,128)(2,1)S(1)}, u32[]{:S(2)}) copy-start(bf16[256,1,1408]{2,0,1:T(8,128)(2,1)S(1)} %get-tuple-element.78) | copy-start | bytes 2162692
  285.3 214.2 %reduce-scatter.22.cloned.1.call-start = ((), (), s32[]{:S(2)}) async-start(), calls=%async_computation.15 | async-start | bytes 221184
  354.9 15.5 %copy-start.121 = (f32[256]{0:T(256)S(1)}, f32[256]{0:T(256)}, u32[]{:S(2)}) copy-start(f32[256]{0:T(256)} %copy-done.120) | copy-start | bytes 3076
  391.5 161.6 %all-reduce.13.cloned.1.call-start = ((), (), s32[]{:S(2)}) async-start(), calls=%async_computation.16 | async-start | bytes 8388608 | tf_op jit(solution)/shard_map/psum | solution.py:163
  398.6 189.8 %reduce-scatter.18.cloned.1.call-start = ((), (), s32[]{:S(2)}) async-start(), calls=%async_computation.13 | async-start | bytes 25952256 | tf_op jit(solution)/shard_map/reduce_scatter | solution.py:264
  410.7 219.6 %reduce-scatter.12.cloned.1.call-start = ((), (), s32[]{:S(2)}) async-start(), calls=%async_computation.10 | async-start | bytes 4718592 | tf_op jit(solution)/shard_map/reduce_scatter | solution.py:260
  415.9 305.1 %reduce-scatter.20.cloned.1.call-start = ((), (), s32[]{:S(2)}) async-start(), calls=%async_computation.14 | async-start | bytes 12976128 | tf_op jit(solution)/shard_map/reduce_scatter | solution.py:265
  423.9 393.4 %reduce-scatter.10.cloned.1.call-start = ((), (), s32[]{:S(2)}) async-start(), calls=%async_computation.9 | async-start | bytes 14155776 | tf_op jit(solution)/shard_map/reduce_scatter | solution.py:258
  432.6 534.9 %reduce-scatter.16.cloned.1.call-start = ((), (), s32[]{:S(2)}) async-start(), calls=%async_computation.12 | async-start | bytes 25952256 | tf_op jit(solution)/shard_map/reduce_scatter | solution.py:263
  454.9 781.1 %reduce-scatter.14.cloned.1.call-start = ((), (), s32[]{:S(2)}) async-start(), calls=%async_computation.11 | async-start | bytes 51904512 | tf_op jit(solution)/shard_map/reduce_scatter | solution.py:262
  (136 other events, 569.7 us)
Sparse Core Ops, SparseCore 0:
  12.5 2.2 sort.21.cloned.1.call-done
  391.6 32.6 reduce-scatter.21
  428.3 146.2 reduce-scatter.17
  578.8 51.4 reduce-scatter.11
  634.2 86.7 reduce-scatter.19
  724.9 92.3 reduce-scatter.9
  821.5 145.9 reduce-scatter.15
  971.7 264.3 reduce-scatter.13
  (1 shorter events, 0.0 us)
Sparse Core Ops, SparseCore 1:
  32.3 88.6 all-reduce.8
  285.4 85.0 all-reduce.10
  398.7 154.3 all-reduce.12
where the time goes:
time: 1250 us; the launch traced here: 1240 us
  waiting for transfers between devices  762 us (61%)
  matrix products  217 us (17%)
  other arithmetic  136 us (11%)
  local copies, waits for them, and re-layouts  73.7 us (6%)
  blocking collectives  36.1 us (3%)
  between operations  18.3 us (1%)
    reduce_scatter x1, waiting for transfers between devices, shards(): lax.psum_scatter(expert_gate_up_grad, 'dp', scatter_dimension=1, tiled=True)  269 us
    reduce_scatter x1, waiting for transfers between devices, shards(): lax.psum_scatter(expert_down_grad, 'dp', scatter_dimension=2, tiled=True)  150 us
    reduce_scatter x1, waiting for transfers between devices, shards(): lax.psum_scatter(qkv_weight_grad, 'dp', scatter_dimension=0, tiled=True)  96.4 us
    reduce_scatter x1, waiting for transfers between devices, shards(): lax.psum_scatter(shared_down_grad, 'dp', scatter_dimension=1, tiled=True)  90.7 us
    psum x1, waiting for transfers between devices, shards(): attn_sum = lax.psum(attn_part, 'tensor')  59.1 us
    scatter-add x8, other arithmetic, shards(): mixture = mixture.at[picked].add(slot_weight[expert][:, None] * out_here)  54.3 us
    scatter-add x8, other arithmetic, shards(): normed_two_grad.at[picked]  53.4 us
    psum x1, waiting for transfers between devices, shards(): mlp_sum = lax.psum(mlp_part, 'tensor')  52.2 us
  transfers between devices with their start and end apart: 10, of which 8 were waited for; matrix products, arithmetic and copies ran while one was open for 17% of the time, Pallas kernels for 0%

commit v1 on v0

v1 whole, which is shorter than its diff:
```python
import functools

import jax
import jax.numpy as jnp
from jax import lax
from jax.experimental import pallas as pl
from jax.experimental.pallas import tpu as pltpu
from jax.sharding import PartitionSpec as P

EPS = 1e-06
ROPE_BASE = 1000000.0
NEG = -1e30
F32 = jnp.float32
BF16 = jnp.bfloat16
VMEM_LIMIT = 60 * 1024 * 1024


def nt(left, right):
    return lax.dot_general(left, right, (((1,), (1,)), ((), ())), preferred_element_type=F32)


def tn(left, right):
    return lax.dot_general(left, right, (((0,), (0,)), ((), ())), preferred_element_type=F32)


def nn(left, right):
    return jnp.dot(left, right, preferred_element_type=F32)


def rms_norm(values_in, gain_vec):
    factor = lax.rsqrt(jnp.mean(values_in * values_in, axis=-1, keepdims=True) + EPS)
    return (values_in * factor * gain_vec, factor)


def norm_back(values_in, factor, gain_vec, upstream):
    scaled = gain_vec * upstream
    inner = jnp.mean(scaled * values_in, axis=-1, keepdims=True)
    return factor * scaled - values_in * factor**3 * inner


def rotate_half(values_in):
    middle = values_in.shape[-1] // 2
    return jnp.concatenate([-values_in[..., middle:], values_in[..., :middle]], axis=-1)


def rotary_apply(values_in, cosine, sine):
    return values_in * cosine[:, None, :] + rotate_half(values_in) * sine[:, None, :]


def rotary_back(upstream, cosine, sine):
    return upstream * cosine[:, None, :] - rotate_half(upstream * sine[:, None, :])


def hidden(w_one, w_two, tokens, branch, route_row):
    units = w_two.shape[0]
    mix = nt(w_one, tokens)
    gate, up = mix[:units], mix[units:]
    back = nt(w_two, branch)
    sigma = 1.0 / (1.0 + jnp.exp(-gate))
    silu = gate * sigma
    act = silu * up
    scaled = back * route_row
    gate_grad = scaled * up * sigma * (1.0 + gate * (1.0 - sigma))
    mix_grad = jnp.concatenate([gate_grad.astype(BF16), (scaled * silu).astype(BF16)], axis=0)
    return act, back, (act * route_row).astype(BF16), mix_grad


def open_row(gate_rows, tokens):
    return 1.0 / (1.0 + jnp.exp(-nt(gate_rows, tokens)[:1]))


def own_kernel(experts, tok_ref, cot_ref, route_ref, gate_ref, w1e_ref, w1s_ref, w2e_ref, w2s_ref,
               out_ref, dx_ref, logit_ref, open_ref):
    step = pl.program_id(0)
    units, width = w2e_ref.shape[-2:]

    @pl.when(step == 0)
    def _():
        out_ref[...] = jnp.zeros_like(out_ref)
        dx_ref[...] = jnp.zeros_like(dx_ref)
        logit_ref[...] = jnp.zeros_like(logit_ref)
        open_ref[...] = open_row(gate_ref[...], tok_ref[...])

    def tile(w_one, w_two, route_row, shared):
        act, back, weighted, mix_grad = hidden(w_one, w_two, tok_ref[...], cot_ref[...], route_row)
        if shared:
            logit_ref[...] += jnp.sum(act * back, axis=0, keepdims=True)
        out_ref[...] += tn(weighted, w_two)
        dx_ref[...] += tn(mix_grad, w_one)

    @pl.when(step < experts)
    def _():
        tile(w1e_ref[...].reshape(2 * units, width), w2e_ref[0], route_ref[0], False)

    @pl.when(step >= experts)
    def _():
        tile(w1s_ref[...].reshape(2 * units, width), w2s_ref[0], open_ref[...], True)

    @pl.when(step == pl.num_programs(0) - 1)
    def _():
        opened = open_ref[...]
        logit = opened * (1.0 - opened) * logit_ref[...]
        logit_ref[...] = logit
        column = jnp.broadcast_to(logit, (8, logit.shape[1])).T[:, :1]
        dx_ref[...] += column * gate_ref[:1].astype(F32)


def own_mlp(tokens, cotangent, route, gate_rows, w1e, w1s, w2e, w2s):
    count, width = tokens.shape
    experts, units = w2e.shape[:2]
    shared = w2s.shape[0]
    last = experts - 1
    whole = lambda *shape: pl.BlockSpec(shape, lambda i: (0,) * len(shape))
    expert = lambda i: jnp.minimum(i, last)
    common = lambda i: jnp.maximum(i - experts, 0)
    return pl.pallas_call(
        functools.partial(own_kernel, experts),
        grid=(experts + shared,),
        in_specs=[
            whole(count, width),
            whole(count, width),
            pl.BlockSpec((1, 1, count), lambda i: (expert(i), 0, 0)),
            whole(*gate_rows.shape),
            pl.BlockSpec((1, 2, units, width), lambda i: (expert(i), 0, 0, 0)),
            pl.BlockSpec((2, 1, units, width), lambda i: (0, common(i), 0, 0)),
            pl.BlockSpec((1, units, width), lambda i: (expert(i), 0, 0)),
            pl.BlockSpec((1, units, width), lambda i: (common(i), 0, 0)),
        ],
        out_specs=[whole(count, width), whole(count, width), whole(1, count)],
        out_shape=[
            jax.ShapeDtypeStruct((count, width), F32),
            jax.ShapeDtypeStruct((count, width), F32),
            jax.ShapeDtypeStruct((1, count), F32),
        ],
        scratch_shapes=[pltpu.VMEM((1, count), F32)],
        compiler_params=pltpu.CompilerParams(
            dimension_semantics=("arbitrary",), vmem_limit_bytes=VMEM_LIMIT
        ),
        cost_estimate=pl.CostEstimate(
            flops=2 * 6 * count * width * units * (experts + shared),
            bytes_accessed=6 * width * units * (experts + shared),
            transcendentals=count * units * (experts + shared),
        ),
        name="own_mlp",
    )(tokens, cotangent, route[:, None, :], gate_rows, w1e, w1s, w2e, w2s)


def grads_kernel(experts_here, where_ref, tok_ref, cot_ref, route_ref, gate_ref, w1e_ref, w1s_ref, w2e_ref,
                 w2s_ref, one_mine_ref, one_peer_ref, two_mine_ref, two_peer_ref):
    step = pl.program_id(0)
    units, width = w2e_ref.shape[-2:]
    blocks, _, count = route_ref.shape
    part = one_mine_ref.shape[-1]
    core = where_ref[0]
    first = pl.multiple_of(where_ref[1] * part, part)
    other = pl.multiple_of(where_ref[2] * part, part)

    for ref in (one_mine_ref, one_peer_ref, two_mine_ref, two_peer_ref):
        ref[...] = jnp.zeros_like(ref)

    def tile(w_one, w_two, row_of):
        def block(number, carry):
            rows = pl.ds(pl.multiple_of(number * count, count), count)
            tokens, branch = tok_ref[rows, :], cot_ref[rows, :]
            _, _, weighted, mix_grad = hidden(w_one, w_two, tokens, branch, row_of(number, tokens))
            for start, one_ref, two_ref in ((first, one_mine_ref, two_mine_ref), (other, one_peer_ref, two_peer_ref)):
                cols = pl.ds(start, part)
                one_ref[...] += nn(mix_grad, tok_ref[rows, cols]).reshape(one_ref.shape)
                two_ref[...] += nn(weighted, cot_ref[rows, cols]).reshape(two_ref.shape)
            return carry

        lax.fori_loop(0, blocks, block, 0)

    @pl.when(step < experts_here)
    def _():
        expert = core * experts_here + step
        tile(w1e_ref[...].reshape(2 * units, width), w2e_ref[0], lambda n, _: route_ref[n, pl.ds(expert, 1), :])

    @pl.when(step >= experts_here)
    def _():
        tile(w1s_ref[...].reshape(2 * units, width), w2s_ref[0], lambda _, tokens: open_row(gate_ref[...], tokens))


def all_grads(where, tokens, cotangent, route, gate_rows, w1e, w1s, w2e, w2s, part):
    total, width = tokens.shape
    experts, units = w2e.shape[:2]
    shared = w2s.shape[0]
    here, here_shared = experts // 2, shared // 2
    expert = lambda i, at: at[0] * here + jnp.minimum(i, here - 1)
    common = lambda i, at: at[0] * here_shared + jnp.maximum(i - here, 0)
    whole = lambda *shape: pl.BlockSpec(shape, lambda i, at: (0,) * len(shape), pipeline_mode=pl.Buffered(1))
    tiles = here + here_shared
    one = jax.ShapeDtypeStruct((tiles, 2, units, part), F32)
    two = jax.ShapeDtypeStruct((tiles, units, part), F32)
    one_spec = pl.BlockSpec((1, 2, units, part), lambda i, at: (i, 0, 0, 0))
    two_spec = pl.BlockSpec((1, units, part), lambda i, at: (i, 0, 0))
    return pl.pallas_call(
        functools.partial(grads_kernel, here),
        grid_spec=pltpu.PrefetchScalarGridSpec(
            num_scalar_prefetch=1,
            grid=(tiles,),
            in_specs=[
                whole(total, width),
                whole(total, width),
                whole(*route.shape),
                whole(*gate_rows.shape),
                pl.BlockSpec((1, 2, units, width), lambda i, at: (expert(i, at), 0, 0, 0)),
                pl.BlockSpec((2, 1, units, width), lambda i, at: (0, common(i, at), 0, 0)),
                pl.BlockSpec((1, units, width), lambda i, at: (expert(i, at), 0, 0)),
                pl.BlockSpec((1, units, width), lambda i, at: (common(i, at), 0, 0)),
            ],
            out_specs=[one_spec, one_spec, two_spec, two_spec],
        ),
        out_shape=[one, one, two, two],
        compiler_params=pltpu.CompilerParams(
            dimension_semantics=("arbitrary",), vmem_limit_bytes=VMEM_LIMIT
        ),
        cost_estimate=pl.CostEstimate(
            flops=2 * 3 * total * (width + 2 * part) * units * tiles,
            bytes_accessed=6 * width * units * tiles + 4 * total * width,
            transcendentals=total * units * tiles,
        ),
        name="all_grads",
    )(where, tokens, cotangent, route, gate_rows, w1e, w1s, w2e, w2s)


def round_kernel(in_ref, out_ref):
    out_ref[...] = in_ref[0].astype(BF16)


def rounded(gathered):
    blocks, count, width = gathered.shape
    return pl.pallas_call(
        round_kernel,
        grid=(blocks,),
        in_specs=[pl.BlockSpec((1, count, width), lambda i: (i, 0, 0))],
        out_specs=pl.BlockSpec((count, width), lambda i: (i, 0)),
        out_shape=jax.ShapeDtypeStruct((blocks * count, width), BF16),
        compiler_params=pltpu.CompilerParams(
            dimension_semantics=("arbitrary",), vmem_limit_bytes=32 * 1024 * 1024
        ),
        name="rounded",
    )(gathered)


def split_kernel(in_ref, out_ref, route_ref):
    count = out_ref.shape[0]
    out_ref[...] = in_ref[0, :count].astype(BF16)
    route_ref[...] = in_ref[0, count:, :count][None]


def split_rounded(gathered, count):
    blocks, rows, width = gathered.shape
    extra = rows - count
    return pl.pallas_call(
        split_kernel,
        grid=(blocks,),
        in_specs=[pl.BlockSpec((1, rows, width), lambda i: (i, 0, 0))],
        out_specs=[
            pl.BlockSpec((count, width), lambda i: (i, 0)),
            pl.BlockSpec((1, extra, count), lambda i: (i, 0, 0)),
        ],
        out_shape=[
            jax.ShapeDtypeStruct((blocks * count, width), BF16),
            jax.ShapeDtypeStruct((blocks, extra, count), F32),
        ],
        compiler_params=pltpu.CompilerParams(
            dimension_semantics=("arbitrary",), vmem_limit_bytes=32 * 1024 * 1024
        ),
        name="split_rounded",
    )(gathered)


def shards(
    n_dp,
    n_tensor,
    layer_input,
    doc_ids,
    expert_ids,
    route_weights,
    attn_gain,
    qkv_weight,
    qkv_bias,
    out_weight,
    mlp_gain,
    expert_gate_up,
    expert_down,
    shared_gate_up,
    shared_down,
    shared_gate,
    cotangent,
):
    count, width = layer_input.shape
    heads_here = qkv_bias.shape[0]
    head_dim = qkv_bias.shape[1] // 3
    experts, units = expert_down.shape[:2]
    shared = shared_down.shape[0] // units
    part = width // n_dp
    scale = head_dim ** (-0.5)
    me = lax.axis_index("dp")
    core = me % 2
    swap = [(i, i ^ 1) for i in range(n_dp)]

    choose = expert_ids[:, :, None] == jnp.arange(experts, dtype=jnp.int32)[None, None, :]
    route = jnp.sum(route_weights[:, :, None] * choose.astype(F32), axis=1).T
    upstream = cotangent.astype(F32)
    cot_all = lax.all_gather(
        jnp.concatenate([upstream, jnp.pad(route, ((0, 0), (0, width - count)))], axis=0), "dp"
    )
    w1e = jnp.transpose(expert_gate_up, (0, 2, 3, 1))
    w1s = jnp.transpose(shared_gate_up, (1, 2, 0)).reshape(2, shared, units, width)
    w2s = shared_down.reshape(shared, units, width)
    gate_rows = jnp.broadcast_to(shared_gate[None, :], (16, width))

    inputs = layer_input.astype(F32)
    gain_one = attn_gain.astype(F32)
    gain_two = mlp_gain.astype(F32)
    normed_one, factor_one = rms_norm(inputs, gain_one)
    normed_one_low = normed_one.astype(BF16)
    projected = nn(normed_one_low, qkv_weight) + qkv_bias.reshape(-1).astype(F32)
    projected = projected.reshape(count, heads_here, 3, head_dim)
    index = jnp.arange(count, dtype=jnp.int32)
    place = (me * count + index - doc_ids).astype(F32)
    freq = ROPE_BASE ** (-(jnp.arange(head_dim // 2, dtype=F32) * 2.0 / head_dim))
    angle = place[:, None] * freq[None, :]
    cosine = jnp.concatenate([jnp.cos(angle), jnp.cos(angle)], axis=-1)
    sine = jnp.concatenate([jnp.sin(angle), jnp.sin(angle)], axis=-1)
    query_low = rotary_apply(projected[:, :, 0], cosine, sine).astype(BF16)
    key_low = rotary_apply(projected[:, :, 1], cosine, sine).astype(BF16)
    value_low = projected[:, :, 2].astype(BF16)
    allowed = (doc_ids[:, None] == doc_ids[None, :]) & (index[None, :] <= index[:, None])
    scores = jnp.einsum("qhd,khd->hqk", query_low, key_low, preferred_element_type=F32) * scale
    scores = jnp.where(allowed[None], scores, NEG)
    exponent = jnp.exp(scores - jnp.max(scores, axis=-1, keepdims=True))
    probs = exponent / jnp.sum(exponent, axis=-1, keepdims=True)
    probs_low = probs.astype(BF16)
    attended = jnp.einsum("hqk,khd->qhd", probs_low, value_low, preferred_element_type=F32)
    attended = attended.astype(BF16).reshape(count, heads_here * head_dim)
    residual = inputs + lax.psum(nn(attended, out_weight), "tensor")
    normed_two, factor_two = rms_norm(residual, gain_two)
    normed_two_low = normed_two.astype(BF16)

    tok_all = lax.all_gather(normed_two_low.astype(F32), "dp")
    mlp_part, normed_two_grad, logit_grad = own_mlp(
        normed_two_low, cotangent, route, gate_rows, w1e, w1s, expert_down, w2s
    )
    normed_two_total = lax.psum(normed_two_grad, "tensor")
    mlp_gain_part = jnp.sum(normed_two_grad * residual * factor_two, axis=0)
    shared_gate_part = jnp.sum(logit_grad[0][:, None] * normed_two_low.astype(F32), axis=0)

    cot_low, route_all = split_rounded(cot_all, count)
    where = jnp.stack([core, me, me ^ 1])
    one_mine, one_peer, two_mine, two_peer = all_grads(
        where, rounded(tok_all), cot_low, route_all, gate_rows, w1e, w1s, expert_down, w2s, part
    )
    one_peer = lax.ppermute(one_peer, "dp", swap)
    two_peer = lax.ppermute(two_peer, "dp", swap)

    def joined(mine, peer):
        return jnp.where(core == 0, jnp.concatenate([mine, peer]), jnp.concatenate([peer, mine]))

    half = experts // 2
    expert_gate_up_grad = jnp.transpose(joined(one_mine[:half], one_peer[:half]), (0, 3, 1, 2))
    expert_down_grad = joined(two_mine[:half], two_peer[:half])
    shared_gate_up_grad = jnp.transpose(joined(one_mine[half:], one_peer[half:]), (3, 1, 0, 2)).reshape(
        part, 2, shared * units
    )
    shared_down_grad = joined(two_mine[half:], two_peer[half:]).reshape(shared * units, part)

    residual_grad = upstream + norm_back(residual, factor_two, gain_two, normed_two_total)
    branch_grad = residual_grad.astype(BF16)
    out_weight_grad = tn(attended, branch_grad)
    out_weight_grad = lax.psum_scatter(out_weight_grad, "dp", scatter_dimension=1, tiled=True)
    attended_grad = nt(branch_grad, out_weight).astype(BF16).reshape(count, heads_here, head_dim)
    prob_grad = jnp.einsum("qhd,khd->hqk", attended_grad, value_low, preferred_element_type=F32)
    inner = jnp.sum(probs * prob_grad, axis=-1, keepdims=True)
    score_low = (probs * (prob_grad - inner) * scale).astype(BF16)
    query_grads = jnp.einsum("hqk,khd->qhd", score_low, key_low, preferred_element_type=F32)
    key_grad = jnp.einsum("hqk,qhd->khd", score_low, query_low, preferred_element_type=F32)
    value_grad = jnp.einsum("hqk,qhd->khd", probs_low, attended_grad, preferred_element_type=F32)
    query_round = lax.optimization_barrier(query_grads.astype(BF16)).astype(F32)
    key_round = lax.optimization_barrier(key_grad.astype(BF16)).astype(F32)
    projected_grad = jnp.stack(
        [rotary_back(query_round, cosine, sine), rotary_back(key_round, cosine, sine), value_grad], axis=2
    )
    projected_grad = projected_grad.astype(BF16).reshape(count, heads_here * 3 * head_dim)
    normed_one_grad = nt(projected_grad, qkv_weight)
    normed_one_total, mlp_sum = lax.psum((normed_one_grad, mlp_part), "tensor")
    qkv_weight_grad = lax.psum_scatter(tn(normed_one_low, projected_grad), "dp", scatter_dimension=0, tiled=True)

    layer_output = (residual + mlp_sum).astype(BF16)
    attn_gain_part = jnp.sum(normed_one_grad * inputs * factor_one, axis=0)
    bias_part = jnp.sum(projected_grad, axis=0, dtype=F32)
    place_of = lax.axis_index("tensor") == jnp.arange(n_tensor)
    small = jnp.concatenate(
        [attn_gain_part, mlp_gain_part, shared_gate_part, (place_of[:, None] * bias_part[None, :]).reshape(-1)]
    )
    small = lax.psum(small, ("dp", "tensor"))
    gains = lax.dynamic_slice(small[: 3 * width].reshape(3, width), (0, me * part), (3, part))
    bias = small[3 * width :].reshape(n_tensor, heads_here, 3 * head_dim)
    bias = lax.dynamic_index_in_dim(bias, lax.axis_index("tensor"), 0, keepdims=False)
    bias_cols = 3 * head_dim // n_dp
    qkv_bias_grad = lax.dynamic_slice(bias, (0, me * bias_cols), (heads_here, bias_cols))
    input_grad = (residual_grad + norm_back(inputs, factor_one, gain_one, normed_one_total)).astype(BF16)
    return (
        layer_output,
        input_grad,
        gains[0],
        qkv_weight_grad,
        qkv_bias_grad,
        out_weight_grad,
        gains[1],
        expert_gate_up_grad,
        expert_down_grad,
        shared_gate_up_grad,
        shared_down_grad,
        gains[2],
    )


def solution(mesh):
    placed = (
        P("dp", None),
        P("dp"),
        P("dp", None),
        P("dp", None),
        P(),
        P(None, "tensor"),
        P("tensor", None),
        P("tensor", None),
        P(),
        P(None, None, None, "tensor"),
        P(None, "tensor", None),
        P(None, None, "tensor"),
        P("tensor", None),
        P(),
        P("dp", None),
    )
    return jax.shard_map(
        functools.partial(shards, mesh.shape["dp"], mesh.shape["tensor"]),
        mesh=mesh,
        in_specs=placed,
        out_specs=(
            P("dp", None),
            P("dp", None),
            P("dp"),
            P("dp", "tensor"),
            P("tensor", "dp"),
            P("tensor", "dp"),
            P("dp"),
            P(None, "dp", None, "tensor"),
            P(None, "tensor", "dp"),
            P("dp", None, "tensor"),
            P("tensor", "dp"),
            P("dp"),
        ),
        check_vma=False,
    )
```

time: 1250 us -> 583 us (0.47)
  waiting for transfers between devices: 762 us -> 192 us
  Pallas kernels: 0 us -> 189 us
  matrix products: 217 us -> 38.1 us
  other arithmetic: 136 us -> 34.2 us
    reduce_scatter x5 -> x1, waiting for transfers between devices: 606 us -> 0.01 us  [shards(): lax.psum_scatter(tn(normed_one_low, projected_grad), 'dp', scatter_dimens...]
    pallas_call x0 -> x4, Pallas kernels: none -> 189 us  [the longest x1 122 us: all_grads(): pl.pallas_call(functools.partial(grads_kernel, here), grid_spec=pltpu.Pre...]
    dot_general x66 -> x9, matrix products: 213 us -> 31.7 us  [the longest x2 9.1 us: tn(): lax.dot_general(left, right, (((0,), (0,)), ((), ())), preferred_element_...]
    scatter-add x16 -> x0, other arithmetic: 108 us -> none  [the longest x8 54.3 us: shards(): mixture = mixture.at[picked].add(slot_weight[expert][:, None] * out_here)]
    all_gather x0 -> x2, waiting for transfers between devices: none -> 50.5 us  [the longest x1 50.5 us: shards(): tok_all = lax.all_gather(normed_two_low.astype(F32), 'dp')]
    gather x19 -> x0, local copies, waits for them, and re-layouts: 43.6 us -> none  [the longest x8 16.3 us: shards(): cotangent[picked].astype(jnp.float32)]
    reduce_scatter x1, waiting for transfers between devices: 36 us -> 0.01 us  [shards(): lax.psum_scatter(out_weight_grad, 'dp', scatter_dimension=1, tiled=True)]
    transpose x0 -> x2, local copies, waits for them, and re-layouts: none -> 30.9 us  [the longest x1 29 us: shards(): jnp.transpose(shared_gate_up, (1, 2, 0)).reshape(2, shared, units, width)]
  transfers between devices with their start and end apart: 10 -> 9, of which waited for: 8 -> 3; matrix products, arithmetic and copies ran while one was open for 17% -> 17% of each run, Pallas kernels for 0% -> 24%
where the time goes in v1:
time: 583 us; the launch traced here: 581 us
  waiting for transfers between devices  192 us (33%)
  Pallas kernels  189 us (32%)
  local copies, waits for them, and re-layouts  69.1 us (12%)
  blocking collectives  41 us (7%)
  matrix products  38.1 us (7%)
  other arithmetic  34.2 us (6%)
  between operations  16 us (3%)
    pallas_call x1, Pallas kernels, all_grads(): pl.pallas_call(functools.partial(grads_kernel, here), grid_spec=pltpu.Pre...  122 us
    psum x1, waiting for transfers between devices, shards(): normed_two_total = lax.psum(normed_two_grad, 'tensor')  81.7 us
    psum x1, waiting for transfers between devices, shards(): residual = inputs + lax.psum(nn(attended, out_weight), 'tensor')  59.1 us
    pallas_call x1, Pallas kernels, own_mlp(): pl.pallas_call(functools.partial(own_kernel, experts), grid=(experts + sh...  51.3 us
    all_gather x1, waiting for transfers between devices, shards(): tok_all = lax.all_gather(normed_two_low.astype(F32), 'dp')  50.5 us
    psum x1, blocking collectives, shards(): small = lax.psum(small, ('dp', 'tensor'))  41 us
    transpose x1, local copies, waits for them, and re-layouts, shards(): jnp.transpose(shared_gate_up, (1, 2, 0)).reshape(2, shared, units, width)  29 us
    unnamed x73, local copies, waits for them, and re-layouts  20.8 us
  transfers between devices with their start and end apart: 9, of which 3 were waited for; matrix products, arithmetic and copies ran while one was open for 17% of the time, Pallas kernels for 24%

profile of v1, /device:TPU:0, one launch (start us, length us, event | category | flops | bytes accessed | tf_op | source)
XLA Modules:
  0.0 580.7 jit_solution(10071724787779695166)
XLA Ops:
  11.7 6.1 %convolution_add_fusion = f32[256,1536]{1,0:T(8,128)} fusion(bf16[2048,1536]{1,0:T(8,128)(2,1)} %param.20, f32[1536]{0:T(1024)S(1)} %reshape.191, bf16[256,2048]{1,0:T(8,128)(2,1)} %param.15, f32[2048]{0:T(1024)S(1)} %convert_element_type.111, f32[256]{0:T(256)S(1)} %get-tuple-element.102), kind=kOutput, calls=%fused_computation.13 | convolution fusion | flops 1613103104 | bytes 8928256 | tf_op jit(solution)/shard_map/dot_general | solution.py:27
  17.8 3.0 copy.81
  24.4 2.2 fusion.34
  26.6 2.6 fusion.61
  31.0 2.0 fusion.62
  33.7 29.0 %copy.88 = bf16[2,1408,2048]{2,1,0:T(8,128)(2,1)} copy(bf16[2,1408,2048]{1,0,2:T(2,128)(2,1)} %bitcast.72) | data formatting | bytes 23068672 | tf_op jit(solution)/shard_map/transpose | solution.py:311
  63.3 59.1 %all-reduce.6.cloned.1.call-done = f32[256,2048]{1,0:T(8,128)} async-done(((f32[256,2048]{1,0:T(8,128)}), f32[256,2048]{1,0:T(8,128)}) %all-reduce.6.cloned.1.call-update) | async-done | bytes 2097168 | tf_op jit(solution)/shard_map/psum | solution.py:339
  122.4 1.9 multiply_reduce_fusion.3
  124.4 2.2 fusion.57
  127.4 51.3 %own_mlp.1 = (f32[256,2048]{1,0:T(8,128)}, f32[256,2048]{1,0:T(8,128)}, f32[1,256]{1,0:T(1,128)}) custom-call(bf16[256,2048]{1,0:T(8,128)(2,1)} %get-tuple-element.73.tok_ref, bf16[256,2048]{1,0:T(8,128)(2,1)} %cot_ref.1, f32[8,1,256]{2,1,0:T(1,128)} %broadcast_in_dim.14.route_ref, bf16[16,2048]{1,0:T(8,128)(2,1)} %broadcast_in_dim.15.gate_ref, ...), custom_call_target="tpu_custom_call" | custom-call | flops 26575110144 | bytes 51904512 | tf_op jit(solution)/shard_map/own_mlp/pallas_call | solution.py:116
  182.6 81.7 %all-reduce.8.cloned.1.call-done = f32[256,2048]{1,0:T(8,128)} async-done(((f32[256,2048]{1,0:T(8,128)}), f32[256,2048]{1,0:T(8,128)}) %all-reduce.8.cloned.1.call-update) | async-done | bytes 2097168 | tf_op jit(solution)/shard_map/psum | solution.py:347
  264.3 3.7 multiply_reduce_fusion.1
  274.8 2.1 fusion.22
  276.9 2.1 fusion.21
  278.9 2.4 convolution_bitcast_fusion
  282.8 7.0 %fusion.63 = f32[256,2048]{1,0:T(8,128)} fusion(bf16[256,1536]{0,1:T(8,128)(2,1)S(1)} %bitcast.81, bf16[2048,1536]{1,0:T(8,128)(2,1)} %param.20), kind=kOutput, calls=%fused_computation.121 | convolution fusion | flops 1610612736 | bytes 9175040 | tf_op jit(solution)/shard_map/dot_general | solution.py:19
  291.5 2.6 fusion.35
  295.5 6.5 %fusion.40 = f32[2048,1536]{1,0:T(8,128)} fusion(bf16[256,1536]{0,1:T(8,128)(2,1)S(1)} %bitcast.82, bf16[256,2048]{1,0:T(8,128)(2,1)S(1)} %copy-done.11, f32[2048]{0:T(1024)S(1)} %convert_element_type.111, f32[256]{0:T(256)S(1)} %get-tuple-element.102), kind=kOutput, calls=%fused_computation.77 | convolution fusion | flops 1612709888 | bytes 14427136 | tf_op jit(solution)/shard_map/dot_general | solution.py:23
  302.6 8.0 %split_rounded.1 = (bf16[2048,2048]{1,0:T(8,128)(2,1)S(1)}, f32[8,8,256]{2,1,0:T(8,128)S(1)}) custom-call(f32[8,264,2048]{2,1,0:T(8,128)} %bitcast.70), custom_call_target="tpu_custom_call" | custom-call | tf_op jit(solution)/shard_map/split_rounded/pallas_call | solution.py:255
  310.6 3.2 copy-done.3
  314.4 50.5 %all-gather.5.cloned.1.call-done = f32[2048,2048]{1,0:T(8,128)} async-done(((f32[256,2048]{1,0:T(8,128)}), f32[2048,2048]{1,0:T(8,128)}) %all-gather.5.cloned.1.call-update) | async-done | bytes 16777232 | tf_op jit(solution)/shard_map/all_gather | solution.py:343
  364.9 8.0 %rounded.1.tok_ref = bf16[2048,2048]{1,0:T(8,128)(2,1)S(1)} custom-call(f32[8,256,2048]{2,1,0:T(8,128)} %bitcast.71), custom_call_target="tpu_custom_call" | custom-call | tf_op jit(solution)/shard_map/rounded/pallas_call | solution.py:233
  373.0 4.2 copy-done.2
  377.1 121.6 %all_grads.1 = (f32[6,2,352,256]{3,2,1,0:T(8,128)}, f32[6,2,352,256]{3,2,1,0:T(8,128)}, f32[6,352,256]{2,1,0:T(8,128)}, f32[6,352,256]{2,1,0:T(8,128)}) custom-call(s32[3]{0:T(128)} %pad_add_fusion.where_ref, bf16[2048,2048]{1,0:T(8,128)(2,1)} %copy-done.2, bf16[2048,2048]{1,0:T(8,128)(2,1)} %copy-done.3, f32[8,8,256]{2,1,0:T(8,128)} %copy-done.4, ...), custom_call_target="tpu_custom_call" | custom-call | flops 66437775360 | bytes 42729472 | tf_op jit(solution)/shard_map/all_grads/pallas_call | solution.py:197
  499.7 2.9 fusion.13
  502.6 41.0 %psum.39 = f32[12288]{0:T(1024)S(1)} all-reduce(f32[12288]{0:T(1024)S(1)} %pad_maximum_fusion.2), channel_id=1, replica_groups=mesh['dp'=8,'tensor'=4] {'dp','tensor'}, use_global_device_ids=true, to_apply=%region_16.17 | all-reduce | flops 12288 | bytes 98304 | tf_op jit(solution)/shard_map/psum | solution.py:398
  545.1 3.0 add_convert_fusion
  550.8 1.9 slice.110
  560.2 1.9 copy.97
  562.1 5.5 copy.98
  567.7 2.3 slice.132
  570.4 3.0 fusion.2
  (149 shorter events, 40.2 us)
Async XLA Ops:
  8.0 23.0 %copy-start = (bf16[512,2048]{1,0:T(8,128)(2,1)S(1)}, bf16[512,2048]{1,0:T(8,128)(2,1)}, u32[]{:S(2)}) copy-start(bf16[512,2048]{1,0:T(8,128)(2,1)} %param.22) | copy-start | bytes 6291460
  8.0 114.4 %all-reduce.6.cloned.1.call-start = ((), (), s32[]{:S(2)}) async-start(), calls=%async_computation.2 | async-start | bytes 4194304 | tf_op jit(solution)/shard_map/psum | solution.py:339
  26.6 2.6 copy-start.23
  26.6 2.6 copy-start.25
  33.1 231.2 %all-reduce.8.cloned.1.call-start = ((), (), s32[]{:S(2)}) async-start(), calls=%async_computation.3 | async-start | bytes 4194304 | tf_op jit(solution)/shard_map/psum | solution.py:347
  33.7 29.0 %copy-start.31 = (f32[256,4]{0,1:T(4,128)S(1)}, f32[256,4]{0,1:T(4,128)}, u32[]{:S(2)}) copy-start(f32[256,4]{0,1:T(4,128)} %param.18) | copy-start | bytes 12292
  33.7 29.0 %copy-start.32 = (s32[256,4]{0,1:T(4,128)S(1)}, s32[256,4]{0,1:T(4,128)}, u32[]{:S(2)}) copy-start(s32[256,4]{0,1:T(4,128)} %param.17) | copy-start | bytes 12292
  33.7 88.7 %copy-start.11 = (bf16[256,2048]{1,0:T(8,128)(2,1)S(1)}, bf16[256,2048]{1,0:T(8,128)(2,1)}, u32[]{:S(2)}) copy-start(bf16[256,2048]{1,0:T(8,128)(2,1)} %param.15) | copy-start | bytes 3145732
  178.7 123.9 %all-gather.7.cloned.1.call-start = ((), (), s32[]{:S(2)}) async-start(), calls=%async_computation.7 | async-start | bytes 19464192 | tf_op jit(solution)/shard_map/all_gather | solution.py:307
  181.7 183.2 %all-gather.5.cloned.1.call-start = ((), (), s32[]{:S(2)}) async-start(), calls=%async_computation.6 | async-start | bytes 18874368 | tf_op jit(solution)/shard_map/all_gather | solution.py:343
  182.3 317.4 %all-reduce.10.cloned.1.call-start = ((), (), s32[]{:S(2)}) async-start(), calls=%async_computation.8 | async-start | bytes 8388608 | tf_op jit(solution)/shard_map/psum | solution.py:388
  264.3 3.7 copy-start.6
  264.3 4.2 copy-start.14
  264.3 4.4 copy-start.15
  272.2 2.5 copy-start.26
  282.8 7.0 %copy-start.17 = (bf16[256,4,3,128]{0,3,2,1:T(8,128)(2,1)}, bf16[256,4,3,128]{0,3,2,1:T(8,128)(2,1)S(1)}, u32[]{:S(2)}) copy-start(bf16[256,4,3,128]{0,3,2,1:T(8,128)(2,1)S(1)} %copy.95) | copy-start | bytes 2359300
  289.9 283.5 %reduce-scatter.5.cloned.1.call-start = ((), (), s32[]{:S(2)}) async-start(), calls=%async_computation.5 | async-start | bytes 4718592 | tf_op jit(solution)/shard_map/reduce_scatter | solution.py:373
  294.1 279.2 %reduce-scatter.3.cloned.1.call-start = ((), (), s32[]{:S(2)}) async-start(), calls=%async_computation.4 | async-start | bytes 14155776 | tf_op jit(solution)/shard_map/reduce_scatter | solution.py:389
  310.6 3.2 copy-start.3
  373.0 4.2 copy-start.2
  377.1 122.0 %copy-start.16 = (bf16[256,2048]{1,0:T(8,128)(2,1)S(1)}, bf16[256,2048]{1,0:T(8,128)(2,1)}, u32[]{:S(2)}) copy-start(bf16[256,2048]{1,0:T(8,128)(2,1)} %get-tuple-element.73.tok_ref) | copy-start | bytes 3145732
  377.1 122.0 %copy-start.33 = (f32[1,256]{1,0:T(1,128)S(1)}, f32[1,256]{1,0:T(1,128)}, u32[]{:S(2)}) copy-start(f32[1,256]{1,0:T(1,128)} %get-tuple-element.23) | copy-start | bytes 3076
  498.7 59.8 %collective-permute-start = (f32[6,2,352,256]{3,2,1,0:T(8,128)}, f32[6,2,352,256]{3,2,1,0:T(8,128)}, u32[]{:S(2)}, u32[]{:S(2)}) collective-permute-start(f32[6,2,352,256]{3,2,1,0:T(8,128)} %get-tuple-element.27), channel_id=1, source_target_pairs={{0,4},{4,0},{8,12},{12,8},{16,20},{20,16},{24,28},{28,24},{1,5},{5... | collective-permute-start | bytes 12976136 | tf_op jit(solution)/shard_map/ppermute | solution.py:356
  499.6 53.1 %collective-permute-start.1 = (f32[6,352,256]{2,1,0:T(8,128)}, f32[6,352,256]{2,1,0:T(8,128)}, u32[]{:S(2)}, u32[]{:S(2)}) collective-permute-start(f32[6,352,256]{2,1,0:T(8,128)} %get-tuple-element.29), channel_id=1, source_target_pairs={{0,4},{4,0},{8,12},{12,8},{16,20},{20,16},{24,28},{28,24},{1,5},{5... | collective-permute-start | bytes 6488072 | tf_op jit(solution)/shard_map/ppermute | solution.py:357
  499.7 45.3 %copy-start.7 = (f32[256,2048]{1,0:T(8,128)S(1)}, f32[256,2048]{1,0:T(8,128)}, u32[]{:S(2)}) copy-start(f32[256,2048]{1,0:T(8,128)} %copy-done.5) | copy-start | bytes 6291460
  499.7 48.3 %copy-start.28 = (f32[256]{0:T(256)S(1)}, f32[256]{0:T(256)}, u32[]{:S(2)}) copy-start(f32[256]{0:T(256)} %get-tuple-element.101) | copy-start | bytes 3076
  545.0 3.0 copy-start.10
  545.0 3.0 copy-start.13
  545.1 5.6 slice-start
  548.1 2.6 slice-start.1
  567.7 2.7 copy-start.12
  570.4 3.0 copy-start.1
  (13 other events, 21.3 us)
Sparse Core Ops, SparseCore 0:
  33.2 89.2 all-reduce.5
  178.8 85.4 all-reduce.7
  290.0 154.5 all-reduce.9
Sparse Core Ops, SparseCore 1:
  181.8 90.8 all-gather.6
  275.2 89.7 all-gather.4
  369.1 51.2 reduce-scatter.4
  424.4 92.7 reduce-scatter.2

commit v2 on v1

v2 whole, which is shorter than its diff:
```python
import functools

import jax
import jax.numpy as jnp
from jax import lax
from jax.experimental import pallas as pl
from jax.experimental.pallas import tpu as pltpu
from jax.sharding import PartitionSpec as P

EPS = 1e-06
ROPE_BASE = 1000000.0
NEG = -1e30
F32 = jnp.float32
BF16 = jnp.bfloat16
VMEM_LIMIT = 60 * 1024 * 1024
BLOCKS = 8
LIGHT = pl.CostEstimate(flops=1 << 20, bytes_accessed=1 << 16, transcendentals=0)


def nt(left, right):
    return lax.dot_general(left, right, (((1,), (1,)), ((), ())), preferred_element_type=F32)


def tn(left, right):
    return lax.dot_general(left, right, (((0,), (0,)), ((), ())), preferred_element_type=F32)


def nn(left, right):
    return jnp.dot(left, right, preferred_element_type=F32)


def norm_back(values_in, factor, gain_vec, upstream):
    scaled = gain_vec * upstream
    inner = jnp.mean(scaled * values_in, axis=-1, keepdims=True)
    return factor * scaled - values_in * factor**3 * inner


def turned(values, cosine, sine):
    return values * cosine + pltpu.roll(values, values.shape[1] // 2, 1) * sine


def turned_back(values, cosine, sine):
    return values * cosine - pltpu.roll(values, values.shape[1] // 2, 1) * sine


def head_probs(queries, keys, row_ref, col_ref):
    count = queries.shape[0]
    scores = nt(queries, keys) * queries.shape[1] ** (-0.5)
    rows = lax.broadcasted_iota(jnp.int32, (count, count), 0)
    cols = lax.broadcasted_iota(jnp.int32, (count, count), 1)
    scores = jnp.where((col_ref[...] == row_ref[...]) & (cols <= rows), scores, NEG)
    exponent = jnp.exp(scores - jnp.max(scores, axis=-1, keepdims=True))
    return exponent / jnp.sum(exponent, axis=-1, keepdims=True)


def split_columns(whole_ref, split_ref):
    part = whole_ref.shape[1] // BLOCKS
    for k in range(BLOCKS):
        split_ref[k % 2, :, k // 2 * part : (k // 2 + 1) * part] = whole_ref[:, k * part : (k + 1) * part]


def attn_kernel(x_ref, gain_ref, weight_ref, bias_ref, cos_ref, sin_ref, row_ref, col_ref, out_weight_ref,
                part_ref, split_ref, qkv_ref, attended_ref, normed_ref):
    head = pl.program_id(0)
    dim = cos_ref.shape[1]

    @pl.when(head == 0)
    def _():
        values = x_ref[...].astype(F32)
        factor = lax.rsqrt(jnp.mean(values * values, axis=-1, keepdims=True) + EPS)
        normed_ref[...] = (values * factor * gain_ref[...]).astype(BF16)
        split_columns(normed_ref, split_ref)

    projected = nn(normed_ref[...], weight_ref[...]) + bias_ref[0]
    queries = turned(projected[:, :dim], cos_ref[...], sin_ref[...]).astype(BF16)
    keys = turned(projected[:, dim : 2 * dim], cos_ref[...], sin_ref[...]).astype(BF16)
    values = projected[:, 2 * dim :].astype(BF16)
    qkv_ref[:, :dim] = queries
    qkv_ref[:, dim : 2 * dim] = keys
    qkv_ref[:, 2 * dim :] = values
    probs = head_probs(queries, keys, row_ref, col_ref)
    cols = pl.ds(pl.multiple_of(head * dim, dim), dim)
    attended_ref[:, cols] = nn(probs.astype(BF16), values).astype(BF16)

    @pl.when(head == pl.num_programs(0) - 1)
    def _():
        part_ref[...] = nn(attended_ref[...], out_weight_ref[...])


def whole(*shape):
    return pl.BlockSpec(shape, lambda *at: (0,) * len(shape))


def attention(x, gain, weight, bias, cosine, sine, row, col, out_weight):
    count, width = x.shape
    heads, _, cols = bias.shape
    return pl.pallas_call(
        attn_kernel,
        grid=(heads,),
        in_specs=[
            whole(count, width),
            whole(1, width),
            pl.BlockSpec((width, cols), lambda h: (0, h)),
            pl.BlockSpec((1, 1, cols), lambda h: (h, 0, 0)),
            whole(*cosine.shape),
            whole(*sine.shape),
            whole(1, count),
            whole(count, 1),
            whole(*out_weight.shape),
        ],
        out_specs=[
            whole(count, width),
            whole(2, count, width // 2),
            pl.BlockSpec((count, cols), lambda h: (0, h)),
            whole(count, out_weight.shape[0]),
        ],
        out_shape=[
            jax.ShapeDtypeStruct((count, width), F32),
            jax.ShapeDtypeStruct((2, count, width // 2), BF16),
            jax.ShapeDtypeStruct((count, heads * cols), BF16),
            jax.ShapeDtypeStruct((count, out_weight.shape[0]), BF16),
        ],
        scratch_shapes=[pltpu.VMEM((count, width), BF16)],
        compiler_params=pltpu.CompilerParams(
            dimension_semantics=("arbitrary",), vmem_limit_bytes=32 * 1024 * 1024
        ),
        cost_estimate=LIGHT,
        name="attention",
    )(x, gain, weight, bias, cosine, sine, row, col, out_weight)


def norm_kernel(x_ref, sum_ref, gain_ref, residual_ref, low_ref, wide_ref):
    residual = x_ref[...].astype(F32) + sum_ref[...]
    factor = lax.rsqrt(jnp.mean(residual * residual, axis=-1, keepdims=True) + EPS)
    low = (residual * factor * gain_ref[...]).astype(BF16)
    residual_ref[...] = residual
    low_ref[...] = low
    wide_ref[...] = low.astype(F32)


def second_norm(x, attn_sum, gain):
    count, width = x.shape
    rows = count // 4
    spec = pl.BlockSpec((rows, width), lambda i: (i, 0))
    return pl.pallas_call(
        norm_kernel,
        grid=(4,),
        in_specs=[spec, spec, whole(1, width)],
        out_specs=[spec, spec, spec],
        out_shape=[
            jax.ShapeDtypeStruct((count, width), F32),
            jax.ShapeDtypeStruct((count, width), BF16),
            jax.ShapeDtypeStruct((count, width), F32),
        ],
        compiler_params=pltpu.CompilerParams(
            dimension_semantics=("arbitrary",), vmem_limit_bytes=32 * 1024 * 1024
        ),
        name="second_norm",
    )(x, attn_sum, gain)


def back_kernel(total_ref, residual_ref, cot_ref, gain_ref, out_weight_ref, qkv_ref, weight_ref, cos_ref, sin_ref,
                row_ref, col_ref, normed_grad_ref, residual_grad_ref, split_ref, projected_grad_ref, bias_ref,
                mlp_gain_ref, branch_ref, attended_grad_ref):
    head = pl.program_id(0)
    dim = cos_ref.shape[1]

    @pl.when(head == 0)
    def _():
        total, residual = total_ref[...], residual_ref[...]
        factor = lax.rsqrt(jnp.mean(residual * residual, axis=-1, keepdims=True) + EPS)
        scaled = gain_ref[...] * total
        inner = jnp.mean(scaled * residual, axis=-1, keepdims=True)
        residual_grad = cot_ref[...].astype(F32) + (factor * scaled - residual * factor**3 * inner)
        residual_grad_ref[...] = residual_grad
        branch_ref[...] = residual_grad.astype(BF16)
        split_columns(branch_ref, split_ref)
        mlp_gain_ref[...] = jnp.sum(total * residual * factor, axis=0, keepdims=True)
        attended_grad = nt(branch_ref[...], out_weight_ref[...]).astype(BF16)
        for k in range(attended_grad_ref.shape[0]):
            attended_grad_ref[k] = attended_grad[:, k * dim : (k + 1) * dim]

    queries, keys, values = qkv_ref[:, :dim], qkv_ref[:, dim : 2 * dim], qkv_ref[:, 2 * dim :]
    attended_grad = attended_grad_ref[head]
    probs = head_probs(queries, keys, row_ref, col_ref)
    prob_grad = nt(attended_grad, values)
    inner = jnp.sum(probs * prob_grad, axis=-1, keepdims=True)
    score = (probs * (prob_grad - inner) * dim ** (-0.5)).astype(BF16)
    query_grad = nn(score, keys).astype(BF16).astype(F32)
    key_grad = tn(score, queries).astype(BF16).astype(F32)
    value_grad = tn(probs.astype(BF16), attended_grad)
    grad = jnp.concatenate(
        [
            turned_back(query_grad, cos_ref[...], sin_ref[...]).astype(BF16),
            turned_back(key_grad, cos_ref[...], sin_ref[...]).astype(BF16),
            value_grad.astype(BF16),
        ],
        axis=1,
    )
    projected_grad_ref[...] = grad
    bias_ref[...] = jnp.sum(grad.astype(F32), axis=0, keepdims=True)
    product = nt(grad, weight_ref[...])

    @pl.when(head == 0)
    def _():
        normed_grad_ref[...] = product

    @pl.when(head > 0)
    def _():
        normed_grad_ref[...] += product


def attention_back(total, residual, cotangent, gain, out_weight, qkv, weight, cosine, sine, row, col):
    count, width = total.shape
    dim = cosine.shape[1]
    cols = 3 * dim
    heads = qkv.shape[1] // cols
    return pl.pallas_call(
        back_kernel,
        grid=(heads,),
        in_specs=[
            whole(count, width),
            whole(count, width),
            whole(count, width),
            whole(1, width),
            whole(*out_weight.shape),
            pl.BlockSpec((count, cols), lambda h: (0, h)),
            pl.BlockSpec((width, cols), lambda h: (0, h)),
            whole(*cosine.shape),
            whole(*sine.shape),
            whole(1, count),
            whole(count, 1),
        ],
        out_specs=[
            whole(count, width),
            whole(count, width),
            whole(2, count, width // 2),
            pl.BlockSpec((count, cols), lambda h: (0, h)),
            pl.BlockSpec((1, cols), lambda h: (0, h)),
            whole(1, width),
        ],
        out_shape=[
            jax.ShapeDtypeStruct((count, width), F32),
            jax.ShapeDtypeStruct((count, width), F32),
            jax.ShapeDtypeStruct((2, count, width // 2), BF16),
            jax.ShapeDtypeStruct((count, heads * cols), BF16),
            jax.ShapeDtypeStruct((1, heads * cols), F32),
            jax.ShapeDtypeStruct((1, width), F32),
        ],
        scratch_shapes=[pltpu.VMEM((count, width), BF16), pltpu.VMEM((heads, count, dim), BF16)],
        compiler_params=pltpu.CompilerParams(
            dimension_semantics=("arbitrary",), vmem_limit_bytes=48 * 1024 * 1024
        ),
        cost_estimate=LIGHT,
        name="attention_back",
    )(total, residual, cotangent, gain, out_weight, qkv, weight, cosine, sine, row, col)


def hidden(w_one, w_two, tokens, branch, route_row):
    units = w_two.shape[0]
    mix = nt(w_one, tokens)
    gate, up = mix[:units], mix[units:]
    back = nt(w_two, branch)
    sigma = lax.logistic(gate)
    silu = gate * sigma
    act = silu * up
    scaled = back * route_row
    gate_grad = scaled * up * (sigma + silu * (1.0 - sigma))
    mix_grad = jnp.concatenate([gate_grad.astype(BF16), (scaled * silu).astype(BF16)], axis=0)
    return act, back, (act * route_row).astype(BF16), mix_grad


def open_row(gate_rows, tokens):
    return lax.logistic(nt(gate_rows, tokens)[:1])


def own_kernel(experts, tok_ref, cot_ref, route_ref, gate_ref, w1_ref, w2_ref, out_ref, dx_ref, logit_ref, open_ref):
    step = pl.program_id(0)
    group, units, width = w2_ref.shape
    shared = step * group >= experts

    @pl.when(step == 0)
    def _():
        out_ref[...] = jnp.zeros_like(out_ref)
        dx_ref[...] = jnp.zeros_like(dx_ref)
        logit_ref[...] = jnp.zeros_like(logit_ref)
        open_ref[...] = open_row(gate_ref[...], tok_ref[...])

    weighted, mix_grads = [], []
    for k in range(group):
        act, back, scaled, mix_grad = hidden(
            w1_ref[k].reshape(2 * units, width),
            w2_ref[k],
            tok_ref[...],
            cot_ref[...],
            jnp.where(shared, open_ref[...], route_ref[k]),
        )
        weighted.append(scaled)
        mix_grads.append(mix_grad)
        logit_ref[...] += jnp.where(shared, jnp.sum(act * back, axis=0, keepdims=True), 0.0)
    out_ref[...] += tn(jnp.concatenate(weighted), w2_ref[...].reshape(group * units, width))
    dx_ref[...] += tn(jnp.concatenate(mix_grads), w1_ref[...].reshape(group * 2 * units, width))

    @pl.when(step == pl.num_programs(0) - 1)
    def _():
        opened = open_ref[...]
        logit = opened * (1.0 - opened) * logit_ref[...]
        logit_ref[...] = logit
        column = jnp.broadcast_to(logit, (8, logit.shape[1])).T[:, :1]
        dx_ref[...] += column * gate_ref[:1].astype(F32)


def own_mlp(tokens, cotangent, route, gate_rows, w1, w2):
    count, width = tokens.shape
    tiles, units = w2.shape[:2]
    experts = route.shape[0]
    group = 2
    return pl.pallas_call(
        functools.partial(own_kernel, experts),
        grid=(tiles // group,),
        in_specs=[
            whole(count, width),
            whole(count, width),
            pl.BlockSpec((group, 1, count), lambda i: (jnp.minimum(i, experts // group - 1), 0, 0)),
            whole(*gate_rows.shape),
            pl.BlockSpec((group, 2, units, width), lambda i: (i, 0, 0, 0)),
            pl.BlockSpec((group, units, width), lambda i: (i, 0, 0)),
        ],
        out_specs=[whole(count, width), whole(count, width), whole(1, count)],
        out_shape=[
            jax.ShapeDtypeStruct((count, width), F32),
            jax.ShapeDtypeStruct((count, width), F32),
            jax.ShapeDtypeStruct((1, count), F32),
        ],
        scratch_shapes=[pltpu.VMEM((1, count), F32)],
        compiler_params=pltpu.CompilerParams(
            dimension_semantics=("arbitrary",), vmem_limit_bytes=VMEM_LIMIT
        ),
        cost_estimate=LIGHT,
        name="own_mlp",
    )(tokens, cotangent, route[:, None, :], gate_rows, w1, w2)


def chip_kernel(pieces, here, at_ref, *refs):
    token_refs, refs = refs[: 2 * pieces], refs[2 * pieces :]
    cot_ref, route_ref, gate_ref, w1_ref, w2_ref = refs[:5]
    mix_grad_ref, weighted_ref, part_ref, tok_ref, open_ref = refs[-5:]
    step = pl.program_id(0)
    units, width = w2_ref.shape[-2:]
    cores, experts, count = route_ref.shape
    core = at_ref[0]

    @pl.when(step == 0)
    def _():
        for owner in range(2):
            base = count * (core if owner == 0 else 1 - core)
            for k, ref in enumerate(token_refs[owner * pieces : (owner + 1) * pieces]):
                rows = ref.shape[0]
                tok_ref[pl.ds(pl.multiple_of(base + k * rows, rows), rows), :] = ref[...].astype(BF16)
        part = part_ref.shape[1]
        part_ref[...] = tok_ref[:, pl.ds(pl.multiple_of(at_ref[1] * part, part), part)]
        open_ref[...] = open_row(gate_ref[...], tok_ref[...])

    expert = jnp.minimum(core * here + step, experts - 1)
    route_row = jnp.concatenate([route_ref[k, pl.ds(expert, 1), :] for k in range(cores)], axis=1)
    _, _, weighted, mix_grad = hidden(
        w1_ref[...].reshape(2 * units, width),
        w2_ref[0],
        tok_ref[...],
        cot_ref[...],
        jnp.where(step >= here, open_ref[...], route_row),
    )
    mix_grad_ref[0] = mix_grad
    weighted_ref[0] = weighted


def chip_hidden(at, mine, peer, cotangent, route, gate_rows, w1, w2, kept, part):
    total, width = cotangent.shape
    tiles, units = w2.shape[:2]
    experts, count = route.shape[1:]
    here, shared = experts // 2, (tiles - experts) // 2
    rows = 2 * count
    own = lambda i, at: jnp.where(i < here, at[0] * here + i, experts + at[0] * shared + i - here)
    pieces = len(mine)
    fixed = lambda *shape: pl.BlockSpec(shape, lambda i, at: (0,) * len(shape))
    shapes = [
        jax.ShapeDtypeStruct((here + shared, 2 * units, total), BF16),
        jax.ShapeDtypeStruct((here + shared, units, total), BF16),
        jax.ShapeDtypeStruct((total, 2 * part), BF16),
    ]
    inputs = [*mine, *peer, cotangent, route, gate_rows, w1, w2]
    return pl.pallas_call(
        functools.partial(chip_kernel, pieces, here),
        grid_spec=pltpu.PrefetchScalarGridSpec(
            num_scalar_prefetch=1,
            grid=(here + shared,),
            in_specs=[
                *[fixed(*v.shape) for v in (*mine, *peer)],
                pl.BlockSpec((rows, width), lambda i, at: (at[2], 0)),
                pl.BlockSpec((2, experts, count), lambda i, at: (at[2], 0, 0)),
                fixed(*gate_rows.shape),
                pl.BlockSpec((1, 2, units, width), lambda i, at: (own(i, at), 0, 0, 0)),
                pl.BlockSpec((1, units, width), lambda i, at: (own(i, at), 0, 0)),
                *[pl.BlockSpec(memory_space=pl.ANY) for _ in kept],
            ],
            out_specs=[
                pl.BlockSpec((1, 2 * units, rows), lambda i, at: (i, 0, at[2])),
                pl.BlockSpec((1, units, rows), lambda i, at: (i, 0, at[2])),
                pl.BlockSpec((rows, 2 * part), lambda i, at: (at[2], 0)),
            ],
            scratch_shapes=[pltpu.VMEM((rows, width), BF16), pltpu.VMEM((1, rows), F32)],
        ),
        out_shape=shapes,
        input_output_aliases={1 + len(inputs) + k: k for k in range(len(kept))},
        compiler_params=pltpu.CompilerParams(
            dimension_semantics=("arbitrary",), vmem_limit_bytes=VMEM_LIMIT
        ),
        cost_estimate=LIGHT,
        name="chip_hidden",
    )(at, *inputs, *kept)


def weights_kernel(at_ref, mix_grad_ref, weighted_ref, tok_ref, cot_ref, one_mine_ref, one_peer_ref, two_mine_ref,
                   two_peer_ref):
    part = one_mine_ref.shape[-1]
    core = at_ref[0]
    one = nn(mix_grad_ref[0], tok_ref[...])
    two = nn(weighted_ref[0], cot_ref[...])
    for value, mine_ref, peer_ref in ((one, one_mine_ref, one_peer_ref), (two, two_mine_ref, two_peer_ref)):
        low, high = value[:, :part], value[:, part:]
        mine_ref[...] = jnp.where(core == 0, low, high).reshape(mine_ref.shape)
        peer_ref[...] = jnp.where(core == 0, high, low).reshape(peer_ref.shape)


def weight_grads(at, mix_grads, weighted, tokens, cotangent):
    tiles, units, total = weighted.shape
    part = tokens.shape[1] // 2
    one = jax.ShapeDtypeStruct((tiles, 2, units, part), F32)
    two = jax.ShapeDtypeStruct((tiles, units, part), F32)
    one_spec = pl.BlockSpec((1, 2, units, part), lambda i, at: (i, 0, 0, 0))
    two_spec = pl.BlockSpec((1, units, part), lambda i, at: (i, 0, 0))
    return pl.pallas_call(
        weights_kernel,
        grid_spec=pltpu.PrefetchScalarGridSpec(
            num_scalar_prefetch=1,
            grid=(tiles,),
            in_specs=[
                pl.BlockSpec((1, 2 * units, total), lambda i, at: (i, 0, 0)),
                pl.BlockSpec((1, units, total), lambda i, at: (i, 0, 0)),
                pl.BlockSpec((total, 2 * part), lambda i, at: (0, 0)),
                pl.BlockSpec((total, 2 * part), lambda i, at: (0, at[1])),
            ],
            out_specs=[one_spec, one_spec, two_spec, two_spec],
        ),
        out_shape=[one, one, two, two],
        compiler_params=pltpu.CompilerParams(
            dimension_semantics=("arbitrary",), vmem_limit_bytes=VMEM_LIMIT
        ),
        cost_estimate=LIGHT,
        name="weight_grads",
    )(at, mix_grads, weighted, tokens, cotangent)


def split_kernel(in_ref, out_ref, route_ref):
    count = out_ref.shape[0]
    out_ref[...] = in_ref[0, :count].astype(BF16)
    route_ref[...] = in_ref[0, count:, :count][None]


def split_rounded(gathered, count):
    blocks, rows, width = gathered.shape
    extra = rows - count
    return pl.pallas_call(
        split_kernel,
        grid=(blocks,),
        in_specs=[pl.BlockSpec((1, rows, width), lambda i: (i, 0, 0))],
        out_specs=[
            pl.BlockSpec((count, width), lambda i: (i, 0)),
            pl.BlockSpec((1, extra, count), lambda i: (i, 0, 0)),
        ],
        out_shape=[
            jax.ShapeDtypeStruct((blocks * count, width), BF16),
            jax.ShapeDtypeStruct((blocks, extra, count), F32),
        ],
        compiler_params=pltpu.CompilerParams(
            dimension_semantics=("arbitrary",), vmem_limit_bytes=32 * 1024 * 1024
        ),
        name="split_rounded",
    )(gathered)


def flip(value, bit):
    return lax.ppermute(value, "dp", [(i, i ^ bit) for i in range(8)])


def after(source, count):
    message = lax.ppermute(source[:8, :128], "dp", [(i, i ^ 1) for i in range(count)])
    return jnp.isnan(message[0, 0]).astype(jnp.int32)


def take(value, number, axis):
    return lax.dynamic_index_in_dim(value, number, axis, keepdims=False)


def scatter_first(held, me):
    along_x, along_y = (me // 2) % 2, me // 4
    half = held.shape[-1] // 256 * 128
    a, b = held[..., :half], held[..., half:]
    return (take(a, along_x, 1), take(a, 1 - along_x, 1), take(b, along_y, 0), take(b, 1 - along_y, 0))


def scatter_second(a, b, me):
    along_x, along_y = (me // 2) % 2, me // 4
    a = take(a, along_y, 0) + flip(take(a, 1 - along_y, 0), 4)
    b = take(b, along_x, 0) + flip(take(b, 1 - along_x, 0), 2)
    return jnp.concatenate([a, b], axis=-1)


def shards(
    n_dp,
    n_tensor,
    layer_input,
    doc_ids,
    expert_ids,
    route_weights,
    attn_gain,
    qkv_weight,
    qkv_bias,
    out_weight,
    mlp_gain,
    expert_gate_up,
    expert_down,
    shared_gate_up,
    shared_down,
    shared_gate,
    cotangent,
):
    count, width = layer_input.shape
    heads_here = qkv_bias.shape[0]
    head_dim = qkv_bias.shape[1] // 3
    experts, units = expert_down.shape[:2]
    shared = shared_down.shape[0] // units
    part = width // n_dp
    me = lax.axis_index("dp")
    core, chip = me % 2, me // 2
    tied = lax.optimization_barrier

    choose = expert_ids[:, :, None] == jnp.arange(experts, dtype=jnp.int32)[None, None, :]
    route = jnp.sum(route_weights[:, :, None] * choose.astype(F32), axis=1).T
    cot_all = lax.all_gather(
        jnp.concatenate([cotangent.astype(F32), jnp.pad(route, ((0, 0), (0, width - count)))], axis=0), "dp"
    )
    gate_rows = jnp.broadcast_to(shared_gate[None, :], (16, width))
    index = jnp.arange(count, dtype=jnp.int32)
    place = (me * count + index - doc_ids).astype(F32)
    freq = ROPE_BASE ** (-(jnp.arange(head_dim // 2, dtype=F32) * 2.0 / head_dim))
    angle = place[:, None] * freq[None, :]
    cosine = jnp.concatenate([jnp.cos(angle), jnp.cos(angle)], axis=-1)
    sine = jnp.concatenate([-jnp.sin(angle), jnp.sin(angle)], axis=-1)
    row, col = doc_ids[None, :], doc_ids[:, None]
    gain_one = attn_gain.astype(F32)[None, :]
    gain_two = mlp_gain.astype(F32)[None, :]
    attn_part, normed_one, qkv, attended = attention(
        layer_input, gain_one, qkv_weight, qkv_bias.astype(F32)[:, None, :], cosine, sine, row, col, out_weight
    )

    attn_part, shared_gate_up = tied((attn_part, shared_gate_up))
    attn_sum = lax.psum(attn_part, "tensor")
    w1 = jnp.concatenate(
        [
            jnp.transpose(expert_gate_up, (0, 2, 3, 1)),
            jnp.transpose(shared_gate_up.reshape(width, 2, shared, units), (2, 1, 3, 0)),
        ]
    )
    w2 = jnp.concatenate([expert_down, shared_down.reshape(shared, units, width)])
    cot_low, route_all = split_rounded(cot_all, count)
    attn_sum, w1, w2, cot_low, route_all = tied((attn_sum, w1, w2, cot_low, route_all))

    residual, tokens, tokens_wide = second_norm(layer_input, attn_sum, gain_two)
    if n_dp == 8:
        over_x, over_y = flip(tokens_wide, 2), flip(tokens_wide, 4)
        beside = flip(tokens_wide, 1)
    else:
        tok_all = lax.all_gather(tokens_wide, "dp")
    mlp_part, normed_two_part, logit_grad = own_mlp(tokens, cotangent, route, gate_rows, w1, w2)
    normed_two_part, mlp_part = tied((normed_two_part, mlp_part))
    normed_two_total = lax.psum(normed_two_part, "tensor")
    line = n_tensor == 4 and n_dp == 8
    if line:
        inwards = lax.ppermute(mlp_part, "tensor", [(0, 1), (3, 2)])

    kept = []
    pair = lambda other: jnp.stack([core, chip, other])
    hide = lambda other, mine, peer, kept: chip_hidden(
        pair(other), mine, peer, cot_low, route_all, gate_rows, w1, w2, kept, part
    )
    if n_dp == 8:
        over_x, over_y, other = tied((over_x, over_y, (chip ^ 1) + after(normed_two_part, n_dp)))
        low, high = flip(over_x[: count // 2], 4), flip(over_y[count // 2 :], 2)
        beside_x, beside_y = flip(over_x, 1), flip(over_y, 1)
        kept = hide(other, [over_x], [beside_x], kept)
        low, high, kept = tied((low, high, kept))
        beside_low, beside_high = flip(low, 1), flip(high, 1)
        kept = hide(chip ^ 2, [over_y], [beside_y], kept)
        kept = hide(chip ^ 3, [low, high], [beside_low, beside_high], kept)
        kept = hide(chip, [tokens_wide], [beside], kept)
    else:
        for k in range(n_dp // 2):
            kept = hide(k, [take(tok_all, 2 * k + core, 0)], [take(tok_all, 2 * k + 1 - core, 0)], kept)
    one_mine, one_peer, two_mine, two_peer = weight_grads(pair(chip), *kept, cot_low)
    if line:
        inwards, one_peer = tied((inwards, one_peer))
    one_mine, one_peer, two_mine, two_peer, normed_two_total = tied(
        (one_mine, one_peer, two_mine, two_peer, normed_two_total)
    )

    normed_one_part, residual_grad, branch_grad, projected_grad, bias_part, mlp_gain_part = attention_back(
        normed_two_total, residual, cotangent, gain_two, out_weight, qkv, qkv_weight, cosine, sine, row, col
    )
    normed_one_total = lax.psum_scatter(normed_one_part, "tensor", scatter_dimension=0, tiled=True)
    few = count // n_tensor
    inputs = layer_input.astype(F32)
    factor_one = lax.rsqrt(jnp.mean(inputs * inputs, axis=-1, keepdims=True) + EPS)
    mine = lambda v: lax.dynamic_slice_in_dim(v, lax.axis_index("tensor") * few, few, 0)
    input_grad = norm_back(mine(inputs), mine(factor_one), gain_one, normed_one_total)
    input_grad = lax.all_gather(input_grad, "tensor", axis=0, tiled=True)
    swap = [(i, i ^ 1) for i in range(n_dp)]
    one_peer, two_peer = lax.ppermute(one_peer, "dp", swap), lax.ppermute(two_peer, "dp", swap)
    attn_gain_part = jnp.sum(normed_one_part * inputs * factor_one, axis=0)
    shared_gate_part = jnp.sum(logit_grad[0][:, None] * tokens.astype(F32), axis=0)
    my_slot = lax.axis_index("tensor") == jnp.arange(n_tensor)
    small = jnp.concatenate(
        [
            attn_gain_part,
            mlp_gain_part[0] * my_slot[0],
            shared_gate_part,
            (my_slot[:, None] * bias_part).reshape(-1),
        ]
    )
    spot = lax.axis_index("tensor")
    if line:
        inwards, projected_grad = tied((inwards, projected_grad))
    if n_dp == 8:
        def products(c):
            return (
                tn(take(normed_one, c, 0), projected_grad).reshape(2, 2, part, -1),
                tn(take(branch_grad, c, 0), attended).reshape(2, 2, part, -1),
            )

        other = 1 - core + after(normed_one_part, n_dp)
        sent = products(other)
        arrived = [flip(v, 1) for v in sent]
        if line:
            mlp_part, sent = tied((mlp_part, sent))
            partial = mlp_part + inwards
            across = lax.ppermute(partial, "tensor", [(1, 2), (2, 1)])
            small, partial = tied((small, partial))
        else:
            small, sent = tied((small, sent))
        small = lax.psum(small, ("dp", "tensor"))
        small, arrived = tied((small, arrived))
        held = products(1 - other)
        firsts = [scatter_first(h + v, me) for h, v in zip(held, arrived, strict=True)]
        moved = [(flip(a_other, 2), flip(b_other, 4)) for _, a_other, _, b_other in firsts]
        if line:
            across, moved = tied((across, moved))
            partial = partial + across
            outwards = lax.ppermute(partial, "tensor", [(1, 0), (2, 3)])
        steps = [(a + a_in, b + b_in) for (a, _, b, _), (a_in, b_in) in zip(firsts, moved, strict=True)]
        qkv_weight_grad, out_weight_grad = [scatter_second(a, b, me) for a, b in steps]
        out_weight_grad = out_weight_grad.T
        input_grad, qkv_weight_grad = tied((input_grad, qkv_weight_grad))
        if line:
            outwards, qkv_weight_grad = tied((outwards, qkv_weight_grad))
    else:
        small = lax.psum(small, ("dp", "tensor"))
        joint = lambda v: v.reshape(2, count, BLOCKS // 2, -1).transpose(1, 2, 0, 3).reshape(count, width)
        out_weight_grad = lax.psum_scatter(tn(attended, joint(branch_grad)), "dp", scatter_dimension=1, tiled=True)
        qkv_weight_grad = lax.psum_scatter(
            tn(joint(normed_one), projected_grad), "dp", scatter_dimension=0, tiled=True
        )

    gains = lax.dynamic_slice(small[: 3 * width].reshape(3, width), (0, me * part), (3, part))
    bias = take(small[3 * width :].reshape(n_tensor, heads_here, 3 * head_dim), lax.axis_index("tensor"), 0)
    bias_cols = 3 * head_dim // n_dp
    qkv_bias_grad = lax.dynamic_slice(bias, (0, me * bias_cols), (heads_here, bias_cols))
    input_grad = (residual_grad + input_grad).astype(BF16)

    if line:
        mlp_sum = jnp.where((spot == 1) | (spot == 2), partial, outwards)
    else:
        mlp_sum = lax.psum(mlp_part, "tensor")
    layer_output = (residual + mlp_sum).astype(BF16)

    def joined(mine, peer):
        return jnp.where(core == 0, jnp.concatenate([mine, peer]), jnp.concatenate([peer, mine]))

    half = experts // 2
    expert_gate_up_grad = jnp.transpose(joined(one_mine[:half], one_peer[:half]), (0, 3, 1, 2))
    expert_down_grad = joined(two_mine[:half], two_peer[:half])
    shared_gate_up_grad = jnp.transpose(joined(one_mine[half:], one_peer[half:]), (3, 1, 0, 2)).reshape(
        part, 2, shared * units
    )
    shared_down_grad = joined(two_mine[half:], two_peer[half:]).reshape(shared * units, part)
    return (
        layer_output,
        input_grad,
        gains[0],
        qkv_weight_grad,
        qkv_bias_grad,
        out_weight_grad,
        gains[1],
        expert_gate_up_grad,
        expert_down_grad,
        shared_gate_up_grad,
        shared_down_grad,
        gains[2],
    )


def solution(mesh):
    placed = (
        P("dp", None),
        P("dp"),
        P("dp", None),
        P("dp", None),
        P(),
        P(None, "tensor"),
        P("tensor", None),
        P("tensor", None),
        P(),
        P(None, None, None, "tensor"),
        P(None, "tensor", None),
        P(None, None, "tensor"),
        P("tensor", None),
        P(),
        P("dp", None),
    )
    return jax.shard_map(
        functools.partial(shards, mesh.shape["dp"], mesh.shape["tensor"]),
        mesh=mesh,
        in_specs=placed,
        out_specs=(
            P("dp", None),
            P("dp", None),
            P("dp"),
            P("dp", "tensor"),
            P("tensor", "dp"),
            P("tensor", "dp"),
            P("dp"),
            P(None, "dp", None, "tensor"),
            P(None, "tensor", "dp"),
            P("dp", None, "tensor"),
            P("tensor", "dp"),
            P("dp"),
        ),
        check_vma=False,
    )
```

time: 583 us -> 588 us (level); the launches traced: 581 us -> 579 us
  waiting for transfers between devices: 192 us -> 66.6 us
  other arithmetic: 34.2 us -> 80.5 us
  blocking collectives: 41 us -> 85.2 us
  local copies, waits for them, and re-layouts: 69.1 us -> 111 us
  matrix products: 38.1 us -> 10.6 us
  starting transfers between devices: 1.57 us -> 24 us
  Pallas kernels: 189 us -> 181 us
    psum x3 -> x2, waiting for transfers between devices: 141 us -> 3.46 us  [the longest x1 3.46 us: shards(): normed_two_total = lax.psum(normed_two_part, 'tensor')]
    ppermute x2 -> x26, waiting for transfers between devices: 0.01 us -> 59.2 us  [the longest x19 34.3 us: flip(): return lax.ppermute(value, 'dp', [(i, i ^ bit) for i in range(8)])]
    all_gather x2, waiting for transfers between devices: 50.5 us -> 3.83 us  [the longest x1 3.82 us: shards(): lax.all_gather(jnp.concatenate([cotangent.astype(F32), jnp.pad(route, ((0...]
    psum x1, blocking collectives: 41 us -> 85.2 us  [shards(): small = lax.psum(small, ('dp', 'tensor'))]
    concatenate x2 -> x5, other arithmetic: 1.53 us -> 34.4 us  [the longest x1 24.6 us: shards(): jnp.concatenate([jnp.transpose(expert_gate_up, (0, 2, 3, 1)), jnp.transpo...]
    transpose x1 -> x0, local copies, waits for them, and re-layouts: 29 us -> none  [shards(): jnp.transpose(shared_gate_up, (1, 2, 0)).reshape(2, shared, units, width)]
    optimization_barrier x0 -> x1, local copies, waits for them, and re-layouts: none -> 28.7 us  [shards(): attn_part, shared_gate_up = tied((attn_part, shared_gate_up))]
    dot_general x9 -> x0, matrix products: 26.5 us -> none  [the longest x2 8.53 us: nt(): lax.dot_general(left, right, (((1,), (1,)), ((), ())), preferred_element_...]
  transfers between devices with their start and end apart: 9 -> 31, of which waited for: 3 -> 10; matrix products, arithmetic and copies ran while one was open for 17% -> 29% of each run, Pallas kernels for 24% -> 29%
where the time goes in v2:
time: 588 us; the launch traced here: 579 us
  Pallas kernels  181 us (31%)
  local copies, waits for them, and re-layouts  111 us (19%)
  blocking collectives  85.2 us (14%)
  other arithmetic  80.5 us (14%)
  waiting for transfers between devices  66.6 us (11%)
  starting transfers between devices  24 us (4%)
  between operations  19.7 us (3%)
  matrix products  10.6 us (2%)
    pallas_call x4, Pallas kernels, chip_hidden(): pl.pallas_call(functools.partial(chip_kernel, pieces, here), grid_spec=pl...  92.4 us
    psum x1, blocking collectives, shards(): small = lax.psum(small, ('dp', 'tensor'))  85.2 us
    pallas_call x1, Pallas kernels, own_mlp(): pl.pallas_call(functools.partial(own_kernel, experts), grid=(tiles // gro...  39.3 us
    ppermute x19, waiting for transfers between devices, flip(): return lax.ppermute(value, 'dp', [(i, i ^ bit) for i in range(8)])  34.3 us
    unnamed x117, local copies, waits for them, and re-layouts  29.6 us
    optimization_barrier x1, local copies, waits for them, and re-layouts, shards(): attn_part, shared_gate_up = tied((attn_part, shared_gate_up))  28.7 us
    concatenate x1, other arithmetic, shards(): jnp.concatenate([jnp.transpose(expert_gate_up, (0, 2, 3, 1)), jnp.transpo...  24.6 us
    ppermute x1, waiting for transfers between devices, shards(): outwards = lax.ppermute(partial, 'tensor', [(1, 0), (2, 3)])  22.2 us
  transfers between devices with their start and end apart: 31, of which 10 were waited for; matrix products, arithmetic and copies ran while one was open for 29% of the time, Pallas kernels for 29%

profile of v2, /device:TPU:0, one launch (start us, length us, event | category | flops | bytes accessed | tf_op | source)
XLA Modules:
  0.0 578.7 jit_solution(12331250124968514955)
XLA Ops:
  13.6 2.8 copy-done.2
  17.1 7.1 %attention.1 = (f32[256,2048]{1,0:T(8,128)S(1)}, bf16[2,256,1024]{2,1,0:T(8,128)(2,1)S(1)}, bf16[256,1536]{1,0:T(8,128)(2,1)S(1)}, bf16[256,512]{1,0:T(8,128)(2,1)S(1)}) custom-call(bf16[256,2048]{1,0:T(8,128)(2,1)S(1)} %copy-done.1, f32[1,2048]{1,0:T(1,128)S(1)} %bitcast.108, bf16[2048,1536]{1,0:T(8,128)(2,1)S(1)} %copy-done.2, ...), custom_call_target="tpu_custom_call" | custom-call | flops 1048576 | bytes 65536 | tf_op jit(solution)/shard_map/attention/pallas_call | solution.py:97
  27.4 28.7 %copy.59 = bf16[2048,2,1408]{0,2,1:T(8,128)(2,1)} copy(bf16[2048,2,1408]{2,1,0:T(2,128)(2,1)} %param.26) | data formatting | bytes 23068672 | tf_op jit(solution)/shard_map/optimization_barrier | solution.py:567
  56.2 12.7 %copy.75 = bf16[2048,2,4,352]{0,3,1,2:T(8,128)(2,1)} copy(bf16[2048,2,4,352]{0,3,2,1:T(8,128)(2,1)} %bitcast.114) | data formatting | bytes 23068672 | tf_op jit(solution)/shard_map/reshape | solution.py:572
  71.4 6.9 %pad_maximum_fusion.1.w2_ref.refs_6_.refs_8_ = bf16[12,352,2048]{2,1,0:T(8,128)(2,1)} fusion(bf16[4,352,2048]{2,1,0:T(8,128)(2,1)S(1)} %bitcast.123, bf16[8,352,2048]{2,1,0:T(8,128)(2,1)S(1)} %bitcast.119), kind=kLoop, calls=%fused_computation.1 | loop fusion | flops 8650752 | bytes 34603008 | tf_op jit(solution)/shard_map/concatenate | solution.py:575
  78.3 24.6 %pad_maximum_fusion.w1_ref.refs_5_.refs_7_ = bf16[12,2,352,2048]{3,2,1,0:T(8,128)(2,1)} fusion(bf16[4,2,352,2048]{3,2,1,0:T(8,128)(2,1)} %bitcast.115, bf16[8,2,352,2048]{3,2,1,0:T(8,128)(2,1)} %bitcast.116), kind=kLoop, calls=%fused_computation | loop fusion | flops 17301504 | bytes 69206016 | tf_op jit(solution)/shard_map/concatenate | solution.py:569
  102.9 3.8 all-gather.6.cloned.1.call-done
  106.7 7.9 %split_rounded.1 = (bf16[2048,2048]{1,0:T(8,128)(2,1)S(1)}, f32[8,8,256]{2,1,0:T(8,128)S(1)}) custom-call(f32[8,264,2048]{2,1,0:T(8,128)} %bitcast.117), custom_call_target="tpu_custom_call" | custom-call | tf_op jit(solution)/shard_map/split_rounded/pallas_call | solution.py:473
  114.6 3.2 copy-done
  127.3 39.3 %own_mlp.1 = (f32[256,2048]{1,0:T(8,128)}, f32[256,2048]{1,0:T(8,128)}, f32[1,256]{1,0:T(1,128)}) custom-call(bf16[256,2048]{1,0:T(8,128)(2,1)} %copy-done.7, bf16[256,2048]{1,0:T(8,128)(2,1)} %cot_ref.3, f32[8,1,256]{2,1,0:T(1,128)} %broadcast_in_dim.44.route_ref, bf16[16,2048]{1,0:T(8,128)(2,1)} %broadcast_in_dim.43.gate_ref.refs_4_.refs_6_, ...), custom_call_target="tpu_custom_call" | custom-call | flops 1048576 | bytes 65536 | tf_op jit(solution)/shard_map/own_mlp/pallas_call | solution.py:318
  179.2 4.8 collective-permute-start.10
  184.8 23.4 %chip_hidden.4 = (bf16[6,704,2048]{2,1,0:T(8,128)(2,1)}, bf16[6,352,2048]{2,1,0:T(8,128)(2,1)}, bf16[2048,512]{1,0:T(8,128)(2,1)}) custom-call(s32[3]{0:T(128)} %pad_add_fusion.3.at_ref, f32[256,2048]{1,0:T(8,128)} %collective-permute-done.1.refs_0_, f32[256,2048]{1,0:T(8,128)} %collective-permute-done.6.refs_1_, bf16[2048,2048]{1,0:T(8,128)(2,1)} %copy-done, ...), custom_call_target="tpu_custom_call" | custom-call | flops 1048576 | bytes 65536 | tf_op jit(solution)/shard_map/chip_hidden/pallas_call | solution.py:392
  210.6 23.0 %chip_hidden.5 = (bf16[6,704,2048]{2,1,0:T(8,128)(2,1)}, bf16[6,352,2048]{2,1,0:T(8,128)(2,1)}, bf16[2048,512]{1,0:T(8,128)(2,1)}) custom-call(s32[3]{0:T(128)} %pad_add_fusion.4.at_ref, f32[256,2048]{1,0:T(8,128)} %collective-permute-done.2.refs_0_, ...), custom_call_target="tpu_custom_call", output_to_operand_aliasing={{0}: (8, {}), {1}: (9, {}), {2}: (10, {})} | custom-call | flops 1048576 | bytes 65536 | tf_op jit(solution)/shard_map/chip_hidden/pallas_call | solution.py:392
  233.5 23.1 %chip_hidden.6 = (bf16[6,704,2048]{2,1,0:T(8,128)(2,1)}, bf16[6,352,2048]{2,1,0:T(8,128)(2,1)}, bf16[2048,512]{1,0:T(8,128)(2,1)}) custom-call(s32[3]{0:T(128)} %pad_add_fusion.2.at_ref, f32[128,2048]{1,0:T(8,128)} %collective-permute-done.4.refs_0_, ...), custom_call_target="tpu_custom_call", output_to_operand_aliasing={{0}: (10, {}), {1}: (11, {}), {2}: (12, {})} | custom-call | flops 1048576 | bytes 65536 | tf_op jit(solution)/shard_map/chip_hidden/pallas_call | solution.py:392
  256.6 23.0 %chip_hidden.7 = (bf16[6,704,2048]{2,1,0:T(8,128)(2,1)}, bf16[6,352,2048]{2,1,0:T(8,128)(2,1)}, bf16[2048,512]{1,0:T(8,128)(2,1)}) custom-call(s32[3]{0:T(128)} %pad_add_fusion.at_ref, f32[256,2048]{1,0:T(8,128)} %copy-done.9, f32[256,2048]{1,0:T(8,128)} %collective-permute-done.refs_1_, ...), custom_call_target="tpu_custom_call", output_to_operand_aliasing={{0}: (8, {}), {1}: (9, {}), {2}: (10, {})} | custom-call | flops 1048576 | bytes 65536 | tf_op jit(solution)/shard_map/chip_hidden/pallas_call | solution.py:392
  279.7 20.1 %weight_grads.1 = (f32[6,2,352,256]{3,2,1,0:T(8,128)}, f32[6,2,352,256]{3,2,1,0:T(8,128)}, f32[6,352,256]{2,1,0:T(8,128)}, f32[6,352,256]{2,1,0:T(8,128)}) custom-call(s32[3]{0:T(128)} %pad_add_fusion.at_ref, bf16[6,704,2048]{2,1,0:T(8,128)(2,1)} %get-tuple-element.120.mix_grad_ref, bf16[6,352,2048]{2,1,0:T(8,128)(2,1)} %get-tuple-element.121.weighted_ref, ...), custom_call_target="tpu_custom_call" | custom-call | flops 1048576 | bytes 65536 | tf_op jit(solution)/shard_map/weight_grads/pallas_call | solution.py:442
  299.8 3.5 all-reduce.6.cloned.1.call-done.total_ref
  305.1 13.3 %attention_back.1 = (f32[256,2048]{1,0:T(8,128)}, f32[256,2048]{1,0:T(8,128)}, bf16[2,256,1024]{2,1,0:T(8,128)(2,1)S(1)}, bf16[256,1536]{1,0:T(8,128)(2,1)S(1)},...) custom-call(f32[256,2048]{1,0:T(8,128)} %all-reduce.6.cloned.1.call-done.total_ref, f32[256,2048]{1,0:T(8,128)} %copy-done.5, ...), custom_call_target="tpu_custom_call" | custom-call | flops 1048576 | bytes 65536 | tf_op jit(solution)/shard_map/attention_back/pallas_call | solution.py:218
  326.5 3.6 fusion.4
  345.8 3.9 add.159
  352.1 85.2 %psum.23 = f32[12288]{0:T(1024)S(1)} all-reduce(f32[12288]{0:T(1024)S(1)} %pad_maximum_fusion.5), channel_id=1, replica_groups=mesh['dp'=8,'tensor'=4] {'dp','tensor'}, use_global_device_ids=true, to_apply=%region_6.7 | all-reduce | flops 12288 | bytes 98304 | tf_op jit(solution)/shard_map/psum | solution.py:660
  439.1 3.5 fusion.2
  450.9 6.0 %add.161 = f32[2,2,256,1536]{3,2,1,0:T(8,128)S(1)} add(f32[2,2,256,1536]{3,2,1,0:T(8,128)} %fusion.2, f32[2,2,256,1536]{3,2,1,0:T(8,128)} %collective-permute-done.13) | non-fusion elementwise | flops 1572864 | bytes 18874368 | tf_op jit(solution)/shard_map/add | solution.py:663
  468.4 3.0 fusion
  479.9 5.5 copy.71
  486.8 18.8 %collective-permute-done.18 = f32[2,256,256]{2,1,0:T(8,128)S(1)} collective-permute-done((f32[2,256,256]{2,1,0:T(8,128)}, f32[2,256,256]{2,1,0:T(8,128)S(1)}, u32[]{:S(2)}, u32[]{:S(2)}) %collective-permute-start.18) | collective-permute-done | bytes 524320 | tf_op jit(solution)/shard_map/ppermute | solution.py:493
  518.1 3.0 add.166
  526.5 6.3 %collective-permute-done.20 = f32[256,768]{1,0:T(8,128)} collective-permute-done((f32[256,768]{1,0:T(8,128)}, f32[256,768]{1,0:T(8,128)}, u32[]{:S(2)}, u32[]{:S(2)}) %collective-permute-start.20) | collective-permute-done | bytes 786464 | tf_op jit(solution)/shard_map/ppermute | solution.py:493
  534.0 6.4 %collective-permute-done.21 = f32[256,768]{1,0:T(8,128)S(1)} collective-permute-done((f32[256,768]{1,0:T(8,128)}, f32[256,768]{1,0:T(8,128)S(1)}, u32[]{:S(2)}, u32[]{:S(2)}) %collective-permute-start.21) | collective-permute-done | bytes 786464 | tf_op jit(solution)/shard_map/ppermute | solution.py:493
  541.8 3.6 add_convert_fusion
  545.4 22.2 %collective-permute-done.19 = f32[256,2048]{1,0:T(8,128)} collective-permute-done((f32[256,2048]{1,0:T(8,128)S(1)}, f32[256,2048]{1,0:T(8,128)}, u32[]{:S(2)}, u32[]{:S(2)}) %collective-permute-start.19) | collective-permute-done | bytes 2097184 | tf_op jit(solution)/shard_map/ppermute | solution.py:668
  567.6 3.0 add_convert_fusion.1
  (265 shorter events, 113.6 us)
Async XLA Ops:
  8.0 98.7 %all-gather.6.cloned.1.call-start = ((), (), s32[]{:S(2)}) async-start(), calls=%async_computation.5 | async-start | bytes 19464192 | tf_op jit(solution)/shard_map/all_gather | solution.py:550
  11.7 106.8 %all-reduce.4.cloned.1.call-start = ((), (), s32[]{:S(2)}) async-start(), calls=%async_computation.1 | async-start | bytes 4194304 | tf_op jit(solution)/shard_map/psum | solution.py:568
  123.3 55.4 %copy-start.9 = (f32[256,2048]{1,0:T(8,128)}, f32[256,2048]{1,0:T(8,128)S(1)}, u32[]{:S(2)}) copy-start(f32[256,2048]{1,0:T(8,128)S(1)} %get-tuple-element.94.refs_0_) | copy-start | bytes 6291460
  123.3 48.5 %collective-permute-start.1 = (f32[256,2048]{1,0:T(8,128)S(1)}, f32[256,2048]{1,0:T(8,128)}, u32[]{:S(2)}, u32[]{:S(2)}) collective-permute-start(f32[256,2048]{1,0:T(8,128)S(1)} %get-tuple-element.94.refs_0_), channel_id=1, source_target_pairs={{0,8},{4,12},{8,0},{12,4},{16,24},{20,28},{24,16},{28,20},{1,9},{5... | collective-permute-start | bytes 6291464 | tf_op jit(solution)/shard_map/ppermute | solution.py:493
  124.8 47.6 %collective-permute-start.2 = (f32[256,2048]{1,0:T(8,128)S(1)}, f32[256,2048]{1,0:T(8,128)}, u32[]{:S(2)}, u32[]{:S(2)}) collective-permute-start(f32[256,2048]{1,0:T(8,128)S(1)} %get-tuple-element.94.refs_0_), channel_id=1, source_target_pairs={{0,16},{4,20},{8,24},{12,28},{16,0},{20,4},{24,8},{28,12},{1,17},{... | collective-permute-start | bytes 6291464 | tf_op jit(solution)/shard_map/ppermute | solution.py:493
  167.9 135.4 %all-reduce.6.cloned.1.call-start = ((), (), s32[]{:S(2)}) async-start(), calls=%async_computation.2 | async-start | bytes 4194304 | tf_op jit(solution)/shard_map/psum | solution.py:587
  167.9 1.5 collective-permute-start.3
  172.4 6.8 %collective-permute-start.6 = (f32[256,2048]{1,0:T(8,128)}, f32[256,2048]{1,0:T(8,128)}, u32[]{:S(2)}, u32[]{:S(2)}) collective-permute-start(f32[256,2048]{1,0:T(8,128)} %collective-permute-done.1.refs_0_), channel_id=1, source_target_pairs={{0,4},{4,0},{8,12},{12,8},{16,20},{20,16},{24,28},{28,24},{1,5},{5... | collective-permute-start | bytes 6291464 | tf_op jit(solution)/shard_map/ppermute | solution.py:493
  174.7 33.5 %collective-permute-start.4 = (f32[128,2048]{1,0:T(8,128)}, f32[128,2048]{1,0:T(8,128)}, u32[]{:S(2)}, u32[]{:S(2)}) collective-permute-start(f32[128,2048]{1,0:T(8,128)} %slice.94), channel_id=1, source_target_pairs={{0,16},{4,20},{8,24},{12,28},{16,0},{20,4},{24,8},{28,12},{1,17},{... | collective-permute-start | bytes 3145736 | tf_op jit(solution)/shard_map/ppermute | solution.py:493
  178.1 30.0 %collective-permute-start.5 = (f32[128,2048]{1,0:T(8,128)}, f32[128,2048]{1,0:T(8,128)}, u32[]{:S(2)}, u32[]{:S(2)}) collective-permute-start(f32[128,2048]{1,0:T(8,128)} %slice.95), channel_id=1, source_target_pairs={{0,8},{4,12},{8,0},{12,4},{16,24},{20,28},{24,16},{28,20},{1,9},{5... | collective-permute-start | bytes 3145736 | tf_op jit(solution)/shard_map/ppermute | solution.py:493
  178.7 31.9 %collective-permute-start.9 = (f32[256,2048]{1,0:T(8,128)}, f32[256,2048]{1,0:T(8,128)}, u32[]{:S(2)}, u32[]{:S(2)}) collective-permute-start(f32[256,2048]{1,0:T(8,128)} %collective-permute-done.2.refs_0_), channel_id=1, source_target_pairs={{0,4},{4,0},{8,12},{12,8},{16,20},{20,16},{24,28},{28,24},{1,5},{5... | collective-permute-start | bytes 6291464 | tf_op jit(solution)/shard_map/ppermute | solution.py:493
  178.7 77.9 %collective-permute-start = (f32[256,2048]{1,0:T(8,128)S(1)}, f32[256,2048]{1,0:T(8,128)}, u32[]{:S(2)}, u32[]{:S(2)}) collective-permute-start(f32[256,2048]{1,0:T(8,128)S(1)} %get-tuple-element.94.refs_0_), channel_id=1, source_target_pairs={{0,4},{4,0},{8,12},{12,8},{16,20},{20,16},{24,28},{28,24},{1,5},{5... | collective-permute-start | bytes 6291464 | tf_op jit(solution)/shard_map/ppermute | solution.py:493
  179.2 120.6 %collective-permute-start.10 = (f32[256,2048]{1,0:T(8,128)}, f32[256,2048]{1,0:T(8,128)}, u32[]{:S(2)}, u32[]{:S(2)}) collective-permute-start(f32[256,2048]{1,0:T(8,128)} %get-tuple-element.141), channel_id=1, source_target_pairs={{0,1},{3,2},{4,5},{7,6},{8,9},{11,10},{12,13},{15,14},{16,17},{19,... | collective-permute-start | bytes 6291464 | tf_op jit(solution)/shard_map/ppermute | solution.py:590
  184.0 265.1 %reduce-scatter.2.cloned.1.call-start = ((), (), s32[]{:S(2)}) async-start(), calls=%async_computation.3 | async-start | bytes 2621440 | tf_op jit(solution)/shard_map/reduce_scatter | solution.py:620
  208.2 25.4 %collective-permute-start.7 = (f32[128,2048]{1,0:T(8,128)}, f32[128,2048]{1,0:T(8,128)}, u32[]{:S(2)}, u32[]{:S(2)}) collective-permute-start(f32[128,2048]{1,0:T(8,128)} %collective-permute-done.4.refs_0_), channel_id=1, source_target_pairs={{0,4},{4,0},{8,12},{12,8},{16,20},{20,16},{24,28},{28,24},{1,5},{5... | collective-permute-start | bytes 3145736 | tf_op jit(solution)/shard_map/ppermute | solution.py:493
  208.3 25.3 %collective-permute-start.8 = (f32[128,2048]{1,0:T(8,128)}, f32[128,2048]{1,0:T(8,128)}, u32[]{:S(2)}, u32[]{:S(2)}) collective-permute-start(f32[128,2048]{1,0:T(8,128)} %collective-permute-done.5.refs_1_), channel_id=1, source_target_pairs={{0,4},{4,0},{8,12},{12,8},{16,20},{20,16},{24,28},{28,24},{1,5},{5... | collective-permute-start | bytes 3145736 | tf_op jit(solution)/shard_map/ppermute | solution.py:493
  321.2 1.2 collective-permute-start.11
  330.1 120.8 %collective-permute-start.13 = (f32[2,2,256,1536]{3,2,1,0:T(8,128)}, f32[2,2,256,1536]{3,2,1,0:T(8,128)}, u32[]{:S(2)}, u32[]{:S(2)}) collective-permute-start(f32[2,2,256,1536]{3,2,1,0:T(8,128)} %fusion.4), channel_id=1, source_target_pairs={{0,4},{4,0},{8,12},{12,8},{16,20},{20,16},{24,28},{28,24},{1,5},{5... | collective-permute-start | bytes 18874376 | tf_op jit(solution)/shard_map/ppermute | solution.py:493
  330.3 211.5 %all-gather.4.cloned.1.call-start = ((), (), s32[]{:S(2)}) async-start(), calls=%async_computation.4 | async-start | bytes 2621440 | tf_op jit(solution)/shard_map/all_gather | solution.py:626
  332.7 109.9 %collective-permute-start.25 = (f32[6,352,256]{2,1,0:T(8,128)}, f32[6,352,256]{2,1,0:T(8,128)}, u32[]{:S(2)}, u32[]{:S(2)}) collective-permute-start(f32[6,352,256]{2,1,0:T(8,128)} %get-tuple-element.161), channel_id=1, source_target_pairs={{0,4},{4,0},{8,12},{12,8},{16,20},{20,16},{24,28},{28,24},{1,5},{5... | collective-permute-start | bytes 6488072 | tf_op jit(solution)/shard_map/ppermute | solution.py:628
  333.1 131.1 %collective-permute-start.24 = (f32[6,2,352,256]{3,2,1,0:T(8,128)}, f32[6,2,352,256]{3,2,1,0:T(8,128)}, u32[]{:S(2)}, u32[]{:S(2)}) collective-permute-start(f32[6,2,352,256]{3,2,1,0:T(8,128)} %get-tuple-element.159), channel_id=1, source_target_pairs={{0,4},{4,0},{8,12},{12,8},{16,20},{20,16},{24,28},{28,24},{1,5},{5... | collective-permute-start | bytes 12976136 | tf_op jit(solution)/shard_map/ppermute | solution.py:628
  345.4 105.4 %collective-permute-start.14 = (f32[2,2,256,512]{3,2,1,0:T(8,128)}, f32[2,2,256,512]{3,2,1,0:T(8,128)}, u32[]{:S(2)}, u32[]{:S(2)}) collective-permute-start(f32[2,2,256,512]{3,2,1,0:T(8,128)} %fusion.8), channel_id=1, source_target_pairs={{0,4},{4,0},{8,12},{12,8},{16,20},{20,16},{24,28},{28,24},{1,5},{5... | collective-permute-start | bytes 6291464 | tf_op jit(solution)/shard_map/ppermute | solution.py:493
  349.7 137.1 %collective-permute-start.12 = (f32[256,2048]{1,0:T(8,128)}, f32[256,2048]{1,0:T(8,128)}, u32[]{:S(2)}, u32[]{:S(2)}) collective-permute-start(f32[256,2048]{1,0:T(8,128)} %add.159), channel_id=1, source_target_pairs={{1,2},{2,1},{5,6},{6,5},{9,10},{10,9},{13,14},{14,13},{17,18},{18,... | collective-permute-start | bytes 6291464 | tf_op jit(solution)/shard_map/ppermute | solution.py:656
  458.8 49.1 %collective-permute-start.16 = (f32[2,256,768]{2,1,0:T(8,128)}, f32[2,256,768]{2,1,0:T(8,128)}, u32[]{:S(2)}, u32[]{:S(2)}) collective-permute-start(f32[2,256,768]{2,1,0:T(8,128)} %dynamic-slice_bitcast_fusion), channel_id=1, source_target_pairs={{0,16},{4,20},{8,24},{12,28},{16,0},{20,4},{24,8},{28,12},{1,17},{... | collective-permute-start | bytes 4718600 | tf_op jit(solution)/shard_map/ppermute | solution.py:493
  462.4 45.6 %collective-permute-start.15 = (f32[2,256,768]{2,1,0:T(8,128)}, f32[2,256,768]{2,1,0:T(8,128)}, u32[]{:S(2)}, u32[]{:S(2)}) collective-permute-start(f32[2,256,768]{2,1,0:T(8,128)} %dynamic-slice_bitcast_fusion.1), channel_id=1, source_target_pairs={{0,8},{4,12},{8,0},{12,4},{16,24},{20,28},{24,16},{28,20},{1,9},{5... | collective-permute-start | bytes 4718600 | tf_op jit(solution)/shard_map/ppermute | solution.py:493
  474.7 30.9 %collective-permute-start.18 = (f32[2,256,256]{2,1,0:T(8,128)}, f32[2,256,256]{2,1,0:T(8,128)S(1)}, u32[]{:S(2)}, u32[]{:S(2)}) collective-permute-start(f32[2,256,256]{2,1,0:T(8,128)} %dynamic-slice_bitcast_fusion.4), channel_id=1, source_target_pairs={{0,16},{4,20},{8,24},{12,28},{16,0},{20,4},{24,8},{28,12},{1,17},{... | collective-permute-start | bytes 1572872 | tf_op jit(solution)/shard_map/ppermute | solution.py:493
  476.5 31.4 %collective-permute-start.17 = (f32[2,256,256]{2,1,0:T(8,128)}, f32[2,256,256]{2,1,0:T(8,128)S(1)}, u32[]{:S(2)}, u32[]{:S(2)}) collective-permute-start(f32[2,256,256]{2,1,0:T(8,128)} %dynamic-slice_bitcast_fusion.5), channel_id=1, source_target_pairs={{0,8},{4,12},{8,0},{12,4},{16,24},{20,28},{24,16},{28,20},{1,9},{5... | collective-permute-start | bytes 1572872 | tf_op jit(solution)/shard_map/ppermute | solution.py:493
  508.9 15.7 %collective-permute-start.22 = (f32[256,256]{0,1:T(8,128)}, f32[256,256]{0,1:T(8,128)}, u32[]{:S(2)}, u32[]{:S(2)}) collective-permute-start(f32[256,256]{0,1:T(8,128)} %bitcast.54), channel_id=1, source_target_pairs={{0,16},{4,20},{8,24},{12,28},{16,0},{20,4},{24,8},{28,12},{1,17},{... | collective-permute-start | bytes 786440 | tf_op jit(solution)/shard_map/ppermute | solution.py:493
  511.2 14.4 %collective-permute-start.23 = (f32[256,256]{0,1:T(8,128)}, f32[256,256]{0,1:T(8,128)S(1)}, u32[]{:S(2)}, u32[]{:S(2)}) collective-permute-start(f32[256,256]{0,1:T(8,128)} %bitcast.57), channel_id=1, source_target_pairs={{0,8},{4,12},{8,0},{12,4},{16,24},{20,28},{24,16},{28,20},{1,9},{5... | collective-permute-start | bytes 786440 | tf_op jit(solution)/shard_map/ppermute | solution.py:493
  515.7 17.0 %collective-permute-start.20 = (f32[256,768]{1,0:T(8,128)}, f32[256,768]{1,0:T(8,128)}, u32[]{:S(2)}, u32[]{:S(2)}) collective-permute-start(f32[256,768]{1,0:T(8,128)} %dynamic-slice_bitcast_fusion.3), channel_id=1, source_target_pairs={{0,16},{4,20},{8,24},{12,28},{16,0},{20,4},{24,8},{28,12},{1,17},{... | collective-permute-start | bytes 2359304 | tf_op jit(solution)/shard_map/ppermute | solution.py:493
  521.1 46.5 %collective-permute-start.19 = (f32[256,2048]{1,0:T(8,128)S(1)}, f32[256,2048]{1,0:T(8,128)}, u32[]{:S(2)}, u32[]{:S(2)}) collective-permute-start(f32[256,2048]{1,0:T(8,128)S(1)} %add.166), channel_id=1, source_target_pairs={{1,0},{2,3},{5,4},{6,7},{9,8},{10,11},{13,12},{14,15},{17,16},{18,... | collective-permute-start | bytes 6291464 | tf_op jit(solution)/shard_map/ppermute | solution.py:668
  523.7 16.7 %collective-permute-start.21 = (f32[256,768]{1,0:T(8,128)}, f32[256,768]{1,0:T(8,128)S(1)}, u32[]{:S(2)}, u32[]{:S(2)}) collective-permute-start(f32[256,768]{1,0:T(8,128)} %dynamic-slice_bitcast_fusion.2), channel_id=1, source_target_pairs={{0,8},{4,12},{8,0},{12,4},{16,24},{20,28},{24,16},{28,20},{1,9},{5... | collective-permute-start | bytes 2359304 | tf_op jit(solution)/shard_map/ppermute | solution.py:493
  (57 other events, 328.1 us)
Sparse Core Ops, SparseCore 0:
  11.8 94.7 all-gather.5
Sparse Core Ops, SparseCore 1:
  27.5 88.6 all-reduce.3
  184.1 119.1 all-reduce.5
  330.4 42.7 reduce-scatter.1
  464.3 44.7 all-gather.3

commit v3 on v2

--- a/solution.py
+++ b/solution.py
@@ -159,7 +159,7 @@
     )(x, attn_sum, gain)
 
 
-def back_kernel(total_ref, residual_ref, cot_ref, gain_ref, out_weight_ref, qkv_ref, weight_ref, cos_ref, sin_ref,
+def back_kernel(inner_ref, held_top_ref, got_top_ref, held_low_ref, got_low_ref, residual_ref, cot_ref, gain_ref, out_weight_ref, qkv_ref, weight_ref, cos_ref, sin_ref,
                 row_ref, col_ref, normed_grad_ref, residual_grad_ref, split_ref, projected_grad_ref, bias_ref,
                 mlp_gain_ref, branch_ref, attended_grad_ref):
     head = pl.program_id(0)
@@ -167,7 +167,12 @@
 
     @pl.when(head == 0)
     def _():
-        total, residual = total_ref[...], residual_ref[...]
+        total = jnp.where(
+            inner_ref[0] == 1,
+            jnp.concatenate([held_top_ref[...], held_low_ref[...]]),
+            jnp.concatenate([got_top_ref[...], got_low_ref[...]]),
+        )
+        residual = residual_ref[...]
         factor = lax.rsqrt(jnp.mean(residual * residual, axis=-1, keepdims=True) + EPS)
         scaled = gain_ref[...] * total
         inner = jnp.mean(scaled * residual, axis=-1, keepdims=True)
@@ -210,8 +215,8 @@
         normed_grad_ref[...] += product
 
 
-def attention_back(total, residual, cotangent, gain, out_weight, qkv, weight, cosine, sine, row, col):
-    count, width = total.shape
+def attention_back(inner, totals, residual, cotangent, gain, out_weight, qkv, weight, cosine, sine, row, col):
+    count, width = residual.shape
     dim = cosine.shape[1]
     cols = 3 * dim
     heads = qkv.shape[1] // cols
@@ -219,7 +224,8 @@
         back_kernel,
         grid=(heads,),
         in_specs=[
-            whole(count, width),
+            pl.BlockSpec(memory_space=pltpu.SMEM),
+            *[whole(count // 2, width)] * 4,
             whole(count, width),
             whole(count, width),
             whole(1, width),
@@ -253,7 +259,7 @@
         ),
         cost_estimate=LIGHT,
         name="attention_back",
-    )(total, residual, cotangent, gain, out_weight, qkv, weight, cosine, sine, row, col)
+    )(inner, *totals, residual, cotangent, gain, out_weight, qkv, weight, cosine, sine, row, col)
 
 
 def hidden(w_one, w_two, tokens, branch, route_row):
@@ -274,15 +280,16 @@
     return lax.logistic(nt(gate_rows, tokens)[:1])
 
 
-def own_kernel(experts, tok_ref, cot_ref, route_ref, gate_ref, w1_ref, w2_ref, out_ref, dx_ref, logit_ref, open_ref):
+def own_kernel(experts, tok_ref, cot_ref, route_ref, gate_ref, w1_ref, w2_ref, out_top_ref, out_low_ref, dx_top_ref,
+               dx_low_ref, logit_ref, open_ref):
     step = pl.program_id(0)
     group, units, width = w2_ref.shape
     shared = step * group >= experts
 
     @pl.when(step == 0)
     def _():
-        out_ref[...] = jnp.zeros_like(out_ref)
-        dx_ref[...] = jnp.zeros_like(dx_ref)
+        for ref in (out_top_ref, out_low_ref, dx_top_ref, dx_low_ref):
+            ref[...] = jnp.zeros_like(ref)
         logit_ref[...] = jnp.zeros_like(logit_ref)
         open_ref[...] = open_row(gate_ref[...], tok_ref[...])
 
@@ -298,8 +305,13 @@
         weighted.append(scaled)
         mix_grads.append(mix_grad)
         logit_ref[...] += jnp.where(shared, jnp.sum(act * back, axis=0, keepdims=True), 0.0)
-    out_ref[...] += tn(jnp.concatenate(weighted), w2_ref[...].reshape(group * units, width))
-    dx_ref[...] += tn(jnp.concatenate(mix_grads), w1_ref[...].reshape(group * 2 * units, width))
+    rows = out_top_ref.shape[0]
+    out = tn(jnp.concatenate(weighted), w2_ref[...].reshape(group * units, width))
+    out_top_ref[...] += out[:rows]
+    out_low_ref[...] += out[rows:]
+    dx = tn(jnp.concatenate(mix_grads), w1_ref[...].reshape(group * 2 * units, width))
+    dx_top_ref[...] += dx[:rows]
+    dx_low_ref[...] += dx[rows:]
 
     @pl.when(step == pl.num_programs(0) - 1)
     def _():
@@ -307,7 +319,8 @@
         logit = opened * (1.0 - opened) * logit_ref[...]
         logit_ref[...] = logit
         column = jnp.broadcast_to(logit, (8, logit.shape[1])).T[:, :1]
-        dx_ref[...] += column * gate_ref[:1].astype(F32)
+        dx_top_ref[...] += column[:rows] * gate_ref[:1].astype(F32)
+        dx_low_ref[...] += column[rows:] * gate_ref[:1].astype(F32)
 
 
 def own_mlp(tokens, cotangent, route, gate_rows, w1, w2):
@@ -326,10 +339,9 @@
             pl.BlockSpec((group, 2, units, width), lambda i: (i, 0, 0, 0)),
             pl.BlockSpec((group, units, width), lambda i: (i, 0, 0)),
         ],
-        out_specs=[whole(count, width), whole(count, width), whole(1, count)],
+        out_specs=[*[whole(count // 2, width)] * 4, whole(1, count)],
         out_shape=[
-            jax.ShapeDtypeStruct((count, width), F32),
-            jax.ShapeDtypeStruct((count, width), F32),
+            *[jax.ShapeDtypeStruct((count // 2, width), F32)] * 4,
             jax.ShapeDtypeStruct((1, count), F32),
         ],
         scratch_shapes=[pltpu.VMEM((1, count), F32)],
@@ -342,78 +354,82 @@
 
 
 def chip_kernel(pieces, here, at_ref, *refs):
-    token_refs, refs = refs[: 2 * pieces], refs[2 * pieces :]
+    token_refs, refs = refs[: sum(pieces)], refs[sum(pieces) :]
     cot_ref, route_ref, gate_ref, w1_ref, w2_ref = refs[:5]
     mix_grad_ref, weighted_ref, part_ref, tok_ref, open_ref = refs[-5:]
-    step = pl.program_id(0)
+    step, which = pl.program_id(0), pl.program_id(1)
     units, width = w2_ref.shape[-2:]
     cores, experts, count = route_ref.shape
     core = at_ref[0]
 
-    @pl.when(step == 0)
-    def _():
-        for owner in range(2):
-            base = count * (core if owner == 0 else 1 - core)
-            for k, ref in enumerate(token_refs[owner * pieces : (owner + 1) * pieces]):
-                rows = ref.shape[0]
-                tok_ref[pl.ds(pl.multiple_of(base + k * rows, rows), rows), :] = ref[...].astype(BF16)
-        part = part_ref.shape[1]
-        part_ref[...] = tok_ref[:, pl.ds(pl.multiple_of(at_ref[1] * part, part), part)]
-        open_ref[...] = open_row(gate_ref[...], tok_ref[...])
-
+    for chip in range(len(pieces) // 2):
+        @pl.when((step == 0) & (which == chip))
+        def _():
+            for owner in range(2):
+                base = count * (core if owner == 0 else 1 - core)
+                first = sum(pieces[: 2 * chip + owner])
+                for k, ref in enumerate(token_refs[first : first + pieces[2 * chip + owner]]):
+                    rows = ref.shape[0]
+                    tok_ref[chip, pl.ds(pl.multiple_of(base + k * rows, rows), rows), :] = ref[...].astype(BF16)
+            open_ref[chip] = open_row(gate_ref[...], tok_ref[chip])
+
+    part = part_ref.shape[1]
+    part_ref[...] = tok_ref[which, :, pl.ds(pl.multiple_of(at_ref[1] * part, part), part)]
     expert = jnp.minimum(core * here + step, experts - 1)
     route_row = jnp.concatenate([route_ref[k, pl.ds(expert, 1), :] for k in range(cores)], axis=1)
     _, _, weighted, mix_grad = hidden(
         w1_ref[...].reshape(2 * units, width),
         w2_ref[0],
-        tok_ref[...],
+        tok_ref[which],
         cot_ref[...],
-        jnp.where(step >= here, open_ref[...], route_row),
+        jnp.where(step >= here, open_ref[which], route_row),
     )
     mix_grad_ref[0] = mix_grad
     weighted_ref[0] = weighted
 
 
-def chip_hidden(at, mine, peer, cotangent, route, gate_rows, w1, w2, kept, part):
+def chip_hidden(at, tokens, cotangent, route, gate_rows, w1, w2, kept, part):
     total, width = cotangent.shape
     tiles, units = w2.shape[:2]
     experts, count = route.shape[1:]
     here, shared = experts // 2, (tiles - experts) // 2
     rows = 2 * count
     own = lambda i, at: jnp.where(i < here, at[0] * here + i, experts + at[0] * shared + i - here)
-    pieces = len(mine)
-    fixed = lambda *shape: pl.BlockSpec(shape, lambda i, at: (0,) * len(shape))
+    chips = len(tokens) // 2
+    pieces = tuple(len(t) for t in tokens)
+    tokens = [v for t in tokens for v in t]
+    fixed = lambda *shape: pl.BlockSpec(shape, lambda i, j, at: (0,) * len(shape), pipeline_mode=pl.Buffered(1))
     shapes = [
         jax.ShapeDtypeStruct((here + shared, 2 * units, total), BF16),
         jax.ShapeDtypeStruct((here + shared, units, total), BF16),
         jax.ShapeDtypeStruct((total, 2 * part), BF16),
     ]
-    inputs = [*mine, *peer, cotangent, route, gate_rows, w1, w2]
+    inputs = [*tokens, cotangent, route, gate_rows, w1, w2]
     return pl.pallas_call(
         functools.partial(chip_kernel, pieces, here),
         grid_spec=pltpu.PrefetchScalarGridSpec(
             num_scalar_prefetch=1,
-            grid=(here + shared,),
+            grid=(here + shared, chips),
             in_specs=[
-                *[fixed(*v.shape) for v in (*mine, *peer)],
-                pl.BlockSpec((rows, width), lambda i, at: (at[2], 0)),
-                pl.BlockSpec((2, experts, count), lambda i, at: (at[2], 0, 0)),
+                *[fixed(*v.shape) for v in tokens],
+                pl.BlockSpec((rows, width), lambda i, j, at: (at[2 + j], 0)),
+                pl.BlockSpec((2, experts, count), lambda i, j, at: (at[2 + j], 0, 0)),
                 fixed(*gate_rows.shape),
-                pl.BlockSpec((1, 2, units, width), lambda i, at: (own(i, at), 0, 0, 0)),
-                pl.BlockSpec((1, units, width), lambda i, at: (own(i, at), 0, 0)),
+                pl.BlockSpec((1, 2, units, width), lambda i, j, at: (own(i, at), 0, 0, 0)),
+                pl.BlockSpec((1, units, width), lambda i, j, at: (own(i, at), 0, 0)),
                 *[pl.BlockSpec(memory_space=pl.ANY) for _ in kept],
             ],
             out_specs=[
-                pl.BlockSpec((1, 2 * units, rows), lambda i, at: (i, 0, at[2])),
-                pl.BlockSpec((1, units, rows), lambda i, at: (i, 0, at[2])),
-                pl.BlockSpec((rows, 2 * part), lambda i, at: (at[2], 0)),
+                pl.BlockSpec((1, 2 * units, rows), lambda i, j, at: (i, 0, at[2 + j])),
+                pl.BlockSpec((1, units, rows), lambda i, j, at: (i, 0, at[2 + j])),
+                pl.BlockSpec((rows, 2 * part), lambda i, j, at: (at[2 + j], 0)),
             ],
-            scratch_shapes=[pltpu.VMEM((rows, width), BF16), pltpu.VMEM((1, rows), F32)],
+            scratch_shapes=[pltpu.VMEM((chips, rows, width), BF16), pltpu.VMEM((chips, 1, rows), F32)],
         ),
         out_shape=shapes,
         input_output_aliases={1 + len(inputs) + k: k for k in range(len(kept))},
         compiler_params=pltpu.CompilerParams(
-            dimension_semantics=("arbitrary",), vmem_limit_bytes=VMEM_LIMIT
+            dimension_semantics=("arbitrary", "arbitrary"), vmem_limit_bytes=VMEM_LIMIT
         ),
         cost_estimate=LIGHT,
         name="chip_hidden",
@@ -493,9 +509,13 @@
     return lax.ppermute(value, "dp", [(i, i ^ bit) for i in range(8)])
 
 
-def after(source, count):
-    message = lax.ppermute(source[:8, :128], "dp", [(i, i ^ 1) for i in range(count)])
-    return jnp.isnan(message[0, 0]).astype(jnp.int32)
+def butterfly(value):
+    value = value + flip(value, 1)
+    for bit in (1, 2):
+        value = value + lax.ppermute(value, "tensor", [(i, i ^ bit) for i in range(4)])
+    for bit in (2, 4):
+        value = value + flip(value, bit)
+    return value
 
 
 def take(value, number, axis):
@@ -582,53 +602,59 @@
         beside = flip(tokens_wide, 1)
     else:
         tok_all = lax.all_gather(tokens_wide, "dp")
-    mlp_part, normed_two_part, logit_grad = own_mlp(tokens, cotangent, route, gate_rows, w1, w2)
-    normed_two_part, mlp_part = tied((normed_two_part, mlp_part))
-    normed_two_total = lax.psum(normed_two_part, "tensor")
+    mlp_top, mlp_low, grad_top, grad_low, logit_grad = own_mlp(tokens, cotangent, route, gate_rows, w1, w2)
     line = n_tensor == 4 and n_dp == 8
+    spot = lax.axis_index("tensor")
+    hide = lambda chips, tokens, kept: chip_hidden(
+        jnp.stack([core, chip, *chips]), tokens, cot_low, route_all, gate_rows, w1, w2, kept, part
+    )
     if line:
-        inwards = lax.ppermute(mlp_part, "tensor", [(0, 1), (3, 2)])
-
-    kept = []
-    pair = lambda other: jnp.stack([core, chip, other])
-    hide = lambda other, mine, peer, kept: chip_hidden(
-        pair(other), mine, peer, cot_low, route_all, gate_rows, w1, w2, kept, part
-    )
-    if n_dp == 8:
-        over_x, over_y, other = tied((over_x, over_y, (chip ^ 1) + after(normed_two_part, n_dp)))
+        is_inner = (spot == 1) | (spot == 2)
+        inwards = lambda v: lax.ppermute(v, "tensor", [(0, 1), (3, 2)])
+        across = lambda v: lax.ppermute(v, "tensor", [(1, 2), (2, 1)])
+        outwards = lambda v: lax.ppermute(v, "tensor", [(1, 0), (2, 3)])
+        ready = jnp.isnan(logit_grad[0, 0]).astype(jnp.int32)
+        over_x, over_y, ready = tied((over_x, over_y, ready))
         low, high = flip(over_x[: count // 2], 4), flip(over_y[count // 2 :], 2)
         beside_x, beside_y = flip(over_x, 1), flip(over_y, 1)
-        kept = hide(other, [over_x], [beside_x], kept)
-        low, high, kept = tied((low, high, kept))
+        got = inwards(grad_top)
+        kept = hide([chip + ready], [[tokens_wide], [beside]], [])
+        got, beside_x, beside_y, grad_low, kept = tied((got, beside_x, beside_y, grad_low, kept))
+        grad_top = grad_top + got
+        got, got_low = across(grad_top), inwards(grad_low)
+        kept = hide([chip ^ 1], [[over_x], [beside_x]], kept)
+        got, got_low, low, high, mlp_top, kept = tied((got, got_low, low, high, mlp_top, kept))
+        grad_top, grad_low = grad_top + got, grad_low + got_low
+        end_top, got_low, got = outwards(grad_top), across(grad_low), inwards(mlp_top)
         beside_low, beside_high = flip(low, 1), flip(high, 1)
-        kept = hide(chip ^ 2, [over_y], [beside_y], kept)
-        kept = hide(chip ^ 3, [low, high], [beside_low, beside_high], kept)
-        kept = hide(chip, [tokens_wide], [beside], kept)
+        kept = hide([chip ^ 2], [[over_y], [beside_y]], kept)
+        end_top, got_low, got, mlp_low, beside_low, beside_high, kept = tied(
+            (end_top, got_low, got, mlp_low, beside_low, beside_high, kept)
+        )
+        grad_low, mlp_top = grad_low + got_low, mlp_top + got
+        end_low, got, got_low = outwards(grad_low), across(mlp_top), inwards(mlp_low)
+        kept = hide([chip ^ 3], [[low, high], [beside_low, beside_high]], kept)
+        end_low, got, got_low, kept = tied((end_low, got, got_low, kept))
+        totals = [grad_top, end_top, grad_low, end_low]
     else:
+        is_inner = spot >= 0
+        kept = []
         for k in range(n_dp // 2):
-            kept = hide(k, [take(tok_all, 2 * k + core, 0)], [take(tok_all, 2 * k + 1 - core, 0)], kept)
-    one_mine, one_peer, two_mine, two_peer = weight_grads(pair(chip), *kept, cot_low)
-    if line:
-        inwards, one_peer = tied((inwards, one_peer))
-    one_mine, one_peer, two_mine, two_peer, normed_two_total = tied(
-        (one_mine, one_peer, two_mine, two_peer, normed_two_total)
-    )
+            kept = hide([k], [[take(tok_all, 2 * k + core, 0)], [take(tok_all, 2 * k + 1 - core, 0)]], kept)
+        totals = [lax.psum(v, "tensor") for v in (grad_top, grad_low)]
+        totals = [totals[0], totals[0], totals[1], totals[1]]
 
     normed_one_part, residual_grad, branch_grad, projected_grad, bias_part, mlp_gain_part = attention_back(
-        normed_two_total, residual, cotangent, gain_two, out_weight, qkv, qkv_weight, cosine, sine, row, col
+        is_inner.astype(jnp.int32)[None], totals, residual, cotangent, gain_two, out_weight, qkv, qkv_weight,
+        cosine, sine, row, col,
     )
     normed_one_total = lax.psum_scatter(normed_one_part, "tensor", scatter_dimension=0, tiled=True)
     few = count // n_tensor
     inputs = layer_input.astype(F32)
     factor_one = lax.rsqrt(jnp.mean(inputs * inputs, axis=-1, keepdims=True) + EPS)
-    mine = lambda v: lax.dynamic_slice_in_dim(v, lax.axis_index("tensor") * few, few, 0)
-    input_grad = norm_back(mine(inputs), mine(factor_one), gain_one, normed_one_total)
-    input_grad = lax.all_gather(input_grad, "tensor", axis=0, tiled=True)
-    swap = [(i, i ^ 1) for i in range(n_dp)]
-    one_peer, two_peer = lax.ppermute(one_peer, "dp", swap), lax.ppermute(two_peer, "dp", swap)
     attn_gain_part = jnp.sum(normed_one_part * inputs * factor_one, axis=0)
     shared_gate_part = jnp.sum(logit_grad[0][:, None] * tokens.astype(F32), axis=0)
-    my_slot = lax.axis_index("tensor") == jnp.arange(n_tensor)
+    my_slot = spot == jnp.arange(n_tensor)
     small = jnp.concatenate(
         [
             attn_gain_part,
@@ -637,59 +663,58 @@
             (my_slot[:, None] * bias_part).reshape(-1),
         ]
     )
-    spot = lax.axis_index("tensor")
+    swap = lambda v: lax.ppermute(v, "dp", [(i, i ^ 1) for i in range(n_dp)])
+    own_rows = lambda v: lax.dynamic_slice_in_dim(v, spot * few, few, 0)
+
     if line:
-        inwards, projected_grad = tied((inwards, projected_grad))
-    if n_dp == 8:
         def products(c):
             return (
                 tn(take(normed_one, c, 0), projected_grad).reshape(2, 2, part, -1),
                 tn(take(branch_grad, c, 0), attended).reshape(2, 2, part, -1),
             )
 
-        other = 1 - core + after(normed_one_part, n_dp)
-        sent = products(other)
-        arrived = [flip(v, 1) for v in sent]
-        if line:
-            mlp_part, sent = tied((mlp_part, sent))
-            partial = mlp_part + inwards
-            across = lax.ppermute(partial, "tensor", [(1, 2), (2, 1)])
-            small, partial = tied((small, partial))
-        else:
-            small, sent = tied((small, sent))
-        small = lax.psum(small, ("dp", "tensor"))
+        arrived = [flip(v, 1) for v in products(1 - core)]
+        small = butterfly(small.reshape(-1, 128)).reshape(-1)
         small, arrived = tied((small, arrived))
-        held = products(1 - other)
+        got, got_low, residual_grad = tied((got, got_low, residual_grad))
+        mlp_top, mlp_low = mlp_top + got, mlp_low + got_low
+        end_top, got_low = outwards(mlp_top), across(mlp_low)
+        held = products(core)
         firsts = [scatter_first(h + v, me) for h, v in zip(held, arrived, strict=True)]
+        firsts, kept = tied((firsts, kept))
         moved = [(flip(a_other, 2), flip(b_other, 4)) for _, a_other, _, b_other in firsts]
-        if line:
-            across, moved = tied((across, moved))
-            partial = partial + across
-            outwards = lax.ppermute(partial, "tensor", [(1, 0), (2, 3)])
+        one_mine, one_peer, two_mine, two_peer = weight_grads(jnp.stack([core, chip]), *kept, cot_low)
+        one_mine, one_peer, normed_one_total = tied((one_mine, one_peer, normed_one_total))
+        one_peer, two_peer = swap(one_peer), swap(two_peer)
+        input_grad = norm_back(own_rows(inputs), own_rows(factor_one), gain_one, normed_one_total)
+        input_grad, moved, end_top, got_low = tied((input_grad, moved, end_top, got_low))
+        input_grad = lax.all_gather(input_grad, "tensor", axis=0, tiled=True)
+        mlp_low = mlp_low + got_low
+        end_low = outwards(mlp_low)
         steps = [(a + a_in, b + b_in) for (a, _, b, _), (a_in, b_in) in zip(firsts, moved, strict=True)]
         qkv_weight_grad, out_weight_grad = [scatter_second(a, b, me) for a, b in steps]
         out_weight_grad = out_weight_grad.T
-        input_grad, qkv_weight_grad = tied((input_grad, qkv_weight_grad))
-        if line:
-            outwards, qkv_weight_grad = tied((outwards, qkv_weight_grad))
+        mlp_sum = jnp.where(
+            is_inner, jnp.concatenate([mlp_top, mlp_low]), jnp.concatenate([end_top, end_low])
+        )
     else:
         small = lax.psum(small, ("dp", "tensor"))
+        one_mine, one_peer, two_mine, two_peer = weight_grads(jnp.stack([core, chip]), *kept, cot_low)
+        one_peer, two_peer = swap(one_peer), swap(two_peer)
+        input_grad = norm_back(own_rows(inputs), own_rows(factor_one), gain_one, normed_one_total)
+        input_grad = lax.all_gather(input_grad, "tensor", axis=0, tiled=True)
         joint = lambda v: v.reshape(2, count, BLOCKS // 2, -1).transpose(1, 2, 0, 3).reshape(count, width)
         out_weight_grad = lax.psum_scatter(tn(attended, joint(branch_grad)), "dp", scatter_dimension=1, tiled=True)
         qkv_weight_grad = lax.psum_scatter(
             tn(joint(normed_one), projected_grad), "dp", scatter_dimension=0, tiled=True
         )
+        mlp_sum = lax.psum(jnp.concatenate([mlp_top, mlp_low]), "tensor")
 
     gains = lax.dynamic_slice(small[: 3 * width].reshape(3, width), (0, me * part), (3, part))
-    bias = take(small[3 * width :].reshape(n_tensor, heads_here, 3 * head_dim), lax.axis_index("tensor"), 0)
+    bias = take(small[3 * width :].reshape(n_tensor, heads_here, 3 * head_dim), spot, 0)
     bias_cols = 3 * head_dim // n_dp
     qkv_bias_grad = lax.dynamic_slice(bias, (0, me * bias_cols), (heads_here, bias_cols))
     input_grad = (residual_grad + input_grad).astype(BF16)
-
-    if line:
-        mlp_sum = jnp.where((spot == 1) | (spot == 2), partial, outwards)
-    else:
-        mlp_sum = lax.psum(mlp_part, "tensor")
     layer_output = (residual + mlp_sum).astype(BF16)
 
     def joined(mine, peer):

time: 588 us -> 551 us (0.937)
  blocking collectives: 85.2 us -> 0 us
  waiting for transfers between devices: 66.6 us -> 90.1 us
  starting transfers between devices: 24 us -> 47.4 us
  other arithmetic: 80.5 us -> 89.6 us
  local copies, waits for them, and re-layouts: 111 us -> 104 us
    psum x1 -> x0, blocking collectives: 85.2 us -> none  [shards(): small = lax.psum(small, ('dp', 'tensor'))]
    ppermute x7 -> x16, waiting for transfers between devices: 24.9 us -> 49.8 us  [the longest x4 36.2 us: shards(): outwards = lambda v: lax.ppermute(v, 'tensor', [(1, 0), (2, 3)])]
    ppermute x7 -> x16, starting transfers between devices: 8.64 us -> 32.6 us  [the longest x4 20 us: shards(): inwards = lambda v: lax.ppermute(v, 'tensor', [(0, 1), (3, 2)])]
    add x2 -> x12, other arithmetic: 6.97 us -> 17.3 us  [the longest x2 5.55 us: shards(): mlp_top, mlp_low = (mlp_top + got, mlp_low + got_low)]
    unnamed x117 -> x113, local copies, waits for them, and re-layouts: 29.6 us -> 24.5 us
    ppermute x19 -> x22, waiting for transfers between devices: 34.3 us -> 36.1 us  [flip(): return lax.ppermute(value, 'dp', [(i, i ^ bit) for i in range(8)])]
    ppermute x19 -> x22, starting transfers between devices: 15 us -> 14.7 us  [flip(): return lax.ppermute(value, 'dp', [(i, i ^ bit) for i in range(8)])]
  transfers between devices with their start and end apart: 31 -> 42, of which waited for: 10 -> 11; matrix products, arithmetic and copies ran while one was open for 29% -> 31% of each run, Pallas kernels for 29% -> 31%
where the time goes in v3:
time: 551 us; the launch traced here: 542 us
  Pallas kernels  182 us (33%)
  local copies, waits for them, and re-layouts  104 us (19%)
  waiting for transfers between devices  90.1 us (16%)
  other arithmetic  89.6 us (16%)
  starting transfers between devices  47.4 us (9%)
  between operations  18.6 us (3%)
  matrix products  10.5 us (2%)
    pallas_call x4, Pallas kernels, chip_hidden(): pl.pallas_call(functools.partial(chip_kernel, pieces, here), grid_spec=pl...  93.5 us
    pallas_call x1, Pallas kernels, own_mlp(): pl.pallas_call(functools.partial(own_kernel, experts), grid=(tiles // gro...  39.3 us
    ppermute x4, waiting for transfers between devices, shards(): outwards = lambda v: lax.ppermute(v, 'tensor', [(1, 0), (2, 3)])  36.2 us
    ppermute x22, waiting for transfers between devices, flip(): return lax.ppermute(value, 'dp', [(i, i ^ bit) for i in range(8)])  36.1 us
    optimization_barrier x1, local copies, waits for them, and re-layouts, shards(): attn_part, shared_gate_up = tied((attn_part, shared_gate_up))  28.8 us
    unnamed x113, local copies, waits for them, and re-layouts  24.5 us
    concatenate x1, other arithmetic, shards(): jnp.concatenate([jnp.transpose(expert_gate_up, (0, 2, 3, 1)), jnp.transpo...  24.1 us
    ppermute x4, starting transfers between devices, shards(): inwards = lambda v: lax.ppermute(v, 'tensor', [(0, 1), (3, 2)])  20 us
  transfers between devices with their start and end apart: 42, of which 11 were waited for; matrix products, arithmetic and copies ran while one was open for 31% of the time, Pallas kernels for 31%

profile of v3, /device:TPU:0, one launch (start us, length us, event | category | flops | bytes accessed | tf_op | source)
XLA Modules:
  0.0 541.6 jit_solution(1794803082902422773)
XLA Ops:
  16.5 7.1 %attention.1 = (f32[256,2048]{1,0:T(8,128)S(1)}, bf16[2,256,1024]{2,1,0:T(8,128)(2,1)S(1)}, bf16[256,1536]{1,0:T(8,128)(2,1)S(1)}, bf16[256,512]{1,0:T(8,128)(2,1)S(1)}) custom-call(bf16[256,2048]{1,0:T(8,128)(2,1)S(1)} %copy-done.1, f32[1,2048]{1,0:T(1,128)S(1)} %bitcast.117, bf16[2048,1536]{1,0:T(8,128)(2,1)S(1)} %copy-done.2, ...), custom_call_target="tpu_custom_call" | custom-call | flops 1048576 | bytes 65536 | tf_op jit(solution)/shard_map/attention/pallas_call | solution.py:97
  26.9 28.8 %copy.59 = bf16[2048,2,1408]{0,2,1:T(8,128)(2,1)} copy(bf16[2048,2,1408]{2,1,0:T(2,128)(2,1)} %param.26) | data formatting | bytes 23068672 | tf_op jit(solution)/shard_map/optimization_barrier | solution.py:587
  55.8 12.8 %copy.75 = bf16[2048,2,4,352]{0,3,1,2:T(8,128)(2,1)} copy(bf16[2048,2,4,352]{0,3,2,1:T(8,128)(2,1)} %bitcast.123) | data formatting | bytes 23068672 | tf_op jit(solution)/shard_map/reshape | solution.py:592
  71.0 6.9 %pad_maximum_fusion.1.w2_ref.refs_6_.refs_8_ = bf16[12,352,2048]{2,1,0:T(8,128)(2,1)} fusion(bf16[4,352,2048]{2,1,0:T(8,128)(2,1)S(1)} %bitcast.134, bf16[8,352,2048]{2,1,0:T(8,128)(2,1)S(1)} %bitcast.130), kind=kLoop, calls=%fused_computation.1 | loop fusion | flops 8650752 | bytes 34603008 | tf_op jit(solution)/shard_map/concatenate | solution.py:595
  77.9 24.1 %pad_maximum_fusion.w1_ref.refs_5_.refs_7_ = bf16[12,2,352,2048]{3,2,1,0:T(8,128)(2,1)} fusion(bf16[4,2,352,2048]{3,2,1,0:T(8,128)(2,1)} %bitcast.124, bf16[8,2,352,2048]{3,2,1,0:T(8,128)(2,1)} %bitcast.127), kind=kLoop, calls=%fused_computation | loop fusion | flops 17301504 | bytes 69206016 | tf_op jit(solution)/shard_map/concatenate | solution.py:589
  102.0 4.2 all-gather.6.cloned.1.call-done
  106.1 7.9 %split_rounded.1 = (bf16[2048,2048]{1,0:T(8,128)(2,1)S(1)}, f32[8,8,256]{2,1,0:T(8,128)S(1)}) custom-call(f32[8,264,2048]{2,1,0:T(8,128)} %bitcast.128), custom_call_target="tpu_custom_call" | custom-call | tf_op jit(solution)/shard_map/split_rounded/pallas_call | solution.py:489
  114.1 3.3 copy-done
  126.7 39.3 %own_mlp.1 = (f32[128,2048]{1,0:T(8,128)}, f32[128,2048]{1,0:T(8,128)}, f32[128,2048]{1,0:T(8,128)}, f32[128,2048]{1,0:T(8,128)}, f32[1,256]{1,0:T(1,128)}) custom-call(bf16[256,2048]{1,0:T(8,128)(2,1)} %copy-done.6, bf16[256,2048]{1,0:T(8,128)(2,1)} %cot_ref.3, f32[8,1,256]{2,1,0:T(1,128)} %broadcast_in_dim.48.route_ref, ...), custom_call_target="tpu_custom_call" | custom-call | flops 1048576 | bytes 65536 | tf_op jit(solution)/shard_map/own_mlp/pallas_call | solution.py:331
  172.3 4.5 collective-permute-start
  184.7 23.3 %chip_hidden.4 = (bf16[6,704,2048]{2,1,0:T(8,128)(2,1)}, bf16[6,352,2048]{2,1,0:T(8,128)(2,1)}, bf16[2048,512]{1,0:T(8,128)(2,1)}) custom-call(s32[3]{0:T(128)} %get-tuple-element.276.at_ref, f32[256,2048]{1,0:T(8,128)} %copy-done.10, f32[256,2048]{1,0:T(8,128)} %collective-permute-done.5.refs_1_, bf16[2048,2048]{1,0:T(8,128)(2,1)} %copy-done, ...), custom_call_target="tpu_custom_call" | custom-call | flops 1048576 | bytes 65536 | tf_op jit(solution)/shard_map/chip_hidden/pallas_call | solution.py:408
  211.4 3.1 collective-permute-start.7
  214.5 23.3 %chip_hidden.5 = (bf16[6,704,2048]{2,1,0:T(8,128)(2,1)}, bf16[6,352,2048]{2,1,0:T(8,128)(2,1)}, bf16[2048,512]{1,0:T(8,128)(2,1)}) custom-call(s32[3]{0:T(128)} %get-tuple-element.275.at_ref, f32[256,2048]{1,0:T(8,128)} %collective-permute-done.1.refs_0_, ...), custom_call_target="tpu_custom_call", output_to_operand_aliasing={{0}: (8, {}), {1}: (9, {}), {2}: (10, {})} | custom-call | flops 1048576 | bytes 65536 | tf_op jit(solution)/shard_map/chip_hidden/pallas_call | solution.py:408
  244.5 5.7 %collective-permute-start.12 = (f32[128,2048]{1,0:T(8,128)}, f32[128,2048]{1,0:T(8,128)}, u32[]{:S(2)}, u32[]{:S(2)}) collective-permute-start(f32[128,2048]{1,0:T(8,128)} %get-tuple-element.147), channel_id=1, source_target_pairs={{0,1},{3,2},{4,5},{7,6},{8,9},{11,10},{12,13},{15,14},{16,17},{19,... | collective-permute-start | bytes 3145736 | tf_op jit(solution)/shard_map/ppermute | solution.py:613
  250.7 23.3 %chip_hidden.6 = (bf16[6,704,2048]{2,1,0:T(8,128)(2,1)}, bf16[6,352,2048]{2,1,0:T(8,128)(2,1)}, bf16[2048,512]{1,0:T(8,128)(2,1)}) custom-call(s32[3]{0:T(128)} %get-tuple-element.274.at_ref, f32[256,2048]{1,0:T(8,128)} %collective-permute-done.2.refs_0_, ...), custom_call_target="tpu_custom_call", output_to_operand_aliasing={{0}: (8, {}), {1}: (9, {}), {2}: (10, {})} | custom-call | flops 1048576 | bytes 65536 | tf_op jit(solution)/shard_map/chip_hidden/pallas_call | solution.py:408
  274.0 3.0 add.184
  281.7 6.7 %collective-permute-start.17 = (f32[128,2048]{1,0:T(8,128)}, f32[128,2048]{1,0:T(8,128)}, u32[]{:S(2)}, u32[]{:S(2)}) collective-permute-start(f32[128,2048]{1,0:T(8,128)} %get-tuple-element.162), channel_id=1, source_target_pairs={{0,1},{3,2},{4,5},{7,6},{8,9},{11,10},{12,13},{15,14},{16,17},{19,... | collective-permute-start | bytes 3145736 | tf_op jit(solution)/shard_map/ppermute | solution.py:613
  292.7 23.5 %chip_hidden.7 = (bf16[6,704,2048]{2,1,0:T(8,128)(2,1)}, bf16[6,352,2048]{2,1,0:T(8,128)(2,1)}, bf16[2048,512]{1,0:T(8,128)(2,1)}) custom-call(s32[3]{0:T(128)} %get-tuple-element.244.at_ref, f32[128,2048]{1,0:T(8,128)} %collective-permute-done.8.refs_0_, ...), custom_call_target="tpu_custom_call", output_to_operand_aliasing={{0}: (10, {}), {1}: (11, {}), {2}: (12, {})} | custom-call | flops 1048576 | bytes 65536 | tf_op jit(solution)/shard_map/chip_hidden/pallas_call | solution.py:408
  318.6 13.4 %attention_back.1 = (f32[256,2048]{1,0:T(8,128)}, f32[256,2048]{1,0:T(8,128)}, bf16[2,256,1024]{2,1,0:T(8,128)(2,1)S(1)}, bf16[256,1536]{1,0:T(8,128)(2,1)S(1)},...) custom-call(s32[1]{0:T(128)} %bitcast.17.inner_ref, f32[128,2048]{1,0:T(8,128)S(1)} %add.182.held_top_ref, ...), custom_call_target="tpu_custom_call" | custom-call | flops 1048576 | bytes 65536 | tf_op jit(solution)/shard_map/attention_back/pallas_call | solution.py:223
  332.1 3.7 fusion.4
  341.5 4.7 collective-permute-done.18
  346.2 6.8 %collective-permute-done.19 = f32[96,128]{1,0:T(8,128)S(1)} collective-permute-done((f32[96,128]{1,0:T(8,128)S(1)}, f32[96,128]{1,0:T(8,128)S(1)}, u32[]{:S(2)}, u32[]{:S(2)}) %collective-permute-start.19) | collective-permute-done | bytes 49184 | tf_op jit(solution)/shard_map/ppermute | solution.py:515
  354.2 6.7 %collective-permute-done.20 = f32[96,128]{1,0:T(8,128)S(1)} collective-permute-done((f32[96,128]{1,0:T(8,128)S(1)}, f32[96,128]{1,0:T(8,128)S(1)}, u32[]{:S(2)}, u32[]{:S(2)}) %collective-permute-start.20) | collective-permute-done | bytes 49184 | tf_op jit(solution)/shard_map/ppermute | solution.py:515
  361.8 4.6 fusion.6
  379.5 3.6 add.198
  391.7 19.7 %weight_grads.1 = (f32[6,2,352,256]{3,2,1,0:T(8,128)}, f32[6,2,352,256]{3,2,1,0:T(8,128)}, f32[6,352,256]{2,1,0:T(8,128)}, f32[6,352,256]{2,1,0:T(8,128)}) custom-call(s32[2]{0:T(128)} %pad_add_fusion.5.at_ref, bf16[6,704,2048]{2,1,0:T(8,128)(2,1)} %get-tuple-element.191.mix_grad_ref, bf16[6,352,2048]{2,1,0:T(8,128)(2,1)} %get-tuple-element.192.weighted_ref, ...), custom_call_target="tpu_custom_call" | custom-call | flops 1048576 | bytes 65536 | tf_op jit(solution)/shard_map/weight_grads/pallas_call | solution.py:458
  416.3 20.4 %collective-permute-done.27 = f32[2,256,256]{2,1,0:T(8,128)S(1)} collective-permute-done((f32[2,256,256]{2,1,0:T(8,128)}, f32[2,256,256]{2,1,0:T(8,128)S(1)}, u32[]{:S(2)}, u32[]{:S(2)}) %collective-permute-start.27) | collective-permute-done | bytes 524320 | tf_op jit(solution)/shard_map/ppermute | solution.py:509
  475.1 3.3 collective-permute-done.33
  479.9 36.2 %collective-permute-done.31 = f32[128,2048]{1,0:T(8,128)S(1)} collective-permute-done((f32[128,2048]{1,0:T(8,128)S(1)}, f32[128,2048]{1,0:T(8,128)S(1)}, u32[]{:S(2)}, u32[]{:S(2)}) %collective-permute-start.31) | collective-permute-done | bytes 1048608 | tf_op jit(solution)/shard_map/ppermute | solution.py:615
  516.1 2.9 fusion.3
  521.5 3.4 copy.71
  527.6 3.0 fusion
  (289 shorter events, 139.7 us)
Async XLA Ops:
  8.0 98.1 %all-gather.6.cloned.1.call-start = ((), (), s32[]{:S(2)}) async-start(), calls=%async_computation.4 | async-start | bytes 19464192 | tf_op jit(solution)/shard_map/all_gather | solution.py:570
  11.2 106.8 %all-reduce.3.cloned.1.call-start = ((), (), s32[]{:S(2)}) async-start(), calls=%async_computation.1 | async-start | bytes 4194304 | tf_op jit(solution)/shard_map/psum | solution.py:588
  26.9 384.5 %reduce-scatter.2.cloned.1.call-start = ((), (), s32[]{:S(2)}) async-start(), calls=%async_computation.2 | async-start | bytes 2621440 | tf_op jit(solution)/shard_map/reduce_scatter | solution.py:651
  122.7 47.9 %collective-permute-start.1 = (f32[256,2048]{1,0:T(8,128)S(1)}, f32[256,2048]{1,0:T(8,128)}, u32[]{:S(2)}, u32[]{:S(2)}) collective-permute-start(f32[256,2048]{1,0:T(8,128)S(1)} %get-tuple-element.126.refs_0_), channel_id=1, source_target_pairs={{0,8},{4,12},{8,0},{12,4},{16,24},{20,28},{24,16},{28,20},{1,9},{5... | collective-permute-start | bytes 6291464 | tf_op jit(solution)/shard_map/ppermute | solution.py:509
  124.2 47.6 %collective-permute-start.2 = (f32[256,2048]{1,0:T(8,128)S(1)}, f32[256,2048]{1,0:T(8,128)}, u32[]{:S(2)}, u32[]{:S(2)}) collective-permute-start(f32[256,2048]{1,0:T(8,128)S(1)} %get-tuple-element.126.refs_0_), channel_id=1, source_target_pairs={{0,16},{4,20},{8,24},{12,28},{16,0},{20,4},{24,8},{28,12},{1,17},{... | collective-permute-start | bytes 6291464 | tf_op jit(solution)/shard_map/ppermute | solution.py:509
  126.1 57.9 %collective-permute-start.5 = (f32[256,2048]{1,0:T(8,128)S(1)}, f32[256,2048]{1,0:T(8,128)}, u32[]{:S(2)}, u32[]{:S(2)}) collective-permute-start(f32[256,2048]{1,0:T(8,128)S(1)} %get-tuple-element.126.refs_0_), channel_id=1, source_target_pairs={{0,4},{4,0},{8,12},{12,8},{16,20},{20,16},{24,28},{28,24},{1,5},{5... | collective-permute-start | bytes 6291464 | tf_op jit(solution)/shard_map/ppermute | solution.py:509
  171.8 36.2 %collective-permute-start.3 = (f32[256,2048]{1,0:T(8,128)}, f32[256,2048]{1,0:T(8,128)}, u32[]{:S(2)}, u32[]{:S(2)}) collective-permute-start(f32[256,2048]{1,0:T(8,128)} %collective-permute-done.1.refs_0_), channel_id=1, source_target_pairs={{0,4},{4,0},{8,12},{12,8},{16,20},{20,16},{24,28},{28,24},{1,5},{5... | collective-permute-start | bytes 6291464 | tf_op jit(solution)/shard_map/ppermute | solution.py:509
  171.8 36.2 %collective-permute-start.4 = (f32[256,2048]{1,0:T(8,128)}, f32[256,2048]{1,0:T(8,128)}, u32[]{:S(2)}, u32[]{:S(2)}) collective-permute-start(f32[256,2048]{1,0:T(8,128)} %collective-permute-done.2.refs_0_), channel_id=1, source_target_pairs={{0,4},{4,0},{8,12},{12,8},{16,20},{20,16},{24,28},{28,24},{1,5},{5... | collective-permute-start | bytes 6291464 | tf_op jit(solution)/shard_map/ppermute | solution.py:509
  172.3 35.7 %collective-permute-start = (f32[128,2048]{1,0:T(8,128)}, f32[128,2048]{1,0:T(8,128)}, u32[]{:S(2)}, u32[]{:S(2)}) collective-permute-start(f32[128,2048]{1,0:T(8,128)} %get-tuple-element.125), channel_id=1, source_target_pairs={{0,1},{3,2},{4,5},{7,6},{8,9},{11,10},{12,13},{15,14},{16,17},{19,... | collective-permute-start | bytes 3145736 | tf_op jit(solution)/shard_map/ppermute | solution.py:613
  182.1 55.8 %collective-permute-start.8 = (f32[128,2048]{1,0:T(8,128)}, f32[128,2048]{1,0:T(8,128)}, u32[]{:S(2)}, u32[]{:S(2)}) collective-permute-start(f32[128,2048]{1,0:T(8,128)} %slice.84), channel_id=1, source_target_pairs={{0,16},{4,20},{8,24},{12,28},{16,0},{20,4},{24,8},{28,12},{1,17},{... | collective-permute-start | bytes 3145736 | tf_op jit(solution)/shard_map/ppermute | solution.py:509
  183.9 53.9 %collective-permute-start.9 = (f32[128,2048]{1,0:T(8,128)}, f32[128,2048]{1,0:T(8,128)}, u32[]{:S(2)}, u32[]{:S(2)}) collective-permute-start(f32[128,2048]{1,0:T(8,128)} %slice.85), channel_id=1, source_target_pairs={{0,8},{4,12},{8,0},{12,4},{16,24},{20,28},{24,16},{28,20},{1,9},{5... | collective-permute-start | bytes 3145736 | tf_op jit(solution)/shard_map/ppermute | solution.py:509
  209.8 28.1 %collective-permute-start.6 = (f32[128,2048]{1,0:T(8,128)S(1)}, f32[128,2048]{1,0:T(8,128)}, u32[]{:S(2)}, u32[]{:S(2)}) collective-permute-start(f32[128,2048]{1,0:T(8,128)S(1)} %add.181), channel_id=1, source_target_pairs={{1,2},{2,1},{5,6},{6,5},{9,10},{10,9},{13,14},{14,13},{17,18},{18,... | collective-permute-start | bytes 3145736 | tf_op jit(solution)/shard_map/ppermute | solution.py:614
  211.4 26.5 %collective-permute-start.7 = (f32[128,2048]{1,0:T(8,128)S(1)}, f32[128,2048]{1,0:T(8,128)}, u32[]{:S(2)}, u32[]{:S(2)}) collective-permute-start(f32[128,2048]{1,0:T(8,128)S(1)} %copy-done.39), channel_id=1, source_target_pairs={{0,1},{3,2},{4,5},{7,6},{8,9},{11,10},{12,13},{15,14},{16,17},{19,... | collective-permute-start | bytes 3145736 | tf_op jit(solution)/shard_map/ppermute | solution.py:613
  240.2 33.8 %collective-permute-start.11 = (f32[128,2048]{1,0:T(8,128)}, f32[128,2048]{1,0:T(8,128)}, u32[]{:S(2)}, u32[]{:S(2)}) collective-permute-start(f32[128,2048]{1,0:T(8,128)} %add.183), channel_id=1, source_target_pairs={{1,2},{2,1},{5,6},{6,5},{9,10},{10,9},{13,14},{14,13},{17,18},{18,... | collective-permute-start | bytes 3145736 | tf_op jit(solution)/shard_map/ppermute | solution.py:614
  243.2 30.8 %collective-permute-start.10 = (f32[128,2048]{1,0:T(8,128)S(1)}, f32[128,2048]{1,0:T(8,128)S(1)}, u32[]{:S(2)}, u32[]{:S(2)}) collective-permute-start(f32[128,2048]{1,0:T(8,128)S(1)} %add.182.held_top_ref), channel_id=1, source_target_pairs={{1,0},{2,3},{5,4},{6,7},{9,8},{10,11},{13,12},{14,15},{17,16},{18,... | collective-permute-start | bytes 3145736 | tf_op jit(solution)/shard_map/ppermute | solution.py:615
  244.5 29.5 %collective-permute-start.12 = (f32[128,2048]{1,0:T(8,128)}, f32[128,2048]{1,0:T(8,128)}, u32[]{:S(2)}, u32[]{:S(2)}) collective-permute-start(f32[128,2048]{1,0:T(8,128)} %get-tuple-element.147), channel_id=1, source_target_pairs={{0,1},{3,2},{4,5},{7,6},{8,9},{11,10},{12,13},{15,14},{16,17},{19,... | collective-permute-start | bytes 3145736 | tf_op jit(solution)/shard_map/ppermute | solution.py:613
  250.2 23.8 %collective-permute-start.13 = (f32[128,2048]{1,0:T(8,128)}, f32[128,2048]{1,0:T(8,128)}, u32[]{:S(2)}, u32[]{:S(2)}) collective-permute-start(f32[128,2048]{1,0:T(8,128)} %collective-permute-done.8.refs_0_), channel_id=1, source_target_pairs={{0,4},{4,0},{8,12},{12,8},{16,20},{20,16},{24,28},{28,24},{1,5},{5... | collective-permute-start | bytes 3145736 | tf_op jit(solution)/shard_map/ppermute | solution.py:509
  250.2 23.9 %collective-permute-start.14 = (f32[128,2048]{1,0:T(8,128)}, f32[128,2048]{1,0:T(8,128)}, u32[]{:S(2)}, u32[]{:S(2)}) collective-permute-start(f32[128,2048]{1,0:T(8,128)} %collective-permute-done.9.refs_1_), channel_id=1, source_target_pairs={{0,4},{4,0},{8,12},{12,8},{16,20},{20,16},{24,28},{28,24},{1,5},{5... | collective-permute-start | bytes 3145736 | tf_op jit(solution)/shard_map/ppermute | solution.py:509
  277.0 39.2 %collective-permute-start.16 = (f32[128,2048]{1,0:T(8,128)}, f32[128,2048]{1,0:T(8,128)}, u32[]{:S(2)}, u32[]{:S(2)}) collective-permute-start(f32[128,2048]{1,0:T(8,128)} %add.184), channel_id=1, source_target_pairs={{1,2},{2,1},{5,6},{6,5},{9,10},{10,9},{13,14},{14,13},{17,18},{18,... | collective-permute-start | bytes 3145736 | tf_op jit(solution)/shard_map/ppermute | solution.py:614
  280.4 35.9 %collective-permute-start.15 = (f32[128,2048]{1,0:T(8,128)S(1)}, f32[128,2048]{1,0:T(8,128)}, u32[]{:S(2)}, u32[]{:S(2)}) collective-permute-start(f32[128,2048]{1,0:T(8,128)S(1)} %add.185.held_low_ref), channel_id=1, source_target_pairs={{1,0},{2,3},{5,4},{6,7},{9,8},{10,11},{13,12},{14,15},{17,16},{18,... | collective-permute-start | bytes 3145736 | tf_op jit(solution)/shard_map/ppermute | solution.py:615
  281.7 34.6 %collective-permute-start.17 = (f32[128,2048]{1,0:T(8,128)}, f32[128,2048]{1,0:T(8,128)}, u32[]{:S(2)}, u32[]{:S(2)}) collective-permute-start(f32[128,2048]{1,0:T(8,128)} %get-tuple-element.162), channel_id=1, source_target_pairs={{0,1},{3,2},{4,5},{7,6},{8,9},{11,10},{12,13},{15,14},{16,17},{19,... | collective-permute-start | bytes 3145736 | tf_op jit(solution)/shard_map/ppermute | solution.py:613
  335.8 41.7 %collective-permute-start.23 = (f32[2,2,256,1536]{3,2,1,0:T(8,128)}, f32[2,2,256,1536]{3,2,1,0:T(8,128)}, u32[]{:S(2)}, u32[]{:S(2)}) collective-permute-start(f32[2,2,256,1536]{3,2,1,0:T(8,128)} %fusion.4), channel_id=1, source_target_pairs={{0,4},{4,0},{8,12},{12,8},{16,20},{20,16},{24,28},{28,24},{1,5},{5... | collective-permute-start | bytes 18874376 | tf_op jit(solution)/shard_map/ppermute | solution.py:509
  338.6 38.9 %collective-permute-start.24 = (f32[2,2,256,512]{3,2,1,0:T(8,128)}, f32[2,2,256,512]{3,2,1,0:T(8,128)}, u32[]{:S(2)}, u32[]{:S(2)}) collective-permute-start(f32[2,2,256,512]{3,2,1,0:T(8,128)} %fusion.10), channel_id=1, source_target_pairs={{0,4},{4,0},{8,12},{12,8},{16,20},{20,16},{24,28},{28,24},{1,5},{5... | collective-permute-start | bytes 6291464 | tf_op jit(solution)/shard_map/ppermute | solution.py:509
  339.1 191.5 %all-gather.4.cloned.1.call-start = ((), (), s32[]{:S(2)}) async-start(), calls=%async_computation.3 | async-start | bytes 2621440 | tf_op jit(solution)/shard_map/all_gather | solution.py:691
  371.5 41.6 %collective-permute-start.29 = (f32[128,2048]{1,0:T(8,128)}, f32[128,2048]{1,0:T(8,128)}, u32[]{:S(2)}, u32[]{:S(2)}) collective-permute-start(f32[128,2048]{1,0:T(8,128)} %add.186), channel_id=1, source_target_pairs={{1,0},{2,3},{5,4},{6,7},{9,8},{10,11},{13,12},{14,15},{17,16},{18,... | collective-permute-start | bytes 3145736 | tf_op jit(solution)/shard_map/ppermute | solution.py:615
  375.6 38.5 %collective-permute-start.30 = (f32[128,2048]{1,0:T(8,128)}, f32[128,2048]{1,0:T(8,128)}, u32[]{:S(2)}, u32[]{:S(2)}) collective-permute-start(f32[128,2048]{1,0:T(8,128)} %add.187), channel_id=1, source_target_pairs={{1,2},{2,1},{5,6},{6,5},{9,10},{10,9},{13,14},{14,13},{17,18},{18,... | collective-permute-start | bytes 3145736 | tf_op jit(solution)/shard_map/ppermute | solution.py:614
  389.5 60.0 %collective-permute-start.25 = (f32[2,256,768]{2,1,0:T(8,128)}, f32[2,256,768]{2,1,0:T(8,128)}, u32[]{:S(2)}, u32[]{:S(2)}) collective-permute-start(f32[2,256,768]{2,1,0:T(8,128)} %get-tuple-element.197), channel_id=1, source_target_pairs={{0,8},{4,12},{8,0},{12,4},{16,24},{20,28},{24,16},{28,20},{1,9},{5... | collective-permute-start | bytes 4718600 | tf_op jit(solution)/shard_map/ppermute | solution.py:509
  390.5 58.9 %collective-permute-start.26 = (f32[2,256,768]{2,1,0:T(8,128)}, f32[2,256,768]{2,1,0:T(8,128)}, u32[]{:S(2)}, u32[]{:S(2)}) collective-permute-start(f32[2,256,768]{2,1,0:T(8,128)} %get-tuple-element.198), channel_id=1, source_target_pairs={{0,16},{4,20},{8,24},{12,28},{16,0},{20,4},{24,8},{28,12},{1,17},{... | collective-permute-start | bytes 4718600 | tf_op jit(solution)/shard_map/ppermute | solution.py:509
  411.4 107.6 %collective-permute-start.36 = (f32[6,2,352,256]{3,2,1,0:T(8,128)}, f32[6,2,352,256]{3,2,1,0:T(8,128)}, u32[]{:S(2)}, u32[]{:S(2)}) collective-permute-start(f32[6,2,352,256]{3,2,1,0:T(8,128)} %get-tuple-element.215), channel_id=1, source_target_pairs={{0,4},{4,0},{8,12},{12,8},{16,20},{20,16},{24,28},{28,24},{1,5},{5... | collective-permute-start | bytes 12976136 | tf_op jit(solution)/shard_map/ppermute | solution.py:666
  413.1 23.6 %collective-permute-start.27 = (f32[2,256,256]{2,1,0:T(8,128)}, f32[2,256,256]{2,1,0:T(8,128)S(1)}, u32[]{:S(2)}, u32[]{:S(2)}) collective-permute-start(f32[2,256,256]{2,1,0:T(8,128)} %get-tuple-element.199), channel_id=1, source_target_pairs={{0,8},{4,12},{8,0},{12,4},{16,24},{20,28},{24,16},{28,20},{1,9},{5... | collective-permute-start | bytes 1572872 | tf_op jit(solution)/shard_map/ppermute | solution.py:509
  414.1 53.0 %collective-permute-start.37 = (f32[6,352,256]{2,1,0:T(8,128)}, f32[6,352,256]{2,1,0:T(8,128)}, u32[]{:S(2)}, u32[]{:S(2)}) collective-permute-start(f32[6,352,256]{2,1,0:T(8,128)} %get-tuple-element.217), channel_id=1, source_target_pairs={{0,4},{4,0},{8,12},{12,8},{16,20},{20,16},{24,28},{28,24},{1,5},{5... | collective-permute-start | bytes 6488072 | tf_op jit(solution)/shard_map/ppermute | solution.py:666
  464.9 51.2 %collective-permute-start.31 = (f32[128,2048]{1,0:T(8,128)S(1)}, f32[128,2048]{1,0:T(8,128)S(1)}, u32[]{:S(2)}, u32[]{:S(2)}) collective-permute-start(f32[128,2048]{1,0:T(8,128)S(1)} %add.205), channel_id=1, source_target_pairs={{1,0},{2,3},{5,4},{6,7},{9,8},{10,11},{13,12},{14,15},{17,16},{18,... | collective-permute-start | bytes 3145736 | tf_op jit(solution)/shard_map/ppermute | solution.py:615
  (66 other events, 521.9 us)
Sparse Core Ops, SparseCore 0:
  11.3 94.7 all-gather.5
Sparse Core Ops, SparseCore 1:
  27.0 88.6 all-reduce.2
  339.2 45.5 reduce-scatter.1
  449.5 56.6 all-gather.3

commit v4 on v3

--- a/solution.py
+++ b/solution.py
@@ -160,7 +160,7 @@
 
 
 def back_kernel(inner_ref, held_top_ref, got_top_ref, held_low_ref, got_low_ref, residual_ref, cot_ref, gain_ref, out_weight_ref, qkv_ref, weight_ref, cos_ref, sin_ref,
-                row_ref, col_ref, normed_grad_ref, residual_grad_ref, split_ref, projected_grad_ref, bias_ref,
+                row_ref, col_ref, x_ref, extra_ref, normed_grad_ref, residual_grad_ref, split_ref, projected_grad_ref, bias_ref,
                 mlp_gain_ref, branch_ref, attended_grad_ref):
     head = pl.program_id(0)
     dim = cos_ref.shape[1]
@@ -205,17 +205,33 @@
     projected_grad_ref[...] = grad
     bias_ref[...] = jnp.sum(grad.astype(F32), axis=0, keepdims=True)
     product = nt(grad, weight_ref[...])
+    groups, few = normed_grad_ref.shape[0], normed_grad_ref.shape[1] - 8
 
     @pl.when(head == 0)
     def _():
-        normed_grad_ref[...] = product
+        for k in range(groups):
+            normed_grad_ref[k, :few] = product[k * few : (k + 1) * few]
 
     @pl.when(head > 0)
     def _():
-        normed_grad_ref[...] += product
-
-
-def attention_back(inner, totals, residual, cotangent, gain, out_weight, qkv, weight, cosine, sine, row, col):
+        for k in range(groups):
+            normed_grad_ref[k, :few] += product[k * few : (k + 1) * few]
+
+    @pl.when(head == pl.num_programs(0) - 1)
+    def _():
+        total = jnp.zeros((1, x_ref.shape[1]), F32)
+        for k in range(groups):
+            x = x_ref[k * few : (k + 1) * few].astype(F32)
+            factor = lax.rsqrt(jnp.mean(x * x, axis=-1, keepdims=True) + EPS)
+            total += jnp.sum(normed_grad_ref[k, :few] * x * factor, axis=0, keepdims=True)
+        rows = lax.broadcasted_iota(jnp.int32, (8, x_ref.shape[1]), 0)
+        small = jnp.where(rows == 0, total, jnp.where(rows == 1, extra_ref[...], 0.0))
+        for k in range(groups):
+            normed_grad_ref[k, few:] = small
+
+
+def attention_back(inner, totals, residual, cotangent, gain, out_weight, qkv, weight, cosine, sine, row, col, x, extra,
+                   groups):
     count, width = residual.shape
     dim = cosine.shape[1]
     cols = 3 * dim
@@ -236,9 +252,11 @@
             whole(*sine.shape),
             whole(1, count),
             whole(count, 1),
+            whole(count, width),
+            whole(1, width),
         ],
         out_specs=[
-            whole(count, width),
+            whole(groups, count // groups + 8, width),
             whole(count, width),
             whole(2, count, width // 2),
             pl.BlockSpec((count, cols), lambda h: (0, h)),
@@ -246,7 +264,7 @@
             whole(1, width),
         ],
         out_shape=[
-            jax.ShapeDtypeStruct((count, width), F32),
+            jax.ShapeDtypeStruct((groups, count // groups + 8, width), F32),
             jax.ShapeDtypeStruct((count, width), F32),
             jax.ShapeDtypeStruct((2, count, width // 2), BF16),
             jax.ShapeDtypeStruct((count, heads * cols), BF16),
@@ -259,7 +277,7 @@
         ),
         cost_estimate=LIGHT,
         name="attention_back",
-    )(inner, *totals, residual, cotangent, gain, out_weight, qkv, weight, cosine, sine, row, col)
+    )(inner, *totals, residual, cotangent, gain, out_weight, qkv, weight, cosine, sine, row, col, x, extra)
 
 
 def hidden(w_one, w_two, tokens, branch, route_row):
@@ -353,36 +371,29 @@
     )(tokens, cotangent, route[:, None, :], gate_rows, w1, w2)
 
 
-def chip_kernel(pieces, here, at_ref, *refs):
-    token_refs, refs = refs[: sum(pieces)], refs[sum(pieces) :]
-    cot_ref, route_ref, gate_ref, w1_ref, w2_ref = refs[:5]
+def chip_kernel(here, at_ref, even_ref, odd_ref, cot_ref, route_ref, gate_ref, w1_ref, w2_ref, *refs):
     mix_grad_ref, weighted_ref, part_ref, tok_ref, open_ref = refs[-5:]
-    step, which = pl.program_id(0), pl.program_id(1)
+    step = pl.program_id(0)
     units, width = w2_ref.shape[-2:]
     cores, experts, count = route_ref.shape
     core = at_ref[0]
 
-    for chip in range(len(pieces) // 2):
-        @pl.when((step == 0) & (which == chip))
-        def _():
-            for owner in range(2):
-                base = count * (core if owner == 0 else 1 - core)
-                first = sum(pieces[: 2 * chip + owner])
-                for k, ref in enumerate(token_refs[first : first + pieces[2 * chip + owner]]):
-                    rows = ref.shape[0]
-                    tok_ref[chip, pl.ds(pl.multiple_of(base + k * rows, rows), rows), :] = ref[...].astype(BF16)
-            open_ref[chip] = open_row(gate_ref[...], tok_ref[chip])
-
-    part = part_ref.shape[1]
-    part_ref[...] = tok_ref[which, :, pl.ds(pl.multiple_of(at_ref[1] * part, part), part)]
+    @pl.when(step == 0)
+    def _():
+        for start, ref in ((at_ref[3], even_ref), (at_ref[4], odd_ref)):
+            tok_ref[pl.ds(pl.multiple_of(start, count), count), :] = ref[...].reshape(count, width).astype(BF16)
+        part = part_ref.shape[1]
+        part_ref[...] = tok_ref[:, pl.ds(pl.multiple_of(at_ref[1] * part, part), part)]
+        open_ref[...] = open_row(gate_ref[...], tok_ref[...])
+
     expert = jnp.minimum(core * here + step, experts - 1)
     route_row = jnp.concatenate([route_ref[k, pl.ds(expert, 1), :] for k in range(cores)], axis=1)
     _, _, weighted, mix_grad = hidden(
         w1_ref[...].reshape(2 * units, width),
         w2_ref[0],
-        tok_ref[which],
+        tok_ref[...],
         cot_ref[...],
-        jnp.where(step >= here, open_ref[which], route_row),
+        jnp.where(step >= here, open_ref[...], route_row),
     )
     mix_grad_ref[0] = mix_grad
     weighted_ref[0] = weighted
@@ -395,10 +406,15 @@
     here, shared = experts // 2, (tiles - experts) // 2
     rows = 2 * count
     own = lambda i, at: jnp.where(i < here, at[0] * here + i, experts + at[0] * shared + i - here)
-    chips = len(tokens) // 2
-    pieces = tuple(len(t) for t in tokens)
-    tokens = [v for t in tokens for v in t]
-    fixed = lambda *shape: pl.BlockSpec(shape, lambda i, j, at: (0,) * len(shape), pipeline_mode=pl.Buffered(1))
+    fixed = lambda *shape: pl.BlockSpec(shape, lambda i, at: (0,) * len(shape))
+    if len(tokens) == 2:
+        sources = [fixed(count, width), fixed(count, width)]
+    else:
+        tokens = [tokens[0], tokens[0]]
+        sources = [
+            pl.BlockSpec((1, count, width), lambda i, at: (2 * at[2], 0, 0)),
+            pl.BlockSpec((1, count, width), lambda i, at: (2 * at[2] + 1, 0, 0)),
+        ]
     shapes = [
         jax.ShapeDtypeStruct((here + shared, 2 * units, total), BF16),
         jax.ShapeDtypeStruct((here + shared, units, total), BF16),
@@ -406,34 +422,122 @@
     ]
     inputs = [*tokens, cotangent, route, gate_rows, w1, w2]
     return pl.pallas_call(
-        functools.partial(chip_kernel, pieces, here),
+        functools.partial(chip_kernel, here),
         grid_spec=pltpu.PrefetchScalarGridSpec(
             num_scalar_prefetch=1,
-            grid=(here + shared, chips),
+            grid=(here + shared,),
             in_specs=[
-                *[fixed(*v.shape) for v in tokens],
-                pl.BlockSpec((rows, width), lambda i, j, at: (at[2 + j], 0)),
-                pl.BlockSpec((2, experts, count), lambda i, j, at: (at[2 + j], 0, 0)),
+                *sources,
+                pl.BlockSpec((rows, width), lambda i, at: (at[2], 0)),
+                pl.BlockSpec((2, experts, count), lambda i, at: (at[2], 0, 0)),
                 fixed(*gate_rows.shape),
-                pl.BlockSpec((1, 2, units, width), lambda i, j, at: (own(i, at), 0, 0, 0)),
-                pl.BlockSpec((1, units, width), lambda i, j, at: (own(i, at), 0, 0)),
+                pl.BlockSpec((1, 2, units, width), lambda i, at: (own(i, at), 0, 0, 0)),
+                pl.BlockSpec((1, units, width), lambda i, at: (own(i, at), 0, 0)),
                 *[pl.BlockSpec(memory_space=pl.ANY) for _ in kept],
             ],
             out_specs=[
-                pl.BlockSpec((1, 2 * units, rows), lambda i, j, at: (i, 0, at[2 + j])),
-                pl.BlockSpec((1, units, rows), lambda i, j, at: (i, 0, at[2 + j])),
-                pl.BlockSpec((rows, 2 * part), lambda i, j, at: (at[2 + j], 0)),
+                pl.BlockSpec((1, 2 * units, rows), lambda i, at: (i, 0, at[2])),
+                pl.BlockSpec((1, units, rows), lambda i, at: (i, 0, at[2])),
+                pl.BlockSpec((rows, 2 * part), lambda i, at: (at[2], 0)),
             ],
-            scratch_shapes=[pltpu.VMEM((chips, rows, width), BF16), pltpu.VMEM((chips, 1, rows), F32)],
+            scratch_shapes=[pltpu.VMEM((rows, width), BF16), pltpu.VMEM((1, rows), F32)],
         ),
         out_shape=shapes,
         input_output_aliases={1 + len(inputs) + k: k for k in range(len(kept))},
         compiler_params=pltpu.CompilerParams(
-            dimension_semantics=("arbitrary", "arbitrary"), vmem_limit_bytes=VMEM_LIMIT
+            dimension_semantics=("arbitrary",), vmem_limit_bytes=VMEM_LIMIT
         ),
         cost_estimate=LIGHT,
         name="chip_hidden",
     )(at, *inputs, *kept)
+
+
+def both_products(normed_ref, projected_ref, branch_ref, attended_ref):
+    return jnp.concatenate(
+        [tn(normed_ref[0], projected_ref[...]), tn(branch_ref[0], attended_ref[...])], axis=1
+    )
+
+
+def sent_kernel(at_ref, normed_ref, projected_ref, branch_ref, attended_ref, out_ref):
+    out_ref[0] = both_products(normed_ref, projected_ref, branch_ref, attended_ref)
+
+
+def held_kernel(at_ref, normed_ref, projected_ref, branch_ref, attended_ref, arrived_ref, *out_refs):
+    block = pl.program_id(0)
+    along_y, along_x = block // 2, lax.rem(block, 2)
+    value = both_products(normed_ref, projected_ref, branch_ref, attended_ref) + arrived_ref[0]
+    half = value.shape[1] // 2
+    x_keep_ref, x_send_ref, y_keep_ref, y_send_ref = out_refs
+    for same, index, columns, keep_ref, send_ref in (
+        (along_x == at_ref[1], along_y, value[:, :half], x_keep_ref, x_send_ref),
+        (along_y == at_ref[2], along_x, value[:, half:], y_keep_ref, y_send_ref),
+    ):
+        @pl.when(same)
+        def _():
+            keep_ref[index] = columns
+
+        @pl.when(jnp.logical_not(same))
+        def _():
+            send_ref[index] = columns
+
+
+def token_products(at, normed, projected, branch, attended, arrived):
+    _, count, half = normed.shape
+    blocks = BLOCKS // 2
+    part = half // blocks
+    cols = projected.shape[1] + attended.shape[1]
+    side = pl.BlockSpec((1, count, part), lambda i, at: (at[0], 0, i))
+    fixed = lambda *shape: pl.BlockSpec(shape, lambda i, at: (0,) * len(shape))
+    block = pl.BlockSpec((1, part, cols), lambda i, at: (i, 0, 0))
+    inputs = [normed, projected, branch, attended]
+    in_specs = [side, fixed(*projected.shape), side, fixed(*attended.shape)]
+    if arrived is None:
+        kernel, out_specs = sent_kernel, block
+        out_shape = jax.ShapeDtypeStruct((blocks, part, cols), F32)
+    else:
+        kernel, out_specs = held_kernel, [fixed(2, part, cols // 2)] * 4
+        out_shape = [jax.ShapeDtypeStruct((2, part, cols // 2), F32)] * 4
+        inputs, in_specs = [*inputs, arrived], [*in_specs, block]
+    return pl.pallas_call(
+        kernel,
+        grid_spec=pltpu.PrefetchScalarGridSpec(
+            num_scalar_prefetch=1, grid=(blocks,), in_specs=in_specs, out_specs=out_specs
+        ),
+        out_shape=out_shape,
+        compiler_params=pltpu.CompilerParams(
+            dimension_semantics=("arbitrary",), vmem_limit_bytes=VMEM_LIMIT
+        ),
+        cost_estimate=LIGHT,
+        name="token_products",
+    )(at, *inputs)
+
+
+def turn_kernel(at_ref, x_keep_ref, x_got_ref, y_keep_ref, y_got_ref, x_own_ref, x_send_ref, y_own_ref, y_send_ref):
+    for mine, keep_ref, got_ref, own_ref, send_ref in (
+        (at_ref[2], x_keep_ref, x_got_ref, x_own_ref, x_send_ref),
+        (at_ref[1], y_keep_ref, y_got_ref, y_own_ref, y_send_ref),
+    ):
+        own_ref[...] = keep_ref[mine] + got_ref[mine]
+        send_ref[...] = keep_ref[1 - mine] + got_ref[1 - mine]
+
+
+def turned_blocks(at, x_keep, x_got, y_keep, y_got):
+    _, part, cols = x_keep.shape
+    rows = part // 4
+    spec = pl.BlockSpec((2, rows, cols), lambda i, at: (0, i, 0))
+    out = pl.BlockSpec((rows, cols), lambda i, at: (i, 0))
+    return pl.pallas_call(
+        turn_kernel,
+        grid_spec=pltpu.PrefetchScalarGridSpec(
+            num_scalar_prefetch=1, grid=(4,), in_specs=[spec] * 4, out_specs=[out] * 4
+        ),
+        out_shape=[jax.ShapeDtypeStruct((part, cols), F32)] * 4,
+        compiler_params=pltpu.CompilerParams(
+            dimension_semantics=("arbitrary",), vmem_limit_bytes=32 * 1024 * 1024
+        ),
+        cost_estimate=LIGHT,
+        name="turned_blocks",
+    )(at, x_keep, x_got, y_keep, y_got)
 
 
 def weights_kernel(at_ref, mix_grad_ref, weighted_ref, tok_ref, cot_ref, one_mine_ref, one_peer_ref, two_mine_ref,
@@ -509,31 +613,8 @@
     return lax.ppermute(value, "dp", [(i, i ^ bit) for i in range(8)])
 
 
-def butterfly(value):
-    value = value + flip(value, 1)
-    for bit in (1, 2):
-        value = value + lax.ppermute(value, "tensor", [(i, i ^ bit) for i in range(4)])
-    for bit in (2, 4):
-        value = value + flip(value, bit)
-    return value
-
-
 def take(value, number, axis):
     return lax.dynamic_index_in_dim(value, number, axis, keepdims=False)
-
-
-def scatter_first(held, me):
-    along_x, along_y = (me // 2) % 2, me // 4
-    half = held.shape[-1] // 256 * 128
-    a, b = held[..., :half], held[..., half:]
-    return (take(a, along_x, 1), take(a, 1 - along_x, 1), take(b, along_y, 0), take(b, 1 - along_y, 0))
-
-
-def scatter_second(a, b, me):
-    along_x, along_y = (me // 2) % 2, me // 4
-    a = take(a, along_y, 0) + flip(take(a, 1 - along_y, 0), 4)
-    b = take(b, along_x, 0) + flip(take(b, 1 - along_x, 0), 2)
-    return jnp.concatenate([a, b], axis=-1)
 
 
 def shards(
@@ -597,112 +678,103 @@
     attn_sum, w1, w2, cot_low, route_all = tied((attn_sum, w1, w2, cot_low, route_all))
 
     residual, tokens, tokens_wide = second_norm(layer_input, attn_sum, gain_two)
-    if n_dp == 8:
-        over_x, over_y = flip(tokens_wide, 2), flip(tokens_wide, 4)
-        beside = flip(tokens_wide, 1)
-    else:
-        tok_all = lax.all_gather(tokens_wide, "dp")
+    swap = lambda v: lax.ppermute(v, "dp", [(i, i ^ 1) for i in range(n_dp)])
+    beside = swap(tokens_wide)
+    tok_all = lax.all_gather(tokens_wide, "dp")
     mlp_top, mlp_low, grad_top, grad_low, logit_grad = own_mlp(tokens, cotangent, route, gate_rows, w1, w2)
     line = n_tensor == 4 and n_dp == 8
     spot = lax.axis_index("tensor")
-    hide = lambda chips, tokens, kept: chip_hidden(
-        jnp.stack([core, chip, *chips]), tokens, cot_low, route_all, gate_rows, w1, w2, kept, part
-    )
+    hide = lambda other, starts, tokens, kept: chip_hidden(
+        jnp.stack([core, chip, other, *starts]), tokens, cot_low, route_all, gate_rows, w1, w2, kept, part
+    )
+    in_order = (jnp.int32(0), jnp.int32(count))
+    beside_starts = (core * count, (1 - core) * count)
+    shared_gate_part = jnp.sum(logit_grad[0][:, None] * tokens.astype(F32), axis=0, keepdims=True)
     if line:
         is_inner = (spot == 1) | (spot == 2)
         inwards = lambda v: lax.ppermute(v, "tensor", [(0, 1), (3, 2)])
         across = lambda v: lax.ppermute(v, "tensor", [(1, 2), (2, 1)])
         outwards = lambda v: lax.ppermute(v, "tensor", [(1, 0), (2, 3)])
         ready = jnp.isnan(logit_grad[0, 0]).astype(jnp.int32)
-        over_x, over_y, ready = tied((over_x, over_y, ready))
-        low, high = flip(over_x[: count // 2], 4), flip(over_y[count // 2 :], 2)
-        beside_x, beside_y = flip(over_x, 1), flip(over_y, 1)
         got = inwards(grad_top)
-        kept = hide([chip + ready], [[tokens_wide], [beside]], [])
-        got, beside_x, beside_y, grad_low, kept = tied((got, beside_x, beside_y, grad_low, kept))
+        kept = hide(chip + ready, beside_starts, [tokens_wide, beside], [])
+        got, grad_low, kept = tied((got, grad_low, kept))
         grad_top = grad_top + got
         got, got_low = across(grad_top), inwards(grad_low)
-        kept = hide([chip ^ 1], [[over_x], [beside_x]], kept)
-        got, got_low, low, high, mlp_top, kept = tied((got, got_low, low, high, mlp_top, kept))
+        got, got_low, mlp_top, tok_all, shared_gate_part, kept = tied(
+            (got, got_low, mlp_top, tok_all, shared_gate_part, kept)
+        )
         grad_top, grad_low = grad_top + got, grad_low + got_low
         end_top, got_low, got = outwards(grad_top), across(grad_low), inwards(mlp_top)
-        beside_low, beside_high = flip(low, 1), flip(high, 1)
-        kept = hide([chip ^ 2], [[over_y], [beside_y]], kept)
-        end_top, got_low, got, mlp_low, beside_low, beside_high, kept = tied(
-            (end_top, got_low, got, mlp_low, beside_low, beside_high, kept)
-        )
+        kept = hide(chip ^ 1, in_order, [tok_all], kept)
+        end_top, got_low, got, mlp_low, kept = tied((end_top, got_low, got, mlp_low, kept))
         grad_low, mlp_top = grad_low + got_low, mlp_top + got
         end_low, got, got_low = outwards(grad_low), across(mlp_top), inwards(mlp_low)
-        kept = hide([chip ^ 3], [[low, high], [beside_low, beside_high]], kept)
+        kept = hide(chip ^ 2, in_order, [tok_all], kept)
         end_low, got, got_low, kept = tied((end_low, got, got_low, kept))
         totals = [grad_top, end_top, grad_low, end_low]
     else:
         is_inner = spot >= 0
         kept = []
         for k in range(n_dp // 2):
-            kept = hide([k], [[take(tok_all, 2 * k + core, 0)], [take(tok_all, 2 * k + 1 - core, 0)]], kept)
+            kept = hide(jnp.int32(k), in_order, [tok_all], kept)
         totals = [lax.psum(v, "tensor") for v in (grad_top, grad_low)]
         totals = [totals[0], totals[0], totals[1], totals[1]]
 
     normed_one_part, residual_grad, branch_grad, projected_grad, bias_part, mlp_gain_part = attention_back(
         is_inner.astype(jnp.int32)[None], totals, residual, cotangent, gain_two, out_weight, qkv, qkv_weight,
-        cosine, sine, row, col,
-    )
-    normed_one_total = lax.psum_scatter(normed_one_part, "tensor", scatter_dimension=0, tiled=True)
+        cosine, sine, row, col, layer_input, shared_gate_part, n_tensor,
+    )
     few = count // n_tensor
-    inputs = layer_input.astype(F32)
-    factor_one = lax.rsqrt(jnp.mean(inputs * inputs, axis=-1, keepdims=True) + EPS)
-    attn_gain_part = jnp.sum(normed_one_part * inputs * factor_one, axis=0)
-    shared_gate_part = jnp.sum(logit_grad[0][:, None] * tokens.astype(F32), axis=0)
-    my_slot = spot == jnp.arange(n_tensor)
-    small = jnp.concatenate(
-        [
-            attn_gain_part,
-            mlp_gain_part[0] * my_slot[0],
-            shared_gate_part,
-            (my_slot[:, None] * bias_part).reshape(-1),
-        ]
-    )
-    swap = lambda v: lax.ppermute(v, "dp", [(i, i ^ 1) for i in range(n_dp)])
+    summed = lax.psum_scatter(normed_one_part.reshape(-1, width), "tensor", scatter_dimension=0, tiled=True)
     own_rows = lambda v: lax.dynamic_slice_in_dim(v, spot * few, few, 0)
 
+    def finish(summed):
+        inputs = own_rows(layer_input).astype(F32)
+        factor = lax.rsqrt(jnp.mean(inputs * inputs, axis=-1, keepdims=True) + EPS)
+        bias_row = jnp.pad(bias_part, ((0, 0), (0, width - bias_part.shape[1])))
+        small = jnp.concatenate([summed[few : few + 2], mlp_gain_part, bias_row])
+        return norm_back(inputs, factor, gain_one, summed[:few]), jnp.pad(small, ((0, 4), (0, 0)))
+
     if line:
-        def products(c):
-            return (
-                tn(take(normed_one, c, 0), projected_grad).reshape(2, 2, part, -1),
-                tn(take(branch_grad, c, 0), attended).reshape(2, 2, part, -1),
-            )
-
-        arrived = [flip(v, 1) for v in products(1 - core)]
-        small = butterfly(small.reshape(-1, 128)).reshape(-1)
-        small, arrived = tied((small, arrived))
-        got, got_low, residual_grad = tied((got, got_low, residual_grad))
+        got, got_low, mlp_top, mlp_low, projected_grad = tied((got, got_low, mlp_top, mlp_low, projected_grad))
         mlp_top, mlp_low = mlp_top + got, mlp_low + got_low
         end_top, got_low = outwards(mlp_top), across(mlp_low)
-        held = products(core)
-        firsts = [scatter_first(h + v, me) for h, v in zip(held, arrived, strict=True)]
-        firsts, kept = tied((firsts, kept))
-        moved = [(flip(a_other, 2), flip(b_other, 4)) for _, a_other, _, b_other in firsts]
-        one_mine, one_peer, two_mine, two_peer = weight_grads(jnp.stack([core, chip]), *kept, cot_low)
-        one_mine, one_peer, normed_one_total = tied((one_mine, one_peer, normed_one_total))
-        one_peer, two_peer = swap(one_peer), swap(two_peer)
-        input_grad = norm_back(own_rows(inputs), own_rows(factor_one), gain_one, normed_one_total)
-        input_grad, moved, end_top, got_low = tied((input_grad, moved, end_top, got_low))
-        input_grad = lax.all_gather(input_grad, "tensor", axis=0, tiled=True)
+        mlp_low, projected_grad = tied((mlp_low, projected_grad))
+        at = jnp.stack([core, chip % 2, chip // 2])
+        other_at = jnp.stack([1 - core, chip % 2, chip // 2])
+        arrived = swap(token_products(other_at, normed_one, projected_grad, branch_grad, attended, None))
+        x_keep, x_send, y_keep, y_send = token_products(
+            at, normed_one, projected_grad, branch_grad, attended, arrived
+        )
+        x_send, y_send, kept, got_low = tied((x_send, y_send, kept, got_low))
         mlp_low = mlp_low + got_low
         end_low = outwards(mlp_low)
-        steps = [(a + a_in, b + b_in) for (a, _, b, _), (a_in, b_in) in zip(firsts, moved, strict=True)]
-        qkv_weight_grad, out_weight_grad = [scatter_second(a, b, me) for a, b in steps]
-        out_weight_grad = out_weight_grad.T
+        x_got, y_got = flip(x_send, 2), flip(y_send, 4)
+        kept = hide(chip ^ 3, in_order, [tok_all], kept)
+        one_mine, one_peer, two_mine, two_peer = weight_grads(jnp.stack([core, chip]), *kept, cot_low)
+        one_mine, one_peer, summed = tied((one_mine, one_peer, summed))
+        one_peer, two_peer = swap(one_peer), swap(two_peer)
+        input_grad, small = finish(summed)
+        input_grad, x_got, y_got, end_top, end_low = tied((input_grad, x_got, y_got, end_top, end_low))
+        input_grad = lax.all_gather(input_grad, "tensor", axis=0, tiled=True)
+        x_own, x_send, y_own, y_send = turned_blocks(at, x_keep, x_got, y_keep, y_got)
+        x_got, y_got = flip(x_send, 4), flip(y_send, 2)
+        small, x_own = tied((small, x_own))
+        for bit in (1, 2, 4):
+            small = small + flip(small, bit)
+        both = jnp.concatenate([x_own + x_got, y_own + y_got], axis=1)
+        cut = projected_grad.shape[1]
+        qkv_weight_grad, out_weight_grad = both[:, :cut], both[:, cut:].T
         mlp_sum = jnp.where(
             is_inner, jnp.concatenate([mlp_top, mlp_low]), jnp.concatenate([end_top, end_low])
         )
     else:
-        small = lax.psum(small, ("dp", "tensor"))
         one_mine, one_peer, two_mine, two_peer = weight_grads(jnp.stack([core, chip]), *kept, cot_low)
         one_peer, two_peer = swap(one_peer), swap(two_peer)
-        input_grad = norm_back(own_rows(inputs), own_rows(factor_one), gain_one, normed_one_total)
+        input_grad, small = finish(summed)
         input_grad = lax.all_gather(input_grad, "tensor", axis=0, tiled=True)
+        small = lax.psum(small, "dp")
         joint = lambda v: v.reshape(2, count, BLOCKS // 2, -1).transpose(1, 2, 0, 3).reshape(count, width)
         out_weight_grad = lax.psum_scatter(tn(attended, joint(branch_grad)), "dp", scatter_dimension=1, tiled=True)
         qkv_weight_grad = lax.psum_scatter(
@@ -710,9 +782,9 @@
         )
         mlp_sum = lax.psum(jnp.concatenate([mlp_top, mlp_low]), "tensor")
 
-    gains = lax.dynamic_slice(small[: 3 * width].reshape(3, width), (0, me * part), (3, part))
-    bias = take(small[3 * width :].reshape(n_tensor, heads_here, 3 * head_dim), spot, 0)
+    attn_gain_grad, shared_gate_grad, mlp_gain_grad = lax.dynamic_slice(small, (0, me * part), (3, part))
     bias_cols = 3 * head_dim // n_dp
+    bias = small[3, : heads_here * 3 * head_dim].reshape(heads_here, 3 * head_dim)
     qkv_bias_grad = lax.dynamic_slice(bias, (0, me * bias_cols), (heads_here, bias_cols))
     input_grad = (residual_grad + input_grad).astype(BF16)
     layer_output = (residual + mlp_sum).astype(BF16)
@@ -730,16 +802,16 @@
     return (
         layer_output,
         input_grad,
-        gains[0],
+        attn_gain_grad,
         qkv_weight_grad,
         qkv_bias_grad,
         out_weight_grad,
-        gains[1],
+        mlp_gain_grad,
         expert_gate_up_grad,
         expert_down_grad,
         shared_gate_up_grad,
         shared_down_grad,
-        gains[2],
+        shared_gate_grad,
     )
 
 

time: 551 us -> 544 us (0.987); the launches traced: 542 us -> 542 us
  waiting for transfers between devices: 90.1 us -> 116 us
  Pallas kernels: 182 us -> 205 us
  other arithmetic: 89.6 us -> 69.9 us
  local copies, waits for them, and re-layouts: 104 us -> 91.9 us
  matrix products: 10.5 us -> 0 us
  starting transfers between devices: 47.4 us -> 41.3 us
    ppermute x4, waiting for transfers between devices: 36.2 us -> 63.4 us  [shards(): outwards = lambda v: lax.ppermute(v, 'tensor', [(1, 0), (2, 3)])]
    ppermute x4, waiting for transfers between devices: 0.01 us -> 20.4 us  [shards(): inwards = lambda v: lax.ppermute(v, 'tensor', [(0, 1), (3, 2)])]
    ppermute x22 -> x7, waiting for transfers between devices: 36.1 us -> 15.8 us  [flip(): return lax.ppermute(value, 'dp', [(i, i ^ bit) for i in range(8)])]
    pallas_call x4 -> x7, Pallas kernels: 93.5 us -> 114 us  [the longest x4 92.4 us: chip_hidden(): pl.pallas_call(functools.partial(chip_kernel, here), grid_spec=pltpu.Pref...]
    ppermute x2 -> x0, waiting for transfers between devices: 13.5 us -> none  [butterfly(): lax.ppermute(value, 'tensor', [(i, i ^ bit) for i in range(4)])]
    ppermute x2 -> x4, waiting for transfers between devices: 0.01 us -> 12.1 us  [shards(): swap = lambda v: lax.ppermute(v, 'dp', [(i, i ^ 1) for i in range(n_dp)])]
    dot_general x4 -> x0, matrix products: 10.5 us -> none  [tn(): lax.dot_general(left, right, (((0,), (0,)), ((), ())), preferred_element_...]
    add x14 -> x5, other arithmetic: 13.1 us -> 2.83 us  [the longest x2 2.8 us: shards(): both = jnp.concatenate([x_own + x_got, y_own + y_got], axis=1)]
  transfers between devices with their start and end apart: 42 -> 28, of which waited for: 11 -> 7; matrix products, arithmetic and copies ran while one was open for 31% -> 23% of each run, Pallas kernels for 31% -> 34%
where the time goes in v4:
time: 544 us; the launch traced here: 542 us
  Pallas kernels  205 us (38%)
  waiting for transfers between devices  116 us (21%)
  local copies, waits for them, and re-layouts  91.9 us (17%)
  other arithmetic  69.9 us (13%)
  starting transfers between devices  41.3 us (8%)
  between operations  17.7 us (3%)
    pallas_call x4, Pallas kernels, chip_hidden(): pl.pallas_call(functools.partial(chip_kernel, here), grid_spec=pltpu.Pref...  92.4 us
    ppermute x4, waiting for transfers between devices, shards(): outwards = lambda v: lax.ppermute(v, 'tensor', [(1, 0), (2, 3)])  63.4 us
    pallas_call x1, Pallas kernels, own_mlp(): pl.pallas_call(functools.partial(own_kernel, experts), grid=(tiles // gro...  40.2 us
    unnamed x110, local copies, waits for them, and re-layouts  30.1 us
    optimization_barrier x1, local copies, waits for them, and re-layouts, shards(): attn_part, shared_gate_up = tied((attn_part, shared_gate_up))  28.7 us
    concatenate x1, other arithmetic, shards(): jnp.concatenate([jnp.transpose(expert_gate_up, (0, 2, 3, 1)), jnp.transpo...  24.2 us
    ppermute x4, starting transfers between devices, shards(): inwards = lambda v: lax.ppermute(v, 'tensor', [(0, 1), (3, 2)])  22.6 us
    ppermute x4, waiting for transfers between devices, shards(): inwards = lambda v: lax.ppermute(v, 'tensor', [(0, 1), (3, 2)])  20.4 us
  transfers between devices with their start and end apart: 28, of which 7 were waited for; matrix products, arithmetic and copies ran while one was open for 23% of the time, Pallas kernels for 34%

profile of v4, /device:TPU:0, one launch (start us, length us, event | category | flops | bytes accessed | tf_op | source)
XLA Modules:
  0.0 542.3 jit_solution(12923418977151419991)
XLA Ops:
  15.8 7.1 %attention.1 = (f32[256,2048]{1,0:T(8,128)S(1)}, bf16[2,256,1024]{2,1,0:T(8,128)(2,1)S(1)}, bf16[256,1536]{1,0:T(8,128)(2,1)S(1)}, bf16[256,512]{1,0:T(8,128)(2,1)S(1)}) custom-call(bf16[256,2048]{1,0:T(8,128)(2,1)S(1)} %copy-done.2, f32[1,2048]{1,0:T(1,128)S(1)} %bitcast.40, bf16[2048,1536]{1,0:T(8,128)(2,1)S(1)} %copy-done.1, ...), custom_call_target="tpu_custom_call" | custom-call | flops 1048576 | bytes 65536 | tf_op jit(solution)/shard_map/attention/pallas_call | solution.py:97
  26.9 28.7 %copy.49 = bf16[2048,2,1408]{0,2,1:T(8,128)(2,1)} copy(bf16[2048,2,1408]{2,1,0:T(2,128)(2,1)} %param.26) | data formatting | bytes 23068672 | tf_op jit(solution)/shard_map/optimization_barrier | solution.py:668
  55.7 12.8 %copy.56 = bf16[2048,2,4,352]{0,3,1,2:T(8,128)(2,1)} copy(bf16[2048,2,4,352]{0,3,2,1:T(8,128)(2,1)} %bitcast.53) | data formatting | bytes 23068672 | tf_op jit(solution)/shard_map/reshape | solution.py:673
  70.8 6.9 %pad_maximum_fusion.1.w2_ref = bf16[12,352,2048]{2,1,0:T(8,128)(2,1)} fusion(bf16[4,352,2048]{2,1,0:T(8,128)(2,1)S(1)} %bitcast.62, bf16[8,352,2048]{2,1,0:T(8,128)(2,1)S(1)} %bitcast.58), kind=kLoop, calls=%fused_computation.1 | loop fusion | flops 8650752 | bytes 34603008 | tf_op jit(solution)/shard_map/concatenate | solution.py:676
  77.7 24.2 %pad_maximum_fusion.w1_ref = bf16[12,2,352,2048]{3,2,1,0:T(8,128)(2,1)} fusion(bf16[4,2,352,2048]{3,2,1,0:T(8,128)(2,1)} %bitcast.54, bf16[8,2,352,2048]{3,2,1,0:T(8,128)(2,1)} %bitcast.55), kind=kLoop, calls=%fused_computation | loop fusion | flops 17301504 | bytes 69206016 | tf_op jit(solution)/shard_map/concatenate | solution.py:670
  101.9 4.4 all-gather.8.cloned.1.call-done
  106.3 7.9 %split_rounded.1 = (bf16[2048,2048]{1,0:T(8,128)(2,1)S(1)}, f32[8,8,256]{2,1,0:T(8,128)S(1)}) custom-call(f32[8,264,2048]{2,1,0:T(8,128)} %bitcast.56), custom_call_target="tpu_custom_call" | custom-call | tf_op jit(solution)/shard_map/split_rounded/pallas_call | solution.py:593
  114.2 3.2 copy-done
  125.2 40.2 %own_mlp.1 = (f32[128,2048]{1,0:T(8,128)}, f32[128,2048]{1,0:T(8,128)}, f32[128,2048]{1,0:T(8,128)}, f32[128,2048]{1,0:T(8,128)}, f32[1,256]{1,0:T(1,128)}) custom-call(bf16[256,2048]{1,0:T(8,128)(2,1)} %copy-done.9, bf16[256,2048]{1,0:T(8,128)(2,1)} %cot_ref.3, f32[8,1,256]{2,1,0:T(1,128)} %broadcast_in_dim.50.route_ref, ...), custom_call_target="tpu_custom_call" | custom-call | flops 1048576 | bytes 65536 | tf_op jit(solution)/shard_map/own_mlp/pallas_call | solution.py:349
  165.4 3.6 collective-permute-start
  173.5 23.0 %chip_hidden.4 = (bf16[6,704,2048]{2,1,0:T(8,128)(2,1)}, bf16[6,352,2048]{2,1,0:T(8,128)(2,1)}, bf16[2048,512]{1,0:T(8,128)(2,1)}) custom-call(s32[5]{0:T(128)} %stack.70.at_ref, f32[256,2048]{1,0:T(8,128)} %get-tuple-element.125.even_ref, f32[256,2048]{1,0:T(8,128)} %copy-done.34, bf16[2048,2048]{1,0:T(8,128)(2,1)} %copy-done, f32[8,8,256]{2,1,0:T(8,128)} %copy-done.20, ...), custom_call_target="tpu_custom_call" | custom-call | flops 1048576 | bytes 65536 | tf_op jit(solution)/shard_map/chip_hidden/pallas_call | solution.py:424
  198.9 4.3 collective-permute-start.3
  204.5 20.4 %collective-permute-done.3 = f32[128,2048]{1,0:T(8,128)} collective-permute-done((f32[128,2048]{1,0:T(8,128)S(1)}, f32[128,2048]{1,0:T(8,128)}, u32[]{:S(2)}, u32[]{:S(2)}) %collective-permute-start.3) | collective-permute-done | bytes 1048608 | tf_op jit(solution)/shard_map/ppermute | solution.py:695
  229.4 6.4 %collective-permute-start.6 = (f32[128,2048]{1,0:T(8,128)}, f32[128,2048]{1,0:T(8,128)}, u32[]{:S(2)}, u32[]{:S(2)}) collective-permute-start(f32[128,2048]{1,0:T(8,128)} %get-tuple-element.139), channel_id=1, source_target_pairs={{0,1},{3,2},{4,5},{7,6},{8,9},{11,10},{12,13},{15,14},{16,17},{19,... | collective-permute-start | bytes 3145736 | tf_op jit(solution)/shard_map/ppermute | solution.py:695
  236.5 23.0 %chip_hidden.5 = (bf16[6,704,2048]{2,1,0:T(8,128)(2,1)}, bf16[6,352,2048]{2,1,0:T(8,128)(2,1)}, bf16[2048,512]{1,0:T(8,128)(2,1)}) custom-call(s32[5]{0:T(128)} %stack.72.at_ref, f32[8,256,2048]{2,1,0:T(8,128)} %bitcast.47, f32[8,256,2048]{2,1,0:T(8,128)} %bitcast.48, ...), custom_call_target="tpu_custom_call", output_to_operand_aliasing={{0}: (8, {}), {1}: (9, {}), {2}: (10, {})} | custom-call | flops 1048576 | bytes 65536 | tf_op jit(solution)/shard_map/chip_hidden/pallas_call | solution.py:424
  266.8 8.3 %collective-permute-start.9 = (f32[128,2048]{1,0:T(8,128)}, f32[128,2048]{1,0:T(8,128)}, u32[]{:S(2)}, u32[]{:S(2)}) collective-permute-start(f32[128,2048]{1,0:T(8,128)} %get-tuple-element.166), channel_id=1, source_target_pairs={{0,1},{3,2},{4,5},{7,6},{8,9},{11,10},{12,13},{15,14},{16,17},{19,... | collective-permute-start | bytes 3145736 | tf_op jit(solution)/shard_map/ppermute | solution.py:695
  276.3 23.3 %chip_hidden.6 = (bf16[6,704,2048]{2,1,0:T(8,128)(2,1)}, bf16[6,352,2048]{2,1,0:T(8,128)(2,1)}, bf16[2048,512]{1,0:T(8,128)(2,1)}) custom-call(s32[5]{0:T(128)} %stack.74.at_ref, f32[8,256,2048]{2,1,0:T(8,128)} %bitcast.49, f32[8,256,2048]{2,1,0:T(8,128)} %bitcast.50, ...), custom_call_target="tpu_custom_call", output_to_operand_aliasing={{0}: (8, {}), {1}: (9, {}), {2}: (10, {})} | custom-call | flops 1048576 | bytes 65536 | tf_op jit(solution)/shard_map/chip_hidden/pallas_call | solution.py:424
  300.8 14.4 %attention_back.1 = (f32[4,72,2048]{2,1,0:T(8,128)}, f32[256,2048]{1,0:T(8,128)}, bf16[2,256,1024]{2,1,0:T(8,128)(2,1)S(1)}, bf16[256,1536]{1,0:T(8,128)(2,1)S(1...) custom-call(s32[1]{0:T(128)} %bitcast.21.inner_ref, f32[128,2048]{1,0:T(8,128)S(1)} %add.103.held_top_ref, ...), custom_call_target="tpu_custom_call" | custom-call | flops 1048576 | bytes 65536 | tf_op jit(solution)/shard_map/attention_back/pallas_call | solution.py:239
  318.7 6.8 %token_products.2 = f32[4,256,2048]{2,1,0:T(8,128)} custom-call(s32[3]{0:T(128)} %add_add_fusion.1.at_ref, bf16[2,256,1024]{2,1,0:T(8,128)(2,1)} %copy-done.7, bf16[256,1536]{1,0:T(8,128)(2,1)} %copy-done.11, bf16[2,256,1024]{2,1,0:T(8,128)(2,1)} %copy-done.8, bf16[256,512]{1,0:T(8,128)(2,1)} %copy-done.23), custom_call_target="tpu_custom_call" | custom-call | flops 1048576 | bytes 65536 | tf_op jit(solution)/shard_map/token_products/pallas_call | solution.py:501
  326.9 12.1 %collective-permute-done.10.arrived_ref = f32[4,256,2048]{2,1,0:T(8,128)} collective-permute-done((f32[4,256,2048]{2,1,0:T(8,128)}, f32[4,256,2048]{2,1,0:T(8,128)}, u32[]{:S(2)}, u32[]{:S(2)}) %collective-permute-start.10) | collective-permute-done | bytes 8388640 | tf_op jit(solution)/shard_map/ppermute | solution.py:681
  339.0 9.9 %token_products.3 = (f32[2,256,1024]{2,1,0:T(8,128)}, f32[2,256,1024]{2,1,0:T(8,128)}, f32[2,256,1024]{2,1,0:T(8,128)}, f32[2,256,1024]{2,1,0:T(8,128)}) custom-call(s32[3]{0:T(128)} %add_add_fusion.at_ref, bf16[2,256,1024]{2,1,0:T(8,128)(2,1)} %copy-done.7, bf16[256,1536]{1,0:T(8,128)(2,1)} %copy-done.11, bf16[2,256,1024]{2,1,0:T(8,128)(2,1)} %copy-done.8, ...), custom_call_target="tpu_custom_call" | custom-call | flops 1048576 | bytes 65536 | tf_op jit(solution)/shard_map/token_products/pallas_call | solution.py:501
  357.1 23.1 %chip_hidden.7 = (bf16[6,704,2048]{2,1,0:T(8,128)(2,1)}, bf16[6,352,2048]{2,1,0:T(8,128)(2,1)}, bf16[2048,512]{1,0:T(8,128)(2,1)}) custom-call(s32[5]{0:T(128)} %stack.82.at_ref, f32[8,256,2048]{2,1,0:T(8,128)} %bitcast.51, f32[8,256,2048]{2,1,0:T(8,128)} %bitcast.52, ...), custom_call_target="tpu_custom_call", output_to_operand_aliasing={{0}: (8, {}), {1}: (9, {}), {2}: (10, {})} | custom-call | flops 1048576 | bytes 65536 | tf_op jit(solution)/shard_map/chip_hidden/pallas_call | solution.py:424
  380.1 19.8 %weight_grads.1 = (f32[6,2,352,256]{3,2,1,0:T(8,128)}, f32[6,2,352,256]{3,2,1,0:T(8,128)}, f32[6,352,256]{2,1,0:T(8,128)}, f32[6,352,256]{2,1,0:T(8,128)}) custom-call(s32[2]{0:T(128)} %pad_add_fusion.at_ref, bf16[6,704,2048]{2,1,0:T(8,128)(2,1)} %get-tuple-element.183.mix_grad_ref, bf16[6,352,2048]{2,1,0:T(8,128)(2,1)} %get-tuple-element.184.weighted_ref, ...), custom_call_target="tpu_custom_call" | custom-call | flops 1048576 | bytes 65536 | tf_op jit(solution)/shard_map/weight_grads/pallas_call | solution.py:562
  404.3 14.2 %collective-permute-done.14 = f32[128,2048]{1,0:T(8,128)} collective-permute-done((f32[128,2048]{1,0:T(8,128)}, f32[128,2048]{1,0:T(8,128)}, u32[]{:S(2)}, u32[]{:S(2)}) %collective-permute-start.14) | collective-permute-done | bytes 1048608 | tf_op jit(solution)/shard_map/ppermute | solution.py:697
  419.5 49.2 %collective-permute-done.15 = f32[128,2048]{1,0:T(8,128)} collective-permute-done((f32[128,2048]{1,0:T(8,128)}, f32[128,2048]{1,0:T(8,128)}, u32[]{:S(2)}, u32[]{:S(2)}) %collective-permute-start.15) | collective-permute-done | bytes 1048608 | tf_op jit(solution)/shard_map/ppermute | solution.py:697
  468.7 3.6 slice.48
  477.5 4.7 turned_blocks.1
  485.1 3.7 fusion.3
  494.7 14.7 %collective-permute-done.17 = f32[8,2048]{1,0:T(8,128)S(1)} collective-permute-done((f32[8,2048]{1,0:T(8,128)S(1)}, f32[8,2048]{1,0:T(8,128)S(1)}, u32[]{:S(2)}, u32[]{:S(2)}) %collective-permute-start.17) | collective-permute-done | bytes 65568 | tf_op jit(solution)/shard_map/ppermute | solution.py:613
  522.7 3.4 copy.54
  528.8 3.0 fusion
  531.8 2.9 add_convert_fusion
  (222 shorter events, 91.4 us)
Async XLA Ops:
  8.0 98.3 %all-gather.8.cloned.1.call-start = ((), (), s32[]{:S(2)}) async-start(), calls=%async_computation.4 | async-start | bytes 19464192 | tf_op jit(solution)/shard_map/all_gather | solution.py:651
  11.2 106.3 %all-reduce.5.cloned.1.call-start = ((), (), s32[]{:S(2)}) async-start(), calls=%async_computation.1 | async-start | bytes 4194304 | tf_op jit(solution)/shard_map/psum | solution.py:669
  26.9 197.9 %all-gather.10.cloned.1.call-start = ((), (), s32[]{:S(2)}) async-start(), calls=%async_computation.5 | async-start | bytes 18874368 | tf_op jit(solution)/shard_map/all_gather | solution.py:683
  123.6 276.3 %reduce-scatter.2.cloned.1.call-start = ((), (), s32[]{:S(2)}) async-start(), calls=%async_computation.2 | async-start | bytes 2949120 | tf_op jit(solution)/shard_map/reduce_scatter | solution.py:729
  123.7 48.5 %collective-permute-start.1 = (f32[256,2048]{1,0:T(8,128)}, f32[256,2048]{1,0:T(8,128)S(1)}, u32[]{:S(2)}, u32[]{:S(2)}) collective-permute-start(f32[256,2048]{1,0:T(8,128)} %get-tuple-element.125.even_ref), channel_id=1, source_target_pairs={{0,4},{4,0},{8,12},{12,8},{16,20},{20,16},{24,28},{28,24},{1,5},{5... | collective-permute-start | bytes 6291464 | tf_op jit(solution)/shard_map/ppermute | solution.py:681
  165.4 31.1 %collective-permute-start = (f32[128,2048]{1,0:T(8,128)}, f32[128,2048]{1,0:T(8,128)}, u32[]{:S(2)}, u32[]{:S(2)}) collective-permute-start(f32[128,2048]{1,0:T(8,128)} %get-tuple-element.122), channel_id=1, source_target_pairs={{0,1},{3,2},{4,5},{7,6},{8,9},{11,10},{12,13},{15,14},{16,17},{19,... | collective-permute-start | bytes 3145736 | tf_op jit(solution)/shard_map/ppermute | solution.py:695
  172.2 24.4 %copy-start.39 = (f32[128,2048]{1,0:T(8,128)S(1)}, f32[128,2048]{1,0:T(8,128)}, u32[]{:S(2)}) copy-start(f32[128,2048]{1,0:T(8,128)} %get-tuple-element.122) | copy-start | bytes 3145732
  198.2 5.3 collective-permute-start.2
  198.9 25.9 %collective-permute-start.3 = (f32[128,2048]{1,0:T(8,128)S(1)}, f32[128,2048]{1,0:T(8,128)}, u32[]{:S(2)}, u32[]{:S(2)}) collective-permute-start(f32[128,2048]{1,0:T(8,128)S(1)} %copy-done.37), channel_id=1, source_target_pairs={{0,1},{3,2},{4,5},{7,6},{8,9},{11,10},{12,13},{15,14},{16,17},{19,... | collective-permute-start | bytes 3145736 | tf_op jit(solution)/shard_map/ppermute | solution.py:695
  226.4 33.2 %copy-start.32 = (f32[128,2048]{1,0:T(8,128)}, f32[128,2048]{1,0:T(8,128)S(1)}, u32[]{:S(2)}) copy-start(f32[128,2048]{1,0:T(8,128)S(1)} %add.102) | copy-start | bytes 3145732
  226.5 33.0 %collective-permute-start.4 = (f32[128,2048]{1,0:T(8,128)S(1)}, f32[128,2048]{1,0:T(8,128)S(1)}, u32[]{:S(2)}, u32[]{:S(2)}) collective-permute-start(f32[128,2048]{1,0:T(8,128)S(1)} %add.103.held_top_ref), channel_id=1, source_target_pairs={{1,0},{2,3},{5,4},{6,7},{9,8},{10,11},{13,12},{14,15},{17,16},{18,... | collective-permute-start | bytes 3145736 | tf_op jit(solution)/shard_map/ppermute | solution.py:697
  227.8 31.7 %collective-permute-start.5 = (f32[128,2048]{1,0:T(8,128)S(1)}, f32[128,2048]{1,0:T(8,128)}, u32[]{:S(2)}, u32[]{:S(2)}) collective-permute-start(f32[128,2048]{1,0:T(8,128)S(1)} %add.102), channel_id=1, source_target_pairs={{1,2},{2,1},{5,6},{6,5},{9,10},{10,9},{13,14},{14,13},{17,18},{18,... | collective-permute-start | bytes 3145736 | tf_op jit(solution)/shard_map/ppermute | solution.py:696
  229.4 30.1 %collective-permute-start.6 = (f32[128,2048]{1,0:T(8,128)}, f32[128,2048]{1,0:T(8,128)}, u32[]{:S(2)}, u32[]{:S(2)}) collective-permute-start(f32[128,2048]{1,0:T(8,128)} %get-tuple-element.139), channel_id=1, source_target_pairs={{0,1},{3,2},{4,5},{7,6},{8,9},{11,10},{12,13},{15,14},{16,17},{19,... | collective-permute-start | bytes 3145736 | tf_op jit(solution)/shard_map/ppermute | solution.py:695
  261.2 38.4 %collective-permute-start.7 = (f32[128,2048]{1,0:T(8,128)S(1)}, f32[128,2048]{1,0:T(8,128)}, u32[]{:S(2)}, u32[]{:S(2)}) collective-permute-start(f32[128,2048]{1,0:T(8,128)S(1)} %add.104.held_low_ref), channel_id=1, source_target_pairs={{1,0},{2,3},{5,4},{6,7},{9,8},{10,11},{13,12},{14,15},{17,16},{18,... | collective-permute-start | bytes 3145736 | tf_op jit(solution)/shard_map/ppermute | solution.py:697
  265.2 34.4 %collective-permute-start.8 = (f32[128,2048]{1,0:T(8,128)}, f32[128,2048]{1,0:T(8,128)}, u32[]{:S(2)}, u32[]{:S(2)}) collective-permute-start(f32[128,2048]{1,0:T(8,128)} %add.105), channel_id=1, source_target_pairs={{1,2},{2,1},{5,6},{6,5},{9,10},{10,9},{13,14},{14,13},{17,18},{18,... | collective-permute-start | bytes 3145736 | tf_op jit(solution)/shard_map/ppermute | solution.py:696
  266.8 32.8 %collective-permute-start.9 = (f32[128,2048]{1,0:T(8,128)}, f32[128,2048]{1,0:T(8,128)}, u32[]{:S(2)}, u32[]{:S(2)}) collective-permute-start(f32[128,2048]{1,0:T(8,128)} %get-tuple-element.166), channel_id=1, source_target_pairs={{0,1},{3,2},{4,5},{7,6},{8,9},{11,10},{12,13},{15,14},{16,17},{19,... | collective-permute-start | bytes 3145736 | tf_op jit(solution)/shard_map/ppermute | solution.py:695
  276.3 23.3 %copy-start.19 = (f32[256,128]{1,0:T(8,128)S(1)}, f32[256,128]{1,0:T(8,128)}, u32[]{:S(2)}) copy-start(f32[256,128]{1,0:T(8,128)} %copy-done.18) | copy-start | bytes 393220
  276.3 23.3 %copy-start.27 = (s32[256]{0:T(256)S(1)}, s32[256]{0:T(256)}, u32[]{:S(2)}) copy-start(s32[256]{0:T(256)} %param.16) | copy-start | bytes 3076
  325.5 13.5 %collective-permute-start.10 = (f32[4,256,2048]{2,1,0:T(8,128)}, f32[4,256,2048]{2,1,0:T(8,128)}, u32[]{:S(2)}, u32[]{:S(2)}) collective-permute-start(f32[4,256,2048]{2,1,0:T(8,128)} %token_products.2), channel_id=1, source_target_pairs={{0,4},{4,0},{8,12},{12,8},{16,20},{20,16},{24,28},{28,24},{1,5},{5... | collective-permute-start | bytes 25165832 | tf_op jit(solution)/shard_map/ppermute | solution.py:681
  325.5 206.3 %all-gather.6.cloned.1.call-start = ((), (), s32[]{:S(2)}) async-start(), calls=%async_computation.3 | async-start | bytes 2621440 | tf_op jit(solution)/shard_map/all_gather | solution.py:760
  325.6 23.3 %collective-permute-start.11 = (f32[128,2048]{1,0:T(8,128)S(1)}, f32[128,2048]{1,0:T(8,128)S(1)}, u32[]{:S(2)}, u32[]{:S(2)}) collective-permute-start(f32[128,2048]{1,0:T(8,128)S(1)} %add.107), channel_id=1, source_target_pairs={{1,2},{2,1},{5,6},{6,5},{9,10},{10,9},{13,14},{14,13},{17,18},{18,... | collective-permute-start | bytes 3145736 | tf_op jit(solution)/shard_map/ppermute | solution.py:696
  349.8 118.9 %collective-permute-start.12 = (f32[2,256,1024]{2,1,0:T(8,128)}, f32[2,256,1024]{2,1,0:T(8,128)S(1)}, u32[]{:S(2)}, u32[]{:S(2)}) collective-permute-start(f32[2,256,1024]{2,1,0:T(8,128)} %get-tuple-element.190), channel_id=1, source_target_pairs={{0,8},{4,12},{8,0},{12,4},{16,24},{20,28},{24,16},{28,20},{1,9},{5... | collective-permute-start | bytes 6291464 | tf_op jit(solution)/shard_map/ppermute | solution.py:613
  351.2 117.5 %collective-permute-start.13 = (f32[2,256,1024]{2,1,0:T(8,128)}, f32[2,256,1024]{2,1,0:T(8,128)}, u32[]{:S(2)}, u32[]{:S(2)}) collective-permute-start(f32[2,256,1024]{2,1,0:T(8,128)} %get-tuple-element.191), channel_id=1, source_target_pairs={{0,16},{4,20},{8,24},{12,28},{16,0},{20,4},{24,8},{28,12},{1,17},{... | collective-permute-start | bytes 6291464 | tf_op jit(solution)/shard_map/ppermute | solution.py:613
  354.9 63.6 %collective-permute-start.14 = (f32[128,2048]{1,0:T(8,128)}, f32[128,2048]{1,0:T(8,128)}, u32[]{:S(2)}, u32[]{:S(2)}) collective-permute-start(f32[128,2048]{1,0:T(8,128)} %add.106), channel_id=1, source_target_pairs={{1,0},{2,3},{5,4},{6,7},{9,8},{10,11},{13,12},{14,15},{17,16},{18,... | collective-permute-start | bytes 3145736 | tf_op jit(solution)/shard_map/ppermute | solution.py:697
  399.9 120.3 %collective-permute-start.21 = (f32[6,2,352,256]{3,2,1,0:T(8,128)}, f32[6,2,352,256]{3,2,1,0:T(8,128)}, u32[]{:S(2)}, u32[]{:S(2)}) collective-permute-start(f32[6,2,352,256]{3,2,1,0:T(8,128)} %get-tuple-element.209), channel_id=1, source_target_pairs={{0,4},{4,0},{8,12},{12,8},{16,20},{20,16},{24,28},{28,24},{1,5},{5... | collective-permute-start | bytes 12976136 | tf_op jit(solution)/shard_map/ppermute | solution.py:681
  402.7 65.9 %collective-permute-start.15 = (f32[128,2048]{1,0:T(8,128)}, f32[128,2048]{1,0:T(8,128)}, u32[]{:S(2)}, u32[]{:S(2)}) collective-permute-start(f32[128,2048]{1,0:T(8,128)} %add.109), channel_id=1, source_target_pairs={{1,0},{2,3},{5,4},{6,7},{9,8},{10,11},{13,12},{14,15},{17,16},{18,... | collective-permute-start | bytes 3145736 | tf_op jit(solution)/shard_map/ppermute | solution.py:697
  418.5 70.3 %collective-permute-start.22 = (f32[6,352,256]{2,1,0:T(8,128)}, f32[6,352,256]{2,1,0:T(8,128)}, u32[]{:S(2)}, u32[]{:S(2)}) collective-permute-start(f32[6,352,256]{2,1,0:T(8,128)} %get-tuple-element.211), channel_id=1, source_target_pairs={{0,4},{4,0},{8,12},{12,8},{16,20},{20,16},{24,28},{28,24},{1,5},{5... | collective-permute-start | bytes 6488072 | tf_op jit(solution)/shard_map/ppermute | solution.py:681
  482.2 8.1 %collective-permute-start.16 = (f32[8,2048]{1,0:T(8,128)S(1)}, f32[8,2048]{1,0:T(8,128)S(1)}, u32[]{:S(2)}, u32[]{:S(2)}) collective-permute-start(f32[8,2048]{1,0:T(8,128)S(1)} %pad.14), channel_id=1, source_target_pairs={{0,4},{4,0},{8,12},{12,8},{16,20},{20,16},{24,28},{28,24},{1,5},{5... | collective-permute-start | bytes 196616 | tf_op jit(solution)/shard_map/ppermute | solution.py:613
  482.2 32.9 %collective-permute-start.20 = (f32[256,1024]{1,0:T(8,128)}, f32[256,1024]{1,0:T(8,128)}, u32[]{:S(2)}, u32[]{:S(2)}) collective-permute-start(f32[256,1024]{1,0:T(8,128)} %get-tuple-element.207), channel_id=1, source_target_pairs={{0,8},{4,12},{8,0},{12,4},{16,24},{20,28},{24,16},{28,20},{1,9},{5... | collective-permute-start | bytes 3145736 | tf_op jit(solution)/shard_map/ppermute | solution.py:613
  483.1 34.5 %collective-permute-start.19 = (f32[256,1024]{1,0:T(8,128)}, f32[256,1024]{1,0:T(8,128)}, u32[]{:S(2)}, u32[]{:S(2)}) collective-permute-start(f32[256,1024]{1,0:T(8,128)} %get-tuple-element.205), channel_id=1, source_target_pairs={{0,16},{4,20},{8,24},{12,28},{16,0},{20,4},{24,8},{28,12},{1,17},{... | collective-permute-start | bytes 3145736 | tf_op jit(solution)/shard_map/ppermute | solution.py:613
  490.4 19.0 %collective-permute-start.17 = (f32[8,2048]{1,0:T(8,128)S(1)}, f32[8,2048]{1,0:T(8,128)S(1)}, u32[]{:S(2)}, u32[]{:S(2)}) collective-permute-start(f32[8,2048]{1,0:T(8,128)S(1)} %add.115), channel_id=1, source_target_pairs={{0,8},{4,12},{8,0},{12,4},{16,24},{20,28},{24,16},{28,20},{1,9},{5... | collective-permute-start | bytes 196616 | tf_op jit(solution)/shard_map/ppermute | solution.py:613
  509.4 4.3 collective-permute-start.18
  (51 other events, 254.9 us)
Sparse Core Ops, SparseCore 0:
  11.5 94.7 all-gather.7
  123.7 89.8 all-gather.9
Sparse Core Ops, SparseCore 1:
  27.0 88.6 all-reduce.4
  325.6 55.8 reduce-scatter.1
  468.8 44.4 all-gather.5

commit v5 on v4

--- a/solution.py
+++ b/solution.py
@@ -298,15 +298,15 @@
     return lax.logistic(nt(gate_rows, tokens)[:1])
 
 
-def own_kernel(experts, tok_ref, cot_ref, route_ref, gate_ref, w1_ref, w2_ref, out_top_ref, out_low_ref, dx_top_ref,
-               dx_low_ref, logit_ref, open_ref):
+def own_kernel(experts, tok_ref, cot_ref, route_ref, gate_ref, w1_ref, w2_ref, out_ref, dx_top_ref, dx_low_ref,
+               logit_ref, open_ref):
     step = pl.program_id(0)
     group, units, width = w2_ref.shape
     shared = step * group >= experts
 
     @pl.when(step == 0)
     def _():
-        for ref in (out_top_ref, out_low_ref, dx_top_ref, dx_low_ref):
+        for ref in (out_ref, dx_top_ref, dx_low_ref):
             ref[...] = jnp.zeros_like(ref)
         logit_ref[...] = jnp.zeros_like(logit_ref)
         open_ref[...] = open_row(gate_ref[...], tok_ref[...])
@@ -323,10 +323,8 @@
         weighted.append(scaled)
         mix_grads.append(mix_grad)
         logit_ref[...] += jnp.where(shared, jnp.sum(act * back, axis=0, keepdims=True), 0.0)
-    rows = out_top_ref.shape[0]
-    out = tn(jnp.concatenate(weighted), w2_ref[...].reshape(group * units, width))
-    out_top_ref[...] += out[:rows]
-    out_low_ref[...] += out[rows:]
+    rows = dx_top_ref.shape[0]
+    out_ref[...] += tn(jnp.concatenate(weighted), w2_ref[...].reshape(group * units, width))
     dx = tn(jnp.concatenate(mix_grads), w1_ref[...].reshape(group * 2 * units, width))
     dx_top_ref[...] += dx[:rows]
     dx_low_ref[...] += dx[rows:]
@@ -357,9 +355,10 @@
             pl.BlockSpec((group, 2, units, width), lambda i: (i, 0, 0, 0)),
             pl.BlockSpec((group, units, width), lambda i: (i, 0, 0)),
         ],
-        out_specs=[*[whole(count // 2, width)] * 4, whole(1, count)],
+        out_specs=[whole(count, width), *[whole(count // 2, width)] * 2, whole(1, count)],
         out_shape=[
-            *[jax.ShapeDtypeStruct((count // 2, width), F32)] * 4,
+            jax.ShapeDtypeStruct((count, width), F32),
+            *[jax.ShapeDtypeStruct((count // 2, width), F32)] * 2,
             jax.ShapeDtypeStruct((1, count), F32),
         ],
         scratch_shapes=[pltpu.VMEM((1, count), F32)],
@@ -540,27 +539,44 @@
     )(at, x_keep, x_got, y_keep, y_got)
 
 
-def weights_kernel(at_ref, mix_grad_ref, weighted_ref, tok_ref, cot_ref, one_mine_ref, one_peer_ref, two_mine_ref,
-                   two_peer_ref):
-    part = one_mine_ref.shape[-1]
-    core = at_ref[0]
-    one = nn(mix_grad_ref[0], tok_ref[...])
-    two = nn(weighted_ref[0], cot_ref[...])
-    for value, mine_ref, peer_ref in ((one, one_mine_ref, one_peer_ref), (two, two_mine_ref, two_peer_ref)):
+def weights_kernel(here, at_ref, mix_grad_ref, weighted_ref, tok_ref, cot_ref, *refs):
+    part = refs[0].shape[-1]
+    expert_refs, shared_refs, peer_refs = refs[:2], refs[2:4], refs[4:]
+    core, step = at_ref[0], pl.program_id(0)
+    products = nn(mix_grad_ref[0], tok_ref[...]), nn(weighted_ref[0], cot_ref[...])
+    for value, expert_ref, shared_ref, peer_ref in zip(products, expert_refs, shared_refs, peer_refs, strict=True):
         low, high = value[:, :part], value[:, part:]
-        mine_ref[...] = jnp.where(core == 0, low, high).reshape(mine_ref.shape)
+        mine = jnp.where(core == 0, low, high)
         peer_ref[...] = jnp.where(core == 0, high, low).reshape(peer_ref.shape)
 
-
-def weight_grads(at, mix_grads, weighted, tokens, cotangent):
+        @pl.when(step < here)
+        def _():
+            expert_ref[...] = mine.reshape(expert_ref.shape)
+
+        @pl.when(step >= here)
+        def _():
+            shared_ref[...] = mine.reshape(shared_ref.shape)
+
+
+def tile_specs(core_of, here, shared, units, part):
+    expert = lambda i, at: core_of(at) * here + jnp.minimum(i, here - 1)
+    common = lambda i, at: core_of(at) * shared + jnp.maximum(i - here, 0)
+    return [
+        pl.BlockSpec((1, 2, units, part), lambda i, at: (expert(i, at), 0, 0, 0)),
+        pl.BlockSpec((1, units, part), lambda i, at: (expert(i, at), 0, 0)),
+        pl.BlockSpec((1, 2, units, part), lambda i, at: (common(i, at), 0, 0, 0)),
+        pl.BlockSpec((1, units, part), lambda i, at: (common(i, at), 0, 0)),
+    ]
+
+
+def weight_grads(at, mix_grads, weighted, tokens, cotangent, here):
     tiles, units, total = weighted.shape
     part = tokens.shape[1] // 2
-    one = jax.ShapeDtypeStruct((tiles, 2, units, part), F32)
-    two = jax.ShapeDtypeStruct((tiles, units, part), F32)
-    one_spec = pl.BlockSpec((1, 2, units, part), lambda i, at: (i, 0, 0, 0))
-    two_spec = pl.BlockSpec((1, units, part), lambda i, at: (i, 0, 0))
+    shared = tiles - here
+    one = lambda count: jax.ShapeDtypeStruct((count, 2, units, part), F32)
+    two = lambda count: jax.ShapeDtypeStruct((count, units, part), F32)
     return pl.pallas_call(
-        weights_kernel,
+        functools.partial(weights_kernel, here),
         grid_spec=pltpu.PrefetchScalarGridSpec(
             num_scalar_prefetch=1,
             grid=(tiles,),
@@ -568,17 +584,60 @@
                 pl.BlockSpec((1, 2 * units, total), lambda i, at: (i, 0, 0)),
                 pl.BlockSpec((1, units, total), lambda i, at: (i, 0, 0)),
                 pl.BlockSpec((total, 2 * part), lambda i, at: (0, 0)),
-                pl.BlockSpec((total, 2 * part), lambda i, at: (0, at[1])),
+                pl.BlockSpec((total, 2 * part), lambda i, at: (0, at[3])),
             ],
-            out_specs=[one_spec, one_spec, two_spec, two_spec],
-        ),
-        out_shape=[one, one, two, two],
+            out_specs=[
+                *tile_specs(lambda at: at[0], here, shared, units, part),
+                pl.BlockSpec((1, 2, units, part), lambda i, at: (i, 0, 0, 0)),
+                pl.BlockSpec((1, units, part), lambda i, at: (i, 0, 0)),
+            ],
+        ),
+        out_shape=[one(2 * here), two(2 * here), one(2 * shared), two(2 * shared), one(tiles), two(tiles)],
         compiler_params=pltpu.CompilerParams(
             dimension_semantics=("arbitrary",), vmem_limit_bytes=VMEM_LIMIT
         ),
         cost_estimate=LIGHT,
         name="weight_grads",
     )(at, mix_grads, weighted, tokens, cotangent)
+
+
+def place_kernel(here, at_ref, one_ref, two_ref, *refs):
+    step = pl.program_id(0)
+    expert_one_ref, expert_two_ref, shared_one_ref, shared_two_ref = refs[-4:]
+
+    @pl.when(step < here)
+    def _():
+        expert_one_ref[...] = one_ref[...]
+        expert_two_ref[...] = two_ref[...]
+
+    @pl.when(step >= here)
+    def _():
+        shared_one_ref[...] = one_ref[...]
+        shared_two_ref[...] = two_ref[...]
+
+
+def place_peer(at, one, two, grads, here):
+    tiles, units, part = two.shape
+    return pl.pallas_call(
+        functools.partial(place_kernel, here),
+        grid_spec=pltpu.PrefetchScalarGridSpec(
+            num_scalar_prefetch=1,
+            grid=(tiles,),
+            in_specs=[
+                pl.BlockSpec((1, 2, units, part), lambda i, at: (i, 0, 0, 0)),
+                pl.BlockSpec((1, units, part), lambda i, at: (i, 0, 0)),
+                *[pl.BlockSpec(memory_space=pl.ANY)] * 4,
+            ],
+            out_specs=tile_specs(lambda at: 1 - at[0], here, tiles - here, units, part),
+        ),
+        out_shape=[jax.ShapeDtypeStruct(g.shape, g.dtype) for g in grads],
+        input_output_aliases={3 + k: k for k in range(4)},
+        compiler_params=pltpu.CompilerParams(
+            dimension_semantics=("arbitrary",), vmem_limit_bytes=32 * 1024 * 1024
+        ),
+        cost_estimate=LIGHT,
+        name="place_peer",
+    )(at, one, two, *grads)
 
 
 def split_kernel(in_ref, out_ref, route_ref):
@@ -681,7 +740,8 @@
     swap = lambda v: lax.ppermute(v, "dp", [(i, i ^ 1) for i in range(n_dp)])
     beside = swap(tokens_wide)
     tok_all = lax.all_gather(tokens_wide, "dp")
-    mlp_top, mlp_low, grad_top, grad_low, logit_grad = own_mlp(tokens, cotangent, route, gate_rows, w1, w2)
+    mlp_part, grad_top, grad_low, logit_grad = own_mlp(tokens, cotangent, route, gate_rows, w1, w2)
+    mlp_sum = lax.psum_scatter(mlp_part, "tensor", scatter_dimension=0, tiled=True)
     line = n_tensor == 4 and n_dp == 8
     spot = lax.axis_index("tensor")
     hide = lambda other, starts, tokens, kept: chip_hidden(
@@ -701,20 +761,21 @@
         got, grad_low, kept = tied((got, grad_low, kept))
         grad_top = grad_top + got
         got, got_low = across(grad_top), inwards(grad_low)
-        got, got_low, mlp_top, tok_all, shared_gate_part, kept = tied(
-            (got, got_low, mlp_top, tok_all, shared_gate_part, kept)
-        )
+        got, got_low, tok_all, shared_gate_part, kept = tied((got, got_low, tok_all, shared_gate_part, kept))
         grad_top, grad_low = grad_top + got, grad_low + got_low
-        end_top, got_low, got = outwards(grad_top), across(grad_low), inwards(mlp_top)
+        grad_top, mlp_sum = tied((grad_top, mlp_sum))
+        mlp_sum = lax.all_gather(mlp_sum, "tensor", axis=0, tiled=True)
+        end_top, got_low = outwards(grad_top), across(grad_low)
         kept = hide(chip ^ 1, in_order, [tok_all], kept)
-        end_top, got_low, got, mlp_low, kept = tied((end_top, got_low, got, mlp_low, kept))
-        grad_low, mlp_top = grad_low + got_low, mlp_top + got
-        end_low, got, got_low = outwards(grad_low), across(mlp_top), inwards(mlp_low)
+        end_top, got_low, kept = tied((end_top, got_low, kept))
+        grad_low = grad_low + got_low
+        end_low = outwards(grad_low)
         kept = hide(chip ^ 2, in_order, [tok_all], kept)
-        end_low, got, got_low, kept = tied((end_low, got, got_low, kept))
+        end_low, mlp_sum, kept = tied((end_low, mlp_sum, kept))
         totals = [grad_top, end_top, grad_low, end_low]
     else:
         is_inner = spot >= 0
+        mlp_sum = lax.all_gather(mlp_sum, "tensor", axis=0, tiled=True)
         kept = []
         for k in range(n_dp // 2):
             kept = hide(jnp.int32(k), in_order, [tok_all], kept)
@@ -723,82 +784,66 @@
 
     normed_one_part, residual_grad, branch_grad, projected_grad, bias_part, mlp_gain_part = attention_back(
         is_inner.astype(jnp.int32)[None], totals, residual, cotangent, gain_two, out_weight, qkv, qkv_weight,
-        cosine, sine, row, col, layer_input, shared_gate_part, n_tensor,
-    )
-    few = count // n_tensor
-    summed = lax.psum_scatter(normed_one_part.reshape(-1, width), "tensor", scatter_dimension=0, tiled=True)
-    own_rows = lambda v: lax.dynamic_slice_in_dim(v, spot * few, few, 0)
+        cosine, sine, row, col, layer_input, shared_gate_part, 1,
+    )
+    summed = lax.psum(normed_one_part.reshape(-1, width), "tensor")
 
     def finish(summed):
-        inputs = own_rows(layer_input).astype(F32)
+        inputs = layer_input.astype(F32)
         factor = lax.rsqrt(jnp.mean(inputs * inputs, axis=-1, keepdims=True) + EPS)
         bias_row = jnp.pad(bias_part, ((0, 0), (0, width - bias_part.shape[1])))
-        small = jnp.concatenate([summed[few : few + 2], mlp_gain_part, bias_row])
-        return norm_back(inputs, factor, gain_one, summed[:few]), jnp.pad(small, ((0, 4), (0, 0)))
+        small = jnp.concatenate([summed[count : count + 2], mlp_gain_part, bias_row])
+        input_grad = (residual_grad + norm_back(inputs, factor, gain_one, summed[:count])).astype(BF16)
+        return input_grad, jnp.pad(small, ((0, 4), (0, 0)))
 
     if line:
-        got, got_low, mlp_top, mlp_low, projected_grad = tied((got, got_low, mlp_top, mlp_low, projected_grad))
-        mlp_top, mlp_low = mlp_top + got, mlp_low + got_low
-        end_top, got_low = outwards(mlp_top), across(mlp_low)
-        mlp_low, projected_grad = tied((mlp_low, projected_grad))
-        at = jnp.stack([core, chip % 2, chip // 2])
-        other_at = jnp.stack([1 - core, chip % 2, chip // 2])
+        at = jnp.stack([core, chip % 2, chip // 2, chip])
+        other_at = jnp.stack([1 - core, chip % 2, chip // 2, chip])
         arrived = swap(token_products(other_at, normed_one, projected_grad, branch_grad, attended, None))
         x_keep, x_send, y_keep, y_send = token_products(
             at, normed_one, projected_grad, branch_grad, attended, arrived
         )
-        x_send, y_send, kept, got_low = tied((x_send, y_send, kept, got_low))
-        mlp_low = mlp_low + got_low
-        end_low = outwards(mlp_low)
+        x_send, y_send, kept = tied((x_send, y_send, kept))
         x_got, y_got = flip(x_send, 2), flip(y_send, 4)
         kept = hide(chip ^ 3, in_order, [tok_all], kept)
-        one_mine, one_peer, two_mine, two_peer = weight_grads(jnp.stack([core, chip]), *kept, cot_low)
-        one_mine, one_peer, summed = tied((one_mine, one_peer, summed))
+        *grads, one_peer, two_peer = weight_grads(at, *kept, cot_low, experts // 2)
+        one_peer, x_got, y_got = tied((one_peer, x_got, y_got))
+        x_own, x_send, y_own, y_send = turned_blocks(at, x_keep, x_got, y_keep, y_got)
+        x_send, y_send, one_peer, two_peer, summed = tied((x_send, y_send, one_peer, two_peer, summed))
+        x_got, y_got = flip(x_send, 4), flip(y_send, 2)
         one_peer, two_peer = swap(one_peer), swap(two_peer)
+        summed, one_peer, two_peer = tied((summed, one_peer, two_peer))
+        expert_one, expert_two, shared_one, shared_two = place_peer(at, one_peer, two_peer, grads, experts // 2)
+        expert_one, summed = tied((expert_one, summed))
         input_grad, small = finish(summed)
-        input_grad, x_got, y_got, end_top, end_low = tied((input_grad, x_got, y_got, end_top, end_low))
-        input_grad = lax.all_gather(input_grad, "tensor", axis=0, tiled=True)
-        x_own, x_send, y_own, y_send = turned_blocks(at, x_keep, x_got, y_keep, y_got)
-        x_got, y_got = flip(x_send, 4), flip(y_send, 2)
-        small, x_own = tied((small, x_own))
         for bit in (1, 2, 4):
             small = small + flip(small, bit)
+        x_got, y_got, input_grad, small, expert_one = tied((x_got, y_got, input_grad, small, expert_one))
         both = jnp.concatenate([x_own + x_got, y_own + y_got], axis=1)
         cut = projected_grad.shape[1]
         qkv_weight_grad, out_weight_grad = both[:, :cut], both[:, cut:].T
-        mlp_sum = jnp.where(
-            is_inner, jnp.concatenate([mlp_top, mlp_low]), jnp.concatenate([end_top, end_low])
-        )
     else:
-        one_mine, one_peer, two_mine, two_peer = weight_grads(jnp.stack([core, chip]), *kept, cot_low)
+        at = jnp.stack([core, core, core, chip])
+        *grads, one_peer, two_peer = weight_grads(at, *kept, cot_low, experts // 2)
         one_peer, two_peer = swap(one_peer), swap(two_peer)
+        expert_one, expert_two, shared_one, shared_two = place_peer(at, one_peer, two_peer, grads, experts // 2)
         input_grad, small = finish(summed)
-        input_grad = lax.all_gather(input_grad, "tensor", axis=0, tiled=True)
         small = lax.psum(small, "dp")
         joint = lambda v: v.reshape(2, count, BLOCKS // 2, -1).transpose(1, 2, 0, 3).reshape(count, width)
         out_weight_grad = lax.psum_scatter(tn(attended, joint(branch_grad)), "dp", scatter_dimension=1, tiled=True)
         qkv_weight_grad = lax.psum_scatter(
             tn(joint(normed_one), projected_grad), "dp", scatter_dimension=0, tiled=True
         )
-        mlp_sum = lax.psum(jnp.concatenate([mlp_top, mlp_low]), "tensor")
 
     attn_gain_grad, shared_gate_grad, mlp_gain_grad = lax.dynamic_slice(small, (0, me * part), (3, part))
     bias_cols = 3 * head_dim // n_dp
     bias = small[3, : heads_here * 3 * head_dim].reshape(heads_here, 3 * head_dim)
     qkv_bias_grad = lax.dynamic_slice(bias, (0, me * bias_cols), (heads_here, bias_cols))
-    input_grad = (residual_grad + input_grad).astype(BF16)
     layer_output = (residual + mlp_sum).astype(BF16)
 
-    def joined(mine, peer):
-        return jnp.where(core == 0, jnp.concatenate([mine, peer]), jnp.concatenate([peer, mine]))
-
-    half = experts // 2
-    expert_gate_up_grad = jnp.transpose(joined(one_mine[:half], one_peer[:half]), (0, 3, 1, 2))
-    expert_down_grad = joined(two_mine[:half], two_peer[:half])
-    shared_gate_up_grad = jnp.transpose(joined(one_mine[half:], one_peer[half:]), (3, 1, 0, 2)).reshape(
-        part, 2, shared * units
-    )
-    shared_down_grad = joined(two_mine[half:], two_peer[half:]).reshape(shared * units, part)
+    expert_gate_up_grad = jnp.transpose(expert_one, (0, 3, 1, 2))
+    shared_gate_up_grad = jnp.transpose(shared_one, (3, 1, 0, 2)).reshape(part, 2, shared * units)
+    shared_down_grad = shared_two.reshape(shared * units, part)
     return (
         layer_output,
         input_grad,
@@ -808,7 +853,7 @@
         out_weight_grad,
         mlp_gain_grad,
         expert_gate_up_grad,
-        expert_down_grad,
+        expert_two,
         shared_gate_up_grad,
         shared_down_grad,
         shared_gate_grad,

time: 544 us -> 507 us (0.932)
  other arithmetic: 69.9 us -> 49.6 us
  starting transfers between devices: 41.3 us -> 23.8 us
  Pallas kernels: 205 us -> 216 us
  local copies, waits for them, and re-layouts: 91.9 us -> 86 us
    ppermute x4 -> x2, waiting for transfers between devices: 63.4 us -> 32.6 us  [shards(): outwards = lambda v: lax.ppermute(v, 'tensor', [(1, 0), (2, 3)])]
    ppermute x4 -> x2, waiting for transfers between devices: 20.4 us -> 41.6 us  [shards(): inwards = lambda v: lax.ppermute(v, 'tensor', [(0, 1), (3, 2)])]
    slice x10 -> x2, local copies, waits for them, and re-layouts: 13.6 us -> 0.12 us  [finish(): small = jnp.concatenate([summed[count:count + 2], mlp_gain_part, bias_row])]
    ppermute x4 -> x2, starting transfers between devices: 22.6 us -> 11 us  [shards(): inwards = lambda v: lax.ppermute(v, 'tensor', [(0, 1), (3, 2)])]
    pallas_call x1 -> x2, Pallas kernels: 19.8 us -> 30.7 us  [the longest x1 23 us: weight_grads(): pl.pallas_call(functools.partial(weights_kernel, here), grid_spec=pltpu.P...]
    add x5 -> x1, other arithmetic: 11.4 us -> 1.43 us  [shards(): grad_low = grad_low + got_low]
    psum x0 -> x1, waiting for transfers between devices: none -> 6.64 us  [shards(): summed = lax.psum(normed_one_part.reshape(-1, width), 'tensor')]
    unnamed x110 -> x104, local copies, waits for them, and re-layouts: 30.1 us -> 36.3 us
  transfers between devices with their start and end apart: 28 -> 23, of which waited for: 7 -> 10; matrix products, arithmetic and copies ran while one was open for 23% -> 19% of each run, Pallas kernels for 34% -> 38%
where the time goes in v5:
time: 507 us; the launch traced here: 506 us
  Pallas kernels  216 us (43%)
  waiting for transfers between devices  112 us (22%)
  local copies, waits for them, and re-layouts  86 us (17%)
  other arithmetic  49.6 us (10%)
  starting transfers between devices  23.8 us (5%)
  between operations  17.6 us (3%)
    pallas_call x4, Pallas kernels, chip_hidden(): pl.pallas_call(functools.partial(chip_kernel, here), grid_spec=pltpu.Pref...  93 us
    ppermute x2, waiting for transfers between devices, shards(): inwards = lambda v: lax.ppermute(v, 'tensor', [(0, 1), (3, 2)])  41.6 us
    pallas_call x1, Pallas kernels, own_mlp(): pl.pallas_call(functools.partial(own_kernel, experts), grid=(tiles // gro...  39.5 us
    unnamed x104, local copies, waits for them, and re-layouts  36.3 us
    ppermute x2, waiting for transfers between devices, shards(): outwards = lambda v: lax.ppermute(v, 'tensor', [(1, 0), (2, 3)])  32.6 us
    optimization_barrier x1, local copies, waits for them, and re-layouts, shards(): attn_part, shared_gate_up = tied((attn_part, shared_gate_up))  28.8 us
    concatenate x1, other arithmetic, shards(): jnp.concatenate([jnp.transpose(expert_gate_up, (0, 2, 3, 1)), jnp.transpo...  24.7 us
    pallas_call x1, Pallas kernels, weight_grads(): pl.pallas_call(functools.partial(weights_kernel, here), grid_spec=pltpu.P...  23 us
  transfers between devices with their start and end apart: 23, of which 10 were waited for; matrix products, arithmetic and copies ran while one was open for 19% of the time, Pallas kernels for 38%

profile of v5, /device:TPU:0, one launch (start us, length us, event | category | flops | bytes accessed | tf_op | source)
XLA Modules:
  0.0 505.5 jit_solution(9898979019457795283)
XLA Ops:
  13.1 2.8 copy-done.3
  15.8 7.1 %attention.1 = (f32[256,2048]{1,0:T(8,128)S(1)}, bf16[2,256,1024]{2,1,0:T(8,128)(2,1)S(1)}, bf16[256,1536]{1,0:T(8,128)(2,1)S(1)}, bf16[256,512]{1,0:T(8,128)(2,1)S(1)}) custom-call(bf16[256,2048]{1,0:T(8,128)(2,1)S(1)} %copy-done.1, f32[1,2048]{1,0:T(1,128)S(1)} %bitcast.39, bf16[2048,1536]{1,0:T(8,128)(2,1)S(1)} %copy-done.3, ...), custom_call_target="tpu_custom_call" | custom-call | flops 1048576 | bytes 65536 | tf_op jit(solution)/shard_map/attention/pallas_call | solution.py:97
  26.9 28.8 %copy.53 = bf16[2048,2,1408]{0,2,1:T(8,128)(2,1)} copy(bf16[2048,2,1408]{2,1,0:T(2,128)(2,1)} %param.26) | data formatting | bytes 23068672 | tf_op jit(solution)/shard_map/optimization_barrier | solution.py:727
  55.7 12.7 %copy.60 = bf16[2048,2,4,352]{0,3,1,2:T(8,128)(2,1)} copy(bf16[2048,2,4,352]{0,3,2,1:T(8,128)(2,1)} %bitcast.52) | data formatting | bytes 23068672 | tf_op jit(solution)/shard_map/reshape | solution.py:732
  70.9 6.9 %pad_maximum_fusion.1.w2_ref = bf16[12,352,2048]{2,1,0:T(8,128)(2,1)} fusion(bf16[4,352,2048]{2,1,0:T(8,128)(2,1)S(1)} %bitcast.61, bf16[8,352,2048]{2,1,0:T(8,128)(2,1)S(1)} %bitcast.57), kind=kLoop, calls=%fused_computation.1 | loop fusion | flops 8650752 | bytes 34603008 | tf_op jit(solution)/shard_map/concatenate | solution.py:735
  77.7 24.7 %pad_maximum_fusion.w1_ref = bf16[12,2,352,2048]{3,2,1,0:T(8,128)(2,1)} fusion(bf16[4,2,352,2048]{3,2,1,0:T(8,128)(2,1)} %bitcast.53, bf16[8,2,352,2048]{3,2,1,0:T(8,128)(2,1)} %bitcast.54), kind=kLoop, calls=%fused_computation | loop fusion | flops 17301504 | bytes 69206016 | tf_op jit(solution)/shard_map/concatenate | solution.py:729
  102.4 3.9 all-gather.8.cloned.1.call-done
  106.3 7.9 %split_rounded.1 = (bf16[2048,2048]{1,0:T(8,128)(2,1)S(1)}, f32[8,8,256]{2,1,0:T(8,128)S(1)}) custom-call(f32[8,264,2048]{2,1,0:T(8,128)} %bitcast.55), custom_call_target="tpu_custom_call" | custom-call | tf_op jit(solution)/shard_map/split_rounded/pallas_call | solution.py:652
  114.2 3.3 copy-done
  119.1 2.2 second_norm.1
  125.0 39.5 %own_mlp.1 = (f32[256,2048]{1,0:T(8,128)}, f32[128,2048]{1,0:T(8,128)}, f32[128,2048]{1,0:T(8,128)}, f32[1,256]{1,0:T(1,128)}) custom-call(bf16[256,2048]{1,0:T(8,128)(2,1)} %copy-done.10, bf16[256,2048]{1,0:T(8,128)(2,1)} %cot_ref.3, f32[8,1,256]{2,1,0:T(1,128)} %broadcast_in_dim.50.route_ref, bf16[16,2048]{1,0:T(8,128)(2,1)} %broadcast_in_dim.51.gate_ref, ...), custom_call_target="tpu_custom_call" | custom-call | flops 1048576 | bytes 65536 | tf_op jit(solution)/shard_map/own_mlp/pallas_call | solution.py:347
  164.8 4.3 collective-permute-start
  173.5 23.1 %chip_hidden.4 = (bf16[6,704,2048]{2,1,0:T(8,128)(2,1)}, bf16[6,352,2048]{2,1,0:T(8,128)(2,1)}, bf16[2048,512]{1,0:T(8,128)(2,1)}) custom-call(s32[5]{0:T(128)} %stack.67.at_ref, f32[256,2048]{1,0:T(8,128)} %get-tuple-element.128.even_ref, f32[256,2048]{1,0:T(8,128)} %copy-done.36, bf16[2048,2048]{1,0:T(8,128)(2,1)} %copy-done, f32[8,8,256]{2,1,0:T(8,128)} %copy-done.23, ...), custom_call_target="tpu_custom_call" | custom-call | flops 1048576 | bytes 65536 | tf_op jit(solution)/shard_map/chip_hidden/pallas_call | solution.py:423
  196.6 16.3 %collective-permute-done = f32[128,2048]{1,0:T(8,128)} collective-permute-done((f32[128,2048]{1,0:T(8,128)}, f32[128,2048]{1,0:T(8,128)}, u32[]{:S(2)}, u32[]{:S(2)}) %collective-permute-start) | collective-permute-done | bytes 1048608 | tf_op jit(solution)/shard_map/ppermute | solution.py:755
  215.0 6.7 %collective-permute-start.3 = (f32[128,2048]{1,0:T(8,128)S(1)}, f32[128,2048]{1,0:T(8,128)}, u32[]{:S(2)}, u32[]{:S(2)}) collective-permute-start(f32[128,2048]{1,0:T(8,128)S(1)} %copy-done.37), channel_id=1, source_target_pairs={{0,1},{3,2},{4,5},{7,6},{8,9},{11,10},{12,13},{15,14},{16,17},{19,... | collective-permute-start | bytes 3145736 | tf_op jit(solution)/shard_map/ppermute | solution.py:755
  222.1 25.3 %collective-permute-done.3 = f32[128,2048]{1,0:T(8,128)} collective-permute-done((f32[128,2048]{1,0:T(8,128)S(1)}, f32[128,2048]{1,0:T(8,128)}, u32[]{:S(2)}, u32[]{:S(2)}) %collective-permute-start.3) | collective-permute-done | bytes 1048608 | tf_op jit(solution)/shard_map/ppermute | solution.py:755
  252.9 23.5 %chip_hidden.5 = (bf16[6,704,2048]{2,1,0:T(8,128)(2,1)}, bf16[6,352,2048]{2,1,0:T(8,128)(2,1)}, bf16[2048,512]{1,0:T(8,128)(2,1)}) custom-call(s32[5]{0:T(128)} %stack.69.at_ref, f32[8,256,2048]{2,1,0:T(8,128)} %bitcast.46, f32[8,256,2048]{2,1,0:T(8,128)} %bitcast.47, ...), custom_call_target="tpu_custom_call", output_to_operand_aliasing={{0}: (8, {}), {1}: (9, {}), {2}: (10, {})} | custom-call | flops 1048576 | bytes 65536 | tf_op jit(solution)/shard_map/chip_hidden/pallas_call | solution.py:423
  276.4 32.2 %collective-permute-done.4.got_top_ref = f32[128,2048]{1,0:T(8,128)S(1)} collective-permute-done((f32[128,2048]{1,0:T(8,128)S(1)}, f32[128,2048]{1,0:T(8,128)S(1)}, u32[]{:S(2)}, u32[]{:S(2)}) %collective-permute-start.4) | collective-permute-done | bytes 1048608 | tf_op jit(solution)/shard_map/ppermute | solution.py:757
  313.8 23.2 %chip_hidden.6 = (bf16[6,704,2048]{2,1,0:T(8,128)(2,1)}, bf16[6,352,2048]{2,1,0:T(8,128)(2,1)}, bf16[2048,512]{1,0:T(8,128)(2,1)}) custom-call(s32[5]{0:T(128)} %stack.71.at_ref, f32[8,256,2048]{2,1,0:T(8,128)} %bitcast.48, f32[8,256,2048]{2,1,0:T(8,128)} %bitcast.49, ...), custom_call_target="tpu_custom_call", output_to_operand_aliasing={{0}: (8, {}), {1}: (9, {}), {2}: (10, {})} | custom-call | flops 1048576 | bytes 65536 | tf_op jit(solution)/shard_map/chip_hidden/pallas_call | solution.py:423
  338.7 14.4 %attention_back.1 = (f32[1,264,2048]{2,1,0:T(8,128)}, f32[256,2048]{1,0:T(8,128)}, bf16[2,256,1024]{2,1,0:T(8,128)(2,1)S(1)}, bf16[256,1536]{1,0:T(8,128)(2,1)S(...) custom-call(s32[1]{0:T(128)} %bitcast.23.inner_ref, f32[128,2048]{1,0:T(8,128)S(1)} %add.90.held_top_ref, ...), custom_call_target="tpu_custom_call" | custom-call | flops 1048576 | bytes 65536 | tf_op jit(solution)/shard_map/attention_back/pallas_call | solution.py:239
  354.9 6.8 %token_products.2 = f32[4,256,2048]{2,1,0:T(8,128)} custom-call(s32[4]{0:T(128)} %add_add_fusion.1.at_ref, bf16[2,256,1024]{2,1,0:T(8,128)(2,1)} %copy-done.8, bf16[256,1536]{1,0:T(8,128)(2,1)} %copy-done.12, bf16[2,256,1024]{2,1,0:T(8,128)(2,1)} %copy-done.9, bf16[256,512]{1,0:T(8,128)(2,1)} %copy-done.28), custom_call_target="tpu_custom_call" | custom-call | flops 1048576 | bytes 65536 | tf_op jit(solution)/shard_map/token_products/pallas_call | solution.py:500
  362.3 12.9 %collective-permute-done.7.arrived_ref = f32[4,256,2048]{2,1,0:T(8,128)} collective-permute-done((f32[4,256,2048]{2,1,0:T(8,128)}, f32[4,256,2048]{2,1,0:T(8,128)}, u32[]{:S(2)}, u32[]{:S(2)}) %collective-permute-start.7) | collective-permute-done | bytes 8388640 | tf_op jit(solution)/shard_map/ppermute | solution.py:740
  375.1 9.8 %token_products.3 = (f32[2,256,1024]{2,1,0:T(8,128)}, f32[2,256,1024]{2,1,0:T(8,128)}, f32[2,256,1024]{2,1,0:T(8,128)}, f32[2,256,1024]{2,1,0:T(8,128)}) custom-call(s32[4]{0:T(128)} %add_add_fusion.at_ref, bf16[2,256,1024]{2,1,0:T(8,128)(2,1)} %copy-done.8, bf16[256,1536]{1,0:T(8,128)(2,1)} %copy-done.12, bf16[2,256,1024]{2,1,0:T(8,128)(2,1)} %copy-done.9, ...), custom_call_target="tpu_custom_call" | custom-call | flops 1048576 | bytes 65536 | tf_op jit(solution)/shard_map/token_products/pallas_call | solution.py:500
  386.8 23.2 %chip_hidden.7 = (bf16[6,704,2048]{2,1,0:T(8,128)(2,1)}, bf16[6,352,2048]{2,1,0:T(8,128)(2,1)}, bf16[2048,512]{1,0:T(8,128)(2,1)}) custom-call(s32[5]{0:T(128)} %stack.78.at_ref, f32[8,256,2048]{2,1,0:T(8,128)} %bitcast.50, f32[8,256,2048]{2,1,0:T(8,128)} %bitcast.51, ...), custom_call_target="tpu_custom_call", output_to_operand_aliasing={{0}: (8, {}), {1}: (9, {}), {2}: (10, {})} | custom-call | flops 1048576 | bytes 65536 | tf_op jit(solution)/shard_map/chip_hidden/pallas_call | solution.py:423
  410.0 23.0 %weight_grads.1 = (f32[8,2,352,256]{3,2,1,0:T(8,128)}, f32[8,352,256]{2,1,0:T(8,128)}, f32[4,2,352,256]{3,2,1,0:T(8,128)}, f32[4,352,256]{2,1,0:T(8,128)}, f32[6...) custom-call(s32[4]{0:T(128)} %add_add_fusion.at_ref, bf16[6,704,2048]{2,1,0:T(8,128)(2,1)} %get-tuple-element.176.mix_grad_ref, ...), custom_call_target="tpu_custom_call" | custom-call | flops 1048576 | bytes 65536 | tf_op jit(solution)/shard_map/weight_grads/pallas_call | solution.py:578
  439.2 4.7 turned_blocks.1
  444.8 6.6 %all-reduce.8.cloned.1.call-done = f32[264,2048]{1,0:T(8,128)} async-done(((f32[264,2048]{1,0:T(8,128)}), f32[264,2048]{1,0:T(8,128)}) %all-reduce.8.cloned.1.call-update) | async-done | bytes 2162704 | tf_op jit(solution)/shard_map/psum | solution.py:789
  452.0 3.1 add_convert_fusion
  458.0 4.2 collective-permute-done.13.two_ref
  462.3 7.7 %place_peer.1 = (f32[8,2,352,256]{3,2,1,0:T(8,128)}, f32[8,352,256]{2,1,0:T(8,128)}, f32[4,2,352,256]{3,2,1,0:T(8,128)S(1)}, f32[4,352,256]{2,1,0:T(8,128)}) custom-call(s32[4]{0:T(128)S(1)} %copy-done.33, f32[6,2,352,256]{3,2,1,0:T(8,128)} %collective-permute-done.12.one_ref, ...), custom_call_target="tpu_custom_call", output_to_operand_aliasing={{0}: (3, {}), {1}: (4, {}), {2}: (5, {}), {3}: (6, {})} | custom-call | flops 1048576 | bytes 65536 | tf_op jit(solution)/shard_map/place_peer/pallas_call | solution.py:621
  473.6 9.3 %collective-permute-done.15 = f32[8,2048]{1,0:T(8,128)S(1)} collective-permute-done((f32[8,2048]{1,0:T(8,128)S(1)}, f32[8,2048]{1,0:T(8,128)S(1)}, u32[]{:S(2)}, u32[]{:S(2)}) %collective-permute-start.15) | collective-permute-done | bytes 65568 | tf_op jit(solution)/shard_map/ppermute | solution.py:672
  487.0 5.6 %copy.58 = f32[256,2,1408]{2,1,0:T(2,128)} copy(f32[256,2,1408]{0,2,1:T(8,128)} %bitcast.58) | data formatting | bytes 5767168
  (190 shorter events, 62.2 us)
Async XLA Ops:
  8.0 98.3 %all-gather.8.cloned.1.call-start = ((), (), s32[]{:S(2)}) async-start(), calls=%async_computation.5 | async-start | bytes 19464192 | tf_op jit(solution)/shard_map/all_gather | solution.py:710
  11.2 106.3 %all-reduce.6.cloned.1.call-start = ((), (), s32[]{:S(2)}) async-start(), calls=%async_computation.1 | async-start | bytes 4194304 | tf_op jit(solution)/shard_map/psum | solution.py:728
  26.9 220.6 %all-gather.10.cloned.1.call-start = ((), (), s32[]{:S(2)}) async-start(), calls=%async_computation.6 | async-start | bytes 18874368 | tf_op jit(solution)/shard_map/all_gather | solution.py:742
  123.7 123.9 %reduce-scatter.2.cloned.1.call-start = ((), (), s32[]{:S(2)}) async-start(), calls=%async_computation.2 | async-start | bytes 2621440 | tf_op jit(solution)/shard_map/reduce_scatter | solution.py:744
  164.5 172.9 %all-gather.6.cloned.1.call-start = ((), (), s32[]{:S(2)}) async-start(), calls=%async_computation.3 | async-start | bytes 2621440 | tf_op jit(solution)/shard_map/all_gather | solution.py:767
  164.6 7.6 %collective-permute-start.1 = (f32[256,2048]{1,0:T(8,128)}, f32[256,2048]{1,0:T(8,128)S(1)}, u32[]{:S(2)}, u32[]{:S(2)}) collective-permute-start(f32[256,2048]{1,0:T(8,128)} %get-tuple-element.128.even_ref), channel_id=1, source_target_pairs={{0,4},{4,0},{8,12},{12,8},{16,20},{20,16},{24,28},{28,24},{1,5},{5... | collective-permute-start | bytes 6291464 | tf_op jit(solution)/shard_map/ppermute | solution.py:740
  164.8 48.0 %collective-permute-start = (f32[128,2048]{1,0:T(8,128)}, f32[128,2048]{1,0:T(8,128)}, u32[]{:S(2)}, u32[]{:S(2)}) collective-permute-start(f32[128,2048]{1,0:T(8,128)} %get-tuple-element.125), channel_id=1, source_target_pairs={{0,1},{3,2},{4,5},{7,6},{8,9},{11,10},{12,13},{15,14},{16,17},{19,... | collective-permute-start | bytes 3145736 | tf_op jit(solution)/shard_map/ppermute | solution.py:755
  172.2 40.7 %copy-start.38 = (f32[128,2048]{1,0:T(8,128)S(1)}, f32[128,2048]{1,0:T(8,128)}, u32[]{:S(2)}) copy-start(f32[128,2048]{1,0:T(8,128)} %get-tuple-element.125) | copy-start | bytes 3145732
  196.6 18.5 %copy-start.37 = (f32[128,2048]{1,0:T(8,128)S(1)}, f32[128,2048]{1,0:T(8,128)}, u32[]{:S(2)}) copy-start(f32[128,2048]{1,0:T(8,128)} %get-tuple-element.134) | copy-start | bytes 3145732
  196.6 25.2 %copy-start.11 = (bf16[256,2048]{1,0:T(8,128)(2,1)S(1)}, bf16[256,2048]{1,0:T(8,128)(2,1)}, u32[]{:S(2)}) copy-start(bf16[256,2048]{1,0:T(8,128)(2,1)} %copy-done.10) | copy-start | bytes 3145732
  196.6 25.2 %copy-start.45 = (f32[1,256]{1,0:T(1,128)S(1)}, f32[1,256]{1,0:T(1,128)}, u32[]{:S(2)}) copy-start(f32[1,256]{1,0:T(1,128)} %get-tuple-element.127) | copy-start | bytes 3076
  214.3 7.8 %collective-permute-start.2 = (f32[128,2048]{1,0:T(8,128)S(1)}, f32[128,2048]{1,0:T(8,128)S(1)}, u32[]{:S(2)}, u32[]{:S(2)}) collective-permute-start(f32[128,2048]{1,0:T(8,128)S(1)} %add.88), channel_id=1, source_target_pairs={{1,2},{2,1},{5,6},{6,5},{9,10},{10,9},{13,14},{14,13},{17,18},{18,... | collective-permute-start | bytes 3145736 | tf_op jit(solution)/shard_map/ppermute | solution.py:756
  215.0 32.4 %collective-permute-start.3 = (f32[128,2048]{1,0:T(8,128)S(1)}, f32[128,2048]{1,0:T(8,128)}, u32[]{:S(2)}, u32[]{:S(2)}) collective-permute-start(f32[128,2048]{1,0:T(8,128)S(1)} %copy-done.37), channel_id=1, source_target_pairs={{0,1},{3,2},{4,5},{7,6},{8,9},{11,10},{12,13},{15,14},{16,17},{19,... | collective-permute-start | bytes 3145736 | tf_op jit(solution)/shard_map/ppermute | solution.py:755
  247.6 203.9 %all-reduce.8.cloned.1.call-start = ((), (), s32[]{:S(2)}) async-start(), calls=%async_computation.4 | async-start | bytes 4325376 | tf_op jit(solution)/shard_map/psum | solution.py:789
  249.3 59.3 %collective-permute-start.4 = (f32[128,2048]{1,0:T(8,128)S(1)}, f32[128,2048]{1,0:T(8,128)S(1)}, u32[]{:S(2)}, u32[]{:S(2)}) collective-permute-start(f32[128,2048]{1,0:T(8,128)S(1)} %add.90.held_top_ref), channel_id=1, source_target_pairs={{1,0},{2,3},{5,4},{6,7},{9,8},{10,11},{13,12},{14,15},{17,16},{18,... | collective-permute-start | bytes 3145736 | tf_op jit(solution)/shard_map/ppermute | solution.py:757
  250.6 59.0 %collective-permute-start.5 = (f32[128,2048]{1,0:T(8,128)S(1)}, f32[128,2048]{1,0:T(8,128)}, u32[]{:S(2)}, u32[]{:S(2)}) collective-permute-start(f32[128,2048]{1,0:T(8,128)S(1)} %add.89), channel_id=1, source_target_pairs={{1,2},{2,1},{5,6},{6,5},{9,10},{10,9},{13,14},{14,13},{17,18},{18,... | collective-permute-start | bytes 3145736 | tf_op jit(solution)/shard_map/ppermute | solution.py:756
  311.0 26.4 %collective-permute-start.6 = (f32[128,2048]{1,0:T(8,128)S(1)}, f32[128,2048]{1,0:T(8,128)}, u32[]{:S(2)}, u32[]{:S(2)}) collective-permute-start(f32[128,2048]{1,0:T(8,128)S(1)} %add.91.held_low_ref), channel_id=1, source_target_pairs={{1,0},{2,3},{5,4},{6,7},{9,8},{10,11},{13,12},{14,15},{17,16},{18,... | collective-permute-start | bytes 3145736 | tf_op jit(solution)/shard_map/ppermute | solution.py:757
  313.8 23.7 %copy-start.20 = (f32[256,128]{1,0:T(8,128)S(1)}, f32[256,128]{1,0:T(8,128)}, u32[]{:S(2)}) copy-start(f32[256,128]{1,0:T(8,128)} %copy-done.19) | copy-start | bytes 393220
  313.8 23.7 %copy-start.22 = (f32[256,128]{1,0:T(8,128)S(1)}, f32[256,128]{1,0:T(8,128)}, u32[]{:S(2)}) copy-start(f32[256,128]{1,0:T(8,128)} %copy-done.21) | copy-start | bytes 393220
  313.8 23.7 %copy-start.30 = (bf16[256,1536]{1,0:T(8,128)(2,1)S(1)}, bf16[256,1536]{1,0:T(8,128)(2,1)}, u32[]{:S(2)}) copy-start(bf16[256,1536]{1,0:T(8,128)(2,1)} %copy-done.29) | copy-start | bytes 2359300
  313.8 23.7 %copy-start.32 = (s32[256]{0:T(256)S(1)}, s32[256]{0:T(256)}, u32[]{:S(2)}) copy-start(s32[256]{0:T(256)} %param.16) | copy-start | bytes 3076
  361.6 13.5 %collective-permute-start.7 = (f32[4,256,2048]{2,1,0:T(8,128)}, f32[4,256,2048]{2,1,0:T(8,128)}, u32[]{:S(2)}, u32[]{:S(2)}) collective-permute-start(f32[4,256,2048]{2,1,0:T(8,128)} %token_products.2), channel_id=1, source_target_pairs={{0,4},{4,0},{8,12},{12,8},{16,20},{20,16},{24,28},{28,24},{1,5},{5... | collective-permute-start | bytes 25165832 | tf_op jit(solution)/shard_map/ppermute | solution.py:740
  385.0 48.1 %collective-permute-start.8 = (f32[2,256,1024]{2,1,0:T(8,128)}, f32[2,256,1024]{2,1,0:T(8,128)S(1)}, u32[]{:S(2)}, u32[]{:S(2)}) collective-permute-start(f32[2,256,1024]{2,1,0:T(8,128)} %get-tuple-element.180), channel_id=1, source_target_pairs={{0,8},{4,12},{8,0},{12,4},{16,24},{20,28},{24,16},{28,20},{1,9},{5... | collective-permute-start | bytes 6291464 | tf_op jit(solution)/shard_map/ppermute | solution.py:672
  386.2 48.1 %collective-permute-start.9 = (f32[2,256,1024]{2,1,0:T(8,128)}, f32[2,256,1024]{2,1,0:T(8,128)}, u32[]{:S(2)}, u32[]{:S(2)}) collective-permute-start(f32[2,256,1024]{2,1,0:T(8,128)} %get-tuple-element.181), channel_id=1, source_target_pairs={{0,16},{4,20},{8,24},{12,28},{16,0},{20,4},{24,8},{28,12},{1,17},{... | collective-permute-start | bytes 6291464 | tf_op jit(solution)/shard_map/ppermute | solution.py:672
  410.0 24.4 %copy-start.33 = (s32[4]{0:T(128)S(1)}, s32[4]{0:T(128)}, u32[]{:S(2)}) copy-start(s32[4]{0:T(128)} %add_add_fusion.at_ref) | copy-start | bytes 52
  451.5 10.8 %collective-permute-start.12 = (f32[6,2,352,256]{3,2,1,0:T(8,128)}, f32[6,2,352,256]{3,2,1,0:T(8,128)}, u32[]{:S(2)}, u32[]{:S(2)}) collective-permute-start(f32[6,2,352,256]{3,2,1,0:T(8,128)} %get-tuple-element.194), channel_id=1, source_target_pairs={{0,4},{4,0},{8,12},{12,8},{16,20},{20,16},{24,28},{28,24},{1,5},{5... | collective-permute-start | bytes 12976136 | tf_op jit(solution)/shard_map/ppermute | solution.py:740
  451.5 10.8 %collective-permute-start.13 = (f32[6,352,256]{2,1,0:T(8,128)}, f32[6,352,256]{2,1,0:T(8,128)}, u32[]{:S(2)}, u32[]{:S(2)}) collective-permute-start(f32[6,352,256]{2,1,0:T(8,128)} %get-tuple-element.195), channel_id=1, source_target_pairs={{0,4},{4,0},{8,12},{12,8},{16,20},{20,16},{24,28},{28,24},{1,5},{5... | collective-permute-start | bytes 6488072 | tf_op jit(solution)/shard_map/ppermute | solution.py:740
  455.1 37.6 %collective-permute-start.10 = (f32[256,1024]{1,0:T(8,128)}, f32[256,1024]{1,0:T(8,128)S(1)}, u32[]{:S(2)}, u32[]{:S(2)}) collective-permute-start(f32[256,1024]{1,0:T(8,128)} %get-tuple-element.190), channel_id=1, source_target_pairs={{0,16},{4,20},{8,24},{12,28},{16,0},{20,4},{24,8},{28,12},{1,17},{... | collective-permute-start | bytes 3145736 | tf_op jit(solution)/shard_map/ppermute | solution.py:672
  456.6 36.1 %collective-permute-start.11 = (f32[256,1024]{1,0:T(8,128)}, f32[256,1024]{1,0:T(8,128)}, u32[]{:S(2)}, u32[]{:S(2)}) collective-permute-start(f32[256,1024]{1,0:T(8,128)} %get-tuple-element.191), channel_id=1, source_target_pairs={{0,8},{4,12},{8,0},{12,4},{16,24},{20,28},{24,16},{28,20},{1,9},{5... | collective-permute-start | bytes 3145736 | tf_op jit(solution)/shard_map/ppermute | solution.py:672
  470.8 1.3 collective-permute-start.14
  472.1 10.9 %collective-permute-start.15 = (f32[8,2048]{1,0:T(8,128)S(1)}, f32[8,2048]{1,0:T(8,128)S(1)}, u32[]{:S(2)}, u32[]{:S(2)}) collective-permute-start(f32[8,2048]{1,0:T(8,128)S(1)} %pad_add_fusion), channel_id=1, source_target_pairs={{0,8},{4,12},{8,0},{12,4},{16,24},{20,28},{24,16},{28,20},{1,9},{5... | collective-permute-start | bytes 196616 | tf_op jit(solution)/shard_map/ppermute | solution.py:672
  483.0 9.6 %collective-permute-start.16 = (f32[8,2048]{1,0:T(8,128)S(1)}, f32[8,2048]{1,0:T(8,128)S(1)}, u32[]{:S(2)}, u32[]{:S(2)}) collective-permute-start(f32[8,2048]{1,0:T(8,128)S(1)} %add.98), channel_id=1, source_target_pairs={{0,16},{4,20},{8,24},{12,28},{16,0},{20,4},{24,8},{28,12},{1,17},{... | collective-permute-start | bytes 196616 | tf_op jit(solution)/shard_map/ppermute | solution.py:672
  (43 other events, 210.5 us)
Sparse Core Ops, SparseCore 0:
  11.5 94.7 all-gather.7
  123.8 89.8 all-gather.9
Sparse Core Ops, SparseCore 1:
  26.9 88.6 all-reduce.5
  164.6 66.3 reduce-scatter.1
  247.7 62.6 all-gather.5
  361.8 89.7 all-reduce.7

commit v6 on v5

--- a/solution.py
+++ b/solution.py
@@ -122,7 +122,7 @@
         ],
         scratch_shapes=[pltpu.VMEM((count, width), BF16)],
         compiler_params=pltpu.CompilerParams(
-            dimension_semantics=("arbitrary",), vmem_limit_bytes=32 * 1024 * 1024
+            dimension_semantics=("arbitrary",), vmem_limit_bytes=VMEM_LIMIT
         ),
         cost_estimate=LIGHT,
         name="attention",
@@ -153,13 +153,13 @@
             jax.ShapeDtypeStruct((count, width), F32),
         ],
         compiler_params=pltpu.CompilerParams(
-            dimension_semantics=("arbitrary",), vmem_limit_bytes=32 * 1024 * 1024
+            dimension_semantics=("arbitrary",), vmem_limit_bytes=VMEM_LIMIT
         ),
         name="second_norm",
     )(x, attn_sum, gain)
 
 
-def back_kernel(inner_ref, held_top_ref, got_top_ref, held_low_ref, got_low_ref, residual_ref, cot_ref, gain_ref, out_weight_ref, qkv_ref, weight_ref, cos_ref, sin_ref,
+def back_kernel(total_ref, residual_ref, cot_ref, gain_ref, out_weight_ref, qkv_ref, weight_ref, cos_ref, sin_ref,
                 row_ref, col_ref, x_ref, extra_ref, normed_grad_ref, residual_grad_ref, split_ref, projected_grad_ref, bias_ref,
                 mlp_gain_ref, branch_ref, attended_grad_ref):
     head = pl.program_id(0)
@@ -167,11 +167,7 @@
 
     @pl.when(head == 0)
     def _():
-        total = jnp.where(
-            inner_ref[0] == 1,
-            jnp.concatenate([held_top_ref[...], held_low_ref[...]]),
-            jnp.concatenate([got_top_ref[...], got_low_ref[...]]),
-        )
+        total = total_ref[...]
         residual = residual_ref[...]
         factor = lax.rsqrt(jnp.mean(residual * residual, axis=-1, keepdims=True) + EPS)
         scaled = gain_ref[...] * total
@@ -230,7 +226,7 @@
             normed_grad_ref[k, few:] = small
 
 
-def attention_back(inner, totals, residual, cotangent, gain, out_weight, qkv, weight, cosine, sine, row, col, x, extra,
+def attention_back(total, residual, cotangent, gain, out_weight, qkv, weight, cosine, sine, row, col, x, extra,
                    groups):
     count, width = residual.shape
     dim = cosine.shape[1]
@@ -240,8 +236,7 @@
         back_kernel,
         grid=(heads,),
         in_specs=[
-            pl.BlockSpec(memory_space=pltpu.SMEM),
-            *[whole(count // 2, width)] * 4,
+            whole(count, width),
             whole(count, width),
             whole(count, width),
             whole(1, width),
@@ -273,11 +268,11 @@
         ],
         scratch_shapes=[pltpu.VMEM((count, width), BF16), pltpu.VMEM((heads, count, dim), BF16)],
         compiler_params=pltpu.CompilerParams(
-            dimension_semantics=("arbitrary",), vmem_limit_bytes=48 * 1024 * 1024
+            dimension_semantics=("arbitrary",), vmem_limit_bytes=VMEM_LIMIT
         ),
         cost_estimate=LIGHT,
         name="attention_back",
-    )(inner, *totals, residual, cotangent, gain, out_weight, qkv, weight, cosine, sine, row, col, x, extra)
+    )(total, residual, cotangent, gain, out_weight, qkv, weight, cosine, sine, row, col, x, extra)
 
 
 def hidden(w_one, w_two, tokens, branch, route_row):
@@ -298,15 +293,15 @@
     return lax.logistic(nt(gate_rows, tokens)[:1])
 
 
-def own_kernel(experts, tok_ref, cot_ref, route_ref, gate_ref, w1_ref, w2_ref, out_ref, dx_top_ref, dx_low_ref,
-               logit_ref, open_ref):
+def own_kernel(experts, tok_ref, cot_ref, route_ref, gate_ref, w1_ref, w2_ref, out_ref, dx_ref, logit_ref,
+               open_ref):
     step = pl.program_id(0)
     group, units, width = w2_ref.shape
     shared = step * group >= experts
 
     @pl.when(step == 0)
     def _():
-        for ref in (out_ref, dx_top_ref, dx_low_ref):
+        for ref in (out_ref, dx_ref):
             ref[...] = jnp.zeros_like(ref)
         logit_ref[...] = jnp.zeros_like(logit_ref)
         open_ref[...] = open_row(gate_ref[...], tok_ref[...])
@@ -323,11 +318,8 @@
         weighted.append(scaled)
         mix_grads.append(mix_grad)
         logit_ref[...] += jnp.where(shared, jnp.sum(act * back, axis=0, keepdims=True), 0.0)
-    rows = dx_top_ref.shape[0]
     out_ref[...] += tn(jnp.concatenate(weighted), w2_ref[...].reshape(group * units, width))
-    dx = tn(jnp.concatenate(mix_grads), w1_ref[...].reshape(group * 2 * units, width))
-    dx_top_ref[...] += dx[:rows]
-    dx_low_ref[...] += dx[rows:]
+    dx_ref[...] += tn(jnp.concatenate(mix_grads), w1_ref[...].reshape(group * 2 * units, width))
 
     @pl.when(step == pl.num_programs(0) - 1)
     def _():
@@ -335,8 +327,7 @@
         logit = opened * (1.0 - opened) * logit_ref[...]
         logit_ref[...] = logit
         column = jnp.broadcast_to(logit, (8, logit.shape[1])).T[:, :1]
-        dx_top_ref[...] += column[:rows] * gate_ref[:1].astype(F32)
-        dx_low_ref[...] += column[rows:] * gate_ref[:1].astype(F32)
+        dx_ref[...] += column * gate_ref[:1].astype(F32)
 
 
 def own_mlp(tokens, cotangent, route, gate_rows, w1, w2):
@@ -355,10 +346,10 @@
             pl.BlockSpec((group, 2, units, width), lambda i: (i, 0, 0, 0)),
             pl.BlockSpec((group, units, width), lambda i: (i, 0, 0)),
         ],
-        out_specs=[whole(count, width), *[whole(count // 2, width)] * 2, whole(1, count)],
+        out_specs=[whole(count, width), whole(count, width), whole(1, count)],
         out_shape=[
             jax.ShapeDtypeStruct((count, width), F32),
-            *[jax.ShapeDtypeStruct((count // 2, width), F32)] * 2,
+            jax.ShapeDtypeStruct((count, width), F32),
             jax.ShapeDtypeStruct((1, count), F32),
         ],
         scratch_shapes=[pltpu.VMEM((1, count), F32)],
@@ -532,7 +523,7 @@
         ),
         out_shape=[jax.ShapeDtypeStruct((part, cols), F32)] * 4,
         compiler_params=pltpu.CompilerParams(
-            dimension_semantics=("arbitrary",), vmem_limit_bytes=32 * 1024 * 1024
+            dimension_semantics=("arbitrary",), vmem_limit_bytes=VMEM_LIMIT
         ),
         cost_estimate=LIGHT,
         name="turned_blocks",
@@ -633,7 +624,7 @@
         out_shape=[jax.ShapeDtypeStruct(g.shape, g.dtype) for g in grads],
         input_output_aliases={3 + k: k for k in range(4)},
         compiler_params=pltpu.CompilerParams(
-            dimension_semantics=("arbitrary",), vmem_limit_bytes=32 * 1024 * 1024
+            dimension_semantics=("arbitrary",), vmem_limit_bytes=VMEM_LIMIT
         ),
         cost_estimate=LIGHT,
         name="place_peer",
@@ -662,7 +653,7 @@
             jax.ShapeDtypeStruct((blocks, extra, count), F32),
         ],
         compiler_params=pltpu.CompilerParams(
-            dimension_semantics=("arbitrary",), vmem_limit_bytes=32 * 1024 * 1024
+            dimension_semantics=("arbitrary",), vmem_limit_bytes=VMEM_LIMIT
         ),
         name="split_rounded",
     )(gathered)
@@ -740,50 +731,29 @@
     swap = lambda v: lax.ppermute(v, "dp", [(i, i ^ 1) for i in range(n_dp)])
     beside = swap(tokens_wide)
     tok_all = lax.all_gather(tokens_wide, "dp")
-    mlp_part, grad_top, grad_low, logit_grad = own_mlp(tokens, cotangent, route, gate_rows, w1, w2)
-    mlp_sum = lax.psum_scatter(mlp_part, "tensor", scatter_dimension=0, tiled=True)
-    line = n_tensor == 4 and n_dp == 8
-    spot = lax.axis_index("tensor")
+    mlp_part, normed_two_part, logit_grad = own_mlp(tokens, cotangent, route, gate_rows, w1, w2)
     hide = lambda other, starts, tokens, kept: chip_hidden(
         jnp.stack([core, chip, other, *starts]), tokens, cot_low, route_all, gate_rows, w1, w2, kept, part
     )
     in_order = (jnp.int32(0), jnp.int32(count))
     beside_starts = (core * count, (1 - core) * count)
     shared_gate_part = jnp.sum(logit_grad[0][:, None] * tokens.astype(F32), axis=0, keepdims=True)
-    if line:
-        is_inner = (spot == 1) | (spot == 2)
-        inwards = lambda v: lax.ppermute(v, "tensor", [(0, 1), (3, 2)])
-        across = lambda v: lax.ppermute(v, "tensor", [(1, 2), (2, 1)])
-        outwards = lambda v: lax.ppermute(v, "tensor", [(1, 0), (2, 3)])
+    normed_two_total = lax.psum(normed_two_part, "tensor")
+    last = n_dp == 8
+    if last:
         ready = jnp.isnan(logit_grad[0, 0]).astype(jnp.int32)
-        got = inwards(grad_top)
         kept = hide(chip + ready, beside_starts, [tokens_wide, beside], [])
-        got, grad_low, kept = tied((got, grad_low, kept))
-        grad_top = grad_top + got
-        got, got_low = across(grad_top), inwards(grad_low)
-        got, got_low, tok_all, shared_gate_part, kept = tied((got, got_low, tok_all, shared_gate_part, kept))
-        grad_top, grad_low = grad_top + got, grad_low + got_low
-        grad_top, mlp_sum = tied((grad_top, mlp_sum))
-        mlp_sum = lax.all_gather(mlp_sum, "tensor", axis=0, tiled=True)
-        end_top, got_low = outwards(grad_top), across(grad_low)
         kept = hide(chip ^ 1, in_order, [tok_all], kept)
-        end_top, got_low, kept = tied((end_top, got_low, kept))
-        grad_low = grad_low + got_low
-        end_low = outwards(grad_low)
         kept = hide(chip ^ 2, in_order, [tok_all], kept)
-        end_low, mlp_sum, kept = tied((end_low, mlp_sum, kept))
-        totals = [grad_top, end_top, grad_low, end_low]
     else:
-        is_inner = spot >= 0
-        mlp_sum = lax.all_gather(mlp_sum, "tensor", axis=0, tiled=True)
         kept = []
         for k in range(n_dp // 2):
             kept = hide(jnp.int32(k), in_order, [tok_all], kept)
-        totals = [lax.psum(v, "tensor") for v in (grad_top, grad_low)]
-        totals = [totals[0], totals[0], totals[1], totals[1]]
+    normed_two_total, mlp_part, shared_gate_part, kept = tied((normed_two_total, mlp_part, shared_gate_part, kept))
+    mlp_sum = lax.psum_scatter(mlp_part, "tensor", scatter_dimension=0, tiled=True)
 
     normed_one_part, residual_grad, branch_grad, projected_grad, bias_part, mlp_gain_part = attention_back(
-        is_inner.astype(jnp.int32)[None], totals, residual, cotangent, gain_two, out_weight, qkv, qkv_weight,
+        normed_two_total, residual, cotangent, gain_two, out_weight, qkv, qkv_weight,
         cosine, sine, row, col, layer_input, shared_gate_part, 1,
     )
     summed = lax.psum(normed_one_part.reshape(-1, width), "tensor")
@@ -796,7 +766,7 @@
         input_grad = (residual_grad + norm_back(inputs, factor, gain_one, summed[:count])).astype(BF16)
         return input_grad, jnp.pad(small, ((0, 4), (0, 0)))
 
-    if line:
+    if last:
         at = jnp.stack([core, chip % 2, chip // 2, chip])
         other_at = jnp.stack([1 - core, chip % 2, chip // 2, chip])
         arrived = swap(token_products(other_at, normed_one, projected_grad, branch_grad, attended, None))
@@ -807,7 +777,8 @@
         x_got, y_got = flip(x_send, 2), flip(y_send, 4)
         kept = hide(chip ^ 3, in_order, [tok_all], kept)
         *grads, one_peer, two_peer = weight_grads(at, *kept, cot_low, experts // 2)
-        one_peer, x_got, y_got = tied((one_peer, x_got, y_got))
+        one_peer, x_got, y_got, mlp_sum = tied((one_peer, x_got, y_got, mlp_sum))
+        mlp_sum = lax.all_gather(mlp_sum, "tensor", axis=0, tiled=True)
         x_own, x_send, y_own, y_send = turned_blocks(at, x_keep, x_got, y_keep, y_got)
         x_send, y_send, one_peer, two_peer, summed = tied((x_send, y_send, one_peer, two_peer, summed))
         x_got, y_got = flip(x_send, 4), flip(y_send, 2)
@@ -822,6 +793,7 @@
         both = jnp.concatenate([x_own + x_got, y_own + y_got], axis=1)
         cut = projected_grad.shape[1]
         qkv_weight_grad, out_weight_grad = both[:, :cut], both[:, cut:].T
+        mlp_sum, qkv_weight_grad = tied((mlp_sum, qkv_weight_grad))
     else:
         at = jnp.stack([core, core, core, chip])
         *grads, one_peer, two_peer = weight_grads(at, *kept, cot_low, experts // 2)
@@ -829,6 +801,7 @@
         expert_one, expert_two, shared_one, shared_two = place_peer(at, one_peer, two_peer, grads, experts // 2)
         input_grad, small = finish(summed)
         small = lax.psum(small, "dp")
+        mlp_sum = lax.all_gather(mlp_sum, "tensor", axis=0, tiled=True)
         joint = lambda v: v.reshape(2, count, BLOCKS // 2, -1).transpose(1, 2, 0, 3).reshape(count, width)
         out_weight_grad = lax.psum_scatter(tn(attended, joint(branch_grad)), "dp", scatter_dimension=1, tiled=True)
         qkv_weight_grad = lax.psum_scatter(

time: 507 us -> 474 us (0.935)
  local copies, waits for them, and re-layouts: 86 us -> 54.8 us
  starting transfers between devices: 23.8 us -> 9.29 us
  Pallas kernels: 216 us -> 229 us
    ppermute x6 -> x0, waiting for transfers between devices: 74.2 us -> none  [the longest x2 41.6 us: shards(): inwards = lambda v: lax.ppermute(v, 'tensor', [(0, 1), (3, 2)])]
    psum x1, waiting for transfers between devices: 6.64 us -> 54 us  [shards(): summed = lax.psum(normed_one_part.reshape(-1, width), 'tensor')]
    unnamed x104 -> x48, local copies, waits for them, and re-layouts: 36.3 us -> 7.83 us
    all_gather x1, waiting for transfers between devices: 0.01 us -> 18.7 us  [shards(): tok_all = lax.all_gather(tokens_wide, 'dp')]
    ppermute x6 -> x0, starting transfers between devices: 16.2 us -> none  [the longest x2 11 us: shards(): inwards = lambda v: lax.ppermute(v, 'tensor', [(0, 1), (3, 2)])]
    all_gather x1, waiting for transfers between devices: 0.01 us -> 5.72 us  [shards(): mlp_sum = lax.all_gather(mlp_sum, 'tensor', axis=0, tiled=True)]
    concatenate x1, other arithmetic: 6.87 us -> 12.1 us  [shards(): jnp.concatenate([expert_down, shared_down.reshape(shared, units, width)])]
  transfers between devices with their start and end apart: 23 -> 18, of which waited for: 10 -> 10; matrix products, arithmetic and copies ran while one was open for 19% -> 21% of each run, Pallas kernels for 38% -> 43%
where the time goes in v6:
time: 474 us; the launch traced here: 472 us
  Pallas kernels  229 us (48%)
  waiting for transfers between devices  108 us (23%)
  local copies, waits for them, and re-layouts  54.8 us (12%)
  other arithmetic  53.9 us (11%)
  between operations  17.4 us (4%)
  starting transfers between devices  9.29 us (2%)
    pallas_call x4, Pallas kernels, chip_hidden(): pl.pallas_call(functools.partial(chip_kernel, here), grid_spec=pltpu.Pref...  92.4 us
    psum x1, waiting for transfers between devices, shards(): summed = lax.psum(normed_one_part.reshape(-1, width), 'tensor')  54 us
    pallas_call x1, Pallas kernels, own_mlp(): pl.pallas_call(functools.partial(own_kernel, experts), grid=(tiles // gro...  39.9 us
    optimization_barrier x1, local copies, waits for them, and re-layouts, shards(): attn_part, shared_gate_up = tied((attn_part, shared_gate_up))  28.9 us
    concatenate x1, other arithmetic, shards(): jnp.concatenate([jnp.transpose(expert_gate_up, (0, 2, 3, 1)), jnp.transpo...  24.7 us
    pallas_call x1, Pallas kernels, weight_grads(): pl.pallas_call(functools.partial(weights_kernel, here), grid_spec=pltpu.P...  22.7 us
    ppermute x4, waiting for transfers between devices, shards(): swap = lambda v: lax.ppermute(v, 'dp', [(i, i ^ 1) for i in range(n_dp)])  19.1 us
    all_gather x1, waiting for transfers between devices, shards(): tok_all = lax.all_gather(tokens_wide, 'dp')  18.7 us
  transfers between devices with their start and end apart: 18, of which 10 were waited for; matrix products, arithmetic and copies ran while one was open for 21% of the time, Pallas kernels for 43%

profile of v6, /device:TPU:0, one launch (start us, length us, event | category | flops | bytes accessed | tf_op | source)
XLA Modules:
  0.0 472.2 jit_solution(12197664788647406329)
XLA Ops:
  14.6 11.3 %attention.1 = (f32[256,2048]{1,0:T(8,128)}, bf16[2,256,1024]{2,1,0:T(8,128)(2,1)}, bf16[256,1536]{1,0:T(8,128)(2,1)}, bf16[256,512]{1,0:T(8,128)(2,1)}) custom-call(bf16[256,2048]{1,0:T(8,128)(2,1)} %x_ref.5, f32[1,2048]{1,0:T(1,128)} %bitcast.55, bf16[2048,1536]{1,0:T(8,128)(2,1)} %weight_ref.3, f32[4,1,384]{2,1,0:T(1,128)} %reshape.77.bias_ref, ...), custom_call_target="tpu_custom_call" | custom-call | flops 1048576 | bytes 65536 | tf_op jit(solution)/shard_map/attention/pallas_call | solution.py:97
  26.6 28.9 %copy.53 = bf16[2048,2,1408]{0,2,1:T(8,128)(2,1)} copy(bf16[2048,2,1408]{2,1,0:T(2,128)(2,1)} %param.26) | data formatting | bytes 23068672 | tf_op jit(solution)/shard_map/optimization_barrier | solution.py:718
  55.5 10.9 %copy.60 = bf16[2048,2,4,352]{0,3,1,2:T(8,128)(2,1)} copy(bf16[2048,2,4,352]{0,3,2,1:T(8,128)(2,1)} %bitcast.43) | data formatting | bytes 23068672 | tf_op jit(solution)/shard_map/reshape | solution.py:723
  66.4 12.1 %pad_maximum_fusion.1.w2_ref = bf16[12,352,2048]{2,1,0:T(8,128)(2,1)} fusion(bf16[4,352,2048]{2,1,0:T(8,128)(2,1)S(1)} %bitcast.51, bf16[8,352,2048]{2,1,0:T(8,128)(2,1)} %param.25), kind=kLoop, calls=%fused_computation.1 | loop fusion | flops 8650752 | bytes 34603008 | tf_op jit(solution)/shard_map/concatenate | solution.py:726
  78.5 24.7 %pad_maximum_fusion.w1_ref = bf16[12,2,352,2048]{3,2,1,0:T(8,128)(2,1)} fusion(bf16[4,2,352,2048]{3,2,1,0:T(8,128)(2,1)} %bitcast.44, bf16[8,2,352,2048]{3,2,1,0:T(8,128)(2,1)} %bitcast.45), kind=kLoop, calls=%fused_computation | loop fusion | flops 17301504 | bytes 69206016 | tf_op jit(solution)/shard_map/concatenate | solution.py:720
  103.2 2.9 all-gather.8.cloned.1.call-done
  106.1 11.1 %split_rounded.1 = (bf16[2048,2048]{1,0:T(8,128)(2,1)}, f32[8,8,256]{2,1,0:T(8,128)}) custom-call(f32[8,264,2048]{2,1,0:T(8,128)} %bitcast.46), custom_call_target="tpu_custom_call" | custom-call | tf_op jit(solution)/shard_map/split_rounded/pallas_call | solution.py:643
  117.2 4.7 %second_norm.1 = (f32[256,2048]{1,0:T(8,128)}, bf16[256,2048]{1,0:T(8,128)(2,1)}, f32[256,2048]{1,0:T(8,128)}) custom-call(bf16[256,2048]{1,0:T(8,128)(2,1)} %x_ref.5, f32[256,2048]{1,0:T(8,128)} %all-reduce.7.cloned.1.call-done.sum_ref, f32[1,2048]{1,0:T(1,128)} %bitcast.56), custom_call_target="tpu_custom_call" | custom-call | tf_op jit(solution)/shard_map/second_norm/pallas_call | solution.py:145
  123.7 39.9 %own_mlp.1 = (f32[256,2048]{1,0:T(8,128)}, f32[256,2048]{1,0:T(8,128)}, f32[1,256]{1,0:T(1,128)}) custom-call(bf16[256,2048]{1,0:T(8,128)(2,1)} %get-tuple-element.112.tok_ref, bf16[256,2048]{1,0:T(8,128)(2,1)} %cot_ref.3, f32[8,1,256]{2,1,0:T(1,128)} %broadcast_in_dim.46.route_ref, bf16[16,2048]{1,0:T(8,128)(2,1)} %broadcast_in_dim.45.gate_ref, ...), custom_call_target="tpu_custom_call" | custom-call | flops 1048576 | bytes 65536 | tf_op jit(solution)/shard_map/own_mlp/pallas_call | solution.py:338
  170.4 23.0 %chip_hidden.4 = (bf16[6,704,2048]{2,1,0:T(8,128)(2,1)}, bf16[6,352,2048]{2,1,0:T(8,128)(2,1)}, bf16[2048,512]{1,0:T(8,128)(2,1)}) custom-call(s32[5]{0:T(128)} %stack.76.at_ref, f32[256,2048]{1,0:T(8,128)} %get-tuple-element.106.even_ref, f32[256,2048]{1,0:T(8,128)} %copy-done.7, bf16[2048,2048]{1,0:T(8,128)(2,1)} %get-tuple-element.107.cot_ref, ...), custom_call_target="tpu_custom_call" | custom-call | flops 1048576 | bytes 65536 | tf_op jit(solution)/shard_map/chip_hidden/pallas_call | solution.py:414
  193.5 18.7 %all-gather.10.cloned.1.call-done = f32[2048,2048]{1,0:T(8,128)} async-done(((f32[256,2048]{1,0:T(8,128)}), f32[2048,2048]{1,0:T(8,128)}) %all-gather.10.cloned.1.call-update) | async-done | bytes 16777232 | tf_op jit(solution)/shard_map/all_gather | solution.py:733
  212.2 23.1 %chip_hidden.5 = (bf16[6,704,2048]{2,1,0:T(8,128)(2,1)}, bf16[6,352,2048]{2,1,0:T(8,128)(2,1)}, bf16[2048,512]{1,0:T(8,128)(2,1)}) custom-call(s32[5]{0:T(128)} %stack.72.at_ref, f32[8,256,2048]{2,1,0:T(8,128)} %bitcast.37, f32[8,256,2048]{2,1,0:T(8,128)} %bitcast.38, ...), custom_call_target="tpu_custom_call", output_to_operand_aliasing={{0}: (8, {}), {1}: (9, {}), {2}: (10, {})} | custom-call | flops 1048576 | bytes 65536 | tf_op jit(solution)/shard_map/chip_hidden/pallas_call | solution.py:414
  235.3 23.1 %chip_hidden.6 = (bf16[6,704,2048]{2,1,0:T(8,128)(2,1)}, bf16[6,352,2048]{2,1,0:T(8,128)(2,1)}, bf16[2048,512]{1,0:T(8,128)(2,1)}) custom-call(s32[5]{0:T(128)} %stack.70.at_ref, f32[8,256,2048]{2,1,0:T(8,128)} %bitcast.39, f32[8,256,2048]{2,1,0:T(8,128)} %bitcast.40, ...), custom_call_target="tpu_custom_call", output_to_operand_aliasing={{0}: (8, {}), {1}: (9, {}), {2}: (10, {})} | custom-call | flops 1048576 | bytes 65536 | tf_op jit(solution)/shard_map/chip_hidden/pallas_call | solution.py:414
  258.5 15.1 %attention_back.1 = (f32[1,264,2048]{2,1,0:T(8,128)}, f32[256,2048]{1,0:T(8,128)}, bf16[2,256,1024]{2,1,0:T(8,128)(2,1)}, bf16[256,1536]{1,0:T(8,128)(2,1)}, f32[1,1536]{1,0:T(1,128)}, /*index=5*/f32[1,2048]{1,0:T(1,128)}) custom-call(f32[256,2048]{1,0:T(8,128)} %all-reduce.9.cloned.1.call-done.total_ref, f32[256,2048]{1,0:T(8,128)} %get-tuple-element.105.residual_ref, ...), custom_call_target="tpu_custom_call" | custom-call | flops 1048576 | bytes 65536 | tf_op jit(solution)/shard_map/attention_back/pallas_call | solution.py:235
  273.6 6.8 %token_products.2 = f32[4,256,2048]{2,1,0:T(8,128)} custom-call(s32[4]{0:T(128)} %add_add_fusion.1.at_ref, bf16[2,256,1024]{2,1,0:T(8,128)(2,1)} %get-tuple-element.111.normed_ref, bf16[256,1536]{1,0:T(8,128)(2,1)} %get-tuple-element.128.projected_ref, bf16[2,256,1024]{2,1,0:T(8,128)(2,1)} %get-tuple-element.129.branch_ref, ...), custom_call_target="tpu_custom_call" | custom-call | flops 1048576 | bytes 65536 | tf_op jit(solution)/shard_map/token_products/pallas_call | solution.py:491
  282.0 11.8 %collective-permute-done.1.arrived_ref = f32[4,256,2048]{2,1,0:T(8,128)} collective-permute-done((f32[4,256,2048]{2,1,0:T(8,128)}, f32[4,256,2048]{2,1,0:T(8,128)}, u32[]{:S(2)}, u32[]{:S(2)}) %collective-permute-start.1) | collective-permute-done | bytes 8388640 | tf_op jit(solution)/shard_map/ppermute | solution.py:731
  293.9 10.2 %token_products.3 = (f32[2,256,1024]{2,1,0:T(8,128)}, f32[2,256,1024]{2,1,0:T(8,128)}, f32[2,256,1024]{2,1,0:T(8,128)}, f32[2,256,1024]{2,1,0:T(8,128)}) custom-call(s32[4]{0:T(128)} %add_add_fusion.at_ref, bf16[2,256,1024]{2,1,0:T(8,128)(2,1)} %get-tuple-element.111.normed_ref, bf16[256,1536]{1,0:T(8,128)(2,1)} %get-tuple-element.128.projected_ref, ...), custom_call_target="tpu_custom_call" | custom-call | flops 1048576 | bytes 65536 | tf_op jit(solution)/shard_map/token_products/pallas_call | solution.py:491
  304.1 1.6 collective-permute-start.2
  306.8 23.1 %chip_hidden.7 = (bf16[6,704,2048]{2,1,0:T(8,128)(2,1)}, bf16[6,352,2048]{2,1,0:T(8,128)(2,1)}, bf16[2048,512]{1,0:T(8,128)(2,1)}) custom-call(s32[5]{0:T(128)} %stack.68.at_ref, f32[8,256,2048]{2,1,0:T(8,128)} %bitcast.41, f32[8,256,2048]{2,1,0:T(8,128)} %bitcast.42, ...), custom_call_target="tpu_custom_call", output_to_operand_aliasing={{0}: (8, {}), {1}: (9, {}), {2}: (10, {})} | custom-call | flops 1048576 | bytes 65536 | tf_op jit(solution)/shard_map/chip_hidden/pallas_call | solution.py:414
  329.9 22.7 %weight_grads.1 = (f32[8,2,352,256]{3,2,1,0:T(8,128)}, f32[8,352,256]{2,1,0:T(8,128)}, f32[4,2,352,256]{3,2,1,0:T(8,128)}, f32[4,352,256]{2,1,0:T(8,128)}, f32[6...) custom-call(s32[4]{0:T(128)} %add_add_fusion.at_ref, bf16[6,704,2048]{2,1,0:T(8,128)(2,1)} %get-tuple-element.139.mix_grad_ref, ...), custom_call_target="tpu_custom_call" | custom-call | flops 1048576 | bytes 65536 | tf_op jit(solution)/shard_map/weight_grads/pallas_call | solution.py:569
  353.9 6.4 %turned_blocks.1 = (f32[256,1024]{1,0:T(8,128)}, f32[256,1024]{1,0:T(8,128)}, f32[256,1024]{1,0:T(8,128)}, f32[256,1024]{1,0:T(8,128)}) custom-call(s32[4]{0:T(128)} %add_add_fusion.at_ref, f32[2,256,1024]{2,1,0:T(8,128)} %get-tuple-element.147.x_keep_ref, f32[2,256,1024]{2,1,0:T(8,128)} %copy-done.8, f32[2,256,1024]{2,1,0:T(8,128)} %get-tuple-element.149.y_keep_ref, ...), custom_call_target="tpu_custom_call" | custom-call | flops 1048576 | bytes 65536 | tf_op jit(solution)/shard_map/turned_blocks/pallas_call | solution.py:519
  360.3 54.0 %all-reduce.11.cloned.1.call-done = f32[264,2048]{1,0:T(8,128)} async-done(((f32[264,2048]{1,0:T(8,128)}), f32[264,2048]{1,0:T(8,128)}) %all-reduce.11.cloned.1.call-update) | async-done | bytes 2162704 | tf_op jit(solution)/shard_map/psum | solution.py:759
  414.9 1.5 collective-permute-start.4
  417.9 6.7 %collective-permute-done.7.two_ref = f32[6,352,256]{2,1,0:T(8,128)S(1)} collective-permute-done((f32[6,352,256]{2,1,0:T(8,128)}, f32[6,352,256]{2,1,0:T(8,128)S(1)}, u32[]{:S(2)}, u32[]{:S(2)}) %collective-permute-start.7) | collective-permute-done | bytes 2162720 | tf_op jit(solution)/shard_map/ppermute | solution.py:731
  426.0 8.1 %place_peer.1 = (f32[8,2,352,256]{3,2,1,0:T(8,128)}, f32[8,352,256]{2,1,0:T(8,128)}, f32[4,2,352,256]{3,2,1,0:T(8,128)}, f32[4,352,256]{2,1,0:T(8,128)}) custom-call(s32[4]{0:T(128)} %add_add_fusion.at_ref, f32[6,2,352,256]{3,2,1,0:T(8,128)} %collective-permute-done.6.one_ref, ...), custom_call_target="tpu_custom_call", output_to_operand_aliasing={{0}: (3, {}), {1}: (4, {}), {2}: (5, {}), {3}: (6, {})} | custom-call | flops 1048576 | bytes 65536 | tf_op jit(solution)/shard_map/place_peer/pallas_call | solution.py:612
  435.6 1.5 collective-permute-start.9
  437.1 5.7 %collective-permute-done.9 = f32[8,2048]{1,0:T(8,128)S(1)} collective-permute-done((f32[8,2048]{1,0:T(8,128)S(1)}, f32[8,2048]{1,0:T(8,128)S(1)}, u32[]{:S(2)}, u32[]{:S(2)}) %collective-permute-start.9) | collective-permute-done | bytes 65568 | tf_op jit(solution)/shard_map/ppermute | solution.py:663
  443.4 1.6 fusion.4
  445.8 3.4 copy.58
  449.3 1.8 add.86
  454.8 5.7 %all-gather.6.cloned.1.call-done = f32[256,2048]{1,0:T(8,128)} async-done(((f32[64,2048]{1,0:T(8,128)}), f32[256,2048]{1,0:T(8,128)}) %all-gather.6.cloned.1.call-update) | async-done | bytes 2097168 | tf_op jit(solution)/shard_map/all_gather | solution.py:781
  460.5 2.8 add_convert_fusion
  (120 shorter events, 29.6 us)
Async XLA Ops:
  8.0 98.1 %all-gather.8.cloned.1.call-start = ((), (), s32[]{:S(2)}) async-start(), calls=%async_computation.6 | async-start | bytes 19464192 | tf_op jit(solution)/shard_map/all_gather | solution.py:701
  11.1 106.1 %all-reduce.7.cloned.1.call-start = ((), (), s32[]{:S(2)}) async-start(), calls=%async_computation.1 | async-start | bytes 4194304 | tf_op jit(solution)/shard_map/psum | solution.py:719
  14.6 11.4 %copy-start.15 = (bf16[2048]{0:T(1024)(128)(2,1)S(1)}, bf16[2048]{0:T(1024)(128)(2,1)}, u32[]{:S(2)}) copy-start(bf16[2048]{0:T(1024)(128)(2,1)} %param.23) | copy-start | bytes 12292
  26.0 186.2 %all-gather.10.cloned.1.call-start = ((), (), s32[]{:S(2)}) async-start(), calls=%async_computation.7 | async-start | bytes 18874368 | tf_op jit(solution)/shard_map/all_gather | solution.py:733
  26.6 39.8 %slice-start.1 = ((s8[5767168]{0:T(1024)(128)(4,1)}), s8[1572864]{0:T(1024)(128)(4,1)S(1)}, s32[]{:S(2)}) async-start(s8[5767168]{0:T(1024)(128)(4,1)} %bitcast.49), calls=%async_computation.9 | async-start | bytes 3145728
  55.5 10.9 %slice-start.2 = ((s8[5767168]{0:T(1024)(128)(4,1)}), s8[4194304]{0:T(1024)(128)(4,1)S(1)}, s32[]{:S(2)}) async-start(s8[5767168]{0:T(1024)(128)(4,1)} %bitcast.49), calls=%async_computation.10 | async-start | bytes 8388608
  117.2 5.8 %copy-start.16 = (bf16[2048]{0:T(1024)(128)(2,1)S(1)}, bf16[2048]{0:T(1024)(128)(2,1)}, u32[]{:S(2)}) copy-start(bf16[2048]{0:T(1024)(128)(2,1)} %param.28) | copy-start | bytes 12292
  122.0 136.4 %all-reduce.9.cloned.1.call-start = ((), (), s32[]{:S(2)}) async-start(), calls=%async_computation.2 | async-start | bytes 4194304 | tf_op jit(solution)/shard_map/psum | solution.py:741
  122.1 47.0 %collective-permute-start = (f32[256,2048]{1,0:T(8,128)}, f32[256,2048]{1,0:T(8,128)S(1)}, u32[]{:S(2)}, u32[]{:S(2)}) collective-permute-start(f32[256,2048]{1,0:T(8,128)} %get-tuple-element.106.even_ref), channel_id=1, source_target_pairs={{0,4},{4,0},{8,12},{12,8},{16,20},{20,16},{24,28},{28,24},{1,5},{5... | collective-permute-start | bytes 6291464 | tf_op jit(solution)/shard_map/ppermute | solution.py:731
  163.6 4.6 copy-start.4
  163.6 189.0 %reduce-scatter.2.cloned.1.call-start = ((), (), s32[]{:S(2)}) async-start(), calls=%async_computation.3 | async-start | bytes 2621440 | tf_op jit(solution)/shard_map/reduce_scatter | solution.py:753
  280.4 13.5 %collective-permute-start.1 = (f32[4,256,2048]{2,1,0:T(8,128)}, f32[4,256,2048]{2,1,0:T(8,128)}, u32[]{:S(2)}, u32[]{:S(2)}) collective-permute-start(f32[4,256,2048]{2,1,0:T(8,128)} %token_products.2), channel_id=1, source_target_pairs={{0,4},{4,0},{8,12},{12,8},{16,20},{20,16},{24,28},{28,24},{1,5},{5... | collective-permute-start | bytes 25165832 | tf_op jit(solution)/shard_map/ppermute | solution.py:731
  280.7 133.7 %all-reduce.11.cloned.1.call-start = ((), (), s32[]{:S(2)}) async-start(), calls=%async_computation.5 | async-start | bytes 4325376 | tf_op jit(solution)/shard_map/psum | solution.py:759
  281.4 179.1 %all-gather.6.cloned.1.call-start = ((), (), s32[]{:S(2)}) async-start(), calls=%async_computation.4 | async-start | bytes 2621440 | tf_op jit(solution)/shard_map/all_gather | solution.py:781
  304.1 48.6 %collective-permute-start.2 = (f32[2,256,1024]{2,1,0:T(8,128)}, f32[2,256,1024]{2,1,0:T(8,128)S(1)}, u32[]{:S(2)}, u32[]{:S(2)}) collective-permute-start(f32[2,256,1024]{2,1,0:T(8,128)} %get-tuple-element.143), channel_id=1, source_target_pairs={{0,8},{4,12},{8,0},{12,4},{16,24},{20,28},{24,16},{28,20},{1,9},{5... | collective-permute-start | bytes 6291464 | tf_op jit(solution)/shard_map/ppermute | solution.py:663
  305.6 47.8 %collective-permute-start.3 = (f32[2,256,1024]{2,1,0:T(8,128)}, f32[2,256,1024]{2,1,0:T(8,128)}, u32[]{:S(2)}, u32[]{:S(2)}) collective-permute-start(f32[2,256,1024]{2,1,0:T(8,128)} %get-tuple-element.144), channel_id=1, source_target_pairs={{0,16},{4,20},{8,24},{12,28},{16,0},{20,4},{24,8},{28,12},{1,17},{... | collective-permute-start | bytes 6291464 | tf_op jit(solution)/shard_map/ppermute | solution.py:663
  414.3 10.8 %collective-permute-start.6 = (f32[6,2,352,256]{3,2,1,0:T(8,128)}, f32[6,2,352,256]{3,2,1,0:T(8,128)}, u32[]{:S(2)}, u32[]{:S(2)}) collective-permute-start(f32[6,2,352,256]{3,2,1,0:T(8,128)} %get-tuple-element.161), channel_id=1, source_target_pairs={{0,4},{4,0},{8,12},{12,8},{16,20},{20,16},{24,28},{28,24},{1,5},{5... | collective-permute-start | bytes 12976136 | tf_op jit(solution)/shard_map/ppermute | solution.py:731
  414.3 10.3 %collective-permute-start.7 = (f32[6,352,256]{2,1,0:T(8,128)}, f32[6,352,256]{2,1,0:T(8,128)S(1)}, u32[]{:S(2)}, u32[]{:S(2)}) collective-permute-start(f32[6,352,256]{2,1,0:T(8,128)} %get-tuple-element.162), channel_id=1, source_target_pairs={{0,4},{4,0},{8,12},{12,8},{16,20},{20,16},{24,28},{28,24},{1,5},{5... | collective-permute-start | bytes 6488072 | tf_op jit(solution)/shard_map/ppermute | solution.py:731
  414.9 34.4 %collective-permute-start.4 = (f32[256,1024]{1,0:T(8,128)}, f32[256,1024]{1,0:T(8,128)}, u32[]{:S(2)}, u32[]{:S(2)}) collective-permute-start(f32[256,1024]{1,0:T(8,128)} %get-tuple-element.157), channel_id=1, source_target_pairs={{0,16},{4,20},{8,24},{12,28},{16,0},{20,4},{24,8},{28,12},{1,17},{... | collective-permute-start | bytes 3145736 | tf_op jit(solution)/shard_map/ppermute | solution.py:663
  416.4 32.9 %collective-permute-start.5 = (f32[256,1024]{1,0:T(8,128)}, f32[256,1024]{1,0:T(8,128)}, u32[]{:S(2)}, u32[]{:S(2)}) collective-permute-start(f32[256,1024]{1,0:T(8,128)} %get-tuple-element.158), channel_id=1, source_target_pairs={{0,8},{4,12},{8,0},{12,4},{16,24},{20,28},{24,16},{28,20},{1,9},{5... | collective-permute-start | bytes 3145736 | tf_op jit(solution)/shard_map/ppermute | solution.py:663
  426.0 8.1 %slice-start = ((f32[264,2048]{1,0:T(8,128)}), f32[2,2048]{1,0:T(2,128)S(1)}, s32[]{:S(2)}) async-start(f32[264,2048]{1,0:T(8,128)} %all-reduce.11.cloned.1.call-done), calls=%async_computation.8 | async-start | bytes 32768 | tf_op jit(solution)/shard_map/slice | solution.py:765
  426.0 8.1 %copy-start.12 = (f32[1,2048]{1,0:T(1,128)S(1)}, f32[1,2048]{1,0:T(1,128)}, u32[]{:S(2)}) copy-start(f32[1,2048]{1,0:T(1,128)} %get-tuple-element.172) | copy-start | bytes 24580
  426.0 8.1 %copy-start.13 = (f32[1,1536]{1,0:T(1,128)S(1)}, f32[1,1536]{1,0:T(1,128)}, u32[]{:S(2)}) copy-start(f32[1,1536]{1,0:T(1,128)} %get-tuple-element.173) | copy-start | bytes 18436
  426.0 8.6 %copy-start = (bf16[256,2048]{1,0:T(8,128)(2,1)S(1)}, bf16[256,2048]{1,0:T(8,128)(2,1)}, u32[]{:S(2)}) copy-start(bf16[256,2048]{1,0:T(8,128)(2,1)} %x_ref.5) | copy-start | bytes 3145732
  426.0 8.6 %copy-start.3 = (f32[264,2048]{1,0:T(8,128)S(1)}, f32[264,2048]{1,0:T(8,128)}, u32[]{:S(2)}) copy-start(f32[264,2048]{1,0:T(8,128)} %all-reduce.11.cloned.1.call-done) | copy-start | bytes 6488068
  426.0 8.6 %copy-start.10 = (f32[2048]{0:T(1024)S(1)}, f32[2048]{0:T(1024)}, u32[]{:S(2)}) copy-start(f32[2048]{0:T(1024)} %convert_element_type.36) | copy-start | bytes 24580
  434.1 9.3 %copy-start.6 = (f32[256,2048]{1,0:T(8,128)S(1)}, f32[256,2048]{1,0:T(8,128)}, u32[]{:S(2)}) copy-start(f32[256,2048]{1,0:T(8,128)} %get-tuple-element.159) | copy-start | bytes 6291460
  434.2 1.4 collective-permute-start.8
  435.6 7.2 %collective-permute-start.9 = (f32[8,2048]{1,0:T(8,128)S(1)}, f32[8,2048]{1,0:T(8,128)S(1)}, u32[]{:S(2)}, u32[]{:S(2)}) collective-permute-start(f32[8,2048]{1,0:T(8,128)S(1)} %pad_add_fusion), channel_id=1, source_target_pairs={{0,8},{4,12},{8,0},{12,4},{16,24},{20,28},{24,16},{28,20},{1,9},{5... | collective-permute-start | bytes 196616 | tf_op jit(solution)/shard_map/ppermute | solution.py:663
  442.8 6.4 %collective-permute-start.10 = (f32[8,2048]{1,0:T(8,128)S(1)}, f32[8,2048]{1,0:T(8,128)S(1)}, u32[]{:S(2)}, u32[]{:S(2)}) collective-permute-start(f32[8,2048]{1,0:T(8,128)S(1)} %add.83), channel_id=1, source_target_pairs={{0,16},{4,20},{8,24},{12,28},{16,0},{20,4},{24,8},{28,12},{1,17},{... | collective-permute-start | bytes 196616 | tf_op jit(solution)/shard_map/ppermute | solution.py:663
  449.3 2.8 copy-start.9
  453.5 7.0 %copy-start.2 = (f32[256,2048]{1,0:T(8,128)S(1)}, f32[256,2048]{1,0:T(8,128)}, u32[]{:S(2)}) copy-start(f32[256,2048]{1,0:T(8,128)} %get-tuple-element.105.residual_ref) | copy-start | bytes 6291460
  (10 other events, 16.7 us)
Sparse Core Ops, SparseCore 0:
  11.3 94.7 all-gather.7
  122.1 89.9 all-gather.9
Sparse Core Ops, SparseCore 1:
  26.0 88.7 all-reduce.6
  163.7 85.4 all-reduce.8
  280.8 43.7 reduce-scatter.1
  327.0 87.3 all-reduce.10
  415.9 44.6 all-gather.5

commit v7 on v6

--- a/solution.py
+++ b/solution.py
@@ -448,14 +448,22 @@
     )
 
 
-def sent_kernel(at_ref, normed_ref, projected_ref, branch_ref, attended_ref, out_ref):
-    out_ref[0] = both_products(normed_ref, projected_ref, branch_ref, attended_ref)
-
-
-def held_kernel(at_ref, normed_ref, projected_ref, branch_ref, attended_ref, arrived_ref, *out_refs):
+def sent_kernel(at_ref, normed_ref, projected_ref, branch_ref, attended_ref, *out_refs):
+    value = both_products(normed_ref, projected_ref, branch_ref, attended_ref)
+    for block, out_ref in enumerate(out_refs):
+        @pl.when(pl.program_id(0) == block)
+        def _():
+            out_ref[...] = value
+
+
+def held_kernel(at_ref, normed_ref, projected_ref, branch_ref, attended_ref, *refs):
     block = pl.program_id(0)
     along_y, along_x = block // 2, lax.rem(block, 2)
-    value = both_products(normed_ref, projected_ref, branch_ref, attended_ref) + arrived_ref[0]
+    arrived_refs, out_refs = refs[:-4], refs[-4:]
+    arrived = arrived_refs[0][...]
+    for k, arrived_ref in enumerate(arrived_refs[1:], 1):
+        arrived = jnp.where(block == k, arrived_ref[...], arrived)
+    value = both_products(normed_ref, projected_ref, branch_ref, attended_ref) + arrived
     half = value.shape[1] // 2
     x_keep_ref, x_send_ref, y_keep_ref, y_send_ref = out_refs
     for same, index, columns, keep_ref, send_ref in (
@@ -478,16 +486,15 @@
     cols = projected.shape[1] + attended.shape[1]
     side = pl.BlockSpec((1, count, part), lambda i, at: (at[0], 0, i))
     fixed = lambda *shape: pl.BlockSpec(shape, lambda i, at: (0,) * len(shape))
-    block = pl.BlockSpec((1, part, cols), lambda i, at: (i, 0, 0))
     inputs = [normed, projected, branch, attended]
     in_specs = [side, fixed(*projected.shape), side, fixed(*attended.shape)]
     if arrived is None:
-        kernel, out_specs = sent_kernel, block
-        out_shape = jax.ShapeDtypeStruct((blocks, part, cols), F32)
+        kernel, out_specs = sent_kernel, [fixed(part, cols)] * blocks
+        out_shape = [jax.ShapeDtypeStruct((part, cols), F32)] * blocks
     else:
         kernel, out_specs = held_kernel, [fixed(2, part, cols // 2)] * 4
         out_shape = [jax.ShapeDtypeStruct((2, part, cols // 2), F32)] * 4
-        inputs, in_specs = [*inputs, arrived], [*in_specs, block]
+        inputs, in_specs = [*inputs, *arrived], [*in_specs, *[fixed(part, cols)] * blocks]
     return pl.pallas_call(
         kernel,
         grid_spec=pltpu.PrefetchScalarGridSpec(
@@ -698,9 +705,8 @@
 
     choose = expert_ids[:, :, None] == jnp.arange(experts, dtype=jnp.int32)[None, None, :]
     route = jnp.sum(route_weights[:, :, None] * choose.astype(F32), axis=1).T
-    cot_all = lax.all_gather(
-        jnp.concatenate([cotangent.astype(F32), jnp.pad(route, ((0, 0), (0, width - count)))], axis=0), "dp"
-    )
+    payload = jnp.concatenate([cotangent.astype(F32), jnp.pad(route, ((0, 0), (0, width - count)))], axis=0)
+    cot_all = lax.all_gather(payload, "dp")
     gate_rows = jnp.broadcast_to(shared_gate[None, :], (16, width))
     index = jnp.arange(count, dtype=jnp.int32)
     place = (me * count + index - doc_ids).astype(F32)
@@ -724,14 +730,16 @@
         ]
     )
     w2 = jnp.concatenate([expert_down, shared_down.reshape(shared, units, width)])
-    cot_low, route_all = split_rounded(cot_all, count)
-    attn_sum, w1, w2, cot_low, route_all = tied((attn_sum, w1, w2, cot_low, route_all))
+    w1, cot_all = tied((w1, cot_all))
+    attn_sum, w1, w2, cot_all = tied((attn_sum, w1, w2, cot_all))
 
     residual, tokens, tokens_wide = second_norm(layer_input, attn_sum, gain_two)
     swap = lambda v: lax.ppermute(v, "dp", [(i, i ^ 1) for i in range(n_dp)])
     beside = swap(tokens_wide)
     tok_all = lax.all_gather(tokens_wide, "dp")
     mlp_part, normed_two_part, logit_grad = own_mlp(tokens, cotangent, route, gate_rows, w1, w2)
+    cot_all, logit_grad = tied((cot_all, logit_grad))
+    cot_low, route_all = split_rounded(cot_all, count)
     hide = lambda other, starts, tokens, kept: chip_hidden(
         jnp.stack([core, chip, other, *starts]), tokens, cot_low, route_all, gate_rows, w1, w2, kept, part
     )
@@ -749,7 +757,7 @@
         kept = []
         for k in range(n_dp // 2):
             kept = hide(jnp.int32(k), in_order, [tok_all], kept)
-    normed_two_total, mlp_part, shared_gate_part, kept = tied((normed_two_total, mlp_part, shared_gate_part, kept))
+    normed_two_total, shared_gate_part, kept = tied((normed_two_total, shared_gate_part, kept))
     mlp_sum = lax.psum_scatter(mlp_part, "tensor", scatter_dimension=0, tiled=True)
 
     normed_one_part, residual_grad, branch_grad, projected_grad, bias_part, mlp_gain_part = attention_back(
@@ -769,11 +777,11 @@
     if last:
         at = jnp.stack([core, chip % 2, chip // 2, chip])
         other_at = jnp.stack([1 - core, chip % 2, chip // 2, chip])
-        arrived = swap(token_products(other_at, normed_one, projected_grad, branch_grad, attended, None))
+        arrived = [swap(v) for v in token_products(other_at, normed_one, projected_grad, branch_grad, attended, None)]
         x_keep, x_send, y_keep, y_send = token_products(
             at, normed_one, projected_grad, branch_grad, attended, arrived
         )
-        x_send, y_send, kept = tied((x_send, y_send, kept))
+        x_send, y_send, kept, mlp_sum = tied((x_send, y_send, kept, mlp_sum))
         x_got, y_got = flip(x_send, 2), flip(y_send, 4)
         kept = hide(chip ^ 3, in_order, [tok_all], kept)
         *grads, one_peer, two_peer = weight_grads(at, *kept, cot_low, experts // 2)

time: 474 us -> 442 us (0.932)
  waiting for transfers between devices: 108 us -> 73 us
  other arithmetic: 53.9 us -> 48.5 us
    psum x1, waiting for transfers between devices: 54 us -> 21.4 us  [shards(): summed = lax.psum(normed_one_part.reshape(-1, width), 'tensor')]
    all_gather x1, waiting for transfers between devices: 18.7 us -> 5.08 us  [shards(): tok_all = lax.all_gather(tokens_wide, 'dp')]
    psum x1, waiting for transfers between devices: 0.01 us -> 9.12 us  [shards(): attn_sum = lax.psum(attn_part, 'tensor')]
    concatenate x1, other arithmetic: 12.1 us -> 6.96 us  [shards(): jnp.concatenate([expert_down, shared_down.reshape(shared, units, width)])]
    unnamed x48 -> x56, local copies, waits for them, and re-layouts: 7.83 us -> 10.3 us
    ppermute x4 -> x7, waiting for transfers between devices: 19.1 us -> 19 us  [shards(): swap = lambda v: lax.ppermute(v, 'dp', [(i, i ^ 1) for i in range(n_dp)])]
  transfers between devices with their start and end apart: 18 -> 21, of which waited for: 10 -> 14; matrix products, arithmetic and copies ran while one was open for 21% -> 21% of each run, Pallas kernels for 43% -> 52%
where the time goes in v7:
time: 442 us; the launch traced here: 440 us
  Pallas kernels  233 us (53%)
  waiting for transfers between devices  73 us (17%)
  local copies, waits for them, and re-layouts  59 us (13%)
  other arithmetic  48.5 us (11%)
  between operations  17.3 us (4%)
  starting transfers between devices  9.81 us (2%)
    pallas_call x4, Pallas kernels, chip_hidden(): pl.pallas_call(functools.partial(chip_kernel, here), grid_spec=pltpu.Pref...  92.5 us
    pallas_call x1, Pallas kernels, own_mlp(): pl.pallas_call(functools.partial(own_kernel, experts), grid=(tiles // gro...  40.9 us
    optimization_barrier x1, local copies, waits for them, and re-layouts, shards(): attn_part, shared_gate_up = tied((attn_part, shared_gate_up))  28.8 us
    concatenate x1, other arithmetic, shards(): jnp.concatenate([jnp.transpose(expert_gate_up, (0, 2, 3, 1)), jnp.transpo...  24.5 us
    pallas_call x1, Pallas kernels, weight_grads(): pl.pallas_call(functools.partial(weights_kernel, here), grid_spec=pltpu.P...  22.5 us
    psum x1, waiting for transfers between devices, shards(): summed = lax.psum(normed_one_part.reshape(-1, width), 'tensor')  21.4 us
    pallas_call x2, Pallas kernels, token_products(): pl.pallas_call(kernel, grid_spec=pltpu.PrefetchScalarGridSpec(num_scalar_...  19.7 us
    ppermute x7, waiting for transfers between devices, shards(): swap = lambda v: lax.ppermute(v, 'dp', [(i, i ^ 1) for i in range(n_dp)])  19 us
  transfers between devices with their start and end apart: 21, of which 14 were waited for; matrix products, arithmetic and copies ran while one was open for 21% of the time, Pallas kernels for 52%

profile of v7, /device:TPU:0, one launch (start us, length us, event | category | flops | bytes accessed | tf_op | source)
XLA Modules:
  0.0 440.2 jit_solution(13274017394995174871)
XLA Ops:
  15.2 11.4 %attention.1 = (f32[256,2048]{1,0:T(8,128)}, bf16[2,256,1024]{2,1,0:T(8,128)(2,1)}, bf16[256,1536]{1,0:T(8,128)(2,1)}, bf16[256,512]{1,0:T(8,128)(2,1)}) custom-call(bf16[256,2048]{1,0:T(8,128)(2,1)} %x_ref.5, f32[1,2048]{1,0:T(1,128)} %bitcast.57, bf16[2048,1536]{1,0:T(8,128)(2,1)} %weight_ref.3, f32[4,1,384]{2,1,0:T(1,128)} %reshape.77.bias_ref, ...), custom_call_target="tpu_custom_call" | custom-call | flops 1048576 | bytes 65536 | tf_op jit(solution)/shard_map/attention/pallas_call | solution.py:97
  26.6 28.8 %copy.53 = bf16[2048,2,1408]{0,2,1:T(8,128)(2,1)} copy(bf16[2048,2,1408]{2,1,0:T(2,128)(2,1)} %param.26) | data formatting | bytes 23068672 | tf_op jit(solution)/shard_map/optimization_barrier | solution.py:724
  55.5 12.8 %copy.60 = bf16[2048,2,4,352]{0,3,1,2:T(8,128)(2,1)} copy(bf16[2048,2,4,352]{0,3,2,1:T(8,128)(2,1)} %bitcast.43) | data formatting | bytes 23068672 | tf_op jit(solution)/shard_map/reshape | solution.py:729
  70.7 7.0 %pad_maximum_fusion.1.w2_ref = bf16[12,352,2048]{2,1,0:T(8,128)(2,1)} fusion(bf16[4,352,2048]{2,1,0:T(8,128)(2,1)S(1)} %bitcast.53, bf16[8,352,2048]{2,1,0:T(8,128)(2,1)S(1)} %bitcast.48), kind=kLoop, calls=%fused_computation.1 | loop fusion | flops 8650752 | bytes 34603008 | tf_op jit(solution)/shard_map/concatenate | solution.py:732
  77.6 24.5 %pad_maximum_fusion.w1_ref = bf16[12,2,352,2048]{3,2,1,0:T(8,128)(2,1)} fusion(bf16[4,2,352,2048]{3,2,1,0:T(8,128)(2,1)} %bitcast.44, bf16[8,2,352,2048]{3,2,1,0:T(8,128)(2,1)} %bitcast.45), kind=kLoop, calls=%fused_computation | loop fusion | flops 17301504 | bytes 69206016 | tf_op jit(solution)/shard_map/concatenate | solution.py:726
  102.1 4.0 all-gather.8.cloned.1.call-done
  106.1 9.1 %all-reduce.7.cloned.1.call-done.sum_ref = f32[256,2048]{1,0:T(8,128)} async-done(((f32[256,2048]{1,0:T(8,128)}), f32[256,2048]{1,0:T(8,128)}) %all-reduce.7.cloned.1.call-update) | async-done | bytes 2097168 | tf_op jit(solution)/shard_map/psum | solution.py:725
  115.3 4.7 %second_norm.1 = (f32[256,2048]{1,0:T(8,128)}, bf16[256,2048]{1,0:T(8,128)(2,1)}, f32[256,2048]{1,0:T(8,128)}) custom-call(bf16[256,2048]{1,0:T(8,128)(2,1)} %x_ref.5, f32[256,2048]{1,0:T(8,128)} %all-reduce.7.cloned.1.call-done.sum_ref, f32[1,2048]{1,0:T(1,128)} %bitcast.58), custom_call_target="tpu_custom_call" | custom-call | tf_op jit(solution)/shard_map/second_norm/pallas_call | solution.py:145
  121.3 40.9 %own_mlp.1 = (f32[256,2048]{1,0:T(8,128)}, f32[256,2048]{1,0:T(8,128)}, f32[1,256]{1,0:T(1,128)}) custom-call(bf16[256,2048]{1,0:T(8,128)(2,1)} %get-tuple-element.115.tok_ref, bf16[256,2048]{1,0:T(8,128)(2,1)} %cot_ref.3, f32[8,1,256]{2,1,0:T(1,128)} %broadcast_in_dim.45.route_ref, bf16[16,2048]{1,0:T(8,128)(2,1)} %broadcast_in_dim.46.gate_ref, ...), custom_call_target="tpu_custom_call" | custom-call | flops 1048576 | bytes 65536 | tf_op jit(solution)/shard_map/own_mlp/pallas_call | solution.py:338
  166.3 11.3 %split_rounded.1 = (bf16[2048,2048]{1,0:T(8,128)(2,1)}, f32[8,8,256]{2,1,0:T(8,128)}) custom-call(f32[8,264,2048]{2,1,0:T(8,128)} %bitcast.46), custom_call_target="tpu_custom_call" | custom-call | tf_op jit(solution)/shard_map/split_rounded/pallas_call | solution.py:650
  180.9 23.1 %chip_hidden.4 = (bf16[6,704,2048]{2,1,0:T(8,128)(2,1)}, bf16[6,352,2048]{2,1,0:T(8,128)(2,1)}, bf16[2048,512]{1,0:T(8,128)(2,1)}) custom-call(s32[5]{0:T(128)} %stack.76.at_ref, f32[256,2048]{1,0:T(8,128)} %get-tuple-element.113.even_ref, f32[256,2048]{1,0:T(8,128)} %collective-permute-done.odd_ref, bf16[2048,2048]{1,0:T(8,128)(2,1)} %get-tuple-element.120.cot_ref, ...), custom_call_target="tpu_custom_call" | custom-call | flops 1048576 | bytes 65536 | tf_op jit(solution)/shard_map/chip_hidden/pallas_call | solution.py:414
  204.0 5.1 %all-gather.10.cloned.1.call-done = f32[2048,2048]{1,0:T(8,128)} async-done(((f32[256,2048]{1,0:T(8,128)}), f32[2048,2048]{1,0:T(8,128)}) %all-gather.10.cloned.1.call-update) | async-done | bytes 16777232 | tf_op jit(solution)/shard_map/all_gather | solution.py:739
  209.1 23.2 %chip_hidden.5 = (bf16[6,704,2048]{2,1,0:T(8,128)(2,1)}, bf16[6,352,2048]{2,1,0:T(8,128)(2,1)}, bf16[2048,512]{1,0:T(8,128)(2,1)}) custom-call(s32[5]{0:T(128)} %stack.72.at_ref, f32[8,256,2048]{2,1,0:T(8,128)} %bitcast.37, f32[8,256,2048]{2,1,0:T(8,128)} %bitcast.38, ...), custom_call_target="tpu_custom_call", output_to_operand_aliasing={{0}: (8, {}), {1}: (9, {}), {2}: (10, {})} | custom-call | flops 1048576 | bytes 65536 | tf_op jit(solution)/shard_map/chip_hidden/pallas_call | solution.py:414
  232.3 23.1 %chip_hidden.6 = (bf16[6,704,2048]{2,1,0:T(8,128)(2,1)}, bf16[6,352,2048]{2,1,0:T(8,128)(2,1)}, bf16[2048,512]{1,0:T(8,128)(2,1)}) custom-call(s32[5]{0:T(128)} %stack.70.at_ref, f32[8,256,2048]{2,1,0:T(8,128)} %bitcast.39, f32[8,256,2048]{2,1,0:T(8,128)} %bitcast.40, ...), custom_call_target="tpu_custom_call", output_to_operand_aliasing={{0}: (8, {}), {1}: (9, {}), {2}: (10, {})} | custom-call | flops 1048576 | bytes 65536 | tf_op jit(solution)/shard_map/chip_hidden/pallas_call | solution.py:414
  255.4 15.1 %attention_back.1 = (f32[1,264,2048]{2,1,0:T(8,128)}, f32[256,2048]{1,0:T(8,128)}, bf16[2,256,1024]{2,1,0:T(8,128)(2,1)}, bf16[256,1536]{1,0:T(8,128)(2,1)}, f32[1,1536]{1,0:T(1,128)}, /*index=5*/f32[1,2048]{1,0:T(1,128)}) custom-call(f32[256,2048]{1,0:T(8,128)} %all-reduce.9.cloned.1.call-done.total_ref, f32[256,2048]{1,0:T(8,128)} %get-tuple-element.112.residual_ref, ...), custom_call_target="tpu_custom_call" | custom-call | flops 1048576 | bytes 65536 | tf_op jit(solution)/shard_map/attention_back/pallas_call | solution.py:235
  270.5 8.2 %token_products.2 = (f32[256,2048]{1,0:T(8,128)}, f32[256,2048]{1,0:T(8,128)}, f32[256,2048]{1,0:T(8,128)}, f32[256,2048]{1,0:T(8,128)}) custom-call(s32[4]{0:T(128)} %add_add_fusion.1.at_ref, bf16[2,256,1024]{2,1,0:T(8,128)(2,1)} %get-tuple-element.122.normed_ref, bf16[256,1536]{1,0:T(8,128)(2,1)} %get-tuple-element.137.projected_ref, ...), custom_call_target="tpu_custom_call" | custom-call | flops 1048576 | bytes 65536 | tf_op jit(solution)/shard_map/token_products/pallas_call | solution.py:498
  280.4 3.1 collective-permute-done.1.refs_0_
  283.6 2.7 collective-permute-done.2.refs_1_
  286.2 3.0 collective-permute-done.3.refs_2_
  289.2 3.0 collective-permute-done.4.refs_3_
  292.2 11.5 %token_products.3 = (f32[2,256,1024]{2,1,0:T(8,128)}, f32[2,256,1024]{2,1,0:T(8,128)}, f32[2,256,1024]{2,1,0:T(8,128)}, f32[2,256,1024]{2,1,0:T(8,128)}) custom-call(s32[4]{0:T(128)} %add_add_fusion.at_ref, bf16[2,256,1024]{2,1,0:T(8,128)(2,1)} %get-tuple-element.122.normed_ref, bf16[256,1536]{1,0:T(8,128)(2,1)} %get-tuple-element.137.projected_ref, ...), custom_call_target="tpu_custom_call" | custom-call | flops 1048576 | bytes 65536 | tf_op jit(solution)/shard_map/token_products/pallas_call | solution.py:498
  306.5 23.1 %chip_hidden.7 = (bf16[6,704,2048]{2,1,0:T(8,128)(2,1)}, bf16[6,352,2048]{2,1,0:T(8,128)(2,1)}, bf16[2048,512]{1,0:T(8,128)(2,1)}) custom-call(s32[5]{0:T(128)} %stack.68.at_ref, f32[8,256,2048]{2,1,0:T(8,128)} %bitcast.41, f32[8,256,2048]{2,1,0:T(8,128)} %bitcast.42, ...), custom_call_target="tpu_custom_call", output_to_operand_aliasing={{0}: (8, {}), {1}: (9, {}), {2}: (10, {})} | custom-call | flops 1048576 | bytes 65536 | tf_op jit(solution)/shard_map/chip_hidden/pallas_call | solution.py:414
  329.6 22.5 %weight_grads.1 = (f32[8,2,352,256]{3,2,1,0:T(8,128)}, f32[8,352,256]{2,1,0:T(8,128)}, f32[4,2,352,256]{3,2,1,0:T(8,128)}, f32[4,352,256]{2,1,0:T(8,128)}, f32[6...) custom-call(s32[4]{0:T(128)} %add_add_fusion.at_ref, bf16[6,704,2048]{2,1,0:T(8,128)(2,1)} %get-tuple-element.153.mix_grad_ref, ...), custom_call_target="tpu_custom_call" | custom-call | flops 1048576 | bytes 65536 | tf_op jit(solution)/shard_map/weight_grads/pallas_call | solution.py:576
  353.4 6.4 %turned_blocks.1 = (f32[256,1024]{1,0:T(8,128)}, f32[256,1024]{1,0:T(8,128)}, f32[256,1024]{1,0:T(8,128)}, f32[256,1024]{1,0:T(8,128)}) custom-call(s32[4]{0:T(128)} %add_add_fusion.at_ref, f32[2,256,1024]{2,1,0:T(8,128)} %get-tuple-element.161.x_keep_ref, f32[2,256,1024]{2,1,0:T(8,128)} %copy-done.8, f32[2,256,1024]{2,1,0:T(8,128)} %get-tuple-element.163.y_keep_ref, ...), custom_call_target="tpu_custom_call" | custom-call | flops 1048576 | bytes 65536 | tf_op jit(solution)/shard_map/turned_blocks/pallas_call | solution.py:526
  359.9 21.4 %all-reduce.11.cloned.1.call-done = f32[264,2048]{1,0:T(8,128)} async-done(((f32[264,2048]{1,0:T(8,128)}), f32[264,2048]{1,0:T(8,128)}) %all-reduce.11.cloned.1.call-update) | async-done | bytes 2162704 | tf_op jit(solution)/shard_map/psum | solution.py:767
  384.8 6.7 %collective-permute-done.10.two_ref = f32[6,352,256]{2,1,0:T(8,128)S(1)} collective-permute-done((f32[6,352,256]{2,1,0:T(8,128)}, f32[6,352,256]{2,1,0:T(8,128)S(1)}, u32[]{:S(2)}, u32[]{:S(2)}) %collective-permute-start.10) | collective-permute-done | bytes 2162720 | tf_op jit(solution)/shard_map/ppermute | solution.py:737
  393.0 8.1 %place_peer.1 = (f32[8,2,352,256]{3,2,1,0:T(8,128)}, f32[8,352,256]{2,1,0:T(8,128)}, f32[4,2,352,256]{3,2,1,0:T(8,128)}, f32[4,352,256]{2,1,0:T(8,128)}) custom-call(s32[4]{0:T(128)} %add_add_fusion.at_ref, f32[6,2,352,256]{3,2,1,0:T(8,128)} %collective-permute-done.9.one_ref, ...), custom_call_target="tpu_custom_call", output_to_operand_aliasing={{0}: (3, {}), {1}: (4, {}), {2}: (5, {}), {3}: (6, {})} | custom-call | flops 1048576 | bytes 65536 | tf_op jit(solution)/shard_map/place_peer/pallas_call | solution.py:619
  404.1 5.7 %collective-permute-done.12 = f32[8,2048]{1,0:T(8,128)S(1)} collective-permute-done((f32[8,2048]{1,0:T(8,128)S(1)}, f32[8,2048]{1,0:T(8,128)S(1)}, u32[]{:S(2)}, u32[]{:S(2)}) %collective-permute-start.12) | collective-permute-done | bytes 65568 | tf_op jit(solution)/shard_map/ppermute | solution.py:670
  412.8 3.4 copy.58
  416.3 1.8 add.85
  420.8 6.7 %all-gather.6.cloned.1.call-done = f32[256,2048]{1,0:T(8,128)} async-done(((f32[64,2048]{1,0:T(8,128)}), f32[256,2048]{1,0:T(8,128)}) %all-gather.6.cloned.1.call-update) | async-done | bytes 2097168 | tf_op jit(solution)/shard_map/all_gather | solution.py:789
  427.5 2.8 add_convert_fusion
  (135 shorter events, 38.7 us)
Async XLA Ops:
  8.0 98.1 %all-gather.8.cloned.1.call-start = ((), (), s32[]{:S(2)}) async-start(), calls=%async_computation.6 | async-start | bytes 19464192 | tf_op jit(solution)/shard_map/all_gather | solution.py:709
  11.1 104.1 %all-reduce.7.cloned.1.call-start = ((), (), s32[]{:S(2)}) async-start(), calls=%async_computation.1 | async-start | bytes 4194304 | tf_op jit(solution)/shard_map/psum | solution.py:725
  26.6 182.5 %all-gather.10.cloned.1.call-start = ((), (), s32[]{:S(2)}) async-start(), calls=%async_computation.7 | async-start | bytes 18874368 | tf_op jit(solution)/shard_map/all_gather | solution.py:739
  55.5 13.4 %slice-start = ((s8[11534336]{0:T(1024)(128)(4,1)}), s8[4194304]{0:T(1024)(128)(4,1)S(1)}, s32[]{:S(2)}) async-start(s8[11534336]{0:T(1024)(128)(4,1)} %bitcast.47), calls=%async_computation.8 | async-start | bytes 8388608
  55.5 13.4 %slice-start.4 = ((s8[5767168]{0:T(1024)(128)(4,1)}), s8[4194304]{0:T(1024)(128)(4,1)S(1)}, s32[]{:S(2)}) async-start(s8[5767168]{0:T(1024)(128)(4,1)} %bitcast.51), calls=%async_computation.12 | async-start | bytes 8388608
  55.5 12.8 %copy-start.16 = (bf16[2048]{0:T(1024)(128)(2,1)S(1)}, bf16[2048]{0:T(1024)(128)(2,1)}, u32[]{:S(2)}) copy-start(bf16[2048]{0:T(1024)(128)(2,1)} %param.23) | copy-start | bytes 12292
  55.5 13.5 %slice-start.1 = ((s8[11534336]{0:T(1024)(128)(4,1)}), s8[4194304]{0:T(1024)(128)(4,1)S(1)}, s32[]{:S(2)}) async-start(s8[11534336]{0:T(1024)(128)(4,1)} %bitcast.47), calls=%async_computation.9 | async-start | bytes 8388608
  55.5 14.6 %slice-start.2 = ((s8[11534336]{0:T(1024)(128)(4,1)}), s8[3145728]{0:T(1024)(128)(4,1)S(1)}, s32[]{:S(2)}) async-start(s8[11534336]{0:T(1024)(128)(4,1)} %bitcast.47), calls=%async_computation.10 | async-start | bytes 6291456
  55.5 15.2 %slice-start.5 = ((s8[5767168]{0:T(1024)(128)(4,1)}), s8[1572864]{0:T(1024)(128)(4,1)S(1)}, s32[]{:S(2)}) async-start(s8[5767168]{0:T(1024)(128)(4,1)} %bitcast.51), calls=%async_computation.13 | async-start | bytes 3145728
  120.0 135.4 %all-reduce.9.cloned.1.call-start = ((), (), s32[]{:S(2)}) async-start(), calls=%async_computation.2 | async-start | bytes 4194304 | tf_op jit(solution)/shard_map/psum | solution.py:749
  162.2 141.5 %reduce-scatter.2.cloned.1.call-start = ((), (), s32[]{:S(2)}) async-start(), calls=%async_computation.3 | async-start | bytes 2621440 | tf_op jit(solution)/shard_map/reduce_scatter | solution.py:761
  162.8 218.5 %all-reduce.11.cloned.1.call-start = ((), (), s32[]{:S(2)}) async-start(), calls=%async_computation.5 | async-start | bytes 4325376 | tf_op jit(solution)/shard_map/psum | solution.py:767
  164.4 16.5 %collective-permute-start = (f32[256,2048]{1,0:T(8,128)S(1)}, f32[256,2048]{1,0:T(8,128)}, u32[]{:S(2)}, u32[]{:S(2)}) collective-permute-start(f32[256,2048]{1,0:T(8,128)S(1)} %copy-done.3), channel_id=1, source_target_pairs={{0,4},{4,0},{8,12},{12,8},{16,20},{20,16},{24,28},{28,24},{1,5},{5... | collective-permute-start | bytes 6291464 | tf_op jit(solution)/shard_map/ppermute | solution.py:737
  166.3 11.3 %copy-start.21 = (f32[1,256]{1,0:T(1,128)S(1)}, f32[1,256]{1,0:T(1,128)}, u32[]{:S(2)}) copy-start(f32[1,256]{1,0:T(1,128)} %get-tuple-element.124) | copy-start | bytes 3076
  166.3 13.7 %copy-start.5 = (bf16[256,2048]{1,0:T(8,128)(2,1)S(1)}, bf16[256,2048]{1,0:T(8,128)(2,1)}, u32[]{:S(2)}) copy-start(bf16[256,2048]{1,0:T(8,128)(2,1)} %get-tuple-element.115.tok_ref) | copy-start | bytes 3145732
  278.7 4.8 %collective-permute-start.1 = (f32[256,2048]{1,0:T(8,128)}, f32[256,2048]{1,0:T(8,128)S(1)}, u32[]{:S(2)}, u32[]{:S(2)}) collective-permute-start(f32[256,2048]{1,0:T(8,128)} %get-tuple-element.140), channel_id=1, source_target_pairs={{0,4},{4,0},{8,12},{12,8},{16,20},{20,16},{24,28},{28,24},{1,5},{5... | collective-permute-start | bytes 6291464 | tf_op jit(solution)/shard_map/ppermute | solution.py:737
  279.0 7.2 %collective-permute-start.2 = (f32[256,2048]{1,0:T(8,128)}, f32[256,2048]{1,0:T(8,128)}, u32[]{:S(2)}, u32[]{:S(2)}) collective-permute-start(f32[256,2048]{1,0:T(8,128)} %get-tuple-element.141), channel_id=1, source_target_pairs={{0,4},{4,0},{8,12},{12,8},{16,20},{20,16},{24,28},{28,24},{1,5},{5... | collective-permute-start | bytes 6291464 | tf_op jit(solution)/shard_map/ppermute | solution.py:737
  279.2 10.0 %collective-permute-start.3 = (f32[256,2048]{1,0:T(8,128)}, f32[256,2048]{1,0:T(8,128)}, u32[]{:S(2)}, u32[]{:S(2)}) collective-permute-start(f32[256,2048]{1,0:T(8,128)} %get-tuple-element.142), channel_id=1, source_target_pairs={{0,4},{4,0},{8,12},{12,8},{16,20},{20,16},{24,28},{28,24},{1,5},{5... | collective-permute-start | bytes 6291464 | tf_op jit(solution)/shard_map/ppermute | solution.py:737
  279.5 12.7 %collective-permute-start.4 = (f32[256,2048]{1,0:T(8,128)}, f32[256,2048]{1,0:T(8,128)}, u32[]{:S(2)}, u32[]{:S(2)}) collective-permute-start(f32[256,2048]{1,0:T(8,128)} %get-tuple-element.143), channel_id=1, source_target_pairs={{0,4},{4,0},{8,12},{12,8},{16,20},{20,16},{24,28},{28,24},{1,5},{5... | collective-permute-start | bytes 6291464 | tf_op jit(solution)/shard_map/ppermute | solution.py:737
  279.8 147.7 %all-gather.6.cloned.1.call-start = ((), (), s32[]{:S(2)}) async-start(), calls=%async_computation.4 | async-start | bytes 2621440 | tf_op jit(solution)/shard_map/all_gather | solution.py:789
  283.5 8.7 %copy-start.9 = (f32[256,2048]{1,0:T(8,128)}, f32[256,2048]{1,0:T(8,128)S(1)}, u32[]{:S(2)}) copy-start(f32[256,2048]{1,0:T(8,128)S(1)} %collective-permute-done.1.refs_0_) | copy-start | bytes 6291460
  303.7 48.4 %collective-permute-start.5 = (f32[2,256,1024]{2,1,0:T(8,128)}, f32[2,256,1024]{2,1,0:T(8,128)S(1)}, u32[]{:S(2)}, u32[]{:S(2)}) collective-permute-start(f32[2,256,1024]{2,1,0:T(8,128)} %get-tuple-element.157), channel_id=1, source_target_pairs={{0,8},{4,12},{8,0},{12,4},{16,24},{20,28},{24,16},{28,20},{1,9},{5... | collective-permute-start | bytes 6291464 | tf_op jit(solution)/shard_map/ppermute | solution.py:670
  305.3 47.7 %collective-permute-start.6 = (f32[2,256,1024]{2,1,0:T(8,128)}, f32[2,256,1024]{2,1,0:T(8,128)}, u32[]{:S(2)}, u32[]{:S(2)}) collective-permute-start(f32[2,256,1024]{2,1,0:T(8,128)} %get-tuple-element.158), channel_id=1, source_target_pairs={{0,16},{4,20},{8,24},{12,28},{16,0},{20,4},{24,8},{28,12},{1,17},{... | collective-permute-start | bytes 6291464 | tf_op jit(solution)/shard_map/ppermute | solution.py:670
  381.3 10.8 %collective-permute-start.9 = (f32[6,2,352,256]{3,2,1,0:T(8,128)}, f32[6,2,352,256]{3,2,1,0:T(8,128)}, u32[]{:S(2)}, u32[]{:S(2)}) collective-permute-start(f32[6,2,352,256]{3,2,1,0:T(8,128)} %get-tuple-element.175), channel_id=1, source_target_pairs={{0,4},{4,0},{8,12},{12,8},{16,20},{20,16},{24,28},{28,24},{1,5},{5... | collective-permute-start | bytes 12976136 | tf_op jit(solution)/shard_map/ppermute | solution.py:737
  381.3 10.3 %collective-permute-start.10 = (f32[6,352,256]{2,1,0:T(8,128)}, f32[6,352,256]{2,1,0:T(8,128)S(1)}, u32[]{:S(2)}, u32[]{:S(2)}) collective-permute-start(f32[6,352,256]{2,1,0:T(8,128)} %get-tuple-element.176), channel_id=1, source_target_pairs={{0,4},{4,0},{8,12},{12,8},{16,20},{20,16},{24,28},{28,24},{1,5},{5... | collective-permute-start | bytes 6488072 | tf_op jit(solution)/shard_map/ppermute | solution.py:737
  381.8 34.4 %collective-permute-start.7 = (f32[256,1024]{1,0:T(8,128)}, f32[256,1024]{1,0:T(8,128)}, u32[]{:S(2)}, u32[]{:S(2)}) collective-permute-start(f32[256,1024]{1,0:T(8,128)} %get-tuple-element.171), channel_id=1, source_target_pairs={{0,16},{4,20},{8,24},{12,28},{16,0},{20,4},{24,8},{28,12},{1,17},{... | collective-permute-start | bytes 3145736 | tf_op jit(solution)/shard_map/ppermute | solution.py:670
  383.4 32.9 %collective-permute-start.8 = (f32[256,1024]{1,0:T(8,128)}, f32[256,1024]{1,0:T(8,128)}, u32[]{:S(2)}, u32[]{:S(2)}) collective-permute-start(f32[256,1024]{1,0:T(8,128)} %get-tuple-element.172), channel_id=1, source_target_pairs={{0,8},{4,12},{8,0},{12,4},{16,24},{20,28},{24,16},{28,20},{1,9},{5... | collective-permute-start | bytes 3145736 | tf_op jit(solution)/shard_map/ppermute | solution.py:670
  393.0 8.6 %copy-start = (bf16[256,2048]{1,0:T(8,128)(2,1)S(1)}, bf16[256,2048]{1,0:T(8,128)(2,1)}, u32[]{:S(2)}) copy-start(bf16[256,2048]{1,0:T(8,128)(2,1)} %x_ref.5) | copy-start | bytes 3145732
  401.1 9.3 %copy-start.7 = (f32[256,2048]{1,0:T(8,128)S(1)}, f32[256,2048]{1,0:T(8,128)}, u32[]{:S(2)}) copy-start(f32[256,2048]{1,0:T(8,128)} %get-tuple-element.173) | copy-start | bytes 6291460
  401.2 1.4 collective-permute-start.11
  402.5 7.2 %collective-permute-start.12 = (f32[8,2048]{1,0:T(8,128)S(1)}, f32[8,2048]{1,0:T(8,128)S(1)}, u32[]{:S(2)}, u32[]{:S(2)}) collective-permute-start(f32[8,2048]{1,0:T(8,128)S(1)} %pad_add_fusion), channel_id=1, source_target_pairs={{0,8},{4,12},{8,0},{12,4},{16,24},{20,28},{24,16},{28,20},{1,9},{5... | collective-permute-start | bytes 196616 | tf_op jit(solution)/shard_map/ppermute | solution.py:670
  409.8 6.4 %collective-permute-start.13 = (f32[8,2048]{1,0:T(8,128)S(1)}, f32[8,2048]{1,0:T(8,128)S(1)}, u32[]{:S(2)}, u32[]{:S(2)}) collective-permute-start(f32[8,2048]{1,0:T(8,128)S(1)} %add.83), channel_id=1, source_target_pairs={{0,16},{4,20},{8,24},{12,28},{16,0},{20,4},{24,8},{28,12},{1,17},{... | collective-permute-start | bytes 196616 | tf_op jit(solution)/shard_map/ppermute | solution.py:670
  (17 other events, 71.2 us)
Sparse Core Ops, SparseCore 0:
  11.3 94.7 all-gather.7
  120.1 88.8 all-gather.9
Sparse Core Ops, SparseCore 1:
  26.7 88.5 all-reduce.6
  162.3 83.8 all-reduce.8
  248.9 42.5 reduce-scatter.1
  293.9 87.3 all-reduce.10
  382.9 44.6 all-gather.5

commit v8 on v7

--- a/solution.py
+++ b/solution.py
@@ -762,17 +762,18 @@
 
     normed_one_part, residual_grad, branch_grad, projected_grad, bias_part, mlp_gain_part = attention_back(
         normed_two_total, residual, cotangent, gain_two, out_weight, qkv, qkv_weight,
-        cosine, sine, row, col, layer_input, shared_gate_part, 1,
-    )
-    summed = lax.psum(normed_one_part.reshape(-1, width), "tensor")
+        cosine, sine, row, col, layer_input, shared_gate_part, n_tensor,
+    )
+    few = count // n_tensor
+    summed = lax.psum_scatter(normed_one_part.reshape(-1, width), "tensor", scatter_dimension=0, tiled=True)
+    own_rows = lambda v: lax.dynamic_slice_in_dim(v, lax.axis_index("tensor") * few, few, 0)
 
     def finish(summed):
-        inputs = layer_input.astype(F32)
+        inputs = own_rows(layer_input).astype(F32)
         factor = lax.rsqrt(jnp.mean(inputs * inputs, axis=-1, keepdims=True) + EPS)
         bias_row = jnp.pad(bias_part, ((0, 0), (0, width - bias_part.shape[1])))
-        small = jnp.concatenate([summed[count : count + 2], mlp_gain_part, bias_row])
-        input_grad = (residual_grad + norm_back(inputs, factor, gain_one, summed[:count])).astype(BF16)
-        return input_grad, jnp.pad(small, ((0, 4), (0, 0)))
+        small = jnp.concatenate([summed[few : few + 2], mlp_gain_part, bias_row])
+        return norm_back(inputs, factor, gain_one, summed[:few]), jnp.pad(small, ((0, 4), (0, 0)))
 
     if last:
         at = jnp.stack([core, chip % 2, chip // 2, chip])
@@ -784,32 +785,33 @@
         x_send, y_send, kept, mlp_sum = tied((x_send, y_send, kept, mlp_sum))
         x_got, y_got = flip(x_send, 2), flip(y_send, 4)
         kept = hide(chip ^ 3, in_order, [tok_all], kept)
+        kept, summed = tied((kept, summed))
+        back, small = finish(summed)
+        back, kept = tied((back, kept))
+        gathered = lax.all_gather(jnp.concatenate([back, mlp_sum]), "tensor")
         *grads, one_peer, two_peer = weight_grads(at, *kept, cot_low, experts // 2)
-        one_peer, x_got, y_got, mlp_sum = tied((one_peer, x_got, y_got, mlp_sum))
-        mlp_sum = lax.all_gather(mlp_sum, "tensor", axis=0, tiled=True)
+        one_peer, x_got, y_got = tied((one_peer, x_got, y_got))
         x_own, x_send, y_own, y_send = turned_blocks(at, x_keep, x_got, y_keep, y_got)
-        x_send, y_send, one_peer, two_peer, summed = tied((x_send, y_send, one_peer, two_peer, summed))
+        x_send, y_send, one_peer, two_peer = tied((x_send, y_send, one_peer, two_peer))
         x_got, y_got = flip(x_send, 4), flip(y_send, 2)
         one_peer, two_peer = swap(one_peer), swap(two_peer)
-        summed, one_peer, two_peer = tied((summed, one_peer, two_peer))
         expert_one, expert_two, shared_one, shared_two = place_peer(at, one_peer, two_peer, grads, experts // 2)
-        expert_one, summed = tied((expert_one, summed))
-        input_grad, small = finish(summed)
+        expert_one, small = tied((expert_one, small))
         for bit in (1, 2, 4):
             small = small + flip(small, bit)
-        x_got, y_got, input_grad, small, expert_one = tied((x_got, y_got, input_grad, small, expert_one))
+        x_got, y_got, small, expert_one = tied((x_got, y_got, small, expert_one))
         both = jnp.concatenate([x_own + x_got, y_own + y_got], axis=1)
         cut = projected_grad.shape[1]
         qkv_weight_grad, out_weight_grad = both[:, :cut], both[:, cut:].T
-        mlp_sum, qkv_weight_grad = tied((mlp_sum, qkv_weight_grad))
+        gathered, qkv_weight_grad = tied((gathered, qkv_weight_grad))
     else:
         at = jnp.stack([core, core, core, chip])
         *grads, one_peer, two_peer = weight_grads(at, *kept, cot_low, experts // 2)
         one_peer, two_peer = swap(one_peer), swap(two_peer)
         expert_one, expert_two, shared_one, shared_two = place_peer(at, one_peer, two_peer, grads, experts // 2)
-        input_grad, small = finish(summed)
+        back, small = finish(summed)
         small = lax.psum(small, "dp")
-        mlp_sum = lax.all_gather(mlp_sum, "tensor", axis=0, tiled=True)
+        gathered = lax.all_gather(jnp.concatenate([back, mlp_sum]), "tensor")
         joint = lambda v: v.reshape(2, count, BLOCKS // 2, -1).transpose(1, 2, 0, 3).reshape(count, width)
         out_weight_grad = lax.psum_scatter(tn(attended, joint(branch_grad)), "dp", scatter_dimension=1, tiled=True)
         qkv_weight_grad = lax.psum_scatter(
@@ -820,7 +822,8 @@
     bias_cols = 3 * head_dim // n_dp
     bias = small[3, : heads_here * 3 * head_dim].reshape(heads_here, 3 * head_dim)
     qkv_bias_grad = lax.dynamic_slice(bias, (0, me * bias_cols), (heads_here, bias_cols))
-    layer_output = (residual + mlp_sum).astype(BF16)
+    input_grad = (residual_grad + gathered[:, :few].reshape(count, width)).astype(BF16)
+    layer_output = (residual + gathered[:, few:].reshape(count, width)).astype(BF16)
 
     expert_gate_up_grad = jnp.transpose(expert_one, (0, 3, 1, 2))
     shared_gate_up_grad = jnp.transpose(shared_one, (3, 1, 0, 2)).reshape(part, 2, shared * units)

time: 442 us -> 440 us (level)
  waiting for transfers between devices: 73 us -> 63.6 us
  other arithmetic: 48.5 us -> 54.8 us
    psum x1 -> x0, waiting for transfers between devices: 21.4 us -> none  [shards(): summed = lax.psum(normed_one_part.reshape(-1, width), 'tensor')]
    reduce_scatter x0 -> x1, waiting for transfers between devices: none -> 11.6 us  [shards(): lax.psum_scatter(normed_one_part.reshape(-1, width), 'tensor', scatter_di...]
    concatenate x1, other arithmetic: 6.96 us -> 12.2 us  [shards(): jnp.concatenate([expert_down, shared_down.reshape(shared, units, width)])]
    unnamed x56 -> x48, local copies, waits for them, and re-layouts: 10.3 us -> 8.94 us
  transfers between devices with their start and end apart: 21 -> 21, of which waited for: 14 -> 13; matrix products, arithmetic and copies ran while one was open for 21% -> 23% of each run, Pallas kernels for 52% -> 52%
where the time goes in v8:
time: 440 us; the launch traced here: 438 us
  Pallas kernels  232 us (53%)
  waiting for transfers between devices  63.6 us (14%)
  local copies, waits for them, and re-layouts  60.8 us (14%)
  other arithmetic  54.8 us (12%)
  between operations  17.4 us (4%)
  starting transfers between devices  9.61 us (2%)
    pallas_call x4, Pallas kernels, chip_hidden(): pl.pallas_call(functools.partial(chip_kernel, here), grid_spec=pltpu.Pref...  92.5 us
    pallas_call x1, Pallas kernels, own_mlp(): pl.pallas_call(functools.partial(own_kernel, experts), grid=(tiles // gro...  40.9 us
    optimization_barrier x1, local copies, waits for them, and re-layouts, shards(): attn_part, shared_gate_up = tied((attn_part, shared_gate_up))  28.9 us
    concatenate x1, other arithmetic, shards(): jnp.concatenate([jnp.transpose(expert_gate_up, (0, 2, 3, 1)), jnp.transpo...  24.2 us
    pallas_call x1, Pallas kernels, weight_grads(): pl.pallas_call(functools.partial(weights_kernel, here), grid_spec=pltpu.P...  22.5 us
    pallas_call x2, Pallas kernels, token_products(): pl.pallas_call(kernel, grid_spec=pltpu.PrefetchScalarGridSpec(num_scalar_...  19.6 us
    ppermute x7, waiting for transfers between devices, shards(): swap = lambda v: lax.ppermute(v, 'dp', [(i, i ^ 1) for i in range(n_dp)])  18.6 us
    pallas_call x1, Pallas kernels, attention_back(): pl.pallas_call(back_kernel, grid=(heads,), in_specs=[whole(count, width),...  15.2 us
  transfers between devices with their start and end apart: 21, of which 13 were waited for; matrix products, arithmetic and copies ran while one was open for 23% of the time, Pallas kernels for 52%

profile of v8, /device:TPU:0, one launch (start us, length us, event | category | flops | bytes accessed | tf_op | source)
XLA Modules:
  0.0 438.5 jit_solution(15759454068099147722)
XLA Ops:
  14.6 11.3 %attention.1 = (f32[256,2048]{1,0:T(8,128)}, bf16[2,256,1024]{2,1,0:T(8,128)(2,1)}, bf16[256,1536]{1,0:T(8,128)(2,1)}, bf16[256,512]{1,0:T(8,128)(2,1)}) custom-call(bf16[256,2048]{1,0:T(8,128)(2,1)} %x_ref.5, f32[1,2048]{1,0:T(1,128)} %bitcast.65, bf16[2048,1536]{1,0:T(8,128)(2,1)} %weight_ref.3, f32[4,1,384]{2,1,0:T(1,128)} %reshape.85.bias_ref, ...), custom_call_target="tpu_custom_call" | custom-call | flops 1048576 | bytes 65536 | tf_op jit(solution)/shard_map/attention/pallas_call | solution.py:97
  26.6 28.9 %copy.53 = bf16[2048,2,1408]{0,2,1:T(8,128)(2,1)} copy(bf16[2048,2,1408]{2,1,0:T(2,128)(2,1)} %param.26) | data formatting | bytes 23068672 | tf_op jit(solution)/shard_map/optimization_barrier | solution.py:724
  55.5 11.2 %copy.60 = bf16[2048,2,4,352]{0,3,1,2:T(8,128)(2,1)} copy(bf16[2048,2,4,352]{0,3,2,1:T(8,128)(2,1)} %bitcast.52) | data formatting | bytes 23068672 | tf_op jit(solution)/shard_map/reshape | solution.py:729
  66.8 12.2 %pad_maximum_fusion.1.w2_ref = bf16[12,352,2048]{2,1,0:T(8,128)(2,1)} fusion(bf16[4,352,2048]{2,1,0:T(8,128)(2,1)S(1)} %bitcast.60, bf16[8,352,2048]{2,1,0:T(8,128)(2,1)} %param.25), kind=kLoop, calls=%fused_computation.1 | loop fusion | flops 8650752 | bytes 34603008 | tf_op jit(solution)/shard_map/concatenate | solution.py:732
  79.0 24.2 %pad_maximum_fusion.w1_ref = bf16[12,2,352,2048]{3,2,1,0:T(8,128)(2,1)} fusion(bf16[4,2,352,2048]{3,2,1,0:T(8,128)(2,1)} %bitcast.53, bf16[8,2,352,2048]{3,2,1,0:T(8,128)(2,1)} %bitcast.54), kind=kLoop, calls=%fused_computation | loop fusion | flops 17301504 | bytes 69206016 | tf_op jit(solution)/shard_map/concatenate | solution.py:726
  103.2 3.1 all-gather.7.cloned.1.call-done
  106.3 8.4 %all-reduce.6.cloned.1.call-done.sum_ref = f32[256,2048]{1,0:T(8,128)} async-done(((f32[256,2048]{1,0:T(8,128)}), f32[256,2048]{1,0:T(8,128)}) %all-reduce.6.cloned.1.call-update) | async-done | bytes 2097168 | tf_op jit(solution)/shard_map/psum | solution.py:725
  114.8 4.7 %second_norm.1 = (f32[256,2048]{1,0:T(8,128)}, bf16[256,2048]{1,0:T(8,128)(2,1)}, f32[256,2048]{1,0:T(8,128)}) custom-call(bf16[256,2048]{1,0:T(8,128)(2,1)} %x_ref.5, f32[256,2048]{1,0:T(8,128)} %all-reduce.6.cloned.1.call-done.sum_ref, f32[1,2048]{1,0:T(1,128)} %bitcast.66), custom_call_target="tpu_custom_call" | custom-call | tf_op jit(solution)/shard_map/second_norm/pallas_call | solution.py:145
  120.8 40.9 %own_mlp.1 = (f32[256,2048]{1,0:T(8,128)}, f32[256,2048]{1,0:T(8,128)}, f32[1,256]{1,0:T(1,128)}) custom-call(bf16[256,2048]{1,0:T(8,128)(2,1)} %get-tuple-element.117.tok_ref, bf16[256,2048]{1,0:T(8,128)(2,1)} %cot_ref.3, f32[8,1,256]{2,1,0:T(1,128)} %broadcast_in_dim.45.route_ref, bf16[16,2048]{1,0:T(8,128)(2,1)} %broadcast_in_dim.46.gate_ref, ...), custom_call_target="tpu_custom_call" | custom-call | flops 1048576 | bytes 65536 | tf_op jit(solution)/shard_map/own_mlp/pallas_call | solution.py:338
  167.0 11.3 %split_rounded.1 = (bf16[2048,2048]{1,0:T(8,128)(2,1)}, f32[8,8,256]{2,1,0:T(8,128)}) custom-call(f32[8,264,2048]{2,1,0:T(8,128)} %bitcast.55), custom_call_target="tpu_custom_call" | custom-call | tf_op jit(solution)/shard_map/split_rounded/pallas_call | solution.py:650
  179.8 23.1 %chip_hidden.4 = (bf16[6,704,2048]{2,1,0:T(8,128)(2,1)}, bf16[6,352,2048]{2,1,0:T(8,128)(2,1)}, bf16[2048,512]{1,0:T(8,128)(2,1)}) custom-call(s32[5]{0:T(128)} %stack.76.at_ref, f32[256,2048]{1,0:T(8,128)} %get-tuple-element.115.even_ref, f32[256,2048]{1,0:T(8,128)} %collective-permute-done.odd_ref, bf16[2048,2048]{1,0:T(8,128)(2,1)} %get-tuple-element.122.cot_ref, ...), custom_call_target="tpu_custom_call" | custom-call | flops 1048576 | bytes 65536 | tf_op jit(solution)/shard_map/chip_hidden/pallas_call | solution.py:414
  202.8 5.8 %all-gather.9.cloned.1.call-done = f32[2048,2048]{1,0:T(8,128)} async-done(((f32[256,2048]{1,0:T(8,128)}), f32[2048,2048]{1,0:T(8,128)}) %all-gather.9.cloned.1.call-update) | async-done | bytes 16777232 | tf_op jit(solution)/shard_map/all_gather | solution.py:739
  208.6 23.2 %chip_hidden.5 = (bf16[6,704,2048]{2,1,0:T(8,128)(2,1)}, bf16[6,352,2048]{2,1,0:T(8,128)(2,1)}, bf16[2048,512]{1,0:T(8,128)(2,1)}) custom-call(s32[5]{0:T(128)} %stack.72.at_ref, f32[8,256,2048]{2,1,0:T(8,128)} %bitcast.46, f32[8,256,2048]{2,1,0:T(8,128)} %bitcast.47, ...), custom_call_target="tpu_custom_call", output_to_operand_aliasing={{0}: (8, {}), {1}: (9, {}), {2}: (10, {})} | custom-call | flops 1048576 | bytes 65536 | tf_op jit(solution)/shard_map/chip_hidden/pallas_call | solution.py:414
  231.8 23.1 %chip_hidden.6 = (bf16[6,704,2048]{2,1,0:T(8,128)(2,1)}, bf16[6,352,2048]{2,1,0:T(8,128)(2,1)}, bf16[2048,512]{1,0:T(8,128)(2,1)}) custom-call(s32[5]{0:T(128)} %stack.70.at_ref, f32[8,256,2048]{2,1,0:T(8,128)} %bitcast.48, f32[8,256,2048]{2,1,0:T(8,128)} %bitcast.49, ...), custom_call_target="tpu_custom_call", output_to_operand_aliasing={{0}: (8, {}), {1}: (9, {}), {2}: (10, {})} | custom-call | flops 1048576 | bytes 65536 | tf_op jit(solution)/shard_map/chip_hidden/pallas_call | solution.py:414
  254.9 15.2 %attention_back.1 = (f32[4,72,2048]{2,1,0:T(8,128)}, f32[256,2048]{1,0:T(8,128)}, bf16[2,256,1024]{2,1,0:T(8,128)(2,1)}, bf16[256,1536]{1,0:T(8,128)(2,1)}, f32[1,1536]{1,0:T(1,128)}, /*index=5*/f32[1,2048]{1,0:T(1,128)}) custom-call(f32[256,2048]{1,0:T(8,128)} %all-reduce.8.cloned.1.call-done.total_ref, f32[256,2048]{1,0:T(8,128)} %get-tuple-element.114.residual_ref, ...), custom_call_target="tpu_custom_call" | custom-call | flops 1048576 | bytes 65536 | tf_op jit(solution)/shard_map/attention_back/pallas_call | solution.py:235
  270.8 8.4 %token_products.2 = (f32[256,2048]{1,0:T(8,128)}, f32[256,2048]{1,0:T(8,128)}, f32[256,2048]{1,0:T(8,128)}, f32[256,2048]{1,0:T(8,128)}) custom-call(s32[4]{0:T(128)} %add_add_fusion.1.at_ref, bf16[2,256,1024]{2,1,0:T(8,128)(2,1)} %get-tuple-element.124.normed_ref, bf16[256,1536]{1,0:T(8,128)(2,1)} %get-tuple-element.139.projected_ref, ...), custom_call_target="tpu_custom_call" | custom-call | flops 1048576 | bytes 65536 | tf_op jit(solution)/shard_map/token_products/pallas_call | solution.py:498
  281.5 2.6 collective-permute-done.1.refs_0_
  284.0 2.7 collective-permute-done.2.refs_1_
  286.7 3.0 collective-permute-done.3.refs_2_
  289.7 3.0 collective-permute-done.4.refs_3_
  292.7 11.3 %token_products.3 = (f32[2,256,1024]{2,1,0:T(8,128)}, f32[2,256,1024]{2,1,0:T(8,128)}, f32[2,256,1024]{2,1,0:T(8,128)}, f32[2,256,1024]{2,1,0:T(8,128)}) custom-call(s32[4]{0:T(128)} %add_add_fusion.at_ref, bf16[2,256,1024]{2,1,0:T(8,128)(2,1)} %get-tuple-element.124.normed_ref, bf16[256,1536]{1,0:T(8,128)(2,1)} %get-tuple-element.139.projected_ref, ...), custom_call_target="tpu_custom_call" | custom-call | flops 1048576 | bytes 65536 | tf_op jit(solution)/shard_map/token_products/pallas_call | solution.py:498
  306.3 23.1 %chip_hidden.7 = (bf16[6,704,2048]{2,1,0:T(8,128)(2,1)}, bf16[6,352,2048]{2,1,0:T(8,128)(2,1)}, bf16[2048,512]{1,0:T(8,128)(2,1)}) custom-call(s32[5]{0:T(128)} %stack.65.at_ref, f32[8,256,2048]{2,1,0:T(8,128)} %bitcast.50, f32[8,256,2048]{2,1,0:T(8,128)} %bitcast.51, ...), custom_call_target="tpu_custom_call", output_to_operand_aliasing={{0}: (8, {}), {1}: (9, {}), {2}: (10, {})} | custom-call | flops 1048576 | bytes 65536 | tf_op jit(solution)/shard_map/chip_hidden/pallas_call | solution.py:414
  329.4 11.6 %reduce-scatter.5.cloned.1.call-done = f32[72,2048]{1,0:T(8,128)} async-done(((f32[288,2048]{1,0:T(8,128)}), f32[72,2048]{1,0:T(8,128)}) %reduce-scatter.5.cloned.1.call-update) | async-done | bytes 589840 | tf_op jit(solution)/shard_map/reduce_scatter | solution.py:768
  344.6 22.5 %weight_grads.1 = (f32[8,2,352,256]{3,2,1,0:T(8,128)}, f32[8,352,256]{2,1,0:T(8,128)}, f32[4,2,352,256]{3,2,1,0:T(8,128)}, f32[4,352,256]{2,1,0:T(8,128)}, f32[6...) custom-call(s32[4]{0:T(128)} %add_add_fusion.at_ref, bf16[6,704,2048]{2,1,0:T(8,128)(2,1)} %get-tuple-element.166.mix_grad_ref, ...), custom_call_target="tpu_custom_call" | custom-call | flops 1048576 | bytes 65536 | tf_op jit(solution)/shard_map/weight_grads/pallas_call | solution.py:576
  368.5 6.5 %turned_blocks.1 = (f32[256,1024]{1,0:T(8,128)}, f32[256,1024]{1,0:T(8,128)}, f32[256,1024]{1,0:T(8,128)}, f32[256,1024]{1,0:T(8,128)}) custom-call(s32[4]{0:T(128)} %add_add_fusion.at_ref, f32[2,256,1024]{2,1,0:T(8,128)} %get-tuple-element.165.x_keep_ref, f32[2,256,1024]{2,1,0:T(8,128)} %copy-done.6, f32[2,256,1024]{2,1,0:T(8,128)} %get-tuple-element.173.y_keep_ref, ...), custom_call_target="tpu_custom_call" | custom-call | flops 1048576 | bytes 65536 | tf_op jit(solution)/shard_map/turned_blocks/pallas_call | solution.py:526
  378.4 6.9 %collective-permute-done.10.two_ref = f32[6,352,256]{2,1,0:T(8,128)S(1)} collective-permute-done((f32[6,352,256]{2,1,0:T(8,128)}, f32[6,352,256]{2,1,0:T(8,128)S(1)}, u32[]{:S(2)}, u32[]{:S(2)}) %collective-permute-start.10) | collective-permute-done | bytes 2162720 | tf_op jit(solution)/shard_map/ppermute | solution.py:737
  386.7 7.8 %place_peer.1 = (f32[8,2,352,256]{3,2,1,0:T(8,128)}, f32[8,352,256]{2,1,0:T(8,128)}, f32[4,2,352,256]{3,2,1,0:T(8,128)}, f32[4,352,256]{2,1,0:T(8,128)}) custom-call(s32[4]{0:T(128)} %add_add_fusion.at_ref, f32[6,2,352,256]{3,2,1,0:T(8,128)} %collective-permute-done.9.one_ref, ...), custom_call_target="tpu_custom_call", output_to_operand_aliasing={{0}: (3, {}), {1}: (4, {}), {2}: (5, {}), {3}: (6, {})} | custom-call | flops 1048576 | bytes 65536 | tf_op jit(solution)/shard_map/place_peer/pallas_call | solution.py:619
  397.3 6.2 %collective-permute-done.12 = f32[8,2048]{1,0:T(8,128)S(1)} collective-permute-done((f32[8,2048]{1,0:T(8,128)S(1)}, f32[8,2048]{1,0:T(8,128)S(1)}, u32[]{:S(2)}, u32[]{:S(2)}) %collective-permute-start.12) | collective-permute-done | bytes 65568 | tf_op jit(solution)/shard_map/ppermute | solution.py:670
  404.1 2.1 copy.56
  406.3 3.4 copy.58
  416.6 8.2 %all-gather.11.cloned.1.call-done = f32[512,2048]{1,0:T(8,128)} async-done(((f32[128,2048]{1,0:T(8,128)}), f32[512,2048]{1,0:T(8,128)}) %all-gather.11.cloned.1.call-update) | async-done | bytes 4194320 | tf_op jit(solution)/shard_map/all_gather | solution.py:791
  424.8 2.6 fusion.7
  (129 shorter events, 42.5 us)
Async XLA Ops:
  8.0 98.3 %all-gather.7.cloned.1.call-start = ((), (), s32[]{:S(2)}) async-start(), calls=%async_computation.6 | async-start | bytes 19464192 | tf_op jit(solution)/shard_map/all_gather | solution.py:709
  11.1 103.6 %all-reduce.6.cloned.1.call-start = ((), (), s32[]{:S(2)}) async-start(), calls=%async_computation.2 | async-start | bytes 4194304 | tf_op jit(solution)/shard_map/psum | solution.py:725
  14.6 11.4 %copy-start.15 = (bf16[2048]{0:T(1024)(128)(2,1)S(1)}, bf16[2048]{0:T(1024)(128)(2,1)}, u32[]{:S(2)}) copy-start(bf16[2048]{0:T(1024)(128)(2,1)} %param.23) | copy-start | bytes 12292
  26.0 182.6 %all-gather.9.cloned.1.call-start = ((), (), s32[]{:S(2)}) async-start(), calls=%async_computation.7 | async-start | bytes 18874368 | tf_op jit(solution)/shard_map/all_gather | solution.py:739
  26.6 40.2 %slice-start = ((s8[5767168]{0:T(1024)(128)(4,1)}), s8[1572864]{0:T(1024)(128)(4,1)S(1)}, s32[]{:S(2)}) async-start(s8[5767168]{0:T(1024)(128)(4,1)} %bitcast.58), calls=%async_computation.9 | async-start | bytes 3145728
  55.5 11.2 %slice-start.1 = ((s8[5767168]{0:T(1024)(128)(4,1)}), s8[4194304]{0:T(1024)(128)(4,1)S(1)}, s32[]{:S(2)}) async-start(s8[5767168]{0:T(1024)(128)(4,1)} %bitcast.58), calls=%async_computation.10 | async-start | bytes 8388608
  114.8 5.4 %copy-start.16 = (bf16[2048]{0:T(1024)(128)(2,1)S(1)}, bf16[2048]{0:T(1024)(128)(2,1)}, u32[]{:S(2)}) copy-start(bf16[2048]{0:T(1024)(128)(2,1)} %param.28) | copy-start | bytes 12292
  119.5 135.4 %all-reduce.8.cloned.1.call-start = ((), (), s32[]{:S(2)}) async-start(), calls=%async_computation.3 | async-start | bytes 4194304 | tf_op jit(solution)/shard_map/psum | solution.py:749
  161.7 142.2 %reduce-scatter.3.cloned.1.call-start = ((), (), s32[]{:S(2)}) async-start(), calls=%async_computation.4 | async-start | bytes 2621440 | tf_op jit(solution)/shard_map/reduce_scatter | solution.py:761
  162.3 178.7 %reduce-scatter.5.cloned.1.call-start = ((), (), s32[]{:S(2)}) async-start(), calls=%async_computation.5 | async-start | bytes 2949120 | tf_op jit(solution)/shard_map/reduce_scatter | solution.py:768
  163.9 15.8 %collective-permute-start = (f32[256,2048]{1,0:T(8,128)S(1)}, f32[256,2048]{1,0:T(8,128)}, u32[]{:S(2)}, u32[]{:S(2)}) collective-permute-start(f32[256,2048]{1,0:T(8,128)S(1)} %copy-done.2), channel_id=1, source_target_pairs={{0,4},{4,0},{8,12},{12,8},{16,20},{20,16},{24,28},{28,24},{1,5},{5... | collective-permute-start | bytes 6291464 | tf_op jit(solution)/shard_map/ppermute | solution.py:737
  167.0 11.9 %copy-start.3 = (bf16[256,2048]{1,0:T(8,128)(2,1)S(1)}, bf16[256,2048]{1,0:T(8,128)(2,1)}, u32[]{:S(2)}) copy-start(bf16[256,2048]{1,0:T(8,128)(2,1)} %get-tuple-element.117.tok_ref) | copy-start | bytes 3145732
  270.1 154.6 %all-gather.11.cloned.1.call-start = ((), (), s32[]{:S(2)}) async-start(), calls=%async_computation.8 | async-start | bytes 5242880 | tf_op jit(solution)/shard_map/all_gather | solution.py:791
  279.2 4.8 %collective-permute-start.1 = (f32[256,2048]{1,0:T(8,128)}, f32[256,2048]{1,0:T(8,128)S(1)}, u32[]{:S(2)}, u32[]{:S(2)}) collective-permute-start(f32[256,2048]{1,0:T(8,128)} %get-tuple-element.142), channel_id=1, source_target_pairs={{0,4},{4,0},{8,12},{12,8},{16,20},{20,16},{24,28},{28,24},{1,5},{5... | collective-permute-start | bytes 6291464 | tf_op jit(solution)/shard_map/ppermute | solution.py:737
  279.5 7.2 %collective-permute-start.2 = (f32[256,2048]{1,0:T(8,128)}, f32[256,2048]{1,0:T(8,128)}, u32[]{:S(2)}, u32[]{:S(2)}) collective-permute-start(f32[256,2048]{1,0:T(8,128)} %get-tuple-element.143), channel_id=1, source_target_pairs={{0,4},{4,0},{8,12},{12,8},{16,20},{20,16},{24,28},{28,24},{1,5},{5... | collective-permute-start | bytes 6291464 | tf_op jit(solution)/shard_map/ppermute | solution.py:737
  279.7 10.0 %collective-permute-start.3 = (f32[256,2048]{1,0:T(8,128)}, f32[256,2048]{1,0:T(8,128)}, u32[]{:S(2)}, u32[]{:S(2)}) collective-permute-start(f32[256,2048]{1,0:T(8,128)} %get-tuple-element.144), channel_id=1, source_target_pairs={{0,4},{4,0},{8,12},{12,8},{16,20},{20,16},{24,28},{28,24},{1,5},{5... | collective-permute-start | bytes 6291464 | tf_op jit(solution)/shard_map/ppermute | solution.py:737
  280.0 12.7 %collective-permute-start.4 = (f32[256,2048]{1,0:T(8,128)}, f32[256,2048]{1,0:T(8,128)}, u32[]{:S(2)}, u32[]{:S(2)}) collective-permute-start(f32[256,2048]{1,0:T(8,128)} %get-tuple-element.145), channel_id=1, source_target_pairs={{0,4},{4,0},{8,12},{12,8},{16,20},{20,16},{24,28},{28,24},{1,5},{5... | collective-permute-start | bytes 6291464 | tf_op jit(solution)/shard_map/ppermute | solution.py:737
  284.0 8.7 %copy-start.7 = (f32[256,2048]{1,0:T(8,128)}, f32[256,2048]{1,0:T(8,128)S(1)}, u32[]{:S(2)}) copy-start(f32[256,2048]{1,0:T(8,128)S(1)} %collective-permute-done.1.refs_0_) | copy-start | bytes 6291460
  304.0 37.0 %copy-start = (bf16[256,2048]{1,0:T(8,128)(2,1)S(1)}, bf16[256,2048]{1,0:T(8,128)(2,1)}, u32[]{:S(2)}) copy-start(bf16[256,2048]{1,0:T(8,128)(2,1)} %x_ref.5) | copy-start | bytes 3145732
  304.0 37.0 %copy-start.10 = (f32[2048]{0:T(1024)S(1)}, f32[2048]{0:T(1024)}, u32[]{:S(2)}) copy-start(f32[2048]{0:T(1024)} %convert_element_type.36) | copy-start | bytes 24580
  304.0 63.2 %collective-permute-start.5 = (f32[2,256,1024]{2,1,0:T(8,128)}, f32[2,256,1024]{2,1,0:T(8,128)S(1)}, u32[]{:S(2)}, u32[]{:S(2)}) collective-permute-start(f32[2,256,1024]{2,1,0:T(8,128)} %get-tuple-element.170), channel_id=1, source_target_pairs={{0,8},{4,12},{8,0},{12,4},{16,24},{20,28},{24,16},{28,20},{1,9},{5... | collective-permute-start | bytes 6291464 | tf_op jit(solution)/shard_map/ppermute | solution.py:670
  305.6 61.6 %collective-permute-start.6 = (f32[2,256,1024]{2,1,0:T(8,128)}, f32[2,256,1024]{2,1,0:T(8,128)}, u32[]{:S(2)}, u32[]{:S(2)}) collective-permute-start(f32[2,256,1024]{2,1,0:T(8,128)} %get-tuple-element.171), channel_id=1, source_target_pairs={{0,16},{4,20},{8,24},{12,28},{16,0},{20,4},{24,8},{28,12},{1,17},{... | collective-permute-start | bytes 6291464 | tf_op jit(solution)/shard_map/ppermute | solution.py:670
  368.5 9.9 %slice-start.2 = ((f32[72,2048]{1,0:T(8,128)}), f32[2,2048]{1,0:T(2,128)S(1)}, s32[]{:S(2)}) async-start(f32[72,2048]{1,0:T(8,128)} %reduce-scatter.5.cloned.1.call-done), calls=%async_computation.11 | async-start | bytes 32768 | tf_op jit(solution)/shard_map/slice | solution.py:775
  368.5 9.9 %copy-start.12 = (f32[1,2048]{1,0:T(1,128)S(1)}, f32[1,2048]{1,0:T(1,128)}, u32[]{:S(2)}) copy-start(f32[1,2048]{1,0:T(1,128)} %get-tuple-element.189) | copy-start | bytes 24580
  368.5 9.9 %copy-start.13 = (f32[1,1536]{1,0:T(1,128)S(1)}, f32[1,1536]{1,0:T(1,128)}, u32[]{:S(2)}) copy-start(f32[1,1536]{1,0:T(1,128)} %get-tuple-element.190) | copy-start | bytes 18436
  375.1 10.8 %collective-permute-start.9 = (f32[6,2,352,256]{3,2,1,0:T(8,128)}, f32[6,2,352,256]{3,2,1,0:T(8,128)}, u32[]{:S(2)}, u32[]{:S(2)}) collective-permute-start(f32[6,2,352,256]{3,2,1,0:T(8,128)} %get-tuple-element.182), channel_id=1, source_target_pairs={{0,4},{4,0},{8,12},{12,8},{16,20},{20,16},{24,28},{28,24},{1,5},{5... | collective-permute-start | bytes 12976136 | tf_op jit(solution)/shard_map/ppermute | solution.py:737
  375.1 10.3 %collective-permute-start.10 = (f32[6,352,256]{2,1,0:T(8,128)}, f32[6,352,256]{2,1,0:T(8,128)S(1)}, u32[]{:S(2)}, u32[]{:S(2)}) collective-permute-start(f32[6,352,256]{2,1,0:T(8,128)} %get-tuple-element.183), channel_id=1, source_target_pairs={{0,4},{4,0},{8,12},{12,8},{16,20},{20,16},{24,28},{28,24},{1,5},{5... | collective-permute-start | bytes 6488072 | tf_op jit(solution)/shard_map/ppermute | solution.py:737
  375.6 34.2 %collective-permute-start.7 = (f32[256,1024]{1,0:T(8,128)}, f32[256,1024]{1,0:T(8,128)}, u32[]{:S(2)}, u32[]{:S(2)}) collective-permute-start(f32[256,1024]{1,0:T(8,128)} %get-tuple-element.180), channel_id=1, source_target_pairs={{0,16},{4,20},{8,24},{12,28},{16,0},{20,4},{24,8},{28,12},{1,17},{... | collective-permute-start | bytes 3145736 | tf_op jit(solution)/shard_map/ppermute | solution.py:670
  377.0 32.7 %collective-permute-start.8 = (f32[256,1024]{1,0:T(8,128)}, f32[256,1024]{1,0:T(8,128)}, u32[]{:S(2)}, u32[]{:S(2)}) collective-permute-start(f32[256,1024]{1,0:T(8,128)} %get-tuple-element.181), channel_id=1, source_target_pairs={{0,8},{4,12},{8,0},{12,4},{16,24},{20,28},{24,16},{28,20},{1,9},{5... | collective-permute-start | bytes 3145736 | tf_op jit(solution)/shard_map/ppermute | solution.py:670
  394.5 1.3 collective-permute-start.11
  395.8 7.7 %collective-permute-start.12 = (f32[8,2048]{1,0:T(8,128)S(1)}, f32[8,2048]{1,0:T(8,128)S(1)}, u32[]{:S(2)}, u32[]{:S(2)}) collective-permute-start(f32[8,2048]{1,0:T(8,128)S(1)} %add.85), channel_id=1, source_target_pairs={{0,8},{4,12},{8,0},{12,4},{16,24},{20,28},{24,16},{28,20},{1,9},{5... | collective-permute-start | bytes 196616 | tf_op jit(solution)/shard_map/ppermute | solution.py:670
  403.5 6.2 %collective-permute-start.13 = (f32[8,2048]{1,0:T(8,128)S(1)}, f32[8,2048]{1,0:T(8,128)S(1)}, u32[]{:S(2)}, u32[]{:S(2)}) collective-permute-start(f32[8,2048]{1,0:T(8,128)S(1)} %add.86), channel_id=1, source_target_pairs={{0,16},{4,20},{8,24},{12,28},{16,0},{20,4},{24,8},{28,12},{1,17},{... | collective-permute-start | bytes 196616 | tf_op jit(solution)/shard_map/ppermute | solution.py:670
  (13 other events, 26.8 us)
Sparse Core Ops, SparseCore 0:
  11.5 94.8 all-gather.6
  119.7 88.8 all-gather.8
Sparse Core Ops, SparseCore 1:
  26.0 88.7 all-reduce.5
  161.8 83.8 all-reduce.7
  248.4 42.5 reduce-scatter.2
  294.0 46.9 reduce-scatter.4
  344.7 80.0 all-gather.10

commit v9 on v8

--- a/solution.py
+++ b/solution.py
@@ -788,7 +788,8 @@
         kept, summed = tied((kept, summed))
         back, small = finish(summed)
         back, kept = tied((back, kept))
-        gathered = lax.all_gather(jnp.concatenate([back, mlp_sum]), "tensor")
+        mlp_sum = lax.all_gather(mlp_sum, "tensor", axis=0, tiled=True)
+        back = lax.all_gather(back, "tensor", axis=0, tiled=True)
         *grads, one_peer, two_peer = weight_grads(at, *kept, cot_low, experts // 2)
         one_peer, x_got, y_got = tied((one_peer, x_got, y_got))
         x_own, x_send, y_own, y_send = turned_blocks(at, x_keep, x_got, y_keep, y_got)
@@ -803,7 +804,7 @@
         both = jnp.concatenate([x_own + x_got, y_own + y_got], axis=1)
         cut = projected_grad.shape[1]
         qkv_weight_grad, out_weight_grad = both[:, :cut], both[:, cut:].T
-        gathered, qkv_weight_grad = tied((gathered, qkv_weight_grad))
+        mlp_sum, qkv_weight_grad = tied((mlp_sum, qkv_weight_grad))
     else:
         at = jnp.stack([core, core, core, chip])
         *grads, one_peer, two_peer = weight_grads(at, *kept, cot_low, experts // 2)
@@ -811,7 +812,8 @@
         expert_one, expert_two, shared_one, shared_two = place_peer(at, one_peer, two_peer, grads, experts // 2)
         back, small = finish(summed)
         small = lax.psum(small, "dp")
-        gathered = lax.all_gather(jnp.concatenate([back, mlp_sum]), "tensor")
+        mlp_sum = lax.all_gather(mlp_sum, "tensor", axis=0, tiled=True)
+        back = lax.all_gather(back, "tensor", axis=0, tiled=True)
         joint = lambda v: v.reshape(2, count, BLOCKS // 2, -1).transpose(1, 2, 0, 3).reshape(count, width)
         out_weight_grad = lax.psum_scatter(tn(attended, joint(branch_grad)), "dp", scatter_dimension=1, tiled=True)
         qkv_weight_grad = lax.psum_scatter(
@@ -822,8 +824,9 @@
     bias_cols = 3 * head_dim // n_dp
     bias = small[3, : heads_here * 3 * head_dim].reshape(heads_here, 3 * head_dim)
     qkv_bias_grad = lax.dynamic_slice(bias, (0, me * bias_cols), (heads_here, bias_cols))
-    input_grad = (residual_grad + gathered[:, :few].reshape(count, width)).astype(BF16)
-    layer_output = (residual + gathered[:, few:].reshape(count, width)).astype(BF16)
+    layer_output = (residual + mlp_sum).astype(BF16)
+    back, layer_output = tied((back, layer_output))
+    input_grad = (residual_grad + back).astype(BF16)
 
     expert_gate_up_grad = jnp.transpose(expert_one, (0, 3, 1, 2))
     shared_gate_up_grad = jnp.transpose(shared_one, (3, 1, 0, 2)).reshape(part, 2, shared * units)

time: 440 us -> 448 us (1.018)
  waiting for transfers between devices: 63.6 us -> 70.3 us
    all_gather x1 -> x2, waiting for transfers between devices: 8.22 us -> 15.4 us  [the longest x1 15.4 us: shards(): back = lax.all_gather(back, 'tensor', axis=0, tiled=True)]
  transfers between devices with their start and end apart: 21 -> 22, of which waited for: 13 -> 13; matrix products, arithmetic and copies ran while one was open for 23% -> 23% of each run, Pallas kernels for 52% -> 51%
where the time goes in v9:
time: 448 us; the launch traced here: 446 us
  Pallas kernels  233 us (52%)
  waiting for transfers between devices  70.3 us (16%)
  other arithmetic  58.2 us (13%)
  local copies, waits for them, and re-layouts  58.1 us (13%)
  between operations  17.2 us (4%)
  starting transfers between devices  9.67 us (2%)
    pallas_call x4, Pallas kernels, chip_hidden(): pl.pallas_call(functools.partial(chip_kernel, here), grid_spec=pltpu.Pref...  92.9 us
    pallas_call x1, Pallas kernels, own_mlp(): pl.pallas_call(functools.partial(own_kernel, experts), grid=(tiles // gro...  40.9 us
    optimization_barrier x1, local copies, waits for them, and re-layouts, shards(): attn_part, shared_gate_up = tied((attn_part, shared_gate_up))  28.9 us
    concatenate x1, other arithmetic, shards(): jnp.concatenate([jnp.transpose(expert_gate_up, (0, 2, 3, 1)), jnp.transpo...  24.2 us
    pallas_call x1, Pallas kernels, weight_grads(): pl.pallas_call(functools.partial(weights_kernel, here), grid_spec=pltpu.P...  22.2 us
    pallas_call x2, Pallas kernels, token_products(): pl.pallas_call(kernel, grid_spec=pltpu.PrefetchScalarGridSpec(num_scalar_...  19.5 us
    ppermute x7, waiting for transfers between devices, shards(): swap = lambda v: lax.ppermute(v, 'dp', [(i, i ^ 1) for i in range(n_dp)])  19.1 us
    pallas_call x1, Pallas kernels, attention_back(): pl.pallas_call(back_kernel, grid=(heads,), in_specs=[whole(count, width),...  15.4 us
  transfers between devices with their start and end apart: 22, of which 13 were waited for; matrix products, arithmetic and copies ran while one was open for 23% of the time, Pallas kernels for 51%

profile of v9, /device:TPU:0, one launch (start us, length us, event | category | flops | bytes accessed | tf_op | source)
XLA Modules:
  0.0 446.0 jit_solution(18117814277456910981)
XLA Ops:
  14.6 11.3 %attention.1 = (f32[256,2048]{1,0:T(8,128)}, bf16[2,256,1024]{2,1,0:T(8,128)(2,1)}, bf16[256,1536]{1,0:T(8,128)(2,1)}, bf16[256,512]{1,0:T(8,128)(2,1)}) custom-call(bf16[256,2048]{1,0:T(8,128)(2,1)} %x_ref.5, f32[1,2048]{1,0:T(1,128)} %bitcast.55, bf16[2048,1536]{1,0:T(8,128)(2,1)} %weight_ref.3, f32[4,1,384]{2,1,0:T(1,128)} %reshape.77.bias_ref, ...), custom_call_target="tpu_custom_call" | custom-call | flops 1048576 | bytes 65536 | tf_op jit(solution)/shard_map/attention/pallas_call | solution.py:97
  26.6 28.9 %copy.53 = bf16[2048,2,1408]{0,2,1:T(8,128)(2,1)} copy(bf16[2048,2,1408]{2,1,0:T(2,128)(2,1)} %param.26) | data formatting | bytes 23068672 | tf_op jit(solution)/shard_map/optimization_barrier | solution.py:724
  55.5 11.2 %copy.60 = bf16[2048,2,4,352]{0,3,1,2:T(8,128)(2,1)} copy(bf16[2048,2,4,352]{0,3,2,1:T(8,128)(2,1)} %bitcast.43) | data formatting | bytes 23068672 | tf_op jit(solution)/shard_map/reshape | solution.py:729
  66.8 12.2 %pad_maximum_fusion.1.w2_ref = bf16[12,352,2048]{2,1,0:T(8,128)(2,1)} fusion(bf16[4,352,2048]{2,1,0:T(8,128)(2,1)S(1)} %bitcast.51, bf16[8,352,2048]{2,1,0:T(8,128)(2,1)} %param.25), kind=kLoop, calls=%fused_computation.1 | loop fusion | flops 8650752 | bytes 34603008 | tf_op jit(solution)/shard_map/concatenate | solution.py:732
  79.0 24.2 %pad_maximum_fusion.w1_ref = bf16[12,2,352,2048]{3,2,1,0:T(8,128)(2,1)} fusion(bf16[4,2,352,2048]{3,2,1,0:T(8,128)(2,1)} %bitcast.44, bf16[8,2,352,2048]{3,2,1,0:T(8,128)(2,1)} %bitcast.45), kind=kLoop, calls=%fused_computation | loop fusion | flops 17301504 | bytes 69206016 | tf_op jit(solution)/shard_map/concatenate | solution.py:726
  103.2 3.1 all-gather.11.cloned.1.call-done
  106.3 8.4 %all-reduce.6.cloned.1.call-done.sum_ref = f32[256,2048]{1,0:T(8,128)} async-done(((f32[256,2048]{1,0:T(8,128)}), f32[256,2048]{1,0:T(8,128)}) %all-reduce.6.cloned.1.call-update) | async-done | bytes 2097168 | tf_op jit(solution)/shard_map/psum | solution.py:725
  114.8 4.7 %second_norm.1 = (f32[256,2048]{1,0:T(8,128)}, bf16[256,2048]{1,0:T(8,128)(2,1)}, f32[256,2048]{1,0:T(8,128)}) custom-call(bf16[256,2048]{1,0:T(8,128)(2,1)} %x_ref.5, f32[256,2048]{1,0:T(8,128)} %all-reduce.6.cloned.1.call-done.sum_ref, f32[1,2048]{1,0:T(1,128)} %bitcast.56), custom_call_target="tpu_custom_call" | custom-call | tf_op jit(solution)/shard_map/second_norm/pallas_call | solution.py:145
  120.8 40.9 %own_mlp.1 = (f32[256,2048]{1,0:T(8,128)}, f32[256,2048]{1,0:T(8,128)}, f32[1,256]{1,0:T(1,128)}) custom-call(bf16[256,2048]{1,0:T(8,128)(2,1)} %get-tuple-element.118.tok_ref, bf16[256,2048]{1,0:T(8,128)(2,1)} %cot_ref.3, f32[8,1,256]{2,1,0:T(1,128)} %broadcast_in_dim.45.route_ref, bf16[16,2048]{1,0:T(8,128)(2,1)} %broadcast_in_dim.46.gate_ref, ...), custom_call_target="tpu_custom_call" | custom-call | flops 1048576 | bytes 65536 | tf_op jit(solution)/shard_map/own_mlp/pallas_call | solution.py:338
  167.0 11.3 %split_rounded.1 = (bf16[2048,2048]{1,0:T(8,128)(2,1)}, f32[8,8,256]{2,1,0:T(8,128)}) custom-call(f32[8,264,2048]{2,1,0:T(8,128)} %bitcast.46), custom_call_target="tpu_custom_call" | custom-call | tf_op jit(solution)/shard_map/split_rounded/pallas_call | solution.py:650
  179.8 23.1 %chip_hidden.4 = (bf16[6,704,2048]{2,1,0:T(8,128)(2,1)}, bf16[6,352,2048]{2,1,0:T(8,128)(2,1)}, bf16[2048,512]{1,0:T(8,128)(2,1)}) custom-call(s32[5]{0:T(128)} %stack.76.at_ref, f32[256,2048]{1,0:T(8,128)} %get-tuple-element.116.even_ref, f32[256,2048]{1,0:T(8,128)} %collective-permute-done.odd_ref, bf16[2048,2048]{1,0:T(8,128)(2,1)} %get-tuple-element.123.cot_ref, ...), custom_call_target="tpu_custom_call" | custom-call | flops 1048576 | bytes 65536 | tf_op jit(solution)/shard_map/chip_hidden/pallas_call | solution.py:414
  202.8 5.8 %all-gather.13.cloned.1.call-done = f32[2048,2048]{1,0:T(8,128)} async-done(((f32[256,2048]{1,0:T(8,128)}), f32[2048,2048]{1,0:T(8,128)}) %all-gather.13.cloned.1.call-update) | async-done | bytes 16777232 | tf_op jit(solution)/shard_map/all_gather | solution.py:739
  208.6 23.2 %chip_hidden.5 = (bf16[6,704,2048]{2,1,0:T(8,128)(2,1)}, bf16[6,352,2048]{2,1,0:T(8,128)(2,1)}, bf16[2048,512]{1,0:T(8,128)(2,1)}) custom-call(s32[5]{0:T(128)} %stack.72.at_ref, f32[8,256,2048]{2,1,0:T(8,128)} %bitcast.37, f32[8,256,2048]{2,1,0:T(8,128)} %bitcast.38, ...), custom_call_target="tpu_custom_call", output_to_operand_aliasing={{0}: (8, {}), {1}: (9, {}), {2}: (10, {})} | custom-call | flops 1048576 | bytes 65536 | tf_op jit(solution)/shard_map/chip_hidden/pallas_call | solution.py:414
  231.8 23.1 %chip_hidden.6 = (bf16[6,704,2048]{2,1,0:T(8,128)(2,1)}, bf16[6,352,2048]{2,1,0:T(8,128)(2,1)}, bf16[2048,512]{1,0:T(8,128)(2,1)}) custom-call(s32[5]{0:T(128)} %stack.70.at_ref, f32[8,256,2048]{2,1,0:T(8,128)} %bitcast.39, f32[8,256,2048]{2,1,0:T(8,128)} %bitcast.40, ...), custom_call_target="tpu_custom_call", output_to_operand_aliasing={{0}: (8, {}), {1}: (9, {}), {2}: (10, {})} | custom-call | flops 1048576 | bytes 65536 | tf_op jit(solution)/shard_map/chip_hidden/pallas_call | solution.py:414
  254.9 15.4 %attention_back.1 = (f32[4,72,2048]{2,1,0:T(8,128)}, f32[256,2048]{1,0:T(8,128)}, bf16[2,256,1024]{2,1,0:T(8,128)(2,1)}, bf16[256,1536]{1,0:T(8,128)(2,1)}, f32[1,1536]{1,0:T(1,128)}, /*index=5*/f32[1,2048]{1,0:T(1,128)}) custom-call(f32[256,2048]{1,0:T(8,128)} %all-reduce.8.cloned.1.call-done.total_ref, f32[256,2048]{1,0:T(8,128)} %get-tuple-element.138.residual_ref, ...), custom_call_target="tpu_custom_call" | custom-call | flops 1048576 | bytes 65536 | tf_op jit(solution)/shard_map/attention_back/pallas_call | solution.py:235
  271.0 8.2 %token_products.2 = (f32[256,2048]{1,0:T(8,128)}, f32[256,2048]{1,0:T(8,128)}, f32[256,2048]{1,0:T(8,128)}, f32[256,2048]{1,0:T(8,128)}) custom-call(s32[4]{0:T(128)} %add_add_fusion.1.at_ref, bf16[2,256,1024]{2,1,0:T(8,128)(2,1)} %get-tuple-element.125.normed_ref, bf16[256,1536]{1,0:T(8,128)(2,1)} %get-tuple-element.141.projected_ref, ...), custom_call_target="tpu_custom_call" | custom-call | flops 1048576 | bytes 65536 | tf_op jit(solution)/shard_map/token_products/pallas_call | solution.py:498
  280.9 3.2 collective-permute-done.1.refs_0_
  284.0 2.7 collective-permute-done.2.refs_1_
  286.7 3.0 collective-permute-done.3.refs_2_
  289.7 3.0 collective-permute-done.4.refs_3_
  292.7 11.3 %token_products.3 = (f32[2,256,1024]{2,1,0:T(8,128)}, f32[2,256,1024]{2,1,0:T(8,128)}, f32[2,256,1024]{2,1,0:T(8,128)}, f32[2,256,1024]{2,1,0:T(8,128)}) custom-call(s32[4]{0:T(128)} %add_add_fusion.at_ref, bf16[2,256,1024]{2,1,0:T(8,128)(2,1)} %get-tuple-element.125.normed_ref, bf16[256,1536]{1,0:T(8,128)(2,1)} %get-tuple-element.141.projected_ref, ...), custom_call_target="tpu_custom_call" | custom-call | flops 1048576 | bytes 65536 | tf_op jit(solution)/shard_map/token_products/pallas_call | solution.py:498
  306.9 23.5 %chip_hidden.7 = (bf16[6,704,2048]{2,1,0:T(8,128)(2,1)}, bf16[6,352,2048]{2,1,0:T(8,128)(2,1)}, bf16[2048,512]{1,0:T(8,128)(2,1)}) custom-call(s32[5]{0:T(128)} %stack.65.at_ref, f32[8,256,2048]{2,1,0:T(8,128)} %bitcast.41, f32[8,256,2048]{2,1,0:T(8,128)} %bitcast.42, ...), custom_call_target="tpu_custom_call", output_to_operand_aliasing={{0}: (8, {}), {1}: (9, {}), {2}: (10, {})} | custom-call | flops 1048576 | bytes 65536 | tf_op jit(solution)/shard_map/chip_hidden/pallas_call | solution.py:414
  330.4 10.6 %reduce-scatter.5.cloned.1.call-done = f32[72,2048]{1,0:T(8,128)} async-done(((f32[288,2048]{1,0:T(8,128)}), f32[72,2048]{1,0:T(8,128)}) %reduce-scatter.5.cloned.1.call-update) | async-done | bytes 589840 | tf_op jit(solution)/shard_map/reduce_scatter | solution.py:768
  344.3 22.2 %weight_grads.1 = (f32[8,2,352,256]{3,2,1,0:T(8,128)}, f32[8,352,256]{2,1,0:T(8,128)}, f32[4,2,352,256]{3,2,1,0:T(8,128)}, f32[4,352,256]{2,1,0:T(8,128)}, f32[6...) custom-call(s32[4]{0:T(128)} %add_add_fusion.at_ref, bf16[6,704,2048]{2,1,0:T(8,128)(2,1)} %get-tuple-element.168.mix_grad_ref, ...), custom_call_target="tpu_custom_call" | custom-call | flops 1048576 | bytes 65536 | tf_op jit(solution)/shard_map/weight_grads/pallas_call | solution.py:576
  367.9 6.5 %turned_blocks.1 = (f32[256,1024]{1,0:T(8,128)}, f32[256,1024]{1,0:T(8,128)}, f32[256,1024]{1,0:T(8,128)}, f32[256,1024]{1,0:T(8,128)}) custom-call(s32[4]{0:T(128)} %add_add_fusion.at_ref, f32[2,256,1024]{2,1,0:T(8,128)} %get-tuple-element.167.x_keep_ref, f32[2,256,1024]{2,1,0:T(8,128)} %copy-done.5, f32[2,256,1024]{2,1,0:T(8,128)} %get-tuple-element.175.y_keep_ref, ...), custom_call_target="tpu_custom_call" | custom-call | flops 1048576 | bytes 65536 | tf_op jit(solution)/shard_map/turned_blocks/pallas_call | solution.py:526
  377.9 6.8 %collective-permute-done.10.two_ref = f32[6,352,256]{2,1,0:T(8,128)S(1)} collective-permute-done((f32[6,352,256]{2,1,0:T(8,128)}, f32[6,352,256]{2,1,0:T(8,128)S(1)}, u32[]{:S(2)}, u32[]{:S(2)}) %collective-permute-start.10) | collective-permute-done | bytes 2162720 | tf_op jit(solution)/shard_map/ppermute | solution.py:737
  386.1 7.8 %place_peer.1 = (f32[8,2,352,256]{3,2,1,0:T(8,128)}, f32[8,352,256]{2,1,0:T(8,128)}, f32[4,2,352,256]{3,2,1,0:T(8,128)}, f32[4,352,256]{2,1,0:T(8,128)}) custom-call(s32[4]{0:T(128)} %add_add_fusion.at_ref, f32[6,2,352,256]{3,2,1,0:T(8,128)} %collective-permute-done.9.one_ref, ...), custom_call_target="tpu_custom_call", output_to_operand_aliasing={{0}: (3, {}), {1}: (4, {}), {2}: (5, {}), {3}: (6, {})} | custom-call | flops 1048576 | bytes 65536 | tf_op jit(solution)/shard_map/place_peer/pallas_call | solution.py:619
  396.7 6.3 %collective-permute-done.12 = f32[8,2048]{1,0:T(8,128)S(1)} collective-permute-done((f32[8,2048]{1,0:T(8,128)S(1)}, f32[8,2048]{1,0:T(8,128)S(1)}, u32[]{:S(2)}, u32[]{:S(2)}) %collective-permute-start.12) | collective-permute-done | bytes 65568 | tf_op jit(solution)/shard_map/ppermute | solution.py:670
  405.7 3.4 copy.58
  415.6 2.8 add_convert_fusion.1
  418.5 15.4 %all-gather.7.cloned.1.call-done = f32[256,2048]{1,0:T(8,128)} async-done(((f32[64,2048]{1,0:T(8,128)}), f32[256,2048]{1,0:T(8,128)}) %all-gather.7.cloned.1.call-update) | async-done | bytes 2097168 | tf_op jit(solution)/shard_map/all_gather | solution.py:792
  434.5 3.5 add_convert_fusion
  (126 shorter events, 41.8 us)
Async XLA Ops:
  8.0 98.3 %all-gather.11.cloned.1.call-start = ((), (), s32[]{:S(2)}) async-start(), calls=%async_computation.8 | async-start | bytes 19464192 | tf_op jit(solution)/shard_map/all_gather | solution.py:709
  11.1 103.6 %all-reduce.6.cloned.1.call-start = ((), (), s32[]{:S(2)}) async-start(), calls=%async_computation.2 | async-start | bytes 4194304 | tf_op jit(solution)/shard_map/psum | solution.py:725
  14.6 11.4 %copy-start.13 = (bf16[2048]{0:T(1024)(128)(2,1)S(1)}, bf16[2048]{0:T(1024)(128)(2,1)}, u32[]{:S(2)}) copy-start(bf16[2048]{0:T(1024)(128)(2,1)} %param.23) | copy-start | bytes 12292
  26.0 182.6 %all-gather.13.cloned.1.call-start = ((), (), s32[]{:S(2)}) async-start(), calls=%async_computation.9 | async-start | bytes 18874368 | tf_op jit(solution)/shard_map/all_gather | solution.py:739
  26.6 40.2 %slice-start = ((s8[5767168]{0:T(1024)(128)(4,1)}), s8[1572864]{0:T(1024)(128)(4,1)S(1)}, s32[]{:S(2)}) async-start(s8[5767168]{0:T(1024)(128)(4,1)} %bitcast.49), calls=%async_computation.10 | async-start | bytes 3145728
  55.5 11.2 %slice-start.1 = ((s8[5767168]{0:T(1024)(128)(4,1)}), s8[4194304]{0:T(1024)(128)(4,1)S(1)}, s32[]{:S(2)}) async-start(s8[5767168]{0:T(1024)(128)(4,1)} %bitcast.49), calls=%async_computation.11 | async-start | bytes 8388608
  119.5 135.4 %all-reduce.8.cloned.1.call-start = ((), (), s32[]{:S(2)}) async-start(), calls=%async_computation.3 | async-start | bytes 4194304 | tf_op jit(solution)/shard_map/psum | solution.py:749
  161.7 142.3 %reduce-scatter.3.cloned.1.call-start = ((), (), s32[]{:S(2)}) async-start(), calls=%async_computation.4 | async-start | bytes 2621440 | tf_op jit(solution)/shard_map/reduce_scatter | solution.py:761
  162.3 178.7 %reduce-scatter.5.cloned.1.call-start = ((), (), s32[]{:S(2)}) async-start(), calls=%async_computation.5 | async-start | bytes 2949120 | tf_op jit(solution)/shard_map/reduce_scatter | solution.py:768
  163.9 15.8 %collective-permute-start = (f32[256,2048]{1,0:T(8,128)S(1)}, f32[256,2048]{1,0:T(8,128)}, u32[]{:S(2)}, u32[]{:S(2)}) collective-permute-start(f32[256,2048]{1,0:T(8,128)S(1)} %copy-done.2), channel_id=1, source_target_pairs={{0,4},{4,0},{8,12},{12,8},{16,20},{20,16},{24,28},{28,24},{1,5},{5... | collective-permute-start | bytes 6291464 | tf_op jit(solution)/shard_map/ppermute | solution.py:737
  167.0 11.9 %copy-start.3 = (bf16[256,2048]{1,0:T(8,128)(2,1)S(1)}, bf16[256,2048]{1,0:T(8,128)(2,1)}, u32[]{:S(2)}) copy-start(bf16[256,2048]{1,0:T(8,128)(2,1)} %get-tuple-element.118.tok_ref) | copy-start | bytes 3145732
  270.4 144.4 %all-gather.9.cloned.1.call-start = ((), (), s32[]{:S(2)}) async-start(), calls=%async_computation.7 | async-start | bytes 2621440 | tf_op jit(solution)/shard_map/all_gather | solution.py:791
  279.2 4.8 %collective-permute-start.1 = (f32[256,2048]{1,0:T(8,128)}, f32[256,2048]{1,0:T(8,128)S(1)}, u32[]{:S(2)}, u32[]{:S(2)}) collective-permute-start(f32[256,2048]{1,0:T(8,128)} %get-tuple-element.144), channel_id=1, source_target_pairs={{0,4},{4,0},{8,12},{12,8},{16,20},{20,16},{24,28},{28,24},{1,5},{5... | collective-permute-start | bytes 6291464 | tf_op jit(solution)/shard_map/ppermute | solution.py:737
  279.5 7.2 %collective-permute-start.2 = (f32[256,2048]{1,0:T(8,128)}, f32[256,2048]{1,0:T(8,128)}, u32[]{:S(2)}, u32[]{:S(2)}) collective-permute-start(f32[256,2048]{1,0:T(8,128)} %get-tuple-element.145), channel_id=1, source_target_pairs={{0,4},{4,0},{8,12},{12,8},{16,20},{20,16},{24,28},{28,24},{1,5},{5... | collective-permute-start | bytes 6291464 | tf_op jit(solution)/shard_map/ppermute | solution.py:737
  279.7 10.0 %collective-permute-start.3 = (f32[256,2048]{1,0:T(8,128)}, f32[256,2048]{1,0:T(8,128)}, u32[]{:S(2)}, u32[]{:S(2)}) collective-permute-start(f32[256,2048]{1,0:T(8,128)} %get-tuple-element.146), channel_id=1, source_target_pairs={{0,4},{4,0},{8,12},{12,8},{16,20},{20,16},{24,28},{28,24},{1,5},{5... | collective-permute-start | bytes 6291464 | tf_op jit(solution)/shard_map/ppermute | solution.py:737
  280.0 12.7 %collective-permute-start.4 = (f32[256,2048]{1,0:T(8,128)}, f32[256,2048]{1,0:T(8,128)}, u32[]{:S(2)}, u32[]{:S(2)}) collective-permute-start(f32[256,2048]{1,0:T(8,128)} %get-tuple-element.147), channel_id=1, source_target_pairs={{0,4},{4,0},{8,12},{12,8},{16,20},{20,16},{24,28},{28,24},{1,5},{5... | collective-permute-start | bytes 6291464 | tf_op jit(solution)/shard_map/ppermute | solution.py:737
  284.0 8.7 %copy-start.6 = (f32[256,2048]{1,0:T(8,128)}, f32[256,2048]{1,0:T(8,128)S(1)}, u32[]{:S(2)}) copy-start(f32[256,2048]{1,0:T(8,128)S(1)} %collective-permute-done.1.refs_0_) | copy-start | bytes 6291460
  304.0 62.6 %collective-permute-start.5 = (f32[2,256,1024]{2,1,0:T(8,128)}, f32[2,256,1024]{2,1,0:T(8,128)S(1)}, u32[]{:S(2)}, u32[]{:S(2)}) collective-permute-start(f32[2,256,1024]{2,1,0:T(8,128)} %get-tuple-element.172), channel_id=1, source_target_pairs={{0,8},{4,12},{8,0},{12,4},{16,24},{20,28},{24,16},{28,20},{1,9},{5... | collective-permute-start | bytes 6291464 | tf_op jit(solution)/shard_map/ppermute | solution.py:670
  305.5 61.1 %collective-permute-start.6 = (f32[2,256,1024]{2,1,0:T(8,128)}, f32[2,256,1024]{2,1,0:T(8,128)}, u32[]{:S(2)}, u32[]{:S(2)}) collective-permute-start(f32[2,256,1024]{2,1,0:T(8,128)} %get-tuple-element.173), channel_id=1, source_target_pairs={{0,16},{4,20},{8,24},{12,28},{16,0},{20,4},{24,8},{28,12},{1,17},{... | collective-permute-start | bytes 6291464 | tf_op jit(solution)/shard_map/ppermute | solution.py:670
  306.8 34.2 %copy-start = (bf16[256,2048]{1,0:T(8,128)(2,1)S(1)}, bf16[256,2048]{1,0:T(8,128)(2,1)}, u32[]{:S(2)}) copy-start(bf16[256,2048]{1,0:T(8,128)(2,1)} %x_ref.5) | copy-start | bytes 3145732
  306.8 34.2 %copy-start.8 = (f32[2048]{0:T(1024)S(1)}, f32[2048]{0:T(1024)}, u32[]{:S(2)}) copy-start(f32[2048]{0:T(1024)} %convert_element_type.37) | copy-start | bytes 24580
  306.8 127.0 %all-gather.7.cloned.1.call-start = ((), (), s32[]{:S(2)}) async-start(), calls=%async_computation.6 | async-start | bytes 2621440 | tf_op jit(solution)/shard_map/all_gather | solution.py:792
  367.9 10.0 %slice-start.2 = ((f32[72,2048]{1,0:T(8,128)}), f32[2,2048]{1,0:T(2,128)S(1)}, s32[]{:S(2)}) async-start(f32[72,2048]{1,0:T(8,128)} %reduce-scatter.5.cloned.1.call-done), calls=%async_computation.12 | async-start | bytes 32768 | tf_op jit(solution)/shard_map/slice | solution.py:775
  367.9 10.0 %copy-start.10 = (f32[1,2048]{1,0:T(1,128)S(1)}, f32[1,2048]{1,0:T(1,128)}, u32[]{:S(2)}) copy-start(f32[1,2048]{1,0:T(1,128)} %get-tuple-element.191) | copy-start | bytes 24580
  367.9 10.0 %copy-start.11 = (f32[1,1536]{1,0:T(1,128)S(1)}, f32[1,1536]{1,0:T(1,128)}, u32[]{:S(2)}) copy-start(f32[1,1536]{1,0:T(1,128)} %get-tuple-element.192) | copy-start | bytes 18436
  374.4 10.8 %collective-permute-start.9 = (f32[6,2,352,256]{3,2,1,0:T(8,128)}, f32[6,2,352,256]{3,2,1,0:T(8,128)}, u32[]{:S(2)}, u32[]{:S(2)}) collective-permute-start(f32[6,2,352,256]{3,2,1,0:T(8,128)} %get-tuple-element.184), channel_id=1, source_target_pairs={{0,4},{4,0},{8,12},{12,8},{16,20},{20,16},{24,28},{28,24},{1,5},{5... | collective-permute-start | bytes 12976136 | tf_op jit(solution)/shard_map/ppermute | solution.py:737
  374.4 10.3 %collective-permute-start.10 = (f32[6,352,256]{2,1,0:T(8,128)}, f32[6,352,256]{2,1,0:T(8,128)S(1)}, u32[]{:S(2)}, u32[]{:S(2)}) collective-permute-start(f32[6,352,256]{2,1,0:T(8,128)} %get-tuple-element.185), channel_id=1, source_target_pairs={{0,4},{4,0},{8,12},{12,8},{16,20},{20,16},{24,28},{28,24},{1,5},{5... | collective-permute-start | bytes 6488072 | tf_op jit(solution)/shard_map/ppermute | solution.py:737
  375.0 34.2 %collective-permute-start.7 = (f32[256,1024]{1,0:T(8,128)}, f32[256,1024]{1,0:T(8,128)}, u32[]{:S(2)}, u32[]{:S(2)}) collective-permute-start(f32[256,1024]{1,0:T(8,128)} %get-tuple-element.182), channel_id=1, source_target_pairs={{0,16},{4,20},{8,24},{12,28},{16,0},{20,4},{24,8},{28,12},{1,17},{... | collective-permute-start | bytes 3145736 | tf_op jit(solution)/shard_map/ppermute | solution.py:670
  376.5 32.7 %collective-permute-start.8 = (f32[256,1024]{1,0:T(8,128)}, f32[256,1024]{1,0:T(8,128)}, u32[]{:S(2)}, u32[]{:S(2)}) collective-permute-start(f32[256,1024]{1,0:T(8,128)} %get-tuple-element.183), channel_id=1, source_target_pairs={{0,8},{4,12},{8,0},{12,4},{16,24},{20,28},{24,16},{28,20},{1,9},{5... | collective-permute-start | bytes 3145736 | tf_op jit(solution)/shard_map/ppermute | solution.py:670
  393.8 1.3 collective-permute-start.11
  395.1 7.8 %collective-permute-start.12 = (f32[8,2048]{1,0:T(8,128)S(1)}, f32[8,2048]{1,0:T(8,128)S(1)}, u32[]{:S(2)}, u32[]{:S(2)}) collective-permute-start(f32[8,2048]{1,0:T(8,128)S(1)} %add.85), channel_id=1, source_target_pairs={{0,8},{4,12},{8,0},{12,4},{16,24},{20,28},{24,16},{28,20},{1,9},{5... | collective-permute-start | bytes 196616 | tf_op jit(solution)/shard_map/ppermute | solution.py:670
  403.0 6.2 %collective-permute-start.13 = (f32[8,2048]{1,0:T(8,128)S(1)}, f32[8,2048]{1,0:T(8,128)S(1)}, u32[]{:S(2)}, u32[]{:S(2)}) collective-permute-start(f32[8,2048]{1,0:T(8,128)S(1)} %add.86), channel_id=1, source_target_pairs={{0,16},{4,20},{8,24},{12,28},{16,0},{20,4},{24,8},{28,12},{1,17},{... | collective-permute-start | bytes 196616 | tf_op jit(solution)/shard_map/ppermute | solution.py:670
  (12 other events, 27.0 us)
Sparse Core Ops, SparseCore 0:
  11.5 94.8 all-gather.10
  119.7 88.8 all-gather.12
Sparse Core Ops, SparseCore 1:
  26.0 88.7 all-reduce.5
  161.8 83.8 all-reduce.7
  248.4 42.5 reduce-scatter.2
  294.0 46.9 reduce-scatter.4
  342.7 45.1 all-gather.8
  389.4 44.3 all-gather.6
